TPU v7x, 32 devices: a whole 2x2x4 slice. The times are simulated.
32 devices in a mesh: expert: 8 (over z, x), tensor: 4 (over y, core).
Axes of the slice: x: 2, y: 2, z: 4, core: 2. Of those that a mesh axis runs over, the one named last changes fastest.
Arguments:
- tokens: bfloat16 [1024, 3584], P('expert', 'tensor'), may hold values from -6 to 6
- routes: int32 [1024, 2], P('expert'), may hold values from 0 to 7, all different within a row; in each aligned block of 128 rows (0 to 127, 128 to 255, ...) at most 40 rows name the same one
- gate_values: float32 [1024, 2], P('expert'), may hold values from 0.05 to 0.5
- probe_rows: bfloat16 [128, 3584], P(None, 'tensor'), may hold values from -6 to 6
- gate_weight: bfloat16 [8, 3584, 2048], P('expert', None, 'tensor'), may hold values from -0.09375 to 0.09375
- up_weight: bfloat16 [8, 3584, 2048], P('expert', None, 'tensor'), may hold values from -0.09375 to 0.09375
- down_weight: bfloat16 [8, 2048, 3584], P('expert', 'tensor'), may hold values from -0.125 to 0.125
- hidden_perm: int32 [8, 2048], P('expert', 'tensor'), may hold values from 0 to 2047, each once within a row
- cluster: int32 [8], replicated, may hold values from 0 to 1, as said below
- owners: int32 [2], replicated, may hold values from 0 to 7, as said below
Outputs:
- mixed: bfloat16 [1024, 3584], P('expert', 'tensor')
- correlation: float32 [8, 2048, 2048], P('expert', 'tensor')
- merged_down: bfloat16 [8, 2048, 3584], P('expert', 'tensor')
Inputs may be any that keep to these rules, and one draw needn't show every extreme that they name: `routes`: each row names 2 different experts. Within the rows of one index of the expert axis no expert is named more than 40 times, and in some such block one expert is named exactly 40 times. `hidden_perm`: each row is a permutation of the 2048 hidden units. Every cluster has at least one expert. owners[c] is an expert of cluster c; the owners are distinct.
All inputs are finite; a program needn't handle non-finite values.
Results may differ from a plain program's by a relative error of at most 0.012.
Values may be sent and summed in bfloat16 or wider, within the bound.
No kernel may reach another device: no remote copies, remote signals or barrier semaphores. Data moves between devices by JAX's collectives and lax.ppermute only.
A program may use at most 128 MiB of HBM per device.

v0:
```python
import jax
import jax.numpy as jnp
from jax import lax
from jax.sharding import PartitionSpec as P


def on_device(
    tokens,
    routes,
    gate_values,
    probe_rows,
    gate_weight,
    up_weight,
    down_weight,
    hidden_perm,
    cluster,
    owners,
):
    expert_count = lax.axis_size("expert")
    tok_rows = routes.shape[0]
    route_width = routes.shape[1]
    capacity = tok_rows * route_width * 5 // (4 * expert_count)
    my_index = lax.axis_index("expert")
    flat_routes = routes.reshape(-1)
    matches = (flat_routes[:, None] == jnp.arange(expert_count, dtype=jnp.int32)[None, :]).astype(
        jnp.int32
    )
    slot_rank = jnp.sum((jnp.cumsum(matches, axis=0) - matches) * matches, axis=1)
    target = flat_routes * capacity + slot_rank
    selector = jnp.arange(expert_count * capacity, dtype=jnp.int32)[:, None] == target[None, :]
    selector = jnp.any(
        selector.reshape(expert_count * capacity, tok_rows, route_width), axis=2
    ).astype(jnp.bfloat16)
    full_tokens, probe_full = (
        lax.all_gather(tokens, "tensor", axis=1, tiled=True),
        lax.all_gather(probe_rows, "tensor", axis=1, tiled=True),
    )
    outgoing = jnp.dot(selector, full_tokens, preferred_element_type=jnp.float32).astype(
        jnp.bfloat16
    )
    expert_rows = lax.all_to_all(outgoing, "expert", split_axis=0, concat_axis=0, tiled=True)
    routed = expert_rows.shape[0]
    stacked = jnp.concatenate([expert_rows, probe_full], axis=0)
    gate_pre = jnp.dot(stacked, gate_weight[0], preferred_element_type=jnp.float32)
    up_pre = jnp.dot(stacked, up_weight[0], preferred_element_type=jnp.float32)
    hidden = (jax.nn.silu(gate_pre) * up_pre).astype(jnp.bfloat16)
    probe_hidden = hidden[routed:]
    partial_sum = jnp.dot(
        hidden[:routed], down_weight[0], preferred_element_type=jnp.float32
    ).astype(jnp.bfloat16)
    returned = (
        lax.psum_scatter(partial_sum, "tensor", scatter_dimension=1, tiled=True)
        .astype(jnp.float32)
        .astype(jnp.bfloat16)
    )
    arrived_home = lax.all_to_all(returned, "expert", split_axis=0, concat_axis=0, tiled=True)
    picked = arrived_home[target].reshape(tok_rows, route_width, arrived_home.shape[1])
    mixed = jnp.sum(gate_values[:, :, None] * picked.astype(jnp.float32), axis=1).astype(
        jnp.bfloat16
    )
    owner_of = owners[cluster]
    my_owner = owner_of[my_index]
    part_rows = lax.all_gather(probe_hidden[None], "expert", axis=0, tiled=True)
    positions = jnp.arange(part_rows.shape[0], dtype=jnp.int32)
    chosen_rows = jnp.where(
        (positions == my_owner)[:, None, None], part_rows.astype(jnp.float32), 0.0
    )
    partner = jnp.sum(chosen_rows, axis=0).astype(jnp.bfloat16)
    partner_full = lax.all_gather(partner, "tensor", axis=1, tiled=True)
    correlation = (
        lax.dot_general(
            probe_hidden, partner_full, (((0,), (0,)), ((), ())), preferred_element_type=jnp.float32
        )
        / probe_hidden.shape[0]
    )
    local_perm = hidden_perm[0]
    own_rows = down_weight[0]
    part_rows = lax.all_gather(own_rows, "tensor", axis=0, tiled=True)
    positions = jnp.arange(part_rows.shape[0], dtype=jnp.int32)
    one_hot = (local_perm[:, None] == positions[None, :]).astype(jnp.bfloat16)
    aligned = jnp.dot(one_hot, part_rows, preferred_element_type=jnp.float32).astype(jnp.bfloat16)
    same_owner = (owner_of[None, :] == jnp.arange(expert_count, dtype=jnp.int32)[:, None]).astype(
        jnp.bfloat16
    )
    size_of = jnp.sum((cluster[:, None] == cluster[None, :]).astype(jnp.float32), axis=1)
    inverse_size = 1.0 / size_of
    cluster_total = jnp.einsum(
        "oj,jrd->ord",
        same_owner,
        lax.all_to_all(aligned[None], "expert", split_axis=1, concat_axis=0, tiled=True),
        preferred_element_type=jnp.float32,
    )
    cluster_mean = (cluster_total * inverse_size[:, None, None]).astype(jnp.bfloat16)
    merged_down = lax.all_to_all(cluster_mean, "expert", split_axis=0, concat_axis=1, tiled=True)
    return (mixed, correlation[None], merged_down)


def solution(mesh):
    in_specs = (
        P("expert", "tensor"),
        P("expert", None),
        P("expert", None),
        P(None, "tensor"),
        P("expert", None, "tensor"),
        P("expert", None, "tensor"),
        P("expert", "tensor", None),
        P("expert", "tensor"),
        P(),
        P(),
    )
    out_specs = (P("expert", "tensor"), P("expert", "tensor", None), P("expert", "tensor", None))
    return jax.shard_map(
        on_device, mesh=mesh, in_specs=in_specs, out_specs=out_specs, check_vma=False
    )
```

profile of v0, /device:TPU:0, one launch (start us, length us, event | category | flops | bytes accessed | tf_op | source)
XLA Modules:
  0.0 431.3 jit_solution(11271069982288683491)
XLA Ops:
  8.0 0.0 copy-start
  8.0 0.0 copy-start.4
  8.0 0.0 copy-start.2
  8.0 0.0 all-gather.7.cloned.1.call-start
  8.1 0.7 all-gather.7.cloned.1.call-update
  8.8 0.1 copy.36
  8.9 0.1 eq.95
  9.0 0.1 eq.91
  9.2 0.6 reduce-window.6
  9.8 0.2 slice_reduce_fusion
  10.0 0.1 fusion.25
  10.1 0.1 reduce_sum.41
  10.3 0.1 copy.39
  10.4 0.1 fusion.23
  10.4 10.8 %all_gather.15 = bf16[128,3584]{1,0:T(8,128)(2,1)S(1)} all-gather(bf16[128,896]{1,0:T(8,128)(2,1)S(1)} %copy-done.2), channel_id=1, replica_groups=mesh['expert'=8,'tensor'=4] {'tensor'}, dimensions={1}, use_global_device_ids=true | all-gather | bytes 1146880 | tf_op jit(solution)/shard_map/all_gather | solution.py:35
  21.2 2.1 convolution_convert_fusion.1
  23.3 5.8 %all-to-all-start = ((bf16[8,40,3584]{2,1,0:T(8,128)(2,1)}), bf16[8,40,3584]{2,1,0:T(8,128)(2,1)S(1)}, u32[]{:S(2)}, u32[]{:S(2)}) async-start(bf16[8,40,3584]{2,1,0:T(8,128)(2,1)} %bitcast.2), calls=%async_computation | async-start | bytes 4587520 | tf_op jit(solution)/shard_map/all_to_all | solution.py:41
  29.1 78.1 %all-gather.7.cloned.1.call-done = bf16[1,2048,3584]{2,1,0:T(8,128)(2,1)} async-done(((bf16[1,512,3584]{2,1,0:T(8,128)(2,1)}), bf16[1,2048,3584]{2,1,0:T(8,128)(2,1)}) %all-gather.7.cloned.1.call-update) | async-done | bytes 14680080 | tf_op jit(solution)/shard_map/all_gather | solution.py:78
  107.2 0.0 copy-done.7
  107.2 11.3 %fusion.5 = bf16[1,512,3584]{2,1,0:T(8,128)(2,1)S(1)} fusion(bf16[1,2048,3584]{2,1,0:T(8,128)(2,1)} %all-gather.7.cloned.1.call-done, s32[512]{0:T(512)S(1)} %bitcast.67), kind=kOutput, calls=%fused_computation.6 | convolution fusion | flops 7519076352 | bytes 18352128 | tf_op jit(solution)/shard_map/dot_general | solution.py:81
  118.5 40.8 %copy.49 = bf16[1,512,3584]{2,0,1:T(2,128)(2,1)} copy(bf16[1,512,3584]{2,1,0:T(8,128)(2,1)S(1)} %fusion.5) | data formatting | bytes 7340032 | tf_op jit(solution)/shard_map/broadcast_in_dim | solution.py:90
  159.3 0.5 broadcast.89
  159.9 25.3 %reduce.2 = bf16[512,3584]{1,0:T(8,128)(2,1)} reduce(bf16[512,1,3584]{2,1,0:T(2,128)(2,1)} %bitcast.57, bf16[]{:T(256)} %broadcast.89), dimensions={1}, to_apply=%bitcast.55.reduce_sub_computation | reduce | bytes 7340034
  185.2 7.4 %reshape.120 = bf16[8,2,114688]{2,1,0:T(2,128)(2,1)} reshape(bf16[512,3584]{1,0:T(8,128)(2,1)} %reduce.2) | data formatting | bytes 7340032
  192.6 0.0 all-to-all-done
  192.6 5.6 %all-to-all-start.2 = ((bf16[8,2,114688]{2,1,0:T(2,128)(2,1)}), bf16[8,2,114688]{2,1,0:T(2,128)(2,1)}, u32[]{:S(2)}, u32[]{:S(2)}) async-start(bf16[8,2,114688]{2,1,0:T(2,128)(2,1)} %reshape.120), calls=%async_computation.2 | async-start | bytes 7340032 | tf_op jit(solution)/shard_map/all_to_all | solution.py:90
  198.2 0.0 reduce-scatter.4.cloned.1.call-start
  198.3 9.2 %all_gather.16 = bf16[128,3584]{1,0:T(8,128)(2,1)S(1)} all-gather(bf16[128,896]{1,0:T(8,128)(2,1)S(1)} %copy-done.3), channel_id=1, replica_groups=mesh['expert'=8,'tensor'=4] {'tensor'}, dimensions={1}, use_global_device_ids=true | all-gather | bytes 1146880 | tf_op jit(solution)/shard_map/all_gather | solution.py:36
  207.5 4.0 fusion.11
  211.6 0.0 copy-start.1
  211.6 1.9 fusion.19
  213.5 0.1 copy-done.1
  213.6 1.4 convolution_convert_fusion
  215.0 2.7 copy.43
  217.7 0.0 reduce-scatter.4.cloned.1.call-update
  217.7 36.3 %reduce-scatter.4.cloned.1.call-done = bf16[896,320]{1,0:T(8,128)(2,1)} async-done(((bf16[3584,320]{1,0:T(8,128)(2,1)}), bf16[896,320]{1,0:T(8,128)(2,1)}) %reduce-scatter.4.cloned.1.call-update) | async-done | bytes 573456
  254.0 2.2 copy.44
  256.2 24.5 %all-to-all-done.2 = bf16[8,2,114688]{2,1,0:T(2,128)(2,1)} async-done(((bf16[8,2,114688]{2,1,0:T(2,128)(2,1)}), bf16[8,2,114688]{2,1,0:T(2,128)(2,1)}, u32[]{:S(2)}, u32[]{:S(2)}) %all-to-all-start.2) | async-done | bytes 3670048 | tf_op jit(solution)/shard_map/all_to_all | solution.py:90
  280.7 3.6 all-to-all-start.1
  284.4 0.0 copy-done
  284.4 0.6 gather_fusion.1
  285.0 0.2 convert_reduce_fusion
  285.2 8.3 %reshape.121 = bf16[512,1,3584]{2,1,0:T(2,128)(2,1)} reshape(bf16[8,2,114688]{2,1,0:T(2,128)(2,1)} %all-to-all-done.2) | data formatting | bytes 7340032
  293.5 3.8 copy.45
  297.4 3.9 multiply_convert_fusion
  301.3 2.9 copy.42
  304.2 0.0 all-to-all-done.1
  304.2 6.1 %all-to-all-start.3 = ((bf16[8,64,3584]{2,1,0:T(8,128)(2,1)}), bf16[8,64,3584]{2,1,0:T(8,128)(2,1)}, u32[]{:S(2)}, u32[]{:S(2)}) async-start(bf16[8,64,3584]{2,1,0:T(8,128)(2,1)} %copy.42), calls=%async_computation.3 | async-start | bytes 7340032 | tf_op jit(solution)/shard_map/all_to_all | solution.py:94
  310.3 0.0 all-gather.5.cloned.1.call-start
  310.4 0.7 slice.22
  311.0 0.0 all-gather.5.cloned.1.call-update
  311.1 0.6 dynamic_slice.3
  311.6 0.1 mul.52
  311.8 0.1 copy.35
  311.9 0.6 iota_compare_fusion.6
  312.6 92.7 %all-gather.5.cloned.1.call-done = bf16[1024,512]{1,0:T(8,128)(2,1)} async-done(((bf16[128,512]{1,0:T(8,128)(2,1)}), bf16[1024,512]{1,0:T(8,128)(2,1)}) %all-gather.5.cloned.1.call-update) | async-done | bytes 1048592 | tf_op jit(solution)/shard_map/all_gather | solution.py:63
  405.3 1.5 fusion.14
  406.8 6.7 %all_gather.18 = bf16[128,2048]{1,0:T(8,128)(2,1)S(1)} all-gather(bf16[128,512]{1,0:T(8,128)(2,1)S(1)} %fusion.14), channel_id=1, replica_groups=mesh['expert'=8,'tensor'=4] {'tensor'}, dimensions={1}, use_global_device_ids=true | all-gather | bytes 655360 | tf_op jit(solution)/shard_map/all_gather | solution.py:69
  413.5 2.7 multiply_bitcast_fusion
  416.2 1.2 gather_fusion
  417.4 0.5 reshape.95
  417.9 1.9 multiply_reduce_fusion
  419.7 0.0 all-to-all-done.3
  419.7 4.1 copy.51
  (20 shorter events, 0.1 us)
Async XLA Ops:
  8.0 276.4 %copy-start = (s32[2]{0:T(128)S(1)}, s32[2]{0:T(128)}, u32[]{:S(2)}) copy-start(s32[2]{0:T(128)} %param.19) | copy-start | bytes 28
  8.0 0.8 copy-start.4
  8.0 2.4 copy-start.2
  8.0 99.1 %all-gather.7.cloned.1.call-start = ((), (), s32[]{:S(2)}) async-start(), calls=%async_computation.6 | async-start | bytes 18350080 | tf_op jit(solution)/shard_map/all_gather | solution.py:78
  21.2 86.0 %copy-start.7 = (s32[1,512]{1,0:T(1,128)S(1)}, s32[1,512]{1,0:T(1,128)}, u32[]{:S(2)}) copy-start(s32[1,512]{1,0:T(1,128)} %param.17) | copy-start | bytes 6148
  23.3 169.3 %all-to-all-start = ((bf16[8,40,3584]{2,1,0:T(8,128)(2,1)}), bf16[8,40,3584]{2,1,0:T(8,128)(2,1)S(1)}, u32[]{:S(2)}, u32[]{:S(2)}) async-start(bf16[8,40,3584]{2,1,0:T(8,128)(2,1)} %bitcast.2), calls=%async_computation | async-start | bytes 4587520 | tf_op jit(solution)/shard_map/all_to_all | solution.py:41
  192.6 5.7 %copy-start.3 = (bf16[128,896]{1,0:T(8,128)(2,1)S(1)}, bf16[128,896]{1,0:T(8,128)(2,1)}, u32[]{:S(2)}) copy-start(bf16[128,896]{1,0:T(8,128)(2,1)} %param.13) | copy-start | bytes 688132
  192.6 88.1 %all-to-all-start.2 = ((bf16[8,2,114688]{2,1,0:T(2,128)(2,1)}), bf16[8,2,114688]{2,1,0:T(2,128)(2,1)}, u32[]{:S(2)}, u32[]{:S(2)}) async-start(bf16[8,2,114688]{2,1,0:T(2,128)(2,1)} %reshape.120), calls=%async_computation.2 | async-start | bytes 7340032 | tf_op jit(solution)/shard_map/all_to_all | solution.py:90
  198.2 55.8 %reduce-scatter.4.cloned.1.call-start = ((), (), s32[]{:S(2)}) async-start(), calls=%async_computation.7 | async-start | bytes 3440640
  207.5 4.0 copy-start.6
  211.6 2.0 copy-start.1
  217.7 66.7 %copy-start.8 = (s32[8]{0:T(128)S(1)}, s32[8]{0:T(128)}, u32[]{:S(2)}) copy-start(s32[8]{0:T(128)} %param.18) | copy-start | bytes 100
  280.7 23.5 %all-to-all-start.1 = ((bf16[8,40,896]{2,1,0:T(8,128)(2,1)}), bf16[8,40,896]{2,1,0:T(8,128)(2,1)S(1)}, u32[]{:S(2)}, u32[]{:S(2)}) async-start(bf16[8,40,896]{2,1,0:T(8,128)(2,1)} %bitcast.7), calls=%async_computation.1 | async-start | bytes 1146880 | tf_op jit(solution)/shard_map/all_to_all | solution.py:56
  304.2 7.6 %copy-start.5 = (f32[128,2]{0,1:T(2,128)S(1)}, f32[128,2]{0,1:T(2,128)}, u32[]{:S(2)}) copy-start(f32[128,2]{0,1:T(2,128)} %param.12) | copy-start | bytes 3076
  304.2 115.5 %all-to-all-start.3 = ((bf16[8,64,3584]{2,1,0:T(8,128)(2,1)}), bf16[8,64,3584]{2,1,0:T(8,128)(2,1)}, u32[]{:S(2)}, u32[]{:S(2)}) async-start(bf16[8,64,3584]{2,1,0:T(8,128)(2,1)} %copy.42), calls=%async_computation.3 | async-start | bytes 7340032 | tf_op jit(solution)/shard_map/all_to_all | solution.py:94
  310.3 94.9 %all-gather.5.cloned.1.call-start = ((), (), s32[]{:S(2)}) async-start(), calls=%async_computation.5 | async-start | bytes 1179648 | tf_op jit(solution)/shard_map/all_gather | solution.py:63
Sparse Core Ops, SparseCore 0:
  10.4 96.7 all-gather.6
  217.8 36.1 reduce-scatter.3
Sparse Core Ops, SparseCore 1:
  313.7 91.5 all-gather.4
where the time goes:
time: 432 us; the launch traced here: 431 us
  waiting for transfers between devices  232 us (54%)
  local copies, waits for them, and re-layouts  77.5 us (18%)
  other arithmetic  30.3 us (7%)
  matrix products  27.4 us (6%)
  blocking collectives  26.8 us (6%)
  starting transfers between devices  21.3 us (5%)
  between operations  15.7 us (4%)
    all_gather x1, waiting for transfers between devices, on_device(): part_rows = lax.all_gather(probe_hidden[None], 'expert', axis=0, tiled=True)  92.7 us
    all_gather x1, waiting for transfers between devices, on_device(): part_rows = lax.all_gather(own_rows, 'tensor', axis=0, tiled=True)  78.1 us
    broadcast_in_dim x1, local copies, waits for them, and re-layouts, on_device(): aligned[None]  40.8 us
    unnamed x4, waiting for transfers between devices  37 us
    unnamed x27, local copies, waits for them, and re-layouts  29.4 us
    unnamed x1, other arithmetic  25.3 us
    all_to_all x1, waiting for transfers between devices, on_device(): lax.all_to_all(aligned[None], 'expert', split_axis=1, concat_axis=0, tile...  24.5 us
    dot_general x1, matrix products, on_device(): jnp.dot(one_hot, part_rows, preferred_element_type=jnp.float32)  11.3 us
  transfers between devices with their start and end apart: 7, of which 4 were waited for; matrix products, arithmetic and copies ran while one was open for 30% of the time, Pallas kernels for 0%

commit v1 on v0

v1 whole, which is shorter than its diff:
```python
import functools

import jax
import jax.numpy as jnp
from jax import lax
from jax.experimental import pallas as pl
from jax.experimental.pallas import tpu as pltpu
from jax.sharding import PartitionSpec as P


def xor_permute(value, axis, size, k):
    return lax.ppermute(value, axis, [(i, i ^ k) for i in range(size)])


def gather_tensor(value, size):
    held = {0: value}
    bit = size // 2
    while bit:
        for k in sorted(held):
            held[k ^ bit] = xor_permute(held[k], "tensor", size, bit)
        bit //= 2
    return [held[k] for k in range(size)]


def scatter_tensor(parts, size):
    held = dict(enumerate(parts))
    bit = 1
    while bit < size:
        for k in sorted(held):
            if k & bit:
                arrived = xor_permute(
                    held.pop(k).astype(jnp.bfloat16), "tensor", size, bit
                )
                held[k ^ bit] = held[k ^ bit] + arrived.astype(jnp.float32)
        bit *= 2
    return held[0]


def ffn_kernel(count, where_ref, *refs):
    parts = refs[:count]
    gate_ref, up_ref, out_ref, gate_sum, up_sum = refs[count:]
    step = pl.program_id(0)

    @pl.when(step == 0)
    def _():
        gate_sum[...] = jnp.zeros_like(gate_sum)
        up_sum[...] = jnp.zeros_like(up_sum)

    for k in range(count):

        @pl.when(step == k)
        def _(k=k):
            rows = parts[k][...]
            gate_sum[...] += jnp.dot(rows, gate_ref[0], preferred_element_type=jnp.float32)
            up_sum[...] += jnp.dot(rows, up_ref[0], preferred_element_type=jnp.float32)

    @pl.when(step == count - 1)
    def _():
        gate = gate_sum[...]
        out_ref[...] = (gate / (1.0 + jnp.exp(-gate)) * up_sum[...]).astype(out_ref.dtype)


def ffn(parts, gate_weight, up_weight, t):
    count = len(parts)
    rows, width = parts[0].shape
    units = gate_weight.shape[2]
    weight_spec = pl.BlockSpec((1, width, units), lambda k, where: (0, where[0] ^ k, 0))
    return pl.pallas_call(
        functools.partial(ffn_kernel, count),
        out_shape=jax.ShapeDtypeStruct((rows, units), jnp.bfloat16),
        grid_spec=pltpu.PrefetchScalarGridSpec(
            num_scalar_prefetch=1,
            grid=(count,),
            in_specs=[pl.BlockSpec((rows, width), lambda k, where: (0, 0))] * count
            + [weight_spec, weight_spec],
            out_specs=pl.BlockSpec((rows, units), lambda k, where: (0, 0)),
            scratch_shapes=[pltpu.VMEM((rows, units), jnp.float32)] * 2,
        ),
        compiler_params=pltpu.CompilerParams(vmem_limit_bytes=48 * 1024 * 1024),
        cost_estimate=pl.CostEstimate(
            flops=4 * rows * width * count * units,
            bytes_accessed=2 * (2 * width * count * units + rows * width * count + rows * units),
            transcendentals=rows * units,
        ),
        name="ffn",
    )(t.reshape(1).astype(jnp.int32), *parts, gate_weight, up_weight)


def chunks_of(width):
    lanes = 128
    if width % lanes or width < 2 * lanes:
        return [(0, width)]
    first = (width // lanes + 1) // 2 * lanes
    return [(0, first), (first, width - first)]


def one_hot_rows(positions, source):
    rows = source.shape[0]
    selector = (positions[:, None] == jnp.arange(rows, dtype=jnp.int32)[None, :]).astype(
        jnp.bfloat16
    )
    return jnp.dot(selector, source, preferred_element_type=jnp.float32).astype(jnp.bfloat16)


def columns_to_device(own, t, nt, off, width):
    block = own.shape[1] // nt
    found = []
    for k in range(nt):
        piece = lax.dynamic_slice(own, (0, (t ^ k) * block + off), (own.shape[0], width))
        found.append(xor_permute(piece, "tensor", nt, k) if k else piece)
    return jnp.concatenate(found, axis=0)


def rows_to_device(pieces, t, nt):
    found = []
    for k in range(nt):
        piece = lax.dynamic_index_in_dim(pieces, t ^ k, 0, keepdims=False)
        found.append(xor_permute(piece, "tensor", nt, k) if k else piece)
    return found


def merge_two(own, perm, cluster, owners, e, t, ne, nt):
    rows, model = own.shape
    half = ne // 2
    block = model // nt
    sub = rows // half
    q, side = e % half, e // half
    placed = ((perm // rows) ^ t) * rows + perm % rows
    placed = placed.reshape(nt, half, sub)
    member = cluster[(e ^ jnp.arange(half, dtype=jnp.int32))]
    inverse = 1.0 / jnp.sum(
        (cluster[None, :] == jnp.arange(2, dtype=jnp.int32)[:, None]).astype(jnp.float32), axis=1
    )
    owner_side = owners // half
    keep = jnp.where(owner_side[0] == side, 0, 1)
    give = jnp.where(owner_side[0] != side, 0, 1)
    spans = chunks_of(block)

    partials = []
    for off, width in spans:
        source = columns_to_device(own, t, nt, off, width)
        arrived = []
        for k in range(half):
            positions = lax.dynamic_index_in_dim(placed, q ^ k, 1, keepdims=False).reshape(-1)
            aligned = one_hot_rows(positions, source)
            arrived.append(xor_permute(aligned, "expert", ne, k) if k else aligned)
        partials.append(arrived)

    def partial_of(arrived, which):
        total = jnp.zeros(arrived[0].shape, jnp.float32)
        for k in range(half):
            total = total + jnp.where(member[k] == which, arrived[k].astype(jnp.float32), 0.0)
        return total

    def finish(partials, kept, given):
        gathered = []
        for arrived, (off, width) in zip(partials, spans):
            sent = partial_of(arrived, given).astype(jnp.bfloat16)
            other = xor_permute(sent, "expert", ne, half)
            mean = (
                (partial_of(arrived, kept) + other.astype(jnp.float32)) * inverse[kept]
            ).astype(jnp.bfloat16)
            back = rows_to_device(mean.reshape(nt, sub, width), t, nt)
            lines = jnp.stack(back)
            gathered.append(
                [xor_permute(lines, "expert", ne, k) if k else lines for k in range(half)]
            )
        mine = owners[kept] == e
        order_t = jnp.arange(nt, dtype=jnp.int32) ^ t
        out = []
        for j in range(half):
            wide = []
            for group in gathered:
                chosen = group[0]
                for k in range(1, half):
                    chosen = jnp.where((q ^ j) == k, group[k], chosen)
                wide.append(chosen)
            out.append(jnp.concatenate(wide, axis=2))
        joined = jnp.stack(out)
        ordered = []
        for b in range(nt):
            chosen = joined[:, 0]
            for k in range(1, nt):
                chosen = jnp.where(order_t[b] == k, joined[:, k], chosen)
            ordered.append(chosen)
        whole = jnp.concatenate(ordered, axis=2).reshape(rows, model)
        return jnp.where(mine, whole, jnp.zeros_like(whole))

    first = finish(partials, keep, give)

    def second(args):
        first, partials = args
        return first + finish(partials, 1, 1)

    return lax.cond(
        owner_side[0] == owner_side[1], second, lambda args: args[0], (first, partials)
    )


def merge_any(own, perm, cluster, owners, e, t, ne, nt):
    rows, model = own.shape
    block = model // nt
    clusters = owners.shape[0]
    sub = rows // ne
    placed = ((perm // rows) ^ t) * rows + perm % rows
    placed = placed.reshape(nt, ne, sub).transpose(1, 0, 2).reshape(-1)
    aligned = one_hot_rows(placed, columns_to_device(own, t, nt, 0, block))
    arrived = lax.all_to_all(aligned, "expert", split_axis=0, concat_axis=0, tiled=True)
    arrived = arrived.reshape(ne, nt, sub, block)
    member = cluster[None, :] == jnp.arange(clusters, dtype=jnp.int32)[:, None]
    inverse = 1.0 / jnp.sum(member.astype(jnp.float32), axis=1)
    means = []
    for c in range(clusters):
        total = jnp.sum(
            jnp.where(member[c][:, None, None, None], arrived.astype(jnp.float32), 0.0), axis=0
        )
        means.append((total * inverse[c]).astype(jnp.bfloat16))
    means = jnp.stack(means, axis=1)
    back = lax.all_to_all(
        means.reshape(nt * clusters * sub, block), "tensor", split_axis=0, concat_axis=0, tiled=True
    ).reshape(nt, clusters, sub, block)
    lines = back.transpose(1, 2, 0, 3).reshape(clusters, sub, model)
    outgoing = jnp.zeros((ne, sub, model), jnp.bfloat16).at[owners].set(lines)
    return lax.all_to_all(
        outgoing.reshape(ne * sub, model), "expert", split_axis=0, concat_axis=0, tiled=True
    )


def on_device(
    tokens,
    routes,
    gate_values,
    probe_rows,
    gate_weight,
    up_weight,
    down_weight,
    hidden_perm,
    cluster,
    owners,
):
    ne = lax.axis_size("expert")
    nt = lax.axis_size("tensor")
    e = lax.axis_index("expert").astype(jnp.int32)
    t = lax.axis_index("tensor").astype(jnp.int32)
    tok_rows, top = routes.shape
    capacity = tok_rows * top * 5 // (4 * ne)
    own = down_weight[0]
    model = own.shape[1]
    block = model // nt

    perm = lax.all_gather(hidden_perm[0], "tensor", axis=0, tiled=True)
    merge = merge_two if ne == 8 and owners.shape[0] == 2 else merge_any
    merged = merge(own, perm, cluster, owners, e, t, ne, nt)

    flat = routes.reshape(-1)
    pairs = jnp.arange(flat.shape[0], dtype=jnp.int32)
    earlier = (flat[:, None] == flat[None, :]) & (pairs[None, :] < pairs[:, None])
    target = flat * capacity + jnp.sum(earlier.astype(jnp.int32), axis=1)
    target = target.reshape(tok_rows, top)
    slots = jnp.arange(ne * capacity, dtype=jnp.int32)
    selector = jnp.zeros((ne * capacity, tok_rows), jnp.bool_)
    for k in range(top):
        selector = selector | (slots[:, None] == target[:, k][None, :])
    outgoing = jnp.dot(
        selector.astype(jnp.bfloat16), tokens, preferred_element_type=jnp.float32
    ).astype(jnp.bfloat16)
    arrived = lax.all_to_all(outgoing, "expert", split_axis=0, concat_axis=0, tiled=True)
    routed = arrived.shape[0]
    stacked = jnp.concatenate([arrived, probe_rows], axis=0)
    hidden = ffn(gather_tensor(stacked, nt), gate_weight, up_weight, t)
    routed_hidden, probe_hidden = hidden[:routed], hidden[routed:]

    parts = [
        jnp.dot(
            routed_hidden,
            lax.dynamic_slice(own, (0, (t ^ k) * block), (own.shape[0], block)),
            preferred_element_type=jnp.float32,
        )
        for k in range(nt)
    ]
    returned = scatter_tensor(parts, nt).astype(jnp.bfloat16)
    home = lax.all_to_all(returned, "expert", split_axis=0, concat_axis=0, tiled=True)
    chooser = (target.T.reshape(-1)[:, None] == slots[None, :]).astype(jnp.bfloat16)
    picked = jnp.dot(chooser, home, preferred_element_type=jnp.float32)
    picked = picked.reshape(top, tok_rows, block)
    mixed = jnp.sum(gate_values.T[:, :, None] * picked, axis=0).astype(jnp.bfloat16)

    everyone = lax.all_gather(probe_hidden, "expert", axis=0)
    partner = lax.dynamic_index_in_dim(everyone, owners[cluster[e]], 0, keepdims=False)
    partner_full = lax.all_gather(partner, "tensor", axis=1, tiled=True)
    correlation = (
        lax.dot_general(
            probe_hidden, partner_full, (((0,), (0,)), ((), ())), preferred_element_type=jnp.float32
        )
        / probe_hidden.shape[0]
    )
    return (mixed, correlation[None], merged[None])


def solution(mesh):
    in_specs = (
        P("expert", "tensor"),
        P("expert", None),
        P("expert", None),
        P(None, "tensor"),
        P("expert", None, "tensor"),
        P("expert", None, "tensor"),
        P("expert", "tensor", None),
        P("expert", "tensor"),
        P(),
        P(),
    )
    out_specs = (P("expert", "tensor"), P("expert", "tensor", None), P("expert", "tensor", None))
    return jax.shard_map(
        on_device, mesh=mesh, in_specs=in_specs, out_specs=out_specs, check_vma=False
    )
```

time: 432 us -> 266 us (0.62)
  waiting for transfers between devices: 232 us -> 89.4 us
  local copies, waits for them, and re-layouts: 77.5 us -> 14.4 us
  starting transfers between devices: 21.3 us -> 41.5 us
  between operations: 15.7 us -> 34.8 us
  other arithmetic: 30.3 us -> 18.4 us
  matrix products: 27.4 us -> 39 us
  Pallas kernels: 0 us -> 6.45 us
  blocking collectives: 26.8 us -> 20.7 us
    all_gather x2 -> x1, waiting for transfers between devices: 171 us -> 17 us  [on_device(): everyone = lax.all_gather(probe_hidden, 'expert', axis=0)]
    ppermute x0 -> x32, waiting for transfers between devices: none -> 72.3 us  [xor_permute(): return lax.ppermute(value, axis, [(i, i ^ k) for i in range(size)])]
    broadcast_in_dim x1 -> x0, local copies, waits for them, and re-layouts: 40.8 us -> none  [on_device(): aligned[None]]
    unnamed x4 -> x1, waiting for transfers between devices: 37 us -> 0.02 us
    ppermute x0 -> x32, starting transfers between devices: none -> 31.5 us  [xor_permute(): return lax.ppermute(value, axis, [(i, i ^ k) for i in range(size)])]
    unnamed x27 -> x65, local copies, waits for them, and re-layouts: 29.4 us -> 0.9 us
    unnamed x1 -> x0, other arithmetic: 25.3 us -> none
    all_to_all x2 -> x0, waiting for transfers between devices: 24.5 us -> none  [the longest x1 24.5 us: on_device(): lax.all_to_all(aligned[None], 'expert', split_axis=1, concat_axis=0, tile...]
  transfers between devices with their start and end apart: 7 -> 35, of which waited for: 4 -> 11; matrix products, arithmetic and copies ran while one was open for 30% -> 25% of each run, Pallas kernels for 0% -> 0%
where the time goes in v1:
time: 266 us; the launch traced here: 265 us
  waiting for transfers between devices  89.4 us (34%)
  starting transfers between devices  41.5 us (16%)
  matrix products  39 us (15%)
  between operations  34.8 us (13%)
  blocking collectives  20.7 us (8%)
  other arithmetic  18.4 us (7%)
  local copies, waits for them, and re-layouts  14.4 us (5%)
  Pallas kernels  6.45 us (2%)
    ppermute x32, waiting for transfers between devices, xor_permute(): return lax.ppermute(value, axis, [(i, i ^ k) for i in range(size)])  72.3 us
    ppermute x32, starting transfers between devices, xor_permute(): return lax.ppermute(value, axis, [(i, i ^ k) for i in range(size)])  31.5 us
    dot_general x8, matrix products, one_hot_rows(): jnp.dot(selector, source, preferred_element_type=jnp.float32)  25.1 us
    all_gather x1, waiting for transfers between devices, on_device(): everyone = lax.all_gather(probe_hidden, 'expert', axis=0)  17 us
    all_gather x1, blocking collectives, on_device(): perm = lax.all_gather(hidden_perm[0], 'tensor', axis=0, tiled=True)  13.6 us
    dot_general x4, matrix products, on_device(): jnp.dot(routed_hidden, lax.dynamic_slice(own, (0, (t ^ k) * block), (own....  7.76 us
    all_gather x1, blocking collectives, on_device(): partner_full = lax.all_gather(partner, 'tensor', axis=1, tiled=True)  7.09 us
    pallas_call x1, Pallas kernels, ffn(): pl.pallas_call(functools.partial(ffn_kernel, count), out_shape=jax.ShapeD...  6.45 us
  transfers between devices with their start and end apart: 35, of which 11 were waited for; matrix products, arithmetic and copies ran while one was open for 25% of the time, Pallas kernels for 0%

profile of v1, /device:TPU:0, one launch (start us, length us, event | category | flops | bytes accessed | tf_op | source)
XLA Modules:
  0.0 264.8 jit_solution(9463716247388653492)
XLA Ops:
  7.2 1.7 dynamic-slice_bitcast_fusion.9
  9.5 2.6 collective-permute-start.21
  12.1 2.3 dynamic-slice_bitcast_fusion.13
  14.8 1.4 collective-permute-start.35
  16.2 0.7 copy.40
  17.0 1.0 eq.499
  18.1 0.8 reduce_sum.30
  18.9 0.9 copy.41
  19.9 1.1 convolution_convert_fusion.2
  21.0 5.8 %all-to-all-start = ((bf16[8,40,896]{2,1,0:T(8,128)(2,1)}), bf16[8,40,896]{2,1,0:T(8,128)(2,1)}, u32[]{:S(2)}, u32[]{:S(2)}) async-start(bf16[8,40,896]{2,1,0:T(8,128)(2,1)} %bitcast.51), calls=%async_computation | async-start | bytes 1146880 | tf_op jit(solution)/shard_map/all_to_all | solution.py:267
  28.8 13.6 %all-gather.2 = s32[1,2048]{1,0:T(1,128)S(1)} all-gather(s32[1,512]{1,0:T(1,128)S(1)} %copy-done.30), channel_id=4, replica_groups=mesh['expert'=8,'tensor'=4] {'tensor'}, dimensions={1}, use_global_device_ids=true | all-gather | bytes 10240 | tf_op jit(solution)/shard_map/all_gather | solution.py:251
  43.3 1.7 collective-permute-start.22
  45.0 2.5 fusion.29
  47.6 1.6 collective-permute-start.36
  49.1 3.3 %fusion.30 = bf16[512,384]{1,0:T(8,128)(2,1)} fusion(s32[512]{0:T(512)S(1)} %bitcast.229, bf16[512,384]{1,0:T(8,128)(2,1)} %collective-permute-done.35, bf16[512,384]{1,0:T(8,128)(2,1)} %collective-permute-done.34, bf16[512,384]{1,0:T(8,128)(2,1)} %collective-permute-done.33, bf16[512,384]{1,0:T(8,128)(2,1)S(1)} %get-tuple-element.99), kind=kOutput, calls=%fused_computation.87 | convolution fusion | flops 812843008 | bytes 1968128 | tf_op jit(solution)/shard_map/dot_general | solution.py:102
  52.4 1.6 collective-permute-start.37
  54.0 3.3 %fusion.31 = bf16[512,384]{1,0:T(8,128)(2,1)} fusion(s32[512]{0:T(512)S(1)} %bitcast.227, bf16[512,384]{1,0:T(8,128)(2,1)} %collective-permute-done.35, bf16[512,384]{1,0:T(8,128)(2,1)} %collective-permute-done.34, bf16[512,384]{1,0:T(8,128)(2,1)} %collective-permute-done.33, bf16[512,384]{1,0:T(8,128)(2,1)S(1)} %get-tuple-element.99), kind=kOutput, calls=%fused_computation.88 | convolution fusion | flops 812843008 | bytes 1968128 | tf_op jit(solution)/shard_map/dot_general | solution.py:102
  57.7 3.5 %fusion.24 = bf16[512,512]{1,0:T(8,128)(2,1)} fusion(s32[512]{0:T(512)S(1)} %bitcast.232, bf16[512,512]{1,0:T(8,128)(2,1)S(1)} %collective-permute-done.22, bf16[512,512]{1,0:T(8,128)(2,1)} %collective-permute-done.21, bf16[512,512]{1,0:T(8,128)(2,1)} %collective-permute-done.20, bf16[512,512]{1,0:T(8,128)(2,1)S(1)} %get-tuple-element.95), kind=kOutput, calls=%fused_computation.81 | convolution fusion | flops 1083441152 | bytes 2623488 | tf_op jit(solution)/shard_map/dot_general | solution.py:102
  61.2 1.5 collective-permute-start.23
  62.7 3.3 %fusion.25 = bf16[512,512]{1,0:T(8,128)(2,1)} fusion(s32[512]{0:T(512)S(1)} %bitcast.230, bf16[512,512]{1,0:T(8,128)(2,1)S(1)} %collective-permute-done.22, bf16[512,512]{1,0:T(8,128)(2,1)} %collective-permute-done.21, bf16[512,512]{1,0:T(8,128)(2,1)} %collective-permute-done.20, bf16[512,512]{1,0:T(8,128)(2,1)S(1)} %get-tuple-element.95), kind=kOutput, calls=%fused_computation.82 | convolution fusion | flops 1083441152 | bytes 2623488 | tf_op jit(solution)/shard_map/dot_general | solution.py:102
  66.0 1.6 collective-permute-start.24
  67.5 3.3 %fusion.26 = bf16[512,512]{1,0:T(8,128)(2,1)} fusion(s32[512]{0:T(512)S(1)} %bitcast.228, bf16[512,512]{1,0:T(8,128)(2,1)S(1)} %collective-permute-done.22, bf16[512,512]{1,0:T(8,128)(2,1)} %collective-permute-done.21, bf16[512,512]{1,0:T(8,128)(2,1)} %collective-permute-done.20, bf16[512,512]{1,0:T(8,128)(2,1)S(1)} %get-tuple-element.95), kind=kOutput, calls=%fused_computation.83 | convolution fusion | flops 1083441152 | bytes 2623488 | tf_op jit(solution)/shard_map/dot_general | solution.py:102
  77.6 3.1 %fusion.59 = (bf16[512,384]{1,0:T(8,128)(2,1)S(1)}, bf16[512,384]{1,0:T(8,128)(2,1)S(1)}) fusion(bf16[512,384]{1,0:T(8,128)(2,1)S(1)} %collective-permute-done.36, bf16[512,384]{1,0:T(8,128)(2,1)S(1)} %collective-permute-done.37, bf16[512,384]{1,0:T(8,128)(2,1)S(1)} %collective-permute-done.38, pred[]{:T(512)S(6)} %eq.544, pred[]{:T(512)S(6)} %eq.543, ...), kind=kOutput, calls=%fused_computation.133 | convolution fusion | flops 815202304 | bytes 3540996 | tf_op jit(solution)/shard_map/dot_general | solution.py:102
  80.7 2.7 %collective-permute-start.39 = (bf16[512,384]{1,0:T(8,128)(2,1)S(1)}, bf16[512,384]{1,0:T(8,128)(2,1)S(1)}, u32[]{:S(2)}, u32[]{:S(2)}) collective-permute-start(bf16[512,384]{1,0:T(8,128)(2,1)S(1)} %get-tuple-element.137), channel_id=1, source_target_pairs={{0,16},{4,20},{8,24},{12,28},{16,0},{20,4},{24,8},{28,12},{1,17},{... | collective-permute-start | bytes 1179656 | tf_op jit(solution)/shard_map/ppermute | solution.py:12
  83.6 9.2 %collective-permute-done.24 = bf16[512,512]{1,0:T(8,128)(2,1)S(1)} collective-permute-done((bf16[512,512]{1,0:T(8,128)(2,1)}, bf16[512,512]{1,0:T(8,128)(2,1)S(1)}, u32[]{:S(2)}, u32[]{:S(2)}) %collective-permute-start.24) | collective-permute-done | bytes 524320 | tf_op jit(solution)/shard_map/ppermute | solution.py:12
  92.8 10.2 %collective-permute-done.25 = bf16[512,512]{1,0:T(8,128)(2,1)S(1)} collective-permute-done((bf16[512,512]{1,0:T(8,128)(2,1)}, bf16[512,512]{1,0:T(8,128)(2,1)S(1)}, u32[]{:S(2)}, u32[]{:S(2)}) %collective-permute-start.25) | collective-permute-done | bytes 524320 | tf_op jit(solution)/shard_map/ppermute | solution.py:12
  102.9 2.9 %fusion.41 = (bf16[512,512]{1,0:T(8,128)(2,1)S(1)}, bf16[512,512]{1,0:T(8,128)(2,1)S(1)}) fusion(bf16[512,512]{1,0:T(8,128)(2,1)S(1)} %collective-permute-done.23, bf16[512,512]{1,0:T(8,128)(2,1)S(1)} %collective-permute-done.24, bf16[512,512]{1,0:T(8,128)(2,1)S(1)} %collective-permute-done.25, pred[]{:T(512)S(6)} %eq.544, pred[]{:T(512)S(6)} %eq.543, ...), kind=kOutput, calls=%fused_computation.98 | convolution fusion | flops 1086586880 | bytes 4720644 | tf_op jit(solution)/shard_map/dot_general | solution.py:102
  105.8 1.9 collective-permute-start.26
  107.8 1.1 fusion.55
  109.5 1.6 collective-permute-start.40
  111.1 3.5 %collective-permute-done.41 = bf16[128,384]{1,0:T(8,128)(2,1)S(1)} collective-permute-done((bf16[128,384]{1,0:T(8,128)(2,1)S(1)}, bf16[128,384]{1,0:T(8,128)(2,1)S(1)}, u32[]{:S(2)}, u32[]{:S(2)}) %collective-permute-start.41) | collective-permute-done | bytes 98336 | tf_op jit(solution)/shard_map/ppermute | solution.py:12
  114.6 1.0 pad_maximum_fusion.8
  115.6 3.3 %collective-permute-start.43 = (bf16[4,128,384]{2,1,0:T(8,128)(2,1)}, bf16[4,128,384]{2,1,0:T(8,128)(2,1)}, u32[]{:S(2)}, u32[]{:S(2)}) collective-permute-start(bf16[4,128,384]{2,1,0:T(8,128)(2,1)} %pad_maximum_fusion.8), channel_id=1, source_target_pairs={{0,12},{4,8},{8,4},{12,0},{16,28},{20,24},{24,20},{28,16},{1,13},{... | collective-permute-start | bytes 1179656 | tf_op jit(solution)/shard_map/ppermute | solution.py:12
  119.4 11.6 %collective-permute-done.26 = bf16[512,512]{1,0:T(8,128)(2,1)S(1)} collective-permute-done((bf16[512,512]{1,0:T(8,128)(2,1)S(1)}, bf16[512,512]{1,0:T(8,128)(2,1)S(1)}, u32[]{:S(2)}, u32[]{:S(2)}) %collective-permute-start.26) | collective-permute-done | bytes 524320 | tf_op jit(solution)/shard_map/ppermute | solution.py:12
  131.0 1.1 fusion.37
  132.2 0.7 constant_dynamic-slice_fusion.3
  133.3 1.1 pad_maximum_fusion.6.refs_0_
  134.5 1.7 collective-permute-start.15
  136.1 3.1 %collective-permute-done.28 = bf16[128,512]{1,0:T(8,128)(2,1)S(1)} collective-permute-done((bf16[128,512]{1,0:T(8,128)(2,1)S(1)}, bf16[128,512]{1,0:T(8,128)(2,1)S(1)}, u32[]{:S(2)}, u32[]{:S(2)}) %collective-permute-start.28) | collective-permute-done | bytes 131104 | tf_op jit(solution)/shard_map/ppermute | solution.py:12
  147.5 0.7 dynamic_slice.152
  150.3 0.7 fusion.89
  154.9 3.5 %collective-permute-done.29 = bf16[128,512]{1,0:T(8,128)(2,1)S(1)} collective-permute-done((bf16[128,512]{1,0:T(8,128)(2,1)}, bf16[128,512]{1,0:T(8,128)(2,1)S(1)}, u32[]{:S(2)}, u32[]{:S(2)}) %collective-permute-start.29) | collective-permute-done | bytes 131104 | tf_op jit(solution)/shard_map/ppermute | solution.py:12
  158.8 2.9 %collective-permute-start.31 = (bf16[4,128,512]{2,1,0:T(8,128)(2,1)S(1)}, bf16[4,128,512]{2,1,0:T(8,128)(2,1)S(1)}, u32[]{:S(2)}, u32[]{:S(2)}) collective-permute-start(bf16[4,128,512]{2,1,0:T(8,128)(2,1)S(1)} %pad_maximum_fusion.7), channel_id=1, source_target_pairs={{0,8},{4,12},{8,0},{12,4},{16,24},{20,28},{24,16},{28,20},{1,9},{5... | collective-permute-start | bytes 1572872 | tf_op jit(solution)/shard_map/ppermute | solution.py:12
  162.3 1.5 select_select_fusion.22
  163.8 1.5 select_select_fusion.23
  165.4 9.1 %collective-permute-done.30 = bf16[4,128,512]{2,1,0:T(8,128)(2,1)S(1)} collective-permute-done((bf16[4,128,512]{2,1,0:T(8,128)(2,1)S(1)}, bf16[4,128,512]{2,1,0:T(8,128)(2,1)S(1)}, u32[]{:S(2)}, u32[]{:S(2)}) %collective-permute-start.30) | collective-permute-done | bytes 524320 | tf_op jit(solution)/shard_map/ppermute | solution.py:12
  174.5 10.6 %collective-permute-done.31 = bf16[4,128,512]{2,1,0:T(8,128)(2,1)S(1)} collective-permute-done((bf16[4,128,512]{2,1,0:T(8,128)(2,1)S(1)}, bf16[4,128,512]{2,1,0:T(8,128)(2,1)S(1)}, u32[]{:S(2)}, u32[]{:S(2)}) %collective-permute-start.31) | collective-permute-done | bytes 524320 | tf_op jit(solution)/shard_map/ppermute | solution.py:12
  185.1 1.1 select_select_fusion.18
  186.9 6.4 %ffn.1 = bf16[448,512]{1,0:T(8,128)(2,1)S(1)} custom-call(s32[1]{0:T(128)} %bitcast.48.where_ref, bf16[448,896]{1,0:T(8,128)(2,1)S(1)} %pad_maximum_fusion.6.refs_0_, bf16[448,896]{1,0:T(8,128)(2,1)S(1)} %collective-permute-done.14.refs_1_, bf16[448,896]{1,0:T(8,128)(2,1)S(1)} %collective-permute-done.15.refs_2_, ...), custom_call_target="tpu_custom_call" | custom-call | flops 3288334336 | bytes 11010048 | tf_op jit(solution)/shard_map/ffn/pallas_call | solution.py:68
  193.4 1.7 convolution_convert_fusion
  195.2 2.1 pad_maximum_fusion.3
  198.0 1.8 convolution_convert_fusion.1
  200.4 1.7 fusion.22
  202.7 1.5 select_select_fusion.15
  204.2 1.6 select_select_fusion.13
  205.8 11.3 %collective-permute-done.19 = bf16[320,896]{1,0:T(8,128)(2,1)S(1)} collective-permute-done((bf16[320,896]{1,0:T(8,128)(2,1)S(1)}, bf16[320,896]{1,0:T(8,128)(2,1)S(1)}, u32[]{:S(2)}, u32[]{:S(2)}) %collective-permute-start.19) | collective-permute-done | bytes 573472 | tf_op jit(solution)/shard_map/ppermute | solution.py:12
  217.1 2.5 fusion.21
  219.6 4.2 %all-to-all-start.1 = ((bf16[8,40,896]{2,1,0:T(8,128)(2,1)}), bf16[8,40,896]{2,1,0:T(8,128)(2,1)}, u32[]{:S(2)}, u32[]{:S(2)}) async-start(bf16[8,40,896]{2,1,0:T(8,128)(2,1)} %bitcast.57), calls=%async_computation.1 | async-start | bytes 1146880 | tf_op jit(solution)/shard_map/all_to_all | solution.py:282
  223.9 3.7 %maximum_select_fusion.1 = bf16[512,3584]{1,0:T(8,128)(2,1)} fusion(bf16[512,896]{1,0:T(8,128)(2,1)} %bitcast.180, bf16[512,896]{1,0:T(8,128)(2,1)} %bitcast.179, bf16[512,896]{1,0:T(8,128)(2,1)} %bitcast.178, bf16[512,896]{1,0:T(8,128)(2,1)} %bitcast.177, pred[]{:T(512)S(6)} %eq.517), kind=kLoop, calls=%fused_computation.52 | loop fusion | flops 16515072 | bytes 7340033 | tf_op jit(solution)/shard_map/jit(_where)/select_n | solution.py:187
  227.9 17.0 %all-gather.5.cloned.1.call-done = bf16[1024,512]{1,0:T(8,128)(2,1)} async-done(((bf16[128,512]{1,0:T(8,128)(2,1)}), bf16[1024,512]{1,0:T(8,128)(2,1)}) %all-gather.5.cloned.1.call-update) | async-done | bytes 1048592 | tf_op jit(solution)/shard_map/all_gather | solution.py:288
  244.9 0.9 constant_dynamic-slice_fusion.8
  245.9 7.1 %all-gather.1 = bf16[1,128,2048]{2,1,0:T(8,128)(2,1)S(1)} all-gather(bf16[1,128,512]{2,1,0:T(8,128)(2,1)S(1)} %constant_dynamic-slice_fusion.8), channel_id=3, replica_groups=mesh['expert'=8,'tensor'=4] {'tensor'}, dimensions={2}, use_global_device_ids=true | all-gather | bytes 655360 | tf_op jit(solution)/shard_map/all_gather | solution.py:290
  253.0 2.7 %multiply_bitcast_fusion = f32[1,512,2048]{2,1,0:T(8,128)} fusion(bf16[1,128,2048]{2,1,0:T(8,128)(2,1)S(1)} %all-gather.1, bf16[448,512]{1,0:T(8,128)(2,1)S(1)} %ffn.1), kind=kOutput, calls=%fused_computation.50 | convolution fusion | flops 269484032 | bytes 4849664 | tf_op jit(solution)/shard_map/dot_general | solution.py:292
  255.7 2.3 fusion.27
  (133 shorter events, 11.1 us)
Async XLA Ops:
  7.2 12.7 %copy-start = (bf16[128,896]{1,0:T(8,128)(2,1)S(1)}, bf16[128,896]{1,0:T(8,128)(2,1)}, u32[]{:S(2)}) copy-start(bf16[128,896]{1,0:T(8,128)(2,1)} %param.12) | copy-start | bytes 688132
  7.2 9.0 %copy-start.29 = (s32[128,2]{0,1:T(2,128)S(1)}, s32[128,2]{0,1:T(2,128)}, u32[]{:S(2)}) copy-start(s32[128,2]{0,1:T(2,128)} %param.13) | copy-start | bytes 3076
  9.0 17.9 %copy-start.31 = (s32[2]{0:T(128)S(1)}, s32[2]{0:T(128)}, u32[]{:S(2)}) copy-start(s32[2]{0:T(128)} %param.21) | copy-start | bytes 28
  9.0 19.8 %copy-start.30 = (s32[1,512]{1,0:T(1,128)S(1)}, s32[1,512]{1,0:T(1,128)}, u32[]{:S(2)}) copy-start(s32[1,512]{1,0:T(1,128)} %param.19) | copy-start | bytes 6148
  9.0 33.5 %copy-start.2 = (s32[8]{0:T(128)S(1)}, s32[8]{0:T(128)}, u32[]{:S(2)}) copy-start(s32[8]{0:T(128)} %param.20) | copy-start | bytes 100
  9.0 48.3 %collective-permute-start.20 = (bf16[512,512]{1,0:T(8,128)(2,1)S(1)}, bf16[512,512]{1,0:T(8,128)(2,1)}, u32[]{:S(2)}, u32[]{:S(2)}) collective-permute-start(bf16[512,512]{1,0:T(8,128)(2,1)S(1)} %get-tuple-element.98), channel_id=1, source_target_pairs={{0,1},{1,0},{2,3},{3,2},{4,5},{5,4},{6,7},{7,6},{8,9},{9,8},{10,11... | collective-permute-start | bytes 1572872 | tf_op jit(solution)/shard_map/ppermute | solution.py:12
  9.5 48.2 %collective-permute-start.21 = (bf16[512,512]{1,0:T(8,128)(2,1)S(1)}, bf16[512,512]{1,0:T(8,128)(2,1)}, u32[]{:S(2)}, u32[]{:S(2)}) collective-permute-start(bf16[512,512]{1,0:T(8,128)(2,1)S(1)} %get-tuple-element.97), channel_id=1, source_target_pairs={{0,2},{1,3},{2,0},{3,1},{4,6},{5,7},{6,4},{7,5},{8,10},{9,11},{10,... | collective-permute-start | bytes 1572872 | tf_op jit(solution)/shard_map/ppermute | solution.py:12
  14.4 39.6 %copy-start.27 = (bf16[512,384]{1,0:T(8,128)(2,1)}, bf16[512,384]{1,0:T(8,128)(2,1)S(1)}, u32[]{:S(2)}) copy-start(bf16[512,384]{1,0:T(8,128)(2,1)S(1)} %get-tuple-element.99) | copy-start | bytes 1179652
  14.4 28.9 %collective-permute-start.33 = (bf16[512,384]{1,0:T(8,128)(2,1)}, bf16[512,384]{1,0:T(8,128)(2,1)}, u32[]{:S(2)}, u32[]{:S(2)}) collective-permute-start(bf16[512,384]{1,0:T(8,128)(2,1)} %get-tuple-element.100), channel_id=1, source_target_pairs={{0,1},{1,0},{2,3},{3,2},{4,5},{5,4},{6,7},{7,6},{8,9},{9,8},{10,11... | collective-permute-start | bytes 1179656 | tf_op jit(solution)/shard_map/ppermute | solution.py:12
  14.5 30.5 %collective-permute-start.34 = (bf16[512,384]{1,0:T(8,128)(2,1)S(1)}, bf16[512,384]{1,0:T(8,128)(2,1)}, u32[]{:S(2)}, u32[]{:S(2)}) collective-permute-start(bf16[512,384]{1,0:T(8,128)(2,1)S(1)} %get-tuple-element.102), channel_id=1, source_target_pairs={{0,2},{1,3},{2,0},{3,1},{4,6},{5,7},{6,4},{7,5},{8,10},{9,11},{10,... | collective-permute-start | bytes 1179656 | tf_op jit(solution)/shard_map/ppermute | solution.py:12
  14.8 30.2 %collective-permute-start.35 = (bf16[512,384]{1,0:T(8,128)(2,1)S(1)}, bf16[512,384]{1,0:T(8,128)(2,1)}, u32[]{:S(2)}, u32[]{:S(2)}) collective-permute-start(bf16[512,384]{1,0:T(8,128)(2,1)S(1)} %get-tuple-element.101), channel_id=1, source_target_pairs={{0,3},{1,2},{2,1},{3,0},{4,7},{5,6},{6,5},{7,4},{8,11},{9,10},{10,... | collective-permute-start | bytes 1179656 | tf_op jit(solution)/shard_map/ppermute | solution.py:12
  21.0 112.3 %all-to-all-start = ((bf16[8,40,896]{2,1,0:T(8,128)(2,1)}), bf16[8,40,896]{2,1,0:T(8,128)(2,1)}, u32[]{:S(2)}, u32[]{:S(2)}) async-start(bf16[8,40,896]{2,1,0:T(8,128)(2,1)} %bitcast.51), calls=%async_computation | async-start | bytes 1146880 | tf_op jit(solution)/shard_map/all_to_all | solution.py:267
  26.8 218.2 %all-gather.5.cloned.1.call-start = ((), (), s32[]{:S(2)}) async-start(), calls=%async_computation.2 | async-start | bytes 1179648 | tf_op jit(solution)/shard_map/all_gather | solution.py:288
  43.3 14.4 %collective-permute-start.22 = (bf16[512,512]{1,0:T(8,128)(2,1)S(1)}, bf16[512,512]{1,0:T(8,128)(2,1)S(1)}, u32[]{:S(2)}, u32[]{:S(2)}) collective-permute-start(bf16[512,512]{1,0:T(8,128)(2,1)S(1)} %get-tuple-element.96), channel_id=1, source_target_pairs={{0,3},{1,2},{2,1},{3,0},{4,7},{5,6},{6,5},{7,4},{8,11},{9,10},{10,... | collective-permute-start | bytes 1572872 | tf_op jit(solution)/shard_map/ppermute | solution.py:12
  47.6 23.3 %collective-permute-start.36 = (bf16[512,384]{1,0:T(8,128)(2,1)S(1)}, bf16[512,384]{1,0:T(8,128)(2,1)S(1)}, u32[]{:S(2)}, u32[]{:S(2)}) collective-permute-start(bf16[512,384]{1,0:T(8,128)(2,1)S(1)} %fusion.29), channel_id=1, source_target_pairs={{0,4},{4,0},{8,12},{12,8},{16,20},{20,16},{24,28},{28,24},{1,5},{5... | collective-permute-start | bytes 1179656 | tf_op jit(solution)/shard_map/ppermute | solution.py:12
  52.4 25.2 %collective-permute-start.37 = (bf16[512,384]{1,0:T(8,128)(2,1)}, bf16[512,384]{1,0:T(8,128)(2,1)S(1)}, u32[]{:S(2)}, u32[]{:S(2)}) collective-permute-start(bf16[512,384]{1,0:T(8,128)(2,1)} %fusion.30), channel_id=1, source_target_pairs={{0,8},{4,12},{8,0},{12,4},{16,24},{20,28},{24,16},{28,20},{1,9},{5... | collective-permute-start | bytes 1179656 | tf_op jit(solution)/shard_map/ppermute | solution.py:12
  57.3 20.3 %collective-permute-start.38 = (bf16[512,384]{1,0:T(8,128)(2,1)}, bf16[512,384]{1,0:T(8,128)(2,1)S(1)}, u32[]{:S(2)}, u32[]{:S(2)}) collective-permute-start(bf16[512,384]{1,0:T(8,128)(2,1)} %fusion.31), channel_id=1, source_target_pairs={{0,12},{4,8},{8,4},{12,0},{16,28},{20,24},{24,20},{28,16},{1,13},{... | collective-permute-start | bytes 1179656 | tf_op jit(solution)/shard_map/ppermute | solution.py:12
  57.7 9.8 %copy-start.32 = (bf16[512,512]{1,0:T(8,128)(2,1)}, bf16[512,512]{1,0:T(8,128)(2,1)S(1)}, u32[]{:S(2)}) copy-start(bf16[512,512]{1,0:T(8,128)(2,1)S(1)} %collective-permute-done.22) | copy-start | bytes 1572868
  61.2 22.4 %collective-permute-start.23 = (bf16[512,512]{1,0:T(8,128)(2,1)}, bf16[512,512]{1,0:T(8,128)(2,1)S(1)}, u32[]{:S(2)}, u32[]{:S(2)}) collective-permute-start(bf16[512,512]{1,0:T(8,128)(2,1)} %fusion.24), channel_id=1, source_target_pairs={{0,4},{4,0},{8,12},{12,8},{16,20},{20,16},{24,28},{28,24},{1,5},{5... | collective-permute-start | bytes 1572872 | tf_op jit(solution)/shard_map/ppermute | solution.py:12
  66.0 26.8 %collective-permute-start.24 = (bf16[512,512]{1,0:T(8,128)(2,1)}, bf16[512,512]{1,0:T(8,128)(2,1)S(1)}, u32[]{:S(2)}, u32[]{:S(2)}) collective-permute-start(bf16[512,512]{1,0:T(8,128)(2,1)} %fusion.25), channel_id=1, source_target_pairs={{0,8},{4,12},{8,0},{12,4},{16,24},{20,28},{24,16},{28,20},{1,9},{5... | collective-permute-start | bytes 1572872 | tf_op jit(solution)/shard_map/ppermute | solution.py:12
  70.8 36.9 %copy-start.8 = (bf16[512,384]{1,0:T(8,128)(2,1)}, bf16[512,384]{1,0:T(8,128)(2,1)S(1)}, u32[]{:S(2)}) copy-start(bf16[512,384]{1,0:T(8,128)(2,1)S(1)} %collective-permute-done.36) | copy-start | bytes 1179652
  70.8 32.1 %collective-permute-start.25 = (bf16[512,512]{1,0:T(8,128)(2,1)}, bf16[512,512]{1,0:T(8,128)(2,1)S(1)}, u32[]{:S(2)}, u32[]{:S(2)}) collective-permute-start(bf16[512,512]{1,0:T(8,128)(2,1)} %fusion.26), channel_id=1, source_target_pairs={{0,12},{4,8},{8,4},{12,0},{16,28},{20,24},{24,20},{28,16},{1,13},{... | collective-permute-start | bytes 1572872 | tf_op jit(solution)/shard_map/ppermute | solution.py:12
  77.6 30.1 %copy-start.10 = (bf16[512,384]{1,0:T(8,128)(2,1)}, bf16[512,384]{1,0:T(8,128)(2,1)S(1)}, u32[]{:S(2)}) copy-start(bf16[512,384]{1,0:T(8,128)(2,1)S(1)} %collective-permute-done.37) | copy-start | bytes 1179652
  77.6 30.1 %copy-start.13 = (bf16[512,384]{1,0:T(8,128)(2,1)}, bf16[512,384]{1,0:T(8,128)(2,1)S(1)}, u32[]{:S(2)}) copy-start(bf16[512,384]{1,0:T(8,128)(2,1)S(1)} %collective-permute-done.38) | copy-start | bytes 1179652
  77.6 25.3 %copy-start.33 = (bf16[512,512]{1,0:T(8,128)(2,1)S(1)}, bf16[512,512]{1,0:T(8,128)(2,1)}, u32[]{:S(2)}) copy-start(bf16[512,512]{1,0:T(8,128)(2,1)} %copy-done.32) | copy-start | bytes 1572868
  80.7 27.1 %copy-start.16 = (bf16[512,384]{1,0:T(8,128)(2,1)}, bf16[512,384]{1,0:T(8,128)(2,1)S(1)}, u32[]{:S(2)}) copy-start(bf16[512,384]{1,0:T(8,128)(2,1)S(1)} %get-tuple-element.157) | copy-start | bytes 1179652
  80.7 27.0 %collective-permute-start.39 = (bf16[512,384]{1,0:T(8,128)(2,1)S(1)}, bf16[512,384]{1,0:T(8,128)(2,1)S(1)}, u32[]{:S(2)}, u32[]{:S(2)}) collective-permute-start(bf16[512,384]{1,0:T(8,128)(2,1)S(1)} %get-tuple-element.137), channel_id=1, source_target_pairs={{0,16},{4,20},{8,24},{12,28},{16,0},{20,4},{24,8},{28,12},{1,17},{... | collective-permute-start | bytes 1179656 | tf_op jit(solution)/shard_map/ppermute | solution.py:12
  102.9 28.1 %copy-start.4 = (bf16[512,512]{1,0:T(8,128)(2,1)}, bf16[512,512]{1,0:T(8,128)(2,1)S(1)}, u32[]{:S(2)}) copy-start(bf16[512,512]{1,0:T(8,128)(2,1)S(1)} %collective-permute-done.25) | copy-start | bytes 1572868
  105.8 27.1 %copy-start.6 = (bf16[512,512]{1,0:T(8,128)(2,1)}, bf16[512,512]{1,0:T(8,128)(2,1)S(1)}, u32[]{:S(2)}) copy-start(bf16[512,512]{1,0:T(8,128)(2,1)S(1)} %get-tuple-element.152) | copy-start | bytes 1572868
  105.8 25.2 %collective-permute-start.26 = (bf16[512,512]{1,0:T(8,128)(2,1)S(1)}, bf16[512,512]{1,0:T(8,128)(2,1)S(1)}, u32[]{:S(2)}, u32[]{:S(2)}) collective-permute-start(bf16[512,512]{1,0:T(8,128)(2,1)S(1)} %get-tuple-element.139), channel_id=1, source_target_pairs={{0,16},{4,20},{8,24},{12,28},{16,0},{20,4},{24,8},{28,12},{1,17},{... | collective-permute-start | bytes 1572872 | tf_op jit(solution)/shard_map/ppermute | solution.py:12
  107.7 25.6 %copy-start.28 = (bf16[128,896]{1,0:T(8,128)(2,1)S(1)}, bf16[128,896]{1,0:T(8,128)(2,1)}, u32[]{:S(2)}) copy-start(bf16[128,896]{1,0:T(8,128)(2,1)} %param.15) | copy-start | bytes 688132
  108.9 5.7 %collective-permute-start.41 = (bf16[128,384]{1,0:T(8,128)(2,1)S(1)}, bf16[128,384]{1,0:T(8,128)(2,1)S(1)}, u32[]{:S(2)}, u32[]{:S(2)}) collective-permute-start(bf16[128,384]{1,0:T(8,128)(2,1)S(1)} %get-tuple-element.117), channel_id=1, source_target_pairs={{0,2},{1,3},{2,0},{3,1},{4,6},{5,7},{6,4},{7,5},{8,10},{9,11},{10,... | collective-permute-start | bytes 294920 | tf_op jit(solution)/shard_map/ppermute | solution.py:12
  109.5 5.1 %collective-permute-start.42 = (bf16[128,384]{1,0:T(8,128)(2,1)S(1)}, bf16[128,384]{1,0:T(8,128)(2,1)S(1)}, u32[]{:S(2)}, u32[]{:S(2)}) collective-permute-start(bf16[128,384]{1,0:T(8,128)(2,1)S(1)} %get-tuple-element.116), channel_id=1, source_target_pairs={{0,3},{1,2},{2,1},{3,0},{4,7},{5,6},{6,5},{7,4},{8,11},{9,10},{10,... | collective-permute-start | bytes 294920 | tf_op jit(solution)/shard_map/ppermute | solution.py:12
  109.5 5.1 %collective-permute-start.40 = (bf16[128,384]{1,0:T(8,128)(2,1)S(1)}, bf16[128,384]{1,0:T(8,128)(2,1)S(1)}, u32[]{:S(2)}, u32[]{:S(2)}) collective-permute-start(bf16[128,384]{1,0:T(8,128)(2,1)S(1)} %get-tuple-element.118), channel_id=1, source_target_pairs={{0,1},{1,0},{2,3},{3,2},{4,5},{5,4},{6,7},{7,6},{8,9},{9,8},{10,11... | collective-permute-start | bytes 294920 | tf_op jit(solution)/shard_map/ppermute | solution.py:12
  114.6 17.6 %copy-start.23 = (bf16[128,384]{1,0:T(8,128)(2,1)}, bf16[128,384]{1,0:T(8,128)(2,1)S(1)}, u32[]{:S(2)}) copy-start(bf16[128,384]{1,0:T(8,128)(2,1)S(1)} %collective-permute-done.41) | copy-start | bytes 294916
  114.6 16.5 %copy-start.25 = (bf16[128,384]{1,0:T(8,128)(2,1)}, bf16[128,384]{1,0:T(8,128)(2,1)S(1)}, u32[]{:S(2)}) copy-start(bf16[128,384]{1,0:T(8,128)(2,1)S(1)} %collective-permute-done.42) | copy-start | bytes 294916
  114.6 16.5 %copy-start.26 = (bf16[128,384]{1,0:T(8,128)(2,1)}, bf16[128,384]{1,0:T(8,128)(2,1)S(1)}, u32[]{:S(2)}) copy-start(bf16[128,384]{1,0:T(8,128)(2,1)S(1)} %collective-permute-done.40) | copy-start | bytes 294916
  115.6 43.2 %collective-permute-start.43 = (bf16[4,128,384]{2,1,0:T(8,128)(2,1)}, bf16[4,128,384]{2,1,0:T(8,128)(2,1)}, u32[]{:S(2)}, u32[]{:S(2)}) collective-permute-start(bf16[4,128,384]{2,1,0:T(8,128)(2,1)} %pad_maximum_fusion.8), channel_id=1, source_target_pairs={{0,12},{4,8},{8,4},{12,0},{16,28},{20,24},{24,20},{28,16},{1,13},{... | collective-permute-start | bytes 1179656 | tf_op jit(solution)/shard_map/ppermute | solution.py:12
  118.8 40.0 %collective-permute-start.44 = (bf16[4,128,384]{2,1,0:T(8,128)(2,1)}, bf16[4,128,384]{2,1,0:T(8,128)(2,1)}, u32[]{:S(2)}, u32[]{:S(2)}) collective-permute-start(bf16[4,128,384]{2,1,0:T(8,128)(2,1)} %pad_maximum_fusion.8), channel_id=1, source_target_pairs={{0,8},{4,12},{8,0},{12,4},{16,24},{20,28},{24,16},{28,20},{1,9},{5... | collective-permute-start | bytes 1179656 | tf_op jit(solution)/shard_map/ppermute | solution.py:12
  118.8 42.9 %collective-permute-start.45 = (bf16[4,128,384]{2,1,0:T(8,128)(2,1)}, bf16[4,128,384]{2,1,0:T(8,128)(2,1)}, u32[]{:S(2)}, u32[]{:S(2)}) collective-permute-start(bf16[4,128,384]{2,1,0:T(8,128)(2,1)} %pad_maximum_fusion.8), channel_id=1, source_target_pairs={{0,4},{4,0},{8,12},{12,8},{16,20},{20,16},{24,28},{28,24},{1,5},{5... | collective-permute-start | bytes 1179656 | tf_op jit(solution)/shard_map/ppermute | solution.py:12
  132.2 30.1 %copy-start.24 = (bf16[128,384]{1,0:T(8,128)(2,1)S(1)}, bf16[128,384]{1,0:T(8,128)(2,1)}, u32[]{:S(2)}) copy-start(bf16[128,384]{1,0:T(8,128)(2,1)} %copy-done.23) | copy-start | bytes 294916
  132.9 1.6 collective-permute-start.27
  132.9 6.3 %collective-permute-start.28 = (bf16[128,512]{1,0:T(8,128)(2,1)S(1)}, bf16[128,512]{1,0:T(8,128)(2,1)S(1)}, u32[]{:S(2)}, u32[]{:S(2)}) collective-permute-start(bf16[128,512]{1,0:T(8,128)(2,1)S(1)} %get-tuple-element.113), channel_id=1, source_target_pairs={{0,2},{1,3},{2,0},{3,1},{4,6},{5,7},{6,4},{7,5},{8,10},{9,11},{10,... | collective-permute-start | bytes 393224 | tf_op jit(solution)/shard_map/ppermute | solution.py:12
  134.5 30.8 %collective-permute-start.15 = (bf16[448,896]{1,0:T(8,128)(2,1)S(1)}, bf16[448,896]{1,0:T(8,128)(2,1)S(1)}, u32[]{:S(2)}, u32[]{:S(2)}) collective-permute-start(bf16[448,896]{1,0:T(8,128)(2,1)S(1)} %pad_maximum_fusion.6.refs_0_), channel_id=1, source_target_pairs={{0,2},{1,3},{2,0},{3,1},{4,6},{5,7},{6,4},{7,5},{8,10},{9,11},{10,... | collective-permute-start | bytes 2408456 | tf_op jit(solution)/shard_map/ppermute | solution.py:12
  139.2 23.1 %copy-start.19 = (bf16[128,512]{1,0:T(8,128)(2,1)}, bf16[128,512]{1,0:T(8,128)(2,1)S(1)}, u32[]{:S(2)}) copy-start(bf16[128,512]{1,0:T(8,128)(2,1)S(1)} %collective-permute-done.28) | copy-start | bytes 393220
  139.2 19.2 %collective-permute-start.29 = (bf16[128,512]{1,0:T(8,128)(2,1)}, bf16[128,512]{1,0:T(8,128)(2,1)S(1)}, u32[]{:S(2)}, u32[]{:S(2)}) collective-permute-start(bf16[128,512]{1,0:T(8,128)(2,1)} %get-tuple-element.112), channel_id=1, source_target_pairs={{0,3},{1,2},{2,1},{3,0},{4,7},{5,6},{6,5},{7,4},{8,11},{9,10},{10,... | collective-permute-start | bytes 393224 | tf_op jit(solution)/shard_map/ppermute | solution.py:12
  158.4 3.9 %copy-start.21 = (bf16[128,512]{1,0:T(8,128)(2,1)}, bf16[128,512]{1,0:T(8,128)(2,1)S(1)}, u32[]{:S(2)}) copy-start(bf16[128,512]{1,0:T(8,128)(2,1)S(1)} %collective-permute-done.29) | copy-start | bytes 393220
  158.4 28.5 %collective-permute-start.14 = (bf16[448,896]{1,0:T(8,128)(2,1)S(1)}, bf16[448,896]{1,0:T(8,128)(2,1)S(1)}, u32[]{:S(2)}, u32[]{:S(2)}) collective-permute-start(bf16[448,896]{1,0:T(8,128)(2,1)S(1)} %pad_maximum_fusion.6.refs_0_), channel_id=1, source_target_pairs={{0,1},{1,0},{2,3},{3,2},{4,5},{5,4},{6,7},{7,6},{8,9},{9,8},{10,11... | collective-permute-start | bytes 2408456 | tf_op jit(solution)/shard_map/ppermute | solution.py:12
  158.7 15.8 %collective-permute-start.30 = (bf16[4,128,512]{2,1,0:T(8,128)(2,1)S(1)}, bf16[4,128,512]{2,1,0:T(8,128)(2,1)S(1)}, u32[]{:S(2)}, u32[]{:S(2)}) collective-permute-start(bf16[4,128,512]{2,1,0:T(8,128)(2,1)S(1)} %pad_maximum_fusion.7), channel_id=1, source_target_pairs={{0,12},{4,8},{8,4},{12,0},{16,28},{20,24},{24,20},{28,16},{1,13},{... | collective-permute-start | bytes 1572872 | tf_op jit(solution)/shard_map/ppermute | solution.py:12
  158.8 26.3 %collective-permute-start.31 = (bf16[4,128,512]{2,1,0:T(8,128)(2,1)S(1)}, bf16[4,128,512]{2,1,0:T(8,128)(2,1)S(1)}, u32[]{:S(2)}, u32[]{:S(2)}) collective-permute-start(bf16[4,128,512]{2,1,0:T(8,128)(2,1)S(1)} %pad_maximum_fusion.7), channel_id=1, source_target_pairs={{0,8},{4,12},{8,0},{12,4},{16,24},{20,28},{24,16},{28,20},{1,9},{5... | collective-permute-start | bytes 1572872 | tf_op jit(solution)/shard_map/ppermute | solution.py:12
  161.8 23.4 %collective-permute-start.32 = (bf16[4,128,512]{2,1,0:T(8,128)(2,1)S(1)}, bf16[4,128,512]{2,1,0:T(8,128)(2,1)S(1)}, u32[]{:S(2)}, u32[]{:S(2)}) collective-permute-start(bf16[4,128,512]{2,1,0:T(8,128)(2,1)S(1)} %pad_maximum_fusion.7), channel_id=1, source_target_pairs={{0,4},{4,0},{8,12},{12,8},{16,20},{20,16},{24,28},{28,24},{1,5},{5... | collective-permute-start | bytes 1572872 | tf_op jit(solution)/shard_map/ppermute | solution.py:12
  165.3 21.2 %copy-start.20 = (bf16[128,512]{1,0:T(8,128)(2,1)S(1)}, bf16[128,512]{1,0:T(8,128)(2,1)}, u32[]{:S(2)}) copy-start(bf16[128,512]{1,0:T(8,128)(2,1)} %copy-done.19) | copy-start | bytes 393220
  165.3 21.2 %copy-start.22 = (bf16[128,512]{1,0:T(8,128)(2,1)S(1)}, bf16[128,512]{1,0:T(8,128)(2,1)}, u32[]{:S(2)}) copy-start(bf16[128,512]{1,0:T(8,128)(2,1)} %copy-done.21) | copy-start | bytes 393220
  165.3 21.6 %collective-permute-start.16 = (bf16[448,896]{1,0:T(8,128)(2,1)S(1)}, bf16[448,896]{1,0:T(8,128)(2,1)S(1)}, u32[]{:S(2)}, u32[]{:S(2)}) collective-permute-start(bf16[448,896]{1,0:T(8,128)(2,1)S(1)} %collective-permute-done.15.refs_2_), channel_id=1, source_target_pairs={{0,1},{1,0},{2,3},{3,2},{4,5},{5,4},{6,7},{7,6},{8,9},{9,8},{10,11... | collective-permute-start | bytes 2408456 | tf_op jit(solution)/shard_map/ppermute | solution.py:12
  195.1 5.3 %collective-permute-start.18 = (bf16[320,896]{1,0:T(8,128)(2,1)S(1)}, bf16[320,896]{1,0:T(8,128)(2,1)S(1)}, u32[]{:S(2)}, u32[]{:S(2)}) collective-permute-start(bf16[320,896]{1,0:T(8,128)(2,1)S(1)} %convolution_convert_fusion), channel_id=1, source_target_pairs={{0,1},{1,0},{2,3},{3,2},{4,5},{5,4},{6,7},{7,6},{8,9},{9,8},{10,11... | collective-permute-start | bytes 1720328 | tf_op jit(solution)/shard_map/ppermute | solution.py:12
  198.0 4.7 %copy-start.3 = (bf16[4,4,128,896]{3,2,1,0:T(8,128)(2,1)S(1)}, bf16[4,4,128,896]{3,2,1,0:T(8,128)(2,1)}, u32[]{:S(2)}) copy-start(bf16[4,4,128,896]{3,2,1,0:T(8,128)(2,1)} %pad_maximum_fusion.3) | copy-start | bytes 11010052
  199.8 5.9 %collective-permute-start.17 = (bf16[320,896]{1,0:T(8,128)(2,1)S(1)}, bf16[320,896]{1,0:T(8,128)(2,1)S(1)}, u32[]{:S(2)}, u32[]{:S(2)}) collective-permute-start(bf16[320,896]{1,0:T(8,128)(2,1)S(1)} %convolution_convert_fusion.1), channel_id=1, source_target_pairs={{0,1},{1,0},{2,3},{3,2},{4,5},{5,4},{6,7},{7,6},{8,9},{9,8},{10,11... | collective-permute-start | bytes 1720328 | tf_op jit(solution)/shard_map/ppermute | solution.py:12
  202.1 15.0 %collective-permute-start.19 = (bf16[320,896]{1,0:T(8,128)(2,1)S(1)}, bf16[320,896]{1,0:T(8,128)(2,1)S(1)}, u32[]{:S(2)}, u32[]{:S(2)}) collective-permute-start(bf16[320,896]{1,0:T(8,128)(2,1)S(1)} %fusion.22), channel_id=1, source_target_pairs={{0,2},{1,3},{2,0},{3,1},{4,6},{5,7},{6,4},{7,5},{8,10},{9,11},{10,... | collective-permute-start | bytes 1720328 | tf_op jit(solution)/shard_map/ppermute | solution.py:12
  219.6 36.1 %all-to-all-start.1 = ((bf16[8,40,896]{2,1,0:T(8,128)(2,1)}), bf16[8,40,896]{2,1,0:T(8,128)(2,1)}, u32[]{:S(2)}, u32[]{:S(2)}) async-start(bf16[8,40,896]{2,1,0:T(8,128)(2,1)} %bitcast.57), calls=%async_computation.1 | async-start | bytes 1146880 | tf_op jit(solution)/shard_map/all_to_all | solution.py:282
  223.8 3.8 %copy-start.5 = (bf16[512,512]{1,0:T(8,128)(2,1)S(1)}, bf16[512,512]{1,0:T(8,128)(2,1)}, u32[]{:S(2)}) copy-start(bf16[512,512]{1,0:T(8,128)(2,1)} %copy-done.4) | copy-start | bytes 1572868
  223.8 3.8 %copy-start.7 = (bf16[512,512]{1,0:T(8,128)(2,1)S(1)}, bf16[512,512]{1,0:T(8,128)(2,1)}, u32[]{:S(2)}) copy-start(bf16[512,512]{1,0:T(8,128)(2,1)} %copy-done.6) | copy-start | bytes 1572868
  223.8 3.8 %copy-start.9 = (bf16[512,384]{1,0:T(8,128)(2,1)S(1)}, bf16[512,384]{1,0:T(8,128)(2,1)}, u32[]{:S(2)}) copy-start(bf16[512,384]{1,0:T(8,128)(2,1)} %copy-done.8) | copy-start | bytes 1179652
  227.9 27.8 %copy-start.34 = (f32[128,2]{0,1:T(2,128)S(1)}, f32[128,2]{0,1:T(2,128)}, u32[]{:S(2)}) copy-start(f32[128,2]{0,1:T(2,128)} %param.14) | copy-start | bytes 3076
  227.9 30.1 %copy-start.1 = (bf16[128,896]{1,0:T(8,128)(2,1)S(1)}, bf16[128,896]{1,0:T(8,128)(2,1)}, u32[]{:S(2)}) copy-start(bf16[128,896]{1,0:T(8,128)(2,1)} %param.12) | copy-start | bytes 688132
  (3 other events, 11.4 us)
Sparse Core Ops, SparseCore 0:
  198.1 46.8 all-gather.4

commit v2 on v1

--- a/solution.py
+++ b/solution.py
@@ -94,12 +94,19 @@
     return [(0, first), (first, width - first)]
 
 
-def one_hot_rows(positions, source):
-    rows = source.shape[0]
-    selector = (positions[:, None] == jnp.arange(rows, dtype=jnp.int32)[None, :]).astype(
+def one_hot(positions, count):
+    selector = (positions[:, None] == jnp.arange(count, dtype=jnp.int32)[None, :]).astype(
         jnp.bfloat16
     )
+    return lax.optimization_barrier(selector)
+
+
+def pick_rows(selector, source):
     return jnp.dot(selector, source, preferred_element_type=jnp.float32).astype(jnp.bfloat16)
+
+
+def after(value, *others):
+    return lax.optimization_barrier((value,) + others)[0]
 
 
 def columns_to_device(own, t, nt, off, width):
@@ -111,15 +118,11 @@
     return jnp.concatenate(found, axis=0)
 
 
-def rows_to_device(pieces, t, nt):
-    found = []
-    for k in range(nt):
-        piece = lax.dynamic_index_in_dim(pieces, t ^ k, 0, keepdims=False)
-        found.append(xor_permute(piece, "tensor", nt, k) if k else piece)
-    return found
-
-
-def merge_two(own, perm, cluster, owners, e, t, ne, nt):
+def rows_to_device(pieces, nt):
+    return [xor_permute(pieces[k], "tensor", nt, k) if k else pieces[k] for k in range(nt)]
+
+
+def merge_two(own, perm, cluster, owners, e, t, ne, nt, beside):
     rows, model = own.shape
     half = ne // 2
     block = model // nt
@@ -135,15 +138,19 @@
     keep = jnp.where(owner_side[0] == side, 0, 1)
     give = jnp.where(owner_side[0] != side, 0, 1)
     spans = chunks_of(block)
+    order = [(q ^ k) for k in range(half)]
+    selectors = [
+        one_hot(lax.dynamic_index_in_dim(placed, j, 1, keepdims=False).reshape(-1), rows * nt)
+        for j in order
+    ]
 
     partials = []
     for off, width in spans:
         source = columns_to_device(own, t, nt, off, width)
-        arrived = []
-        for k in range(half):
-            positions = lax.dynamic_index_in_dim(placed, q ^ k, 1, keepdims=False).reshape(-1)
-            aligned = one_hot_rows(positions, source)
-            arrived.append(xor_permute(aligned, "expert", ne, k) if k else aligned)
+        arrived = [None] * half
+        for k in list(range(1, half)) + [0]:
+            aligned = pick_rows(selectors[k], source)
+            arrived[k] = xor_permute(aligned, "expert", ne, k) if k else aligned
         partials.append(arrived)
 
     def partial_of(arrived, which):
@@ -152,16 +159,17 @@
             total = total + jnp.where(member[k] == which, arrived[k].astype(jnp.float32), 0.0)
         return total
 
-    def finish(partials, kept, given):
+    def finish(partials, kept, given, beside=()):
         gathered = []
-        for arrived, (off, width) in zip(partials, spans):
+        for place, (arrived, (off, width)) in enumerate(zip(partials, spans)):
             sent = partial_of(arrived, given).astype(jnp.bfloat16)
+            if place < len(beside):
+                sent = after(sent, beside[place])
             other = xor_permute(sent, "expert", ne, half)
             mean = (
                 (partial_of(arrived, kept) + other.astype(jnp.float32)) * inverse[kept]
             ).astype(jnp.bfloat16)
-            back = rows_to_device(mean.reshape(nt, sub, width), t, nt)
-            lines = jnp.stack(back)
+            lines = jnp.stack(rows_to_device(mean.reshape(nt, sub, width), nt))
             gathered.append(
                 [xor_permute(lines, "expert", ne, k) if k else lines for k in range(half)]
             )
@@ -186,7 +194,7 @@
         whole = jnp.concatenate(ordered, axis=2).reshape(rows, model)
         return jnp.where(mine, whole, jnp.zeros_like(whole))
 
-    first = finish(partials, keep, give)
+    first = finish(partials, keep, give, beside)
 
     def second(args):
         first, partials = args
@@ -197,14 +205,16 @@
     )
 
 
-def merge_any(own, perm, cluster, owners, e, t, ne, nt):
+def merge_any(own, perm, cluster, owners, e, t, ne, nt, beside):
     rows, model = own.shape
     block = model // nt
     clusters = owners.shape[0]
     sub = rows // ne
     placed = ((perm // rows) ^ t) * rows + perm % rows
     placed = placed.reshape(nt, ne, sub).transpose(1, 0, 2).reshape(-1)
-    aligned = one_hot_rows(placed, columns_to_device(own, t, nt, 0, block))
+    aligned = pick_rows(
+        one_hot(placed, rows * nt), columns_to_device(own, t, nt, 0, block)
+    )
     arrived = lax.all_to_all(aligned, "expert", split_axis=0, concat_axis=0, tiled=True)
     arrived = arrived.reshape(ne, nt, sub, block)
     member = cluster[None, :] == jnp.arange(clusters, dtype=jnp.int32)[:, None]
@@ -215,10 +225,8 @@
             jnp.where(member[c][:, None, None, None], arrived.astype(jnp.float32), 0.0), axis=0
         )
         means.append((total * inverse[c]).astype(jnp.bfloat16))
-    means = jnp.stack(means, axis=1)
-    back = lax.all_to_all(
-        means.reshape(nt * clusters * sub, block), "tensor", split_axis=0, concat_axis=0, tiled=True
-    ).reshape(nt, clusters, sub, block)
+    back = jnp.stack(rows_to_device(jnp.stack(means, axis=1), nt))
+    back = jnp.take(back, jnp.arange(nt, dtype=jnp.int32) ^ t, axis=0)
     lines = back.transpose(1, 2, 0, 3).reshape(clusters, sub, model)
     outgoing = jnp.zeros((ne, sub, model), jnp.bfloat16).at[owners].set(lines)
     return lax.all_to_all(
@@ -248,9 +256,7 @@
     model = own.shape[1]
     block = model // nt
 
-    perm = lax.all_gather(hidden_perm[0], "tensor", axis=0, tiled=True)
-    merge = merge_two if ne == 8 and owners.shape[0] == 2 else merge_any
-    merged = merge(own, perm, cluster, owners, e, t, ne, nt)
+    perm = jnp.concatenate(gather_tensor(hidden_perm[0], nt))
 
     flat = routes.reshape(-1)
     pairs = jnp.arange(flat.shape[0], dtype=jnp.int32)
@@ -285,6 +291,9 @@
     picked = picked.reshape(top, tok_rows, block)
     mixed = jnp.sum(gate_values.T[:, :, None] * picked, axis=0).astype(jnp.bfloat16)
 
+    merge = merge_two if ne == 8 and owners.shape[0] == 2 else merge_any
+    merged = merge(own, perm, cluster, owners, e, t, ne, nt, (hidden, returned))
+
     everyone = lax.all_gather(probe_hidden, "expert", axis=0)
     partner = lax.dynamic_index_in_dim(everyone, owners[cluster[e]], 0, keepdims=False)
     partner_full = lax.all_gather(partner, "tensor", axis=1, tiled=True)

time: 266 us -> 234 us (0.88)
  waiting for transfers between devices: 89.4 us -> 63.5 us
  blocking collectives: 20.7 us -> 6.87 us
  local copies, waits for them, and re-layouts: 14.4 us -> 18.4 us
    all_gather x1, waiting for transfers between devices: 17 us -> 0.01 us  [on_device(): everyone = lax.all_gather(probe_hidden, 'expert', axis=0)]
    all_gather x1 -> x0, blocking collectives: 13.6 us -> none  [on_device(): perm = lax.all_gather(hidden_perm[0], 'tensor', axis=0, tiled=True)]
    ppermute x32 -> x35, waiting for transfers between devices: 72.3 us -> 63.5 us  [xor_permute(): return lax.ppermute(value, axis, [(i, i ^ k) for i in range(size)])]
    select_n x0 -> x4, local copies, waits for them, and re-layouts: none -> 3.77 us  [finish(): chosen = jnp.where(order_t[b] == k, joined[:, k], chosen)]
    convert_element_type x0 -> x4, other arithmetic: none -> 3.33 us  [one_hot(): (positions[:, None] == jnp.arange(count, dtype=jnp.int32)[None, :]).astyp...]
    ppermute x32 -> x35, starting transfers between devices: 31.5 us -> 32 us  [xor_permute(): return lax.ppermute(value, axis, [(i, i ^ k) for i in range(size)])]
  transfers between devices with their start and end apart: 35 -> 38, of which waited for: 11 -> 9; matrix products, arithmetic and copies ran while one was open for 25% -> 31% of each run, Pallas kernels for 0% -> 3%
where the time goes in v2:
time: 234 us; the launch traced here: 232 us
  waiting for transfers between devices  63.5 us (27%)
  starting transfers between devices  42.4 us (18%)
  matrix products  39.2 us (17%)
  between operations  34.6 us (15%)
  other arithmetic  20.2 us (9%)
  local copies, waits for them, and re-layouts  18.4 us (8%)
  Pallas kernels  6.91 us (3%)
  blocking collectives  6.87 us (3%)
    ppermute x35, waiting for transfers between devices, xor_permute(): return lax.ppermute(value, axis, [(i, i ^ k) for i in range(size)])  63.5 us
    ppermute x35, starting transfers between devices, xor_permute(): return lax.ppermute(value, axis, [(i, i ^ k) for i in range(size)])  32 us
    dot_general x8, matrix products, pick_rows(): jnp.dot(selector, source, preferred_element_type=jnp.float32)  27.1 us
    pallas_call x1, Pallas kernels, ffn(): pl.pallas_call(functools.partial(ffn_kernel, count), out_shape=jax.ShapeD...  6.91 us
    all_gather x1, blocking collectives, on_device(): partner_full = lax.all_gather(partner, 'tensor', axis=1, tiled=True)  6.87 us
    dot_general x4, matrix products, on_device(): jnp.dot(routed_hidden, lax.dynamic_slice(own, (0, (t ^ k) * block), (own....  6.06 us
    all_to_all x1, starting transfers between devices, on_device(): lax.all_to_all(outgoing, 'expert', split_axis=0, concat_axis=0, tiled=True)  5.81 us
    dynamic_slice x2, local copies, waits for them, and re-layouts, columns_to_device(): lax.dynamic_slice(own, (0, (t ^ k) * block + off), (own.shape[0], width))  5.34 us
  transfers between devices with their start and end apart: 38, of which 9 were waited for; matrix products, arithmetic and copies ran while one was open for 31% of the time, Pallas kernels for 3%

profile of v2, /device:TPU:0, one launch (start us, length us, event | category | flops | bytes accessed | tf_op | source)
XLA Modules:
  0.0 232.1 jit_solution(12818727405761601026)
XLA Ops:
  7.2 3.0 %collective-permute-start.21 = (s32[512]{0:T(512)}, s32[512]{0:T(512)S(1)}, u32[]{:S(2)}, u32[]{:S(2)}) collective-permute-start(s32[512]{0:T(512)} %bitcast.209), channel_id=1, source_target_pairs={{0,2},{1,3},{2,0},{3,1},{4,6},{5,7},{6,4},{7,5},{8,10},{9,11},{10,... | collective-permute-start | bytes 6152 | tf_op jit(solution)/shard_map/ppermute | solution.py:12
  10.2 2.8 %dynamic-slice_bitcast_fusion.3 = (bf16[512,512]{1,0:T(8,128)(2,1)S(1)}, bf16[512,512]{1,0:T(8,128)(2,1)}, bf16[512,512]{1,0:T(8,128)(2,1)}, bf16[512,512]{1,0:T(8,128)(2,1)}) fusion(bf16[1,512,3584]{2,1,0:T(8,128)(2,1)} %param.18, s32[]{:T(128)S(6)} %select_n.781, s32[]{:T(128)S(6)} %select_n.784, s32[]{:T(128)S(6)} %select_n.783, s32[]{:T(128)S(6)} %select_n.782), kind=kLoop, calls=%fused_computation.125 | loop fusion | bytes 4194320 | tf_op jit(solution)/shard_map/dynamic_slice | solution.py:116
  13.6 1.3 collective-permute-start.25
  15.6 1.1 convolution_convert_fusion.2
  16.7 5.8 %all-to-all-start = ((bf16[8,40,896]{2,1,0:T(8,128)(2,1)}), bf16[8,40,896]{2,1,0:T(8,128)(2,1)S(1)}, u32[]{:S(2)}, u32[]{:S(2)}) async-start(bf16[8,40,896]{2,1,0:T(8,128)(2,1)} %bitcast.42), calls=%async_computation | async-start | bytes 1146880 | tf_op jit(solution)/shard_map/all_to_all | solution.py:273
  24.6 2.6 %dynamic-slice_bitcast_fusion.7 = (bf16[512,384]{1,0:T(8,128)(2,1)}, bf16[512,384]{1,0:T(8,128)(2,1)}, bf16[512,384]{1,0:T(8,128)(2,1)}, bf16[512,384]{1,0:T(8,128)(2,1)}) fusion(bf16[1,512,3584]{2,1,0:T(8,128)(2,1)} %param.18, s32[]{:T(128)S(6)} %select_n.826, s32[]{:T(128)S(6)} %select_n.827, s32[]{:T(128)S(6)} %select_n.829, s32[]{:T(128)S(6)} %select_n.828), kind=kLoop, calls=%fused_computation.134 | loop fusion | bytes 3145744 | tf_op jit(solution)/shard_map/dynamic_slice | solution.py:116
  36.4 2.1 fusion.7
  38.9 1.2 collective-permute-start.38
  40.2 3.5 %convolution_convert_fusion.5 = bf16[512,512]{0,1:T(8,128)(2,1)} fusion(bf16[512,2048]{1,0:T(8,128)(2,1)S(1)} %fusion.5, bf16[512,512]{1,0:T(8,128)(2,1)} %collective-permute-done.25, bf16[512,512]{1,0:T(8,128)(2,1)} %collective-permute-done.24, bf16[512,512]{1,0:T(8,128)(2,1)} %collective-permute-done.23, bf16[512,512]{1,0:T(8,128)(2,1)S(1)} %get-tuple-element.174), kind=kOutput, calls=%fused_computation.64 | convolution fusion | flops 1082392576 | bytes 4718592 | tf_op jit(solution)/shard_map/dot_general | solution.py:105
  43.7 1.7 collective-permute-start.26
  45.4 3.6 %convolution_convert_fusion.4 = bf16[512,512]{0,1:T(8,128)(2,1)} fusion(bf16[512,2048]{1,0:T(8,128)(2,1)S(1)} %fusion.6, bf16[512,512]{1,0:T(8,128)(2,1)} %collective-permute-done.25, bf16[512,512]{1,0:T(8,128)(2,1)} %collective-permute-done.24, bf16[512,512]{1,0:T(8,128)(2,1)} %collective-permute-done.23, bf16[512,512]{1,0:T(8,128)(2,1)} %copy-done.33), kind=kOutput, calls=%fused_computation.63 | convolution fusion | flops 1082392576 | bytes 4718592 | tf_op jit(solution)/shard_map/dot_general | solution.py:105
  49.1 1.2 collective-permute-start.15
  50.3 3.4 %convolution_convert_fusion.3 = bf16[512,512]{0,1:T(8,128)(2,1)S(1)} fusion(bf16[512,2048]{1,0:T(8,128)(2,1)} %fusion.7, bf16[512,512]{1,0:T(8,128)(2,1)} %collective-permute-done.25, bf16[512,512]{1,0:T(8,128)(2,1)} %collective-permute-done.24, bf16[512,512]{1,0:T(8,128)(2,1)} %collective-permute-done.23, bf16[512,512]{1,0:T(8,128)(2,1)} %copy-done.33), kind=kOutput, calls=%fused_computation.62 | convolution fusion | flops 1082392576 | bytes 4718592 | tf_op jit(solution)/shard_map/dot_general | solution.py:105
  53.8 1.5 collective-permute-start.27
  55.5 3.2 %convolution_convert_fusion.9 = bf16[512,384]{0,1:T(8,128)(2,1)} fusion(bf16[512,2048]{1,0:T(8,128)(2,1)S(1)} %copy-done.13, bf16[512,384]{1,0:T(8,128)(2,1)} %collective-permute-done.38, bf16[512,384]{1,0:T(8,128)(2,1)} %collective-permute-done.37, bf16[512,384]{1,0:T(8,128)(2,1)} %collective-permute-done.36, bf16[512,384]{1,0:T(8,128)(2,1)S(1)} %copy-done.35), kind=kOutput, calls=%fused_computation.69 | convolution fusion | flops 811794432 | bytes 4063232 | tf_op jit(solution)/shard_map/dot_general | solution.py:105
  58.6 1.0 collective-permute-start.14
  59.7 13.3 %collective-permute-done.15.refs_2_ = bf16[448,896]{1,0:T(8,128)(2,1)S(1)} collective-permute-done((bf16[448,896]{1,0:T(8,128)(2,1)S(1)}, bf16[448,896]{1,0:T(8,128)(2,1)S(1)}, u32[]{:S(2)}, u32[]{:S(2)}) %collective-permute-start.15) | collective-permute-done | bytes 802848 | tf_op jit(solution)/shard_map/ppermute | solution.py:12
  72.9 3.0 %convolution_convert_fusion.8 = bf16[512,384]{0,1:T(8,128)(2,1)} fusion(bf16[512,2048]{1,0:T(8,128)(2,1)S(1)} %copy-done.11, bf16[512,384]{1,0:T(8,128)(2,1)} %collective-permute-done.38, bf16[512,384]{1,0:T(8,128)(2,1)} %collective-permute-done.37, bf16[512,384]{1,0:T(8,128)(2,1)} %collective-permute-done.36, bf16[512,384]{1,0:T(8,128)(2,1)S(1)} %copy-done.35), kind=kOutput, calls=%fused_computation.68 | convolution fusion | flops 811794432 | bytes 4063232 | tf_op jit(solution)/shard_map/dot_general | solution.py:105
  76.0 1.5 collective-permute-start.39
  77.5 1.6 collective-permute-start.40
  79.1 3.1 %fusion.21 = (bf16[512,512]{0,1:T(8,128)(2,1)S(1)}, bf16[512,512]{0,1:T(8,128)(2,1)S(1)}) fusion(bf16[512,512]{0,1:T(8,128)(2,1)S(1)} %collective-permute-done.26, bf16[512,512]{0,1:T(8,128)(2,1)S(1)} %collective-permute-done.27, bf16[512,512]{0,1:T(8,128)(2,1)S(1)} %collective-permute-done.28, pred[]{:T(512)S(6)} %eq.516, pred[]{:T(512)S(6)} %eq.515, ...), kind=kOutput, calls=%fused_computation.80 | convolution fusion | flops 1085538304 | bytes 6815748 | tf_op jit(solution)/shard_map/dot_general | solution.py:105
  82.2 6.9 %ffn.1 = bf16[448,512]{1,0:T(8,128)(2,1)S(1)} custom-call(s32[1]{0:T(128)} %bitcast.39.where_ref, bf16[448,896]{1,0:T(8,128)(2,1)S(1)} %pad_maximum_fusion.6.refs_0_, bf16[448,896]{1,0:T(8,128)(2,1)S(1)} %collective-permute-done.14.refs_1_, bf16[448,896]{1,0:T(8,128)(2,1)S(1)} %collective-permute-done.15.refs_2_, ...), custom_call_target="tpu_custom_call" | custom-call | flops 3288334336 | bytes 11010048 | tf_op jit(solution)/shard_map/ffn/pallas_call | solution.py:68
  89.1 2.6 %collective-permute-start.29 = (bf16[512,512]{0,1:T(8,128)(2,1)S(1)}, bf16[512,512]{0,1:T(8,128)(2,1)S(1)}, u32[]{:S(2)}, u32[]{:S(2)}) collective-permute-start(bf16[512,512]{0,1:T(8,128)(2,1)S(1)} %get-tuple-element.60), channel_id=1, source_target_pairs={{0,16},{4,20},{8,24},{12,28},{16,0},{20,4},{24,8},{28,12},{1,17},{... | collective-permute-start | bytes 1572872 | tf_op jit(solution)/shard_map/ppermute | solution.py:12
  91.7 3.1 %convolution_convert_fusion.7 = bf16[512,384]{0,1:T(8,128)(2,1)} fusion(bf16[512,2048]{1,0:T(8,128)(2,1)S(1)} %copy-done.9, bf16[512,384]{1,0:T(8,128)(2,1)} %collective-permute-done.38, bf16[512,384]{1,0:T(8,128)(2,1)} %collective-permute-done.37, bf16[512,384]{1,0:T(8,128)(2,1)} %collective-permute-done.36, bf16[512,384]{1,0:T(8,128)(2,1)S(1)} %copy-done.35), kind=kOutput, calls=%fused_computation.67 | convolution fusion | flops 811794432 | bytes 4063232 | tf_op jit(solution)/shard_map/dot_general | solution.py:105
  94.8 1.7 collective-permute-start.41
  97.1 17.9 %collective-permute-done.29 = bf16[512,512]{0,1:T(8,128)(2,1)S(1)} collective-permute-done((bf16[512,512]{0,1:T(8,128)(2,1)S(1)}, bf16[512,512]{0,1:T(8,128)(2,1)S(1)}, u32[]{:S(2)}, u32[]{:S(2)}) %collective-permute-start.29) | collective-permute-done | bytes 524320 | tf_op jit(solution)/shard_map/ppermute | solution.py:12
  115.1 1.1 fusion.17
  116.4 1.3 convolution_convert_fusion.1
  119.1 1.2 collective-permute-start.32
  120.3 1.7 fusion.10
  122.0 2.8 %collective-permute-done.31 = bf16[128,512]{0,1:T(8,128)(2,1)S(1)} collective-permute-done((bf16[128,512]{0,1:T(8,128)(2,1)S(1)}, bf16[128,512]{0,1:T(8,128)(2,1)S(1)}, u32[]{:S(2)}, u32[]{:S(2)}) %collective-permute-start.31) | collective-permute-done | bytes 131104 | tf_op jit(solution)/shard_map/ppermute | solution.py:12
  124.8 2.0 collective-permute-done.32
  127.4 0.9 pad_maximum_fusion.7
  128.3 0.8 collective-permute-start.33
  129.1 1.7 collective-permute-start.34
  130.8 1.0 collective-permute-start.35
  131.8 4.2 %fusion.39 = (bf16[512,384]{0,1:T(8,128)(2,1)}, bf16[512,384]{0,1:T(8,128)(2,1)}) fusion(bf16[512,384]{0,1:T(8,128)(2,1)} %collective-permute-done.39, bf16[512,384]{0,1:T(8,128)(2,1)} %collective-permute-done.40, bf16[512,384]{0,1:T(8,128)(2,1)S(1)} %collective-permute-done.41, pred[]{:T(512)S(6)} %eq.516, pred[]{:T(512)S(6)} %eq.515, pred[]{:T(512)S(6)} %eq.514, ...), kind=kOutput, calls=%fused_computation.115 | convolution fusion | flops 814153728 | bytes 5636100 | tf_op jit(solution)/shard_map/dot_general | solution.py:105
  136.0 5.9 %collective-permute-done.19 = bf16[320,896]{1,0:T(8,128)(2,1)S(1)} collective-permute-done((bf16[320,896]{1,0:T(8,128)(2,1)S(1)}, bf16[320,896]{1,0:T(8,128)(2,1)S(1)}, u32[]{:S(2)}, u32[]{:S(2)}) %collective-permute-start.19) | collective-permute-done | bytes 573472 | tf_op jit(solution)/shard_map/ppermute | solution.py:12
  141.9 2.5 %fusion.9 = bf16[320,896]{1,0:T(8,128)(2,1)} fusion(bf16[320,896]{1,0:T(8,128)(2,1)S(1)} %collective-permute-done.19, bf16[320,896]{1,0:T(8,128)(2,1)S(1)} %collective-permute-done.17, bf16[1,512,3584]{2,1,0:T(8,128)(2,1)} %param.18, s32[]{:T(128)S(6)} %select_n.781, bf16[448,512]{1,0:T(8,128)(2,1)S(1)} %ffn.1), kind=kOutput, calls=%fused_computation.51 | convolution fusion | flops 295034880 | bytes 2965508 | tf_op jit(solution)/shard_map/dot_general | solution.py:280
  159.8 4.5 %all-to-all-start.1 = ((bf16[8,40,896]{2,1,0:T(8,128)(2,1)}), bf16[8,40,896]{2,1,0:T(8,128)(2,1)}, u32[]{:S(2)}, u32[]{:S(2)}) async-start(bf16[8,40,896]{2,1,0:T(8,128)(2,1)} %bitcast.48), calls=%async_computation.1 | async-start | bytes 1146880 | tf_op jit(solution)/shard_map/all_to_all | solution.py:288
  164.3 10.2 %collective-permute-done.34 = bf16[4,128,512]{1,2,0:T(8,128)(2,1)S(1)} collective-permute-done((bf16[4,128,512]{1,2,0:T(8,128)(2,1)}, bf16[4,128,512]{1,2,0:T(8,128)(2,1)S(1)}, u32[]{:S(2)}, u32[]{:S(2)}) %collective-permute-start.34) | collective-permute-done | bytes 524320 | tf_op jit(solution)/shard_map/ppermute | solution.py:12
  174.6 1.2 select_select_fusion.18
  175.8 2.2 fusion.35
  178.2 1.1 collective-permute-start.44
  179.3 0.7 collective-permute-start.45
  180.0 1.1 select_select_fusion.19
  181.2 2.6 %collective-permute-done.44 = bf16[128,384]{0,1:T(8,128)(2,1)S(1)} collective-permute-done((bf16[128,384]{0,1:T(8,128)(2,1)S(1)}, bf16[128,384]{0,1:T(8,128)(2,1)S(1)}, u32[]{:S(2)}, u32[]{:S(2)}) %collective-permute-start.44) | collective-permute-done | bytes 98336 | tf_op jit(solution)/shard_map/ppermute | solution.py:12
  183.8 1.2 collective-permute-done.45
  185.0 0.8 pad_maximum_fusion.8
  185.8 0.8 collective-permute-start.46
  186.7 2.4 %collective-permute-start.47 = (bf16[4,128,384]{1,2,0:T(8,128)(2,1)}, bf16[4,128,384]{1,2,0:T(8,128)(2,1)S(1)}, u32[]{:S(2)}, u32[]{:S(2)}) collective-permute-start(bf16[4,128,384]{1,2,0:T(8,128)(2,1)} %pad_maximum_fusion.8), channel_id=1, source_target_pairs={{0,8},{4,12},{8,0},{12,4},{16,24},{20,28},{24,16},{28,20},{1,9},{5... | collective-permute-start | bytes 1179656 | tf_op jit(solution)/shard_map/ppermute | solution.py:12
  189.3 0.9 constant_dynamic-slice_fusion.4
  190.3 6.9 %all-gather.1 = bf16[1,128,2048]{2,1,0:T(8,128)(2,1)S(1)} all-gather(bf16[1,128,512]{2,1,0:T(8,128)(2,1)S(1)} %constant_dynamic-slice_fusion.4), channel_id=3, replica_groups=mesh['expert'=8,'tensor'=4] {'tensor'}, dimensions={2}, use_global_device_ids=true | all-gather | bytes 655360 | tf_op jit(solution)/shard_map/all_gather | solution.py:299
  197.1 2.7 %multiply_bitcast_fusion = f32[1,512,2048]{2,1,0:T(8,128)} fusion(bf16[1,128,2048]{2,1,0:T(8,128)(2,1)S(1)} %all-gather.1, bf16[448,512]{1,0:T(8,128)(2,1)S(1)} %ffn.1), kind=kOutput, calls=%fused_computation.36 | convolution fusion | flops 269484032 | bytes 4849664 | tf_op jit(solution)/shard_map/dot_general | solution.py:301
  199.9 7.5 %collective-permute-done.47 = bf16[4,128,384]{1,2,0:T(8,128)(2,1)S(1)} collective-permute-done((bf16[4,128,384]{1,2,0:T(8,128)(2,1)}, bf16[4,128,384]{1,2,0:T(8,128)(2,1)S(1)}, u32[]{:S(2)}, u32[]{:S(2)}) %collective-permute-start.47) | collective-permute-done | bytes 393248 | tf_op jit(solution)/shard_map/ppermute | solution.py:12
  207.4 1.2 select_select_fusion.22
  208.7 1.2 select_select_fusion.23
  210.1 0.7 pad_maximum_fusion.3
  210.9 1.8 copy-done.3
  213.5 1.3 copy.101
  214.8 2.2 select_select_fusion.13
  217.0 1.3 copy.103
  218.9 3.4 %maximum_select_fusion.1 = bf16[512,3584]{1,0:T(8,128)(2,1)} fusion(bf16[512,896]{1,0:T(8,128)(2,1)S(1)} %bitcast.165, bf16[512,896]{1,0:T(8,128)(2,1)} %bitcast.164, bf16[512,896]{1,0:T(8,128)(2,1)S(1)} %bitcast.162, bf16[512,896]{1,0:T(8,128)(2,1)} %bitcast.163, pred[]{:T(512)S(6)} %eq.489), kind=kLoop, calls=%fused_computation.42 | loop fusion | flops 16515072 | bytes 7340033 | tf_op jit(solution)/shard_map/jit(_where)/select_n | solution.py:195
  223.0 2.3 fusion.11
  (166 shorter events, 14.1 us)
Async XLA Ops:
  7.2 8.4 %copy-start = (bf16[128,896]{1,0:T(8,128)(2,1)S(1)}, bf16[128,896]{1,0:T(8,128)(2,1)}, u32[]{:S(2)}) copy-start(bf16[128,896]{1,0:T(8,128)(2,1)} %param.12) | copy-start | bytes 688132
  7.2 7.7 %copy-start.38 = (s32[128,2]{0,1:T(2,128)S(1)}, s32[128,2]{0,1:T(2,128)}, u32[]{:S(2)}) copy-start(s32[128,2]{0,1:T(2,128)} %param.13) | copy-start | bytes 3076
  7.2 20.0 %collective-permute-start.21 = (s32[512]{0:T(512)}, s32[512]{0:T(512)S(1)}, u32[]{:S(2)}, u32[]{:S(2)}) collective-permute-start(s32[512]{0:T(512)} %bitcast.209), channel_id=1, source_target_pairs={{0,2},{1,3},{2,0},{3,1},{4,6},{5,7},{6,4},{7,5},{8,10},{9,11},{10,... | collective-permute-start | bytes 6152 | tf_op jit(solution)/shard_map/ppermute | solution.py:12
  10.2 24.6 %collective-permute-start.20 = (s32[512]{0:T(512)}, s32[512]{0:T(512)S(1)}, u32[]{:S(2)}, u32[]{:S(2)}) collective-permute-start(s32[512]{0:T(512)} %bitcast.210), channel_id=1, source_target_pairs={{0,1},{1,0},{2,3},{3,2},{4,5},{5,4},{6,7},{7,6},{8,9},{9,8},{10,11... | collective-permute-start | bytes 6152 | tf_op jit(solution)/shard_map/ppermute | solution.py:12
  10.2 12.4 %copy-start.40 = (s32[2]{0:T(128)S(1)}, s32[2]{0:T(128)}, u32[]{:S(2)}) copy-start(s32[2]{0:T(128)} %param.21) | copy-start | bytes 28
  10.2 13.0 %copy-start.2 = (s32[8]{0:T(128)S(1)}, s32[8]{0:T(128)}, u32[]{:S(2)}) copy-start(s32[8]{0:T(128)} %param.20) | copy-start | bytes 100
  13.0 27.2 %copy-start.33 = (bf16[512,512]{1,0:T(8,128)(2,1)}, bf16[512,512]{1,0:T(8,128)(2,1)S(1)}, u32[]{:S(2)}) copy-start(bf16[512,512]{1,0:T(8,128)(2,1)S(1)} %get-tuple-element.174) | copy-start | bytes 1572868
  13.0 22.5 %copy-start.39 = (s32[1,512]{1,0:T(1,128)S(1)}, s32[1,512]{1,0:T(1,128)}, u32[]{:S(2)}) copy-start(s32[1,512]{1,0:T(1,128)} %param.19) | copy-start | bytes 6148
  13.0 25.9 %collective-permute-start.23 = (bf16[512,512]{1,0:T(8,128)(2,1)}, bf16[512,512]{1,0:T(8,128)(2,1)}, u32[]{:S(2)}, u32[]{:S(2)}) collective-permute-start(bf16[512,512]{1,0:T(8,128)(2,1)} %get-tuple-element.177), channel_id=1, source_target_pairs={{0,1},{1,0},{2,3},{3,2},{4,5},{5,4},{6,7},{7,6},{8,9},{9,8},{10,11... | collective-permute-start | bytes 1572872 | tf_op jit(solution)/shard_map/ppermute | solution.py:12
  13.5 26.7 %collective-permute-start.24 = (bf16[512,512]{1,0:T(8,128)(2,1)}, bf16[512,512]{1,0:T(8,128)(2,1)}, u32[]{:S(2)}, u32[]{:S(2)}) collective-permute-start(bf16[512,512]{1,0:T(8,128)(2,1)} %get-tuple-element.176), channel_id=1, source_target_pairs={{0,2},{1,3},{2,0},{3,1},{4,6},{5,7},{6,4},{7,5},{8,10},{9,11},{10,... | collective-permute-start | bytes 1572872 | tf_op jit(solution)/shard_map/ppermute | solution.py:12
  13.6 26.6 %collective-permute-start.25 = (bf16[512,512]{1,0:T(8,128)(2,1)}, bf16[512,512]{1,0:T(8,128)(2,1)}, u32[]{:S(2)}, u32[]{:S(2)}) collective-permute-start(bf16[512,512]{1,0:T(8,128)(2,1)} %get-tuple-element.175), channel_id=1, source_target_pairs={{0,3},{1,2},{2,1},{3,0},{4,7},{5,6},{6,5},{7,4},{8,11},{9,10},{10,... | collective-permute-start | bytes 1572872 | tf_op jit(solution)/shard_map/ppermute | solution.py:12
  16.7 32.3 %all-to-all-start = ((bf16[8,40,896]{2,1,0:T(8,128)(2,1)}), bf16[8,40,896]{2,1,0:T(8,128)(2,1)S(1)}, u32[]{:S(2)}, u32[]{:S(2)}) async-start(bf16[8,40,896]{2,1,0:T(8,128)(2,1)} %bitcast.42), calls=%async_computation | async-start | bytes 1146880 | tf_op jit(solution)/shard_map/all_to_all | solution.py:273
  22.5 166.8 %all-gather.4.cloned.1.call-start = ((), (), s32[]{:S(2)}) async-start(), calls=%async_computation.2 | async-start | bytes 1179648 | tf_op jit(solution)/shard_map/all_gather | solution.py:297
  24.6 10.8 %copy-start.43 = (f32[2]{0:T(128)}, f32[2]{0:T(128)S(1)}, u32[]{:S(2)}) copy-start(f32[2]{0:T(128)S(1)} %broadcast_divide_fusion) | copy-start | bytes 28
  27.2 7.7 %collective-permute-start.22 = (s32[512]{0:T(512)S(1)}, s32[512]{0:T(512)S(1)}, u32[]{:S(2)}, u32[]{:S(2)}) collective-permute-start(s32[512]{0:T(512)S(1)} %collective-permute-done.21), channel_id=1, source_target_pairs={{0,1},{1,0},{2,3},{3,2},{4,5},{5,4},{6,7},{7,6},{8,9},{9,8},{10,11... | collective-permute-start | bytes 6152 | tf_op jit(solution)/shard_map/ppermute | solution.py:12
  34.8 19.0 %collective-permute-start.36 = (bf16[512,384]{1,0:T(8,128)(2,1)}, bf16[512,384]{1,0:T(8,128)(2,1)}, u32[]{:S(2)}, u32[]{:S(2)}) collective-permute-start(bf16[512,384]{1,0:T(8,128)(2,1)} %get-tuple-element.179), channel_id=1, source_target_pairs={{0,1},{1,0},{2,3},{3,2},{4,5},{5,4},{6,7},{7,6},{8,9},{9,8},{10,11... | collective-permute-start | bytes 1179656 | tf_op jit(solution)/shard_map/ppermute | solution.py:12
  34.9 20.5 %collective-permute-start.37 = (bf16[512,384]{1,0:T(8,128)(2,1)}, bf16[512,384]{1,0:T(8,128)(2,1)}, u32[]{:S(2)}, u32[]{:S(2)}) collective-permute-start(bf16[512,384]{1,0:T(8,128)(2,1)} %get-tuple-element.181), channel_id=1, source_target_pairs={{0,2},{1,3},{2,0},{3,1},{4,6},{5,7},{6,4},{7,5},{8,10},{9,11},{10,... | collective-permute-start | bytes 1179656 | tf_op jit(solution)/shard_map/ppermute | solution.py:12
  36.4 9.0 %copy-start.10 = (bf16[512,2048]{1,0:T(8,128)(2,1)}, bf16[512,2048]{1,0:T(8,128)(2,1)S(1)}, u32[]{:S(2)}) copy-start(bf16[512,2048]{1,0:T(8,128)(2,1)S(1)} %fusion.6) | copy-start | bytes 6291460
  38.9 40.1 %copy-start.8 = (bf16[512,2048]{1,0:T(8,128)(2,1)}, bf16[512,2048]{1,0:T(8,128)(2,1)S(1)}, u32[]{:S(2)}) copy-start(bf16[512,2048]{1,0:T(8,128)(2,1)S(1)} %fusion.4) | copy-start | bytes 6291460
  38.9 16.5 %collective-permute-start.38 = (bf16[512,384]{1,0:T(8,128)(2,1)}, bf16[512,384]{1,0:T(8,128)(2,1)}, u32[]{:S(2)}, u32[]{:S(2)}) collective-permute-start(bf16[512,384]{1,0:T(8,128)(2,1)} %get-tuple-element.180), channel_id=1, source_target_pairs={{0,3},{1,2},{2,1},{3,0},{4,7},{5,6},{6,5},{7,4},{8,11},{9,10},{10,... | collective-permute-start | bytes 1179656 | tf_op jit(solution)/shard_map/ppermute | solution.py:12
  43.7 32.2 %collective-permute-start.26 = (bf16[512,512]{0,1:T(8,128)(2,1)}, bf16[512,512]{0,1:T(8,128)(2,1)S(1)}, u32[]{:S(2)}, u32[]{:S(2)}) collective-permute-start(bf16[512,512]{0,1:T(8,128)(2,1)} %convolution_convert_fusion.5), channel_id=1, source_target_pairs={{0,4},{4,0},{8,12},{12,8},{16,20},{20,16},{24,28},{28,24},{1,5},{5... | collective-permute-start | bytes 1572872 | tf_op jit(solution)/shard_map/ppermute | solution.py:12
  49.1 23.8 %collective-permute-start.15 = (bf16[448,896]{1,0:T(8,128)(2,1)S(1)}, bf16[448,896]{1,0:T(8,128)(2,1)S(1)}, u32[]{:S(2)}, u32[]{:S(2)}) collective-permute-start(bf16[448,896]{1,0:T(8,128)(2,1)S(1)} %pad_maximum_fusion.6.refs_0_), channel_id=1, source_target_pairs={{0,2},{1,3},{2,0},{3,1},{4,6},{5,7},{6,4},{7,5},{8,10},{9,11},{10,... | collective-permute-start | bytes 2408456 | tf_op jit(solution)/shard_map/ppermute | solution.py:12
  53.8 23.6 %collective-permute-start.27 = (bf16[512,512]{0,1:T(8,128)(2,1)S(1)}, bf16[512,512]{0,1:T(8,128)(2,1)S(1)}, u32[]{:S(2)}, u32[]{:S(2)}) collective-permute-start(bf16[512,512]{0,1:T(8,128)(2,1)S(1)} %copy-done.41), channel_id=1, source_target_pairs={{0,8},{4,12},{8,0},{12,4},{16,24},{20,28},{24,16},{28,20},{1,9},{5... | collective-permute-start | bytes 1572872 | tf_op jit(solution)/shard_map/ppermute | solution.py:12
  55.3 23.7 %collective-permute-start.28 = (bf16[512,512]{0,1:T(8,128)(2,1)S(1)}, bf16[512,512]{0,1:T(8,128)(2,1)S(1)}, u32[]{:S(2)}, u32[]{:S(2)}) collective-permute-start(bf16[512,512]{0,1:T(8,128)(2,1)S(1)} %convolution_convert_fusion.3), channel_id=1, source_target_pairs={{0,12},{4,8},{8,4},{12,0},{16,28},{20,24},{24,20},{28,16},{1,13},{... | collective-permute-start | bytes 1572872 | tf_op jit(solution)/shard_map/ppermute | solution.py:12
  55.4 17.5 %copy-start.11 = (bf16[512,2048]{1,0:T(8,128)(2,1)S(1)}, bf16[512,2048]{1,0:T(8,128)(2,1)}, u32[]{:S(2)}) copy-start(bf16[512,2048]{1,0:T(8,128)(2,1)} %copy-done.10) | copy-start | bytes 6291460
  58.6 20.4 %copy-start.34 = (bf16[512,512]{1,0:T(8,128)(2,1)S(1)}, bf16[512,512]{1,0:T(8,128)(2,1)}, u32[]{:S(2)}) copy-start(bf16[512,512]{1,0:T(8,128)(2,1)} %copy-done.33) | copy-start | bytes 1572868
  58.6 23.5 %collective-permute-start.14 = (bf16[448,896]{1,0:T(8,128)(2,1)S(1)}, bf16[448,896]{1,0:T(8,128)(2,1)S(1)}, u32[]{:S(2)}, u32[]{:S(2)}) collective-permute-start(bf16[448,896]{1,0:T(8,128)(2,1)S(1)} %pad_maximum_fusion.6.refs_0_), channel_id=1, source_target_pairs={{0,1},{1,0},{2,3},{3,2},{4,5},{5,4},{6,7},{7,6},{8,9},{9,8},{10,11... | collective-permute-start | bytes 2408456 | tf_op jit(solution)/shard_map/ppermute | solution.py:12
  72.9 9.2 %collective-permute-start.16 = (bf16[448,896]{1,0:T(8,128)(2,1)S(1)}, bf16[448,896]{1,0:T(8,128)(2,1)S(1)}, u32[]{:S(2)}, u32[]{:S(2)}) collective-permute-start(bf16[448,896]{1,0:T(8,128)(2,1)S(1)} %collective-permute-done.15.refs_2_), channel_id=1, source_target_pairs={{0,1},{1,0},{2,3},{3,2},{4,5},{5,4},{6,7},{7,6},{8,9},{9,8},{10,11... | collective-permute-start | bytes 2408456 | tf_op jit(solution)/shard_map/ppermute | solution.py:12
  76.0 39.1 %copy-start.14 = (bf16[512,512]{0,1:T(8,128)(2,1)}, bf16[512,512]{0,1:T(8,128)(2,1)S(1)}, u32[]{:S(2)}) copy-start(bf16[512,512]{0,1:T(8,128)(2,1)S(1)} %collective-permute-done.26) | copy-start | bytes 1572868
  76.0 52.3 %collective-permute-start.39 = (bf16[512,384]{0,1:T(8,128)(2,1)}, bf16[512,384]{0,1:T(8,128)(2,1)}, u32[]{:S(2)}, u32[]{:S(2)}) collective-permute-start(bf16[512,384]{0,1:T(8,128)(2,1)} %convolution_convert_fusion.9), channel_id=1, source_target_pairs={{0,4},{4,0},{8,12},{12,8},{16,20},{20,16},{24,28},{28,24},{1,5},{5... | collective-permute-start | bytes 1179656 | tf_op jit(solution)/shard_map/ppermute | solution.py:12
  77.5 37.6 %copy-start.16 = (bf16[512,512]{0,1:T(8,128)(2,1)}, bf16[512,512]{0,1:T(8,128)(2,1)S(1)}, u32[]{:S(2)}) copy-start(bf16[512,512]{0,1:T(8,128)(2,1)S(1)} %collective-permute-done.27) | copy-start | bytes 1572868
  77.5 51.7 %collective-permute-start.40 = (bf16[512,384]{0,1:T(8,128)(2,1)}, bf16[512,384]{0,1:T(8,128)(2,1)}, u32[]{:S(2)}, u32[]{:S(2)}) collective-permute-start(bf16[512,384]{0,1:T(8,128)(2,1)} %convolution_convert_fusion.8), channel_id=1, source_target_pairs={{0,8},{4,12},{8,0},{12,4},{16,24},{20,28},{24,16},{28,20},{1,9},{5... | collective-permute-start | bytes 1179656 | tf_op jit(solution)/shard_map/ppermute | solution.py:12
  79.0 36.0 %copy-start.18 = (bf16[512,512]{0,1:T(8,128)(2,1)}, bf16[512,512]{0,1:T(8,128)(2,1)S(1)}, u32[]{:S(2)}) copy-start(bf16[512,512]{0,1:T(8,128)(2,1)S(1)} %collective-permute-done.28) | copy-start | bytes 1572868
  82.1 32.9 %copy-start.19 = (bf16[512,512]{0,1:T(8,128)(2,1)}, bf16[512,512]{0,1:T(8,128)(2,1)S(1)}, u32[]{:S(2)}) copy-start(bf16[512,512]{0,1:T(8,128)(2,1)S(1)} %get-tuple-element.231) | copy-start | bytes 1572868
  82.2 9.6 %copy-start.9 = (bf16[512,2048]{1,0:T(8,128)(2,1)S(1)}, bf16[512,2048]{1,0:T(8,128)(2,1)}, u32[]{:S(2)}) copy-start(bf16[512,2048]{1,0:T(8,128)(2,1)} %fusion.7) | copy-start | bytes 6291460
  89.1 7.5 %copy-start.4 = (bf16[1,512,3584]{2,1,0:T(8,128)(2,1)S(1)}, bf16[1,512,3584]{2,1,0:T(8,128)(2,1)}, u32[]{:S(2)}) copy-start(bf16[1,512,3584]{2,1,0:T(8,128)(2,1)} %param.18) | copy-start | bytes 11010052
  89.1 26.0 %collective-permute-start.29 = (bf16[512,512]{0,1:T(8,128)(2,1)S(1)}, bf16[512,512]{0,1:T(8,128)(2,1)S(1)}, u32[]{:S(2)}, u32[]{:S(2)}) collective-permute-start(bf16[512,512]{0,1:T(8,128)(2,1)S(1)} %get-tuple-element.60), channel_id=1, source_target_pairs={{0,16},{4,20},{8,24},{12,28},{16,0},{20,4},{24,8},{28,12},{1,17},{... | collective-permute-start | bytes 1572872 | tf_op jit(solution)/shard_map/ppermute | solution.py:12
  94.8 36.0 %collective-permute-start.41 = (bf16[512,384]{0,1:T(8,128)(2,1)}, bf16[512,384]{0,1:T(8,128)(2,1)S(1)}, u32[]{:S(2)}, u32[]{:S(2)}) collective-permute-start(bf16[512,384]{0,1:T(8,128)(2,1)} %convolution_convert_fusion.7), channel_id=1, source_target_pairs={{0,12},{4,8},{8,4},{12,0},{16,28},{20,24},{24,20},{28,16},{1,13},{... | collective-permute-start | bytes 1179656 | tf_op jit(solution)/shard_map/ppermute | solution.py:12
  97.1 21.3 %collective-permute-start.18 = (bf16[320,896]{1,0:T(8,128)(2,1)S(1)}, bf16[320,896]{1,0:T(8,128)(2,1)S(1)}, u32[]{:S(2)}, u32[]{:S(2)}) collective-permute-start(bf16[320,896]{1,0:T(8,128)(2,1)S(1)} %convolution_convert_fusion), channel_id=1, source_target_pairs={{0,1},{1,0},{2,3},{3,2},{4,5},{5,4},{6,7},{7,6},{8,9},{9,8},{10,11... | collective-permute-start | bytes 1720328 | tf_op jit(solution)/shard_map/ppermute | solution.py:12
  116.2 15.6 %copy-start.36 = (bf16[512,384]{1,0:T(8,128)(2,1)S(1)}, bf16[512,384]{1,0:T(8,128)(2,1)}, u32[]{:S(2)}) copy-start(bf16[512,384]{1,0:T(8,128)(2,1)} %get-tuple-element.178) | copy-start | bytes 1179652
  116.3 2.8 %collective-permute-start.30 = (bf16[128,512]{0,1:T(8,128)(2,1)S(1)}, bf16[128,512]{0,1:T(8,128)(2,1)S(1)}, u32[]{:S(2)}, u32[]{:S(2)}) collective-permute-start(bf16[128,512]{0,1:T(8,128)(2,1)S(1)} %get-tuple-element.193), channel_id=1, source_target_pairs={{0,1},{1,0},{2,3},{3,2},{4,5},{5,4},{6,7},{7,6},{8,9},{9,8},{10,11... | collective-permute-start | bytes 393224 | tf_op jit(solution)/shard_map/ppermute | solution.py:12
  118.4 6.4 %collective-permute-start.31 = (bf16[128,512]{0,1:T(8,128)(2,1)S(1)}, bf16[128,512]{0,1:T(8,128)(2,1)S(1)}, u32[]{:S(2)}, u32[]{:S(2)}) collective-permute-start(bf16[128,512]{0,1:T(8,128)(2,1)S(1)} %get-tuple-element.192), channel_id=1, source_target_pairs={{0,2},{1,3},{2,0},{3,1},{4,6},{5,7},{6,4},{7,5},{8,10},{9,11},{10,... | collective-permute-start | bytes 393224 | tf_op jit(solution)/shard_map/ppermute | solution.py:12
  119.1 7.6 %collective-permute-start.32 = (bf16[128,512]{0,1:T(8,128)(2,1)S(1)}, bf16[128,512]{0,1:T(8,128)(2,1)S(1)}, u32[]{:S(2)}, u32[]{:S(2)}) collective-permute-start(bf16[128,512]{0,1:T(8,128)(2,1)S(1)} %get-tuple-element.191), channel_id=1, source_target_pairs={{0,3},{1,2},{2,1},{3,0},{4,7},{5,6},{6,5},{7,4},{8,11},{9,10},{10,... | collective-permute-start | bytes 393224 | tf_op jit(solution)/shard_map/ppermute | solution.py:12
  124.8 11.2 %copy-start.25 = (bf16[128,512]{0,1:T(8,128)(2,1)}, bf16[128,512]{0,1:T(8,128)(2,1)S(1)}, u32[]{:S(2)}) copy-start(bf16[128,512]{0,1:T(8,128)(2,1)S(1)} %collective-permute-done.31) | copy-start | bytes 393220
  124.8 11.2 %collective-permute-start.17 = (bf16[320,896]{1,0:T(8,128)(2,1)}, bf16[320,896]{1,0:T(8,128)(2,1)S(1)}, u32[]{:S(2)}, u32[]{:S(2)}) collective-permute-start(bf16[320,896]{1,0:T(8,128)(2,1)} %convolution_convert_fusion.1), channel_id=1, source_target_pairs={{0,1},{1,0},{2,3},{3,2},{4,5},{5,4},{6,7},{7,6},{8,9},{9,8},{10,11... | collective-permute-start | bytes 1720328 | tf_op jit(solution)/shard_map/ppermute | solution.py:12
  126.8 9.2 %copy-start.27 = (bf16[128,512]{0,1:T(8,128)(2,1)}, bf16[128,512]{0,1:T(8,128)(2,1)S(1)}, u32[]{:S(2)}) copy-start(bf16[128,512]{0,1:T(8,128)(2,1)S(1)} %collective-permute-done.32) | copy-start | bytes 393220
  126.8 15.1 %collective-permute-start.19 = (bf16[320,896]{1,0:T(8,128)(2,1)S(1)}, bf16[320,896]{1,0:T(8,128)(2,1)S(1)}, u32[]{:S(2)}, u32[]{:S(2)}) collective-permute-start(bf16[320,896]{1,0:T(8,128)(2,1)S(1)} %fusion.10), channel_id=1, source_target_pairs={{0,2},{1,3},{2,0},{3,1},{4,6},{5,7},{6,4},{7,5},{8,10},{9,11},{10,... | collective-permute-start | bytes 1720328 | tf_op jit(solution)/shard_map/ppermute | solution.py:12
  128.3 36.1 %collective-permute-start.33 = (bf16[4,128,512]{1,2,0:T(8,128)(2,1)}, bf16[4,128,512]{1,2,0:T(8,128)(2,1)S(1)}, u32[]{:S(2)}, u32[]{:S(2)}) collective-permute-start(bf16[4,128,512]{1,2,0:T(8,128)(2,1)} %pad_maximum_fusion.7), channel_id=1, source_target_pairs={{0,12},{4,8},{8,4},{12,0},{16,28},{20,24},{24,20},{28,16},{1,13},{... | collective-permute-start | bytes 1572872 | tf_op jit(solution)/shard_map/ppermute | solution.py:12
  129.1 45.5 %collective-permute-start.34 = (bf16[4,128,512]{1,2,0:T(8,128)(2,1)}, bf16[4,128,512]{1,2,0:T(8,128)(2,1)S(1)}, u32[]{:S(2)}, u32[]{:S(2)}) collective-permute-start(bf16[4,128,512]{1,2,0:T(8,128)(2,1)} %pad_maximum_fusion.7), channel_id=1, source_target_pairs={{0,8},{4,12},{8,0},{12,4},{16,24},{20,28},{24,16},{28,20},{1,9},{5... | collective-permute-start | bytes 1572872 | tf_op jit(solution)/shard_map/ppermute | solution.py:12
  130.8 43.8 %collective-permute-start.35 = (bf16[4,128,512]{1,2,0:T(8,128)(2,1)}, bf16[4,128,512]{1,2,0:T(8,128)(2,1)S(1)}, u32[]{:S(2)}, u32[]{:S(2)}) collective-permute-start(bf16[4,128,512]{1,2,0:T(8,128)(2,1)} %pad_maximum_fusion.7), channel_id=1, source_target_pairs={{0,4},{4,0},{8,12},{12,8},{16,20},{20,16},{24,28},{28,24},{1,5},{5... | collective-permute-start | bytes 1572872 | tf_op jit(solution)/shard_map/ppermute | solution.py:12
  144.4 31.3 %collective-permute-start.42 = (bf16[512,384]{0,1:T(8,128)(2,1)}, bf16[512,384]{0,1:T(8,128)(2,1)}, u32[]{:S(2)}, u32[]{:S(2)}) collective-permute-start(bf16[512,384]{0,1:T(8,128)(2,1)} %get-tuple-element.61), channel_id=1, source_target_pairs={{0,16},{4,20},{8,24},{12,28},{16,0},{20,4},{24,8},{28,12},{1,17},{... | collective-permute-start | bytes 1179656 | tf_op jit(solution)/shard_map/ppermute | solution.py:12
  159.8 62.6 %all-to-all-start.1 = ((bf16[8,40,896]{2,1,0:T(8,128)(2,1)}), bf16[8,40,896]{2,1,0:T(8,128)(2,1)}, u32[]{:S(2)}, u32[]{:S(2)}) async-start(bf16[8,40,896]{2,1,0:T(8,128)(2,1)} %bitcast.48), calls=%async_computation.1 | async-start | bytes 1146880 | tf_op jit(solution)/shard_map/all_to_all | solution.py:288
  164.3 11.5 %copy-start.22 = (bf16[512,384]{0,1:T(8,128)(2,1)S(1)}, bf16[512,384]{0,1:T(8,128)(2,1)}, u32[]{:S(2)}) copy-start(bf16[512,384]{0,1:T(8,128)(2,1)} %copy-done.21) | copy-start | bytes 1179652
  164.3 11.5 %copy-start.23 = (bf16[512,384]{0,1:T(8,128)(2,1)S(1)}, bf16[512,384]{0,1:T(8,128)(2,1)}, u32[]{:S(2)}) copy-start(bf16[512,384]{0,1:T(8,128)(2,1)} %get-tuple-element.236) | copy-start | bytes 1179652
  164.3 15.7 %copy-start.26 = (bf16[128,512]{0,1:T(8,128)(2,1)S(1)}, bf16[128,512]{0,1:T(8,128)(2,1)}, u32[]{:S(2)}) copy-start(bf16[128,512]{0,1:T(8,128)(2,1)} %copy-done.25) | copy-start | bytes 393220
  164.3 15.7 %copy-start.28 = (bf16[128,512]{0,1:T(8,128)(2,1)S(1)}, bf16[128,512]{0,1:T(8,128)(2,1)}, u32[]{:S(2)}) copy-start(bf16[128,512]{0,1:T(8,128)(2,1)} %copy-done.27) | copy-start | bytes 393220
  178.1 3.1 %collective-permute-start.43 = (bf16[128,384]{0,1:T(8,128)(2,1)S(1)}, bf16[128,384]{0,1:T(8,128)(2,1)S(1)}, u32[]{:S(2)}, u32[]{:S(2)}) collective-permute-start(bf16[128,384]{0,1:T(8,128)(2,1)S(1)} %get-tuple-element.197), channel_id=1, source_target_pairs={{0,1},{1,0},{2,3},{3,2},{4,5},{5,4},{6,7},{7,6},{8,9},{9,8},{10,11... | collective-permute-start | bytes 294920 | tf_op jit(solution)/shard_map/ppermute | solution.py:12
  178.2 5.7 %collective-permute-start.44 = (bf16[128,384]{0,1:T(8,128)(2,1)S(1)}, bf16[128,384]{0,1:T(8,128)(2,1)S(1)}, u32[]{:S(2)}, u32[]{:S(2)}) collective-permute-start(bf16[128,384]{0,1:T(8,128)(2,1)S(1)} %get-tuple-element.196), channel_id=1, source_target_pairs={{0,2},{1,3},{2,0},{3,1},{4,6},{5,7},{6,4},{7,5},{8,10},{9,11},{10,... | collective-permute-start | bytes 294920 | tf_op jit(solution)/shard_map/ppermute | solution.py:12
  179.3 5.7 %collective-permute-start.45 = (bf16[128,384]{0,1:T(8,128)(2,1)S(1)}, bf16[128,384]{0,1:T(8,128)(2,1)S(1)}, u32[]{:S(2)}, u32[]{:S(2)}) collective-permute-start(bf16[128,384]{0,1:T(8,128)(2,1)S(1)} %get-tuple-element.195), channel_id=1, source_target_pairs={{0,3},{1,2},{2,1},{3,0},{4,7},{5,6},{6,5},{7,4},{8,11},{9,10},{10,... | collective-permute-start | bytes 294920 | tf_op jit(solution)/shard_map/ppermute | solution.py:12
  185.8 14.0 %collective-permute-start.46 = (bf16[4,128,384]{1,2,0:T(8,128)(2,1)}, bf16[4,128,384]{1,2,0:T(8,128)(2,1)S(1)}, u32[]{:S(2)}, u32[]{:S(2)}) collective-permute-start(bf16[4,128,384]{1,2,0:T(8,128)(2,1)} %pad_maximum_fusion.8), channel_id=1, source_target_pairs={{0,12},{4,8},{8,4},{12,0},{16,28},{20,24},{24,20},{28,16},{1,13},{... | collective-permute-start | bytes 1179656 | tf_op jit(solution)/shard_map/ppermute | solution.py:12
  186.7 20.7 %copy-start.30 = (bf16[128,384]{0,1:T(8,128)(2,1)S(1)}, bf16[128,384]{0,1:T(8,128)(2,1)}, u32[]{:S(2)}) copy-start(bf16[128,384]{0,1:T(8,128)(2,1)} %copy-done.29) | copy-start | bytes 294916
  186.7 20.7 %collective-permute-start.47 = (bf16[4,128,384]{1,2,0:T(8,128)(2,1)}, bf16[4,128,384]{1,2,0:T(8,128)(2,1)S(1)}, u32[]{:S(2)}, u32[]{:S(2)}) collective-permute-start(bf16[4,128,384]{1,2,0:T(8,128)(2,1)} %pad_maximum_fusion.8), channel_id=1, source_target_pairs={{0,8},{4,12},{8,0},{12,4},{16,24},{20,28},{24,16},{28,20},{1,9},{5... | collective-permute-start | bytes 1179656 | tf_op jit(solution)/shard_map/ppermute | solution.py:12
  189.1 18.4 %copy-start.32 = (bf16[128,384]{0,1:T(8,128)(2,1)S(1)}, bf16[128,384]{0,1:T(8,128)(2,1)}, u32[]{:S(2)}) copy-start(bf16[128,384]{0,1:T(8,128)(2,1)} %copy-done.31) | copy-start | bytes 294916
  189.1 18.3 %collective-permute-start.48 = (bf16[4,128,384]{1,2,0:T(8,128)(2,1)}, bf16[4,128,384]{1,2,0:T(8,128)(2,1)}, u32[]{:S(2)}, u32[]{:S(2)}) collective-permute-start(bf16[4,128,384]{1,2,0:T(8,128)(2,1)} %pad_maximum_fusion.8), channel_id=1, source_target_pairs={{0,4},{4,0},{8,12},{12,8},{16,20},{20,16},{24,28},{28,24},{1,5},{5... | collective-permute-start | bytes 1179656 | tf_op jit(solution)/shard_map/ppermute | solution.py:12
  (16 other events, 54.3 us)
Sparse Core Ops, SparseCore 0:
  118.5 52.3 all-gather.3

commit v3 on v2

--- a/solution.py
+++ b/solution.py
@@ -115,97 +115,258 @@
     for k in range(nt):
         piece = lax.dynamic_slice(own, (0, (t ^ k) * block + off), (own.shape[0], width))
         found.append(xor_permute(piece, "tensor", nt, k) if k else piece)
-    return jnp.concatenate(found, axis=0)
+    return found
 
 
 def rows_to_device(pieces, nt):
     return [xor_permute(pieces[k], "tensor", nt, k) if k else pieces[k] for k in range(nt)]
 
 
-def merge_two(own, perm, cluster, owners, e, t, ne, nt, beside):
-    rows, model = own.shape
-    half = ne // 2
-    block = model // nt
-    sub = rows // half
-    q, side = e % half, e // half
-    placed = ((perm // rows) ^ t) * rows + perm % rows
-    placed = placed.reshape(nt, half, sub)
-    member = cluster[(e ^ jnp.arange(half, dtype=jnp.int32))]
-    inverse = 1.0 / jnp.sum(
-        (cluster[None, :] == jnp.arange(2, dtype=jnp.int32)[:, None]).astype(jnp.float32), axis=1
-    )
-    owner_side = owners // half
-    keep = jnp.where(owner_side[0] == side, 0, 1)
-    give = jnp.where(owner_side[0] != side, 0, 1)
-    spans = chunks_of(block)
-    order = [(q ^ k) for k in range(half)]
-    selectors = [
-        one_hot(lax.dynamic_index_in_dim(placed, j, 1, keepdims=False).reshape(-1), rows * nt)
-        for j in order
-    ]
-
-    partials = []
-    for off, width in spans:
-        source = columns_to_device(own, t, nt, off, width)
-        arrived = [None] * half
-        for k in list(range(1, half)) + [0]:
-            aligned = pick_rows(selectors[k], source)
-            arrived[k] = xor_permute(aligned, "expert", ne, k) if k else aligned
-        partials.append(arrived)
-
-    def partial_of(arrived, which):
-        total = jnp.zeros(arrived[0].shape, jnp.float32)
+T_AT, Q_AT, KEEP_AT, GIVE_AT, MINE_AT, MEMBER_AT = range(6)
+BIG_VMEM = 48 * 1024 * 1024
+
+
+def full_spec(shape):
+    return pl.BlockSpec(shape, memory_space=pltpu.VMEM)
+
+
+def align_kernel(nt, half, sub, flags_ref, place_ref, *refs):
+    sources, outs = refs[:nt], refs[nt:]
+    rows, width = sources[0].shape
+    lane = lax.broadcasted_iota(jnp.int32, (rows, rows), 1)
+    q = flags_ref[Q_AT]
+    for k in range(half):
+        first = pl.multiple_of((q ^ k) * sub, sub)
+        place = jnp.concatenate(
+            [place_ref[pl.ds(first + b * half * sub, sub), :] for b in range(nt)], axis=0
+        )
+        total = jnp.zeros((rows, width), jnp.float32)
+        for m in range(nt):
+            selector = jnp.where(place - m * rows == lane, 1.0, 0.0).astype(jnp.bfloat16)
+            total = total + jnp.dot(
+                selector, sources[m][...], preferred_element_type=jnp.float32
+            )
+        outs[k][...] = total.astype(jnp.bfloat16)
+
+
+def align(flags, place, sources, half, sub):
+    nt = len(sources)
+    rows, width = sources[0].shape
+    piece = jax.ShapeDtypeStruct((rows, width), jnp.bfloat16)
+    return pl.pallas_call(
+        functools.partial(align_kernel, nt, half, sub),
+        out_shape=[piece] * half,
+        in_specs=[pl.BlockSpec(memory_space=pltpu.SMEM), full_spec(place.shape)]
+        + [full_spec((rows, width))] * nt,
+        out_specs=[full_spec((rows, width))] * half,
+        compiler_params=pltpu.CompilerParams(vmem_limit_bytes=BIG_VMEM),
+        cost_estimate=pl.CostEstimate(
+            flops=2 * half * nt * rows * rows * width,
+            bytes_accessed=2 * (half + nt) * rows * width,
+            transcendentals=0,
+        ),
+        name="align",
+    )(flags, place, *sources)
+
+
+def sums_kernel(half, flags_ref, *refs):
+    parts, sent_ref, kept_ref = refs[:half], refs[half], refs[half + 1]
+    keep, give = flags_ref[KEEP_AT], flags_ref[GIVE_AT]
+    sent = jnp.zeros(sent_ref.shape, jnp.float32)
+    kept = jnp.zeros(kept_ref.shape, jnp.float32)
+    for k in range(half):
+        member = flags_ref[MEMBER_AT + k]
+        part = parts[k][...].astype(jnp.float32)
+        sent = sent + jnp.where(member == give, part, 0.0)
+        kept = kept + jnp.where(member == keep, part, 0.0)
+    sent_ref[...] = sent.astype(sent_ref.dtype)
+    kept_ref[...] = kept
+
+
+def sums(flags, parts, tile=64):
+    rows, width = parts[0].shape
+    tile = min(tile, rows)
+    spec = pl.BlockSpec((tile, width), lambda i: (i, 0))
+    return pl.pallas_call(
+        functools.partial(sums_kernel, len(parts)),
+        grid=(rows // tile,),
+        out_shape=[
+            jax.ShapeDtypeStruct((rows, width), jnp.bfloat16),
+            jax.ShapeDtypeStruct((rows, width), jnp.float32),
+        ],
+        in_specs=[pl.BlockSpec(memory_space=pltpu.SMEM)] + [spec] * len(parts),
+        out_specs=[spec, spec],
+        cost_estimate=pl.CostEstimate(
+            flops=2 * len(parts) * rows * width,
+            bytes_accessed=2 * (len(parts) + 3) * rows * width,
+            transcendentals=0,
+        ),
+        name="sums",
+    )(flags, *parts)
+
+
+def mean_kernel(scale_ref, kept_ref, other_ref, *outs):
+    sub = outs[0].shape[0]
+    scale = scale_ref[0]
+    for m, out in enumerate(outs):
+        at = pl.ds(m * sub, sub)
+        total = kept_ref[at, :] + other_ref[at, :].astype(jnp.float32)
+        out[...] = (total * scale).astype(out.dtype)
+
+
+def mean_of(scale, kept, other, nt):
+    rows, width = kept.shape
+    sub = rows // nt
+    return pl.pallas_call(
+        mean_kernel,
+        out_shape=[jax.ShapeDtypeStruct((sub, width), jnp.bfloat16)] * nt,
+        in_specs=[pl.BlockSpec(memory_space=pltpu.SMEM)] + [full_spec((rows, width))] * 2,
+        out_specs=[full_spec((sub, width))] * nt,
+        compiler_params=pltpu.CompilerParams(vmem_limit_bytes=BIG_VMEM),
+        cost_estimate=pl.CostEstimate(
+            flops=2 * rows * width, bytes_accessed=8 * rows * width, transcendentals=0
+        ),
+        name="mean",
+    )(scale, kept, other)
+
+
+def assemble_kernel(half, nt, spans, flags_ref, *refs):
+    count = half * len(spans)
+    groups, out_ref, blank, sems, blank_sems = refs[:count], *refs[count:]
+    sub = blank.shape[0]
+    block = out_ref.shape[1] // nt
+    mine = flags_ref[MINE_AT] != 0
+
+    @pl.when(mine)
+    def _():
+        copies = []
         for k in range(half):
-            total = total + jnp.where(member[k] == which, arrived[k].astype(jnp.float32), 0.0)
-        return total
-
-    def finish(partials, kept, given, beside=()):
-        gathered = []
-        for place, (arrived, (off, width)) in enumerate(zip(partials, spans)):
-            sent = partial_of(arrived, given).astype(jnp.bfloat16)
-            if place < len(beside):
-                sent = after(sent, beside[place])
-            other = xor_permute(sent, "expert", ne, half)
-            mean = (
-                (partial_of(arrived, kept) + other.astype(jnp.float32)) * inverse[kept]
-            ).astype(jnp.bfloat16)
-            lines = jnp.stack(rows_to_device(mean.reshape(nt, sub, width), nt))
-            gathered.append(
-                [xor_permute(lines, "expert", ne, k) if k else lines for k in range(half)]
+            at = pl.multiple_of((flags_ref[Q_AT] ^ k) * sub, sub)
+            for m in range(nt):
+                left = pl.multiple_of((flags_ref[T_AT] ^ m) * block, 128)
+                for c, (off, width) in enumerate(spans):
+                    copies.append(
+                        pltpu.make_async_copy(
+                            groups[c * half + k].at[m],
+                            out_ref.at[pl.ds(at, sub), pl.ds(left + off, width)],
+                            sems.at[len(copies)],
+                        )
+                    )
+        for copy in copies:
+            copy.start()
+        for copy in copies:
+            copy.wait()
+
+    @pl.when(jnp.logical_not(mine))
+    def _():
+        blank[...] = jnp.zeros_like(blank)
+        copies = [
+            pltpu.make_async_copy(
+                blank, out_ref.at[pl.ds(j * sub, sub), :], blank_sems.at[j]
             )
-        mine = owners[kept] == e
-        order_t = jnp.arange(nt, dtype=jnp.int32) ^ t
-        out = []
-        for j in range(half):
-            wide = []
-            for group in gathered:
-                chosen = group[0]
-                for k in range(1, half):
-                    chosen = jnp.where((q ^ j) == k, group[k], chosen)
-                wide.append(chosen)
-            out.append(jnp.concatenate(wide, axis=2))
-        joined = jnp.stack(out)
-        ordered = []
-        for b in range(nt):
-            chosen = joined[:, 0]
-            for k in range(1, nt):
-                chosen = jnp.where(order_t[b] == k, joined[:, k], chosen)
-            ordered.append(chosen)
-        whole = jnp.concatenate(ordered, axis=2).reshape(rows, model)
-        return jnp.where(mine, whole, jnp.zeros_like(whole))
-
-    first = finish(partials, keep, give, beside)
-
-    def second(args):
-        first, partials = args
-        return first + finish(partials, 1, 1)
-
-    return lax.cond(
-        owner_side[0] == owner_side[1], second, lambda args: args[0], (first, partials)
-    )
-
-
-def merge_any(own, perm, cluster, owners, e, t, ne, nt, beside):
+            for j in range(half)
+        ]
+        for copy in copies:
+            copy.start()
+        for copy in copies:
+            copy.wait()
+
+
+def assemble(flags, gathered, spans, rows, model):
+    half = len(gathered[0])
+    nt, sub = gathered[0][0].shape[:2]
+    anywhere = pl.BlockSpec(memory_space=pl.ANY)
+    groups = [piece for group in gathered for piece in group]
+    return pl.pallas_call(
+        functools.partial(assemble_kernel, half, nt, spans),
+        out_shape=jax.ShapeDtypeStruct((rows, model), jnp.bfloat16),
+        in_specs=[pl.BlockSpec(memory_space=pltpu.SMEM)] + [anywhere] * len(groups),
+        out_specs=anywhere,
+        scratch_shapes=[
+            pltpu.VMEM((sub, model), jnp.bfloat16),
+            pltpu.SemaphoreType.DMA((half * nt * len(spans),)),
+            pltpu.SemaphoreType.DMA((half,)),
+        ],
+        cost_estimate=pl.CostEstimate(
+            flops=0, bytes_accessed=4 * rows * model, transcendentals=0
+        ),
+        name="assemble",
+    )(flags, *groups)
+
+
+class TwoClusters:
+    def __init__(self, own, perm, cluster, owners, e, t, ne, nt):
+        self.own, self.t, self.ne, self.nt = own, t, ne, nt
+        rows, model = own.shape
+        half = self.half = ne // 2
+        self.sub = rows // half
+        self.spans = chunks_of(model // nt)
+        self.cluster, self.owners, self.e = cluster, owners, e
+        q, side = e % half, e // half
+        self.place = (((perm // rows) ^ t) * rows + perm % rows).reshape(-1, 1)
+        experts = jnp.arange(ne, dtype=jnp.int32)
+        near = (e ^ jnp.arange(half, dtype=jnp.int32))[:, None] == experts[None, :]
+        member = jnp.sum(jnp.where(near, cluster[None, :], 0), axis=1)
+        sides = owners // half
+        keep = jnp.where(sides[0:1] == side, 0, 1)
+        give = jnp.where(sides[0:1] != side, 0, 1)
+        mine = jnp.where(jnp.where(keep == 0, owners[0:1], owners[1:2]) == e, 1, 0)
+        self.flags = jnp.concatenate(
+            [t.reshape(1), q.reshape(1), keep, give, mine, member]
+        ).astype(jnp.int32)
+        self.sizes = jnp.sum(
+            (cluster[None, :] == jnp.arange(2, dtype=jnp.int32)[:, None]).astype(jnp.float32),
+            axis=1,
+        )
+        self.scale = 1.0 / jnp.where(keep == 0, self.sizes[0:1], self.sizes[1:2])
+        self.sources = [
+            columns_to_device(own, t, nt, off, width) for off, width in self.spans
+        ]
+
+    def send_aligned(self, c):
+        pieces = align(self.flags, self.place, self.sources[c], self.half, self.sub)
+        sent = [
+            xor_permute(piece, "expert", self.ne, k) if k else piece
+            for k, piece in enumerate(pieces)
+        ]
+        return pieces[0], sent
+
+    def back_and_out(self, pieces, *others):
+        lines = jnp.stack(rows_to_device(pieces, self.nt))
+        if others:
+            lines = after(lines, *others)
+        return [
+            xor_permute(lines, "expert", self.ne, k) if k else lines for k in range(self.half)
+        ]
+
+    def finish(self, gathered, arrived):
+        rows, model = self.own.shape
+        first = assemble(self.flags, gathered, self.spans, rows, model)
+        sides = self.owners // self.half
+
+        def second(args):
+            first, arrived = args
+            near = self.cluster[self.e ^ jnp.arange(self.half, dtype=jnp.int32)]
+            again = []
+            for parts in arrived:
+                total = jnp.zeros(parts[0].shape, jnp.float32)
+                for k in range(self.half):
+                    total = total + jnp.where(near[k] == 1, parts[k].astype(jnp.float32), 0.0)
+                other = xor_permute(total.astype(jnp.bfloat16), "expert", self.ne, self.half)
+                scale = (1.0 / self.sizes[1]).reshape(1)
+                again.append(self.back_and_out(mean_of(scale, total, other, self.nt)))
+            mine = jnp.where(self.owners[1:2] == self.e, 1, 0).astype(jnp.int32)
+            flags = jnp.concatenate(
+                [self.flags[:MINE_AT], mine, self.flags[MINE_AT + 1 :]]
+            )
+            return first + assemble(flags, again, self.spans, rows, model)
+
+        return lax.cond(
+            sides[0] == sides[1], second, lambda args: args[0], (first, arrived)
+        )
+
+
+def merge_any(own, perm, cluster, owners, e, t, ne, nt):
     rows, model = own.shape
     block = model // nt
     clusters = owners.shape[0]
@@ -213,7 +374,7 @@
     placed = ((perm // rows) ^ t) * rows + perm % rows
     placed = placed.reshape(nt, ne, sub).transpose(1, 0, 2).reshape(-1)
     aligned = pick_rows(
-        one_hot(placed, rows * nt), columns_to_device(own, t, nt, 0, block)
+        one_hot(placed, rows * nt), jnp.concatenate(columns_to_device(own, t, nt, 0, block))
     )
     arrived = lax.all_to_all(aligned, "expert", split_axis=0, concat_axis=0, tiled=True)
     arrived = arrived.reshape(ne, nt, sub, block)
@@ -257,6 +418,9 @@
     block = model // nt
 
     perm = jnp.concatenate(gather_tensor(hidden_perm[0], nt))
+    two = None
+    if ne == 8 and owners.shape[0] == 2:
+        two = TwoClusters(own, perm, cluster, owners, e, t, ne, nt)
 
     flat = routes.reshape(-1)
     pairs = jnp.arange(flat.shape[0], dtype=jnp.int32)
@@ -272,11 +436,26 @@
     ).astype(jnp.bfloat16)
     arrived = lax.all_to_all(outgoing, "expert", split_axis=0, concat_axis=0, tiled=True)
     routed = arrived.shape[0]
-    stacked = jnp.concatenate([arrived, probe_rows], axis=0)
-    hidden = ffn(gather_tensor(stacked, nt), gate_weight, up_weight, t)
+    stacked = gather_tensor(jnp.concatenate([arrived, probe_rows], axis=0), nt)
+
+    if two is not None:
+        parts, others, kept, marks = [], [], [], []
+        for c in range(len(two.spans)):
+            mark, sent = two.send_aligned(c)
+            marks.append(mark)
+            parts.append(sent)
+        stacked = list(lax.optimization_barrier((*stacked, *marks))[:nt])
+    hidden = ffn(stacked, gate_weight, up_weight, t)
     routed_hidden, probe_hidden = hidden[:routed], hidden[routed:]
-
-    parts = [
+    if two is not None:
+        for c in range(len(two.spans)):
+            given, own_sum = sums(two.flags, parts[c])
+            if c == 0:
+                given = after(given, hidden)
+            others.append(xor_permute(given, "expert", ne, two.half))
+            kept.append(own_sum)
+
+    partials = [
         jnp.dot(
             routed_hidden,
             lax.dynamic_slice(own, (0, (t ^ k) * block), (own.shape[0], block)),
@@ -284,18 +463,18 @@
         )
         for k in range(nt)
     ]
-    returned = scatter_tensor(parts, nt).astype(jnp.bfloat16)
+    returned = scatter_tensor(partials, nt).astype(jnp.bfloat16)
     home = lax.all_to_all(returned, "expert", split_axis=0, concat_axis=0, tiled=True)
     chooser = (target.T.reshape(-1)[:, None] == slots[None, :]).astype(jnp.bfloat16)
     picked = jnp.dot(chooser, home, preferred_element_type=jnp.float32)
     picked = picked.reshape(top, tok_rows, block)
     mixed = jnp.sum(gate_values.T[:, :, None] * picked, axis=0).astype(jnp.bfloat16)
 
-    merge = merge_two if ne == 8 and owners.shape[0] == 2 else merge_any
-    merged = merge(own, perm, cluster, owners, e, t, ne, nt, (hidden, returned))
-
     everyone = lax.all_gather(probe_hidden, "expert", axis=0)
-    partner = lax.dynamic_index_in_dim(everyone, owners[cluster[e]], 0, keepdims=False)
+    at_owner = jnp.arange(ne, dtype=jnp.int32) == owners[cluster[e]]
+    partner = jnp.sum(
+        jnp.where(at_owner[:, None, None], everyone.astype(jnp.float32), 0.0), axis=0
+    ).astype(jnp.bfloat16)
     partner_full = lax.all_gather(partner, "tensor", axis=1, tiled=True)
     correlation = (
         lax.dot_general(
@@ -303,6 +482,15 @@
         )
         / probe_hidden.shape[0]
     )
+    if two is not None:
+        gathered = []
+        for c in range(len(two.spans)):
+            means = mean_of(two.scale, kept[c], others[c], nt)
+            gathered.append(two.back_and_out(means, *((returned,) if c == 0 else ())))
+        gathered[-1][0] = after(gathered[-1][0], mixed, correlation)
+        merged = two.finish(gathered, parts)
+    else:
+        merged = merge_any(own, perm, cluster, owners, e, t, ne, nt)
     return (mixed, correlation[None], merged[None])
 
 

time: 234 us -> 377 us (1.61)
  Pallas kernels: 6.91 us -> 142 us
  waiting for transfers between devices: 63.5 us -> 116 us
  matrix products: 39.2 us -> 16.6 us
  between operations: 34.6 us -> 21.5 us
  other arithmetic: 20.2 us -> 7.49 us
    pallas_call x0 -> x7, Pallas kernels: none -> 135 us  [the longest x1 113 us: assemble(): pl.pallas_call(functools.partial(assemble_kernel, half, nt, spans), out_s...]
    ppermute x35, waiting for transfers between devices: 63.5 us -> 109 us  [xor_permute(): return lax.ppermute(value, axis, [(i, i ^ k) for i in range(size)])]
    dot_general x8 -> x0, matrix products: 27.1 us -> none  [pick_rows(): jnp.dot(selector, source, preferred_element_type=jnp.float32)]
    select_n x9 -> x1, other arithmetic: 10.5 us -> 0.01 us  [__init__(): sides = owners // half]
    unnamed x85 -> x57, local copies, waits for them, and re-layouts: 2.76 us -> 9.78 us
    convert_element_type x6 -> x0, other arithmetic: 6.69 us -> none  [the longest x2 3.36 us: finish(): mean = ((partial_of(arrived, kept) + other.astype(jnp.float32)) * inverse...]
    all_to_all x1, waiting for transfers between devices: 0.01 us -> 6.5 us  [on_device(): lax.all_to_all(outgoing, 'expert', split_axis=0, concat_axis=0, tiled=True)]
    dot_general x4, matrix products: 6.06 us -> 10.4 us  [on_device(): jnp.dot(routed_hidden, lax.dynamic_slice(own, (0, (t ^ k) * block), (own....]
  transfers between devices with their start and end apart: 38 -> 38, of which waited for: 9 -> 14; matrix products, arithmetic and copies ran while one was open for 31% -> 8% of each run, Pallas kernels for 3% -> 6%
where the time goes in v3:
time: 377 us; the launch traced here: 375 us
  Pallas kernels  142 us (38%)
  waiting for transfers between devices  116 us (31%)
  starting transfers between devices  45.2 us (12%)
  between operations  21.5 us (6%)
  local copies, waits for them, and re-layouts  19.9 us (5%)
  matrix products  16.6 us (4%)
  other arithmetic  7.49 us (2%)
  blocking collectives  6.51 us (2%)
    pallas_call x1, Pallas kernels, assemble(): pl.pallas_call(functools.partial(assemble_kernel, half, nt, spans), out_s...  113 us
    ppermute x35, waiting for transfers between devices, xor_permute(): return lax.ppermute(value, axis, [(i, i ^ k) for i in range(size)])  109 us
    ppermute x35, starting transfers between devices, xor_permute(): return lax.ppermute(value, axis, [(i, i ^ k) for i in range(size)])  33.6 us
    pallas_call x2, Pallas kernels, align(): pl.pallas_call(functools.partial(align_kernel, nt, half, sub), out_shape=...  11.1 us
    pallas_call x2, Pallas kernels, sums(): pl.pallas_call(functools.partial(sums_kernel, len(parts)), grid=(rows //...  10.7 us
    dot_general x4, matrix products, on_device(): jnp.dot(routed_hidden, lax.dynamic_slice(own, (0, (t ^ k) * block), (own....  10.4 us
    unnamed x57, local copies, waits for them, and re-layouts  9.78 us
  transfers between devices with their start and end apart: 38, of which 14 were waited for; matrix products, arithmetic and copies ran while one was open for 8% of the time, Pallas kernels for 6%

profile of v3, /device:TPU:0, one launch (start us, length us, event | category | flops | bytes accessed | tf_op | source)
XLA Modules:
  0.0 375.0 jit_solution(3833024440119940077)
XLA Ops:
  7.2 0.8 copy.45
  8.5 0.7 multiply_add_fusion
  9.3 1.1 convolution_convert_fusion.2
  10.4 7.3 %all-to-all-start = ((bf16[8,40,896]{2,1,0:T(8,128)(2,1)}), bf16[8,40,896]{2,1,0:T(8,128)(2,1)S(1)}, u32[]{:S(2)}, u32[]{:S(2)}) async-start(bf16[8,40,896]{2,1,0:T(8,128)(2,1)} %bitcast.22), calls=%async_computation | async-start | bytes 1146880 | tf_op jit(solution)/shard_map/all_to_all | solution.py:437
  17.7 1.6 collective-permute-start.18
  19.3 2.5 dynamic-slice_bitcast_fusion.4
  22.4 1.5 collective-permute-start.24
  24.0 2.7 dynamic-slice_bitcast_fusion
  26.7 6.5 %all-to-all-done = bf16[8,40,896]{2,1,0:T(8,128)(2,1)S(1)} async-done(((bf16[8,40,896]{2,1,0:T(8,128)(2,1)}), bf16[8,40,896]{2,1,0:T(8,128)(2,1)S(1)}, u32[]{:S(2)}, u32[]{:S(2)}) %all-to-all-start) | async-done | bytes 573472 | tf_op jit(solution)/shard_map/all_to_all | solution.py:437
  33.2 1.6 collective-permute-start.15
  42.3 1.3 copy.47
  43.6 1.5 collective-permute-start.21
  45.6 14.1 %collective-permute-done.15.refs_2_ = bf16[448,896]{1,0:T(8,128)(2,1)S(1)} collective-permute-done((bf16[448,896]{1,0:T(8,128)(2,1)S(1)}, bf16[448,896]{1,0:T(8,128)(2,1)S(1)}, u32[]{:S(2)}, u32[]{:S(2)}) %collective-permute-start.15) | collective-permute-done | bytes 802848 | tf_op jit(solution)/shard_map/ppermute | solution.py:12
  59.7 2.2 fusion.5.place_ref
  61.9 5.7 %align.3 = (bf16[512,384]{1,0:T(8,128)(2,1)}, bf16[512,384]{1,0:T(8,128)(2,1)S(1)}, bf16[512,384]{1,0:T(8,128)(2,1)S(1)}, bf16[512,384]{1,0:T(8,128)(2,1)S(1)}) custom-call(s32[9]{0:T(128)S(1)} %concatenate.52.flags_ref, s32[2048,1]{1,0:T(8,128)S(1)} %fusion.5.place_ref, bf16[512,384]{1,0:T(8,128)(2,1)S(1)} %get-tuple-element.132.refs_0_, ...), custom_call_target="tpu_custom_call" | custom-call | flops 3221225472 | bytes 3145728 | tf_op jit(solution)/shard_map/align/pallas_call | solution.py:156
  67.7 0.8 copy-done.6
  68.4 0.8 copy-done.8
  69.2 0.7 copy-done.10
  70.0 0.8 copy-done.4
  70.7 10.8 %collective-permute-done.21.refs_2_ = bf16[512,512]{1,0:T(8,128)(2,1)S(1)} collective-permute-done((bf16[512,512]{1,0:T(8,128)(2,1)}, bf16[512,512]{1,0:T(8,128)(2,1)S(1)}, u32[]{:S(2)}, u32[]{:S(2)}) %collective-permute-start.21) | collective-permute-done | bytes 524320 | tf_op jit(solution)/shard_map/ppermute | solution.py:12
  81.6 1.0 copy-done.5
  82.6 5.4 %align.2 = (bf16[512,512]{1,0:T(8,128)(2,1)}, bf16[512,512]{1,0:T(8,128)(2,1)}, bf16[512,512]{1,0:T(8,128)(2,1)}, bf16[512,512]{1,0:T(8,128)(2,1)S(1)}) custom-call(s32[9]{0:T(128)S(1)} %concatenate.52.flags_ref, s32[2048,1]{1,0:T(8,128)S(1)} %fusion.5.place_ref, bf16[512,512]{1,0:T(8,128)(2,1)S(1)} %get-tuple-element.136.refs_0_, ...), custom_call_target="tpu_custom_call" | custom-call | flops 4294967296 | bytes 4194304 | tf_op jit(solution)/shard_map/align/pallas_call | solution.py:156
  88.0 6.6 %ffn.1 = bf16[448,512]{1,0:T(8,128)(2,1)S(1)} custom-call(s32[1]{0:T(128)} %bitcast.19.where_ref, bf16[448,896]{1,0:T(8,128)(2,1)S(1)} %pad_maximum_fusion.2.refs_0_, bf16[448,896]{1,0:T(8,128)(2,1)S(1)} %collective-permute-done.14.refs_1_, bf16[448,896]{1,0:T(8,128)(2,1)S(1)} %collective-permute-done.15.refs_2_, ...), custom_call_target="tpu_custom_call" | custom-call | flops 3288334336 | bytes 11010048 | tf_op jit(solution)/shard_map/ffn/pallas_call | solution.py:68
  94.7 2.6 convolution_convert_fusion
  97.3 1.9 collective-permute-start.29
  99.2 1.5 collective-permute-start.30
  101.6 1.9 collective-permute-start.39
  103.5 2.5 convolution_convert_fusion.1
  106.0 7.8 %collective-permute-done.29.refs_1_ = bf16[512,512]{1,0:T(8,128)(2,1)S(1)} collective-permute-done((bf16[512,512]{1,0:T(8,128)(2,1)}, bf16[512,512]{1,0:T(8,128)(2,1)S(1)}, u32[]{:S(2)}, u32[]{:S(2)}) %collective-permute-start.29) | collective-permute-done | bytes 524320 | tf_op jit(solution)/shard_map/ppermute | solution.py:12
  113.7 1.8 collective-permute-start.40
  115.6 1.0 collective-permute-done.30.refs_2_
  116.6 1.8 collective-permute-start.41
  118.4 2.7 add_convert_fusion.1
  121.1 10.0 %collective-permute-done.31.refs_3_ = bf16[512,512]{1,0:T(8,128)(2,1)S(1)} collective-permute-done((bf16[512,512]{1,0:T(8,128)(2,1)S(1)}, bf16[512,512]{1,0:T(8,128)(2,1)S(1)}, u32[]{:S(2)}, u32[]{:S(2)}) %collective-permute-start.31) | collective-permute-done | bytes 524320 | tf_op jit(solution)/shard_map/ppermute | solution.py:12
  131.0 0.8 copy-done.16
  131.8 5.4 %sums.2 = (bf16[512,512]{1,0:T(8,128)(2,1)}, f32[512,512]{1,0:T(8,128)}) custom-call(s32[9]{0:T(128)S(1)} %concatenate.52.flags_ref, bf16[512,512]{1,0:T(8,128)(2,1)S(1)} %copy-done.13, bf16[512,512]{1,0:T(8,128)(2,1)S(1)} %collective-permute-done.29.refs_1_, bf16[512,512]{1,0:T(8,128)(2,1)} %collective-permute-done.30.refs_2_, bf16[512,512]{1,0:T(8,128)(2,1)} %copy-done.16), custom_call_target="tpu_custom_call" | custom-call | flops 2097152 | bytes 3670016 | tf_op jit(solution)/shard_map/sums/pallas_call | solution.py:190
  137.7 3.0 collective-permute-start.32
  140.7 17.2 %collective-permute-done.40.refs_2_ = bf16[512,384]{1,0:T(8,128)(2,1)} collective-permute-done((bf16[512,384]{1,0:T(8,128)(2,1)S(1)}, bf16[512,384]{1,0:T(8,128)(2,1)}, u32[]{:S(2)}, u32[]{:S(2)}) %collective-permute-start.40) | collective-permute-done | bytes 393248 | tf_op jit(solution)/shard_map/ppermute | solution.py:12
  157.8 7.1 %collective-permute-done.41.refs_3_ = bf16[512,384]{1,0:T(8,128)(2,1)} collective-permute-done((bf16[512,384]{1,0:T(8,128)(2,1)S(1)}, bf16[512,384]{1,0:T(8,128)(2,1)}, u32[]{:S(2)}, u32[]{:S(2)}) %collective-permute-start.41) | collective-permute-done | bytes 393248 | tf_op jit(solution)/shard_map/ppermute | solution.py:12
  165.0 5.3 %sums.3 = (bf16[512,384]{1,0:T(8,128)(2,1)}, f32[512,384]{1,0:T(8,128)}) custom-call(s32[9]{0:T(128)S(1)} %concatenate.52.flags_ref, bf16[512,384]{1,0:T(8,128)(2,1)} %get-tuple-element.158.refs_0_, bf16[512,384]{1,0:T(8,128)(2,1)} %collective-permute-done.39.refs_1_, bf16[512,384]{1,0:T(8,128)(2,1)} %collective-permute-done.40.refs_2_, ...), custom_call_target="tpu_custom_call" | custom-call | flops 1572864 | bytes 2752512 | tf_op jit(solution)/shard_map/sums/pallas_call | solution.py:190
  170.3 1.4 collective-permute-start.42
  173.8 16.3 %collective-permute-done.42.other_ref = bf16[512,384]{1,0:T(8,128)(2,1)S(1)} collective-permute-done((bf16[512,384]{1,0:T(8,128)(2,1)}, bf16[512,384]{1,0:T(8,128)(2,1)S(1)}, u32[]{:S(2)}, u32[]{:S(2)}) %collective-permute-start.42) | collective-permute-done | bytes 393248 | tf_op jit(solution)/shard_map/ppermute | solution.py:12
  190.0 1.1 copy-done.3
  191.8 1.4 collective-permute-start.45
  193.2 1.2 copy-done.2
  195.4 2.7 add_convert_fusion
  198.1 4.3 %all-to-all-start.1 = ((bf16[8,40,896]{2,1,0:T(8,128)(2,1)}), bf16[8,40,896]{2,1,0:T(8,128)(2,1)}, u32[]{:S(2)}, u32[]{:S(2)}) async-start(bf16[8,40,896]{2,1,0:T(8,128)(2,1)} %bitcast.44), calls=%async_computation.1 | async-start | bytes 1146880 | tf_op jit(solution)/shard_map/all_to_all | solution.py:467
  202.3 1.1 collective-permute-start.35
  205.4 0.8 pad_maximum_fusion.4.refs_4_
  206.2 2.5 collective-permute-start.48
  208.7 1.2 collective-permute-start.47
  210.6 1.0 pad_maximum_fusion.3.refs_0_
  211.6 0.9 collective-permute-start.38
  213.0 2.2 collective-permute-start.36
  215.2 1.5 fusion.1
  216.7 6.5 %all_gather.11 = bf16[128,2048]{1,0:T(8,128)(2,1)S(1)} all-gather(bf16[128,512]{1,0:T(8,128)(2,1)S(1)} %fusion.1), channel_id=1, replica_groups=mesh['expert'=8,'tensor'=4] {'tensor'}, dimensions={1}, use_global_device_ids=true | all-gather | bytes 655360 | tf_op jit(solution)/shard_map/all_gather | solution.py:478
  223.5 1.0 collective-permute-start.46
  224.5 2.7 convolution_multiply_fusion
  227.3 2.3 fusion.2
  229.5 2.0 collective-permute-done.47.refs_6_
  231.6 21.6 %collective-permute-done.46.refs_5_ = bf16[4,128,384]{2,1,0:T(8,128)(2,1)} collective-permute-done((bf16[4,128,384]{2,1,0:T(8,128)(2,1)}, bf16[4,128,384]{2,1,0:T(8,128)(2,1)}, u32[]{:S(2)}, u32[]{:S(2)}) %collective-permute-start.46) | collective-permute-done | bytes 393248 | tf_op jit(solution)/shard_map/ppermute | solution.py:12
  253.1 0.9 collective-permute-done.37.refs_2_
  254.0 113.1 %assemble.3 = bf16[512,3584]{1,0:T(8,128)(2,1)} custom-call(s32[9]{0:T(128)S(1)} %concatenate.52.flags_ref, bf16[4,128,512]{2,1,0:T(8,128)(2,1)} %copy-done.18, bf16[4,128,512]{2,1,0:T(8,128)(2,1)} %collective-permute-done.36.refs_1_, bf16[4,128,512]{2,1,0:T(8,128)(2,1)} %collective-permute-done.37.refs_2_, bf16[4,128,512]{2,1,0:T(8,128)(2,1)} %copy-done.22, ...), custom_call_target="tpu_custom_call" | custom-call | bytes 7340032 | tf_op jit(solution)/shard_map/assemble/pallas_call | solution.py:280
  367.2 0.9 copy-done.1
  (113 shorter events, 10.6 us)
Async XLA Ops:
  7.2 2.1 copy-start
  10.4 22.8 %all-to-all-start = ((bf16[8,40,896]{2,1,0:T(8,128)(2,1)}), bf16[8,40,896]{2,1,0:T(8,128)(2,1)S(1)}, u32[]{:S(2)}, u32[]{:S(2)}) async-start(bf16[8,40,896]{2,1,0:T(8,128)(2,1)} %bitcast.22), calls=%async_computation | async-start | bytes 1146880 | tf_op jit(solution)/shard_map/all_to_all | solution.py:437
  17.6 197.6 %all-gather.3.cloned.1.call-start = ((), (), s32[]{:S(2)}) async-start(), calls=%async_computation.2 | async-start | bytes 1179648 | tf_op jit(solution)/shard_map/all_gather | solution.py:473
  17.7 19.9 %collective-permute-start.18 = (s32[512]{0:T(512)}, s32[512]{0:T(512)S(1)}, u32[]{:S(2)}, u32[]{:S(2)}) collective-permute-start(s32[512]{0:T(512)} %bitcast.114), channel_id=1, source_target_pairs={{0,2},{1,3},{2,0},{3,1},{4,6},{5,7},{6,4},{7,5},{8,10},{9,11},{10,... | collective-permute-start | bytes 6152 | tf_op jit(solution)/shard_map/ppermute | solution.py:12
  19.3 19.1 %collective-permute-start.17 = (s32[512]{0:T(512)}, s32[512]{0:T(512)S(1)}, u32[]{:S(2)}, u32[]{:S(2)}) collective-permute-start(s32[512]{0:T(512)} %bitcast.115), channel_id=1, source_target_pairs={{0,1},{1,0},{2,3},{3,2},{4,5},{5,4},{6,7},{7,6},{8,9},{9,8},{10,11... | collective-permute-start | bytes 6152 | tf_op jit(solution)/shard_map/ppermute | solution.py:12
  19.3 13.9 %copy-start.30 = (bf16[128,896]{1,0:T(8,128)(2,1)S(1)}, bf16[128,896]{1,0:T(8,128)(2,1)}, u32[]{:S(2)}) copy-start(bf16[128,896]{1,0:T(8,128)(2,1)} %param.15) | copy-start | bytes 688132
  21.8 13.1 %copy-start.33 = (s32[2]{0:T(128)S(1)}, s32[2]{0:T(128)}, u32[]{:S(2)}) copy-start(s32[2]{0:T(128)} %param.21) | copy-start | bytes 28
  21.8 13.1 %copy-start.12 = (s32[8]{0:T(128)S(1)}, s32[8]{0:T(128)}, u32[]{:S(2)}) copy-start(s32[8]{0:T(128)} %param.20) | copy-start | bytes 100
  21.8 20.5 %copy-start.34 = (s32[1,512]{1,0:T(1,128)S(1)}, s32[1,512]{1,0:T(1,128)}, u32[]{:S(2)}) copy-start(s32[1,512]{1,0:T(1,128)} %param.19) | copy-start | bytes 6148
  21.8 21.8 %collective-permute-start.25 = (bf16[512,384]{1,0:T(8,128)(2,1)}, bf16[512,384]{1,0:T(8,128)(2,1)S(1)}, u32[]{:S(2)}, u32[]{:S(2)}) collective-permute-start(bf16[512,384]{1,0:T(8,128)(2,1)} %get-tuple-element.129), channel_id=1, source_target_pairs={{0,3},{1,2},{2,1},{3,0},{4,7},{5,6},{6,5},{7,4},{8,11},{9,10},{10,... | collective-permute-start | bytes 1179656 | tf_op jit(solution)/shard_map/ppermute | solution.py:12
  22.4 22.7 %collective-permute-start.24 = (bf16[512,384]{1,0:T(8,128)(2,1)}, bf16[512,384]{1,0:T(8,128)(2,1)}, u32[]{:S(2)}, u32[]{:S(2)}) collective-permute-start(bf16[512,384]{1,0:T(8,128)(2,1)} %get-tuple-element.130), channel_id=1, source_target_pairs={{0,2},{1,3},{2,0},{3,1},{4,6},{5,7},{6,4},{7,5},{8,10},{9,11},{10,... | collective-permute-start | bytes 1179656 | tf_op jit(solution)/shard_map/ppermute | solution.py:12
  33.2 26.5 %collective-permute-start.15 = (bf16[448,896]{1,0:T(8,128)(2,1)S(1)}, bf16[448,896]{1,0:T(8,128)(2,1)S(1)}, u32[]{:S(2)}, u32[]{:S(2)}) collective-permute-start(bf16[448,896]{1,0:T(8,128)(2,1)S(1)} %pad_maximum_fusion.2.refs_0_), channel_id=1, source_target_pairs={{0,2},{1,3},{2,0},{3,1},{4,6},{5,7},{6,4},{7,5},{8,10},{9,11},{10,... | collective-permute-start | bytes 2408456 | tf_op jit(solution)/shard_map/ppermute | solution.py:12
  37.6 7.8 %collective-permute-start.23 = (bf16[512,384]{1,0:T(8,128)(2,1)}, bf16[512,384]{1,0:T(8,128)(2,1)}, u32[]{:S(2)}, u32[]{:S(2)}) collective-permute-start(bf16[512,384]{1,0:T(8,128)(2,1)} %get-tuple-element.131), channel_id=1, source_target_pairs={{0,1},{1,0},{2,3},{3,2},{4,5},{5,4},{6,7},{7,6},{8,9},{9,8},{10,11... | collective-permute-start | bytes 1179656 | tf_op jit(solution)/shard_map/ppermute | solution.py:12
  38.3 3.8 %collective-permute-start.19 = (s32[512]{0:T(512)S(1)}, s32[512]{0:T(512)S(1)}, u32[]{:S(2)}, u32[]{:S(2)}) collective-permute-start(s32[512]{0:T(512)S(1)} %collective-permute-done.18), channel_id=1, source_target_pairs={{0,1},{1,0},{2,3},{3,2},{4,5},{5,4},{6,7},{7,6},{8,9},{9,8},{10,11... | collective-permute-start | bytes 6152 | tf_op jit(solution)/shard_map/ppermute | solution.py:12
  42.1 27.9 %collective-permute-start.22 = (bf16[512,512]{1,0:T(8,128)(2,1)}, bf16[512,512]{1,0:T(8,128)(2,1)S(1)}, u32[]{:S(2)}, u32[]{:S(2)}) collective-permute-start(bf16[512,512]{1,0:T(8,128)(2,1)} %get-tuple-element.133), channel_id=1, source_target_pairs={{0,3},{1,2},{2,1},{3,0},{4,7},{5,6},{6,5},{7,4},{8,11},{9,10},{10,... | collective-permute-start | bytes 1572872 | tf_op jit(solution)/shard_map/ppermute | solution.py:12
  43.6 38.0 %collective-permute-start.21 = (bf16[512,512]{1,0:T(8,128)(2,1)}, bf16[512,512]{1,0:T(8,128)(2,1)S(1)}, u32[]{:S(2)}, u32[]{:S(2)}) collective-permute-start(bf16[512,512]{1,0:T(8,128)(2,1)} %get-tuple-element.134), channel_id=1, source_target_pairs={{0,2},{1,3},{2,0},{3,1},{4,6},{5,7},{6,4},{7,5},{8,10},{9,11},{10,... | collective-permute-start | bytes 1572872 | tf_op jit(solution)/shard_map/ppermute | solution.py:12
  45.1 36.4 %collective-permute-start.20 = (bf16[512,512]{1,0:T(8,128)(2,1)}, bf16[512,512]{1,0:T(8,128)(2,1)S(1)}, u32[]{:S(2)}, u32[]{:S(2)}) collective-permute-start(bf16[512,512]{1,0:T(8,128)(2,1)} %get-tuple-element.135), channel_id=1, source_target_pairs={{0,1},{1,0},{2,3},{3,2},{4,5},{5,4},{6,7},{7,6},{8,9},{9,8},{10,11... | collective-permute-start | bytes 1572872 | tf_op jit(solution)/shard_map/ppermute | solution.py:12
  45.3 42.7 %collective-permute-start.14 = (bf16[448,896]{1,0:T(8,128)(2,1)S(1)}, bf16[448,896]{1,0:T(8,128)(2,1)S(1)}, u32[]{:S(2)}, u32[]{:S(2)}) collective-permute-start(bf16[448,896]{1,0:T(8,128)(2,1)S(1)} %pad_maximum_fusion.2.refs_0_), channel_id=1, source_target_pairs={{0,1},{1,0},{2,3},{3,2},{4,5},{5,4},{6,7},{7,6},{8,9},{9,8},{10,11... | collective-permute-start | bytes 2408456 | tf_op jit(solution)/shard_map/ppermute | solution.py:12
  59.7 28.3 %collective-permute-start.16 = (bf16[448,896]{1,0:T(8,128)(2,1)S(1)}, bf16[448,896]{1,0:T(8,128)(2,1)S(1)}, u32[]{:S(2)}, u32[]{:S(2)}) collective-permute-start(bf16[448,896]{1,0:T(8,128)(2,1)S(1)} %collective-permute-done.15.refs_2_), channel_id=1, source_target_pairs={{0,1},{1,0},{2,3},{3,2},{4,5},{5,4},{6,7},{7,6},{8,9},{9,8},{10,11... | collective-permute-start | bytes 2408456 | tf_op jit(solution)/shard_map/ppermute | solution.py:12
  67.7 0.8 copy-start.6
  68.4 0.8 copy-start.8
  69.2 0.8 copy-start.10
  70.0 0.8 copy-start.4
  81.6 1.0 copy-start.5
  88.0 13.6 %copy-start.11 = (bf16[512,384]{1,0:T(8,128)(2,1)S(1)}, bf16[512,384]{1,0:T(8,128)(2,1)}, u32[]{:S(2)}) copy-start(bf16[512,384]{1,0:T(8,128)(2,1)} %copy-done.10) | copy-start | bytes 1179652
  94.7 19.1 %copy-start.9 = (bf16[512,384]{1,0:T(8,128)(2,1)S(1)}, bf16[512,384]{1,0:T(8,128)(2,1)}, u32[]{:S(2)}) copy-start(bf16[512,384]{1,0:T(8,128)(2,1)} %copy-done.8) | copy-start | bytes 1179652
  94.7 21.9 %copy-start.7 = (bf16[512,384]{1,0:T(8,128)(2,1)S(1)}, bf16[512,384]{1,0:T(8,128)(2,1)}, u32[]{:S(2)}) copy-start(bf16[512,384]{1,0:T(8,128)(2,1)} %copy-done.6) | copy-start | bytes 1179652
  94.7 37.1 %copy-start.13 = (bf16[512,512]{1,0:T(8,128)(2,1)S(1)}, bf16[512,512]{1,0:T(8,128)(2,1)}, u32[]{:S(2)}) copy-start(bf16[512,512]{1,0:T(8,128)(2,1)} %get-tuple-element.154.refs_0_) | copy-start | bytes 1572868
  97.3 21.1 %collective-permute-start.27 = (bf16[320,896]{1,0:T(8,128)(2,1)}, bf16[320,896]{1,0:T(8,128)(2,1)}, u32[]{:S(2)}, u32[]{:S(2)}) collective-permute-start(bf16[320,896]{1,0:T(8,128)(2,1)} %convolution_convert_fusion), channel_id=1, source_target_pairs={{0,1},{1,0},{2,3},{3,2},{4,5},{5,4},{6,7},{7,6},{8,9},{9,8},{10,11... | collective-permute-start | bytes 1720328 | tf_op jit(solution)/shard_map/ppermute | solution.py:12
  97.3 16.4 %collective-permute-start.29 = (bf16[512,512]{1,0:T(8,128)(2,1)}, bf16[512,512]{1,0:T(8,128)(2,1)S(1)}, u32[]{:S(2)}, u32[]{:S(2)}) collective-permute-start(bf16[512,512]{1,0:T(8,128)(2,1)} %get-tuple-element.99), channel_id=1, source_target_pairs={{0,4},{4,0},{8,12},{12,8},{16,20},{20,16},{24,28},{28,24},{1,5},{5... | collective-permute-start | bytes 1572872 | tf_op jit(solution)/shard_map/ppermute | solution.py:12
  99.2 17.4 %collective-permute-start.30 = (bf16[512,512]{1,0:T(8,128)(2,1)}, bf16[512,512]{1,0:T(8,128)(2,1)}, u32[]{:S(2)}, u32[]{:S(2)}) collective-permute-start(bf16[512,512]{1,0:T(8,128)(2,1)} %get-tuple-element.100), channel_id=1, source_target_pairs={{0,8},{4,12},{8,0},{12,4},{16,24},{20,28},{24,16},{28,20},{1,9},{5... | collective-permute-start | bytes 1572872 | tf_op jit(solution)/shard_map/ppermute | solution.py:12
  101.4 29.6 %collective-permute-start.31 = (bf16[512,512]{1,0:T(8,128)(2,1)S(1)}, bf16[512,512]{1,0:T(8,128)(2,1)S(1)}, u32[]{:S(2)}, u32[]{:S(2)}) collective-permute-start(bf16[512,512]{1,0:T(8,128)(2,1)S(1)} %get-tuple-element.101), channel_id=1, source_target_pairs={{0,12},{4,8},{8,4},{12,0},{16,28},{20,24},{24,20},{28,16},{1,13},{... | collective-permute-start | bytes 1572872 | tf_op jit(solution)/shard_map/ppermute | solution.py:12
  101.6 36.1 %collective-permute-start.39 = (bf16[512,384]{1,0:T(8,128)(2,1)S(1)}, bf16[512,384]{1,0:T(8,128)(2,1)}, u32[]{:S(2)}, u32[]{:S(2)}) collective-permute-start(bf16[512,384]{1,0:T(8,128)(2,1)S(1)} %copy-done.11), channel_id=1, source_target_pairs={{0,4},{4,0},{8,12},{12,8},{16,20},{20,16},{24,28},{28,24},{1,5},{5... | collective-permute-start | bytes 1179656 | tf_op jit(solution)/shard_map/ppermute | solution.py:12
  113.7 23.5 %copy-start.14 = (bf16[512,512]{1,0:T(8,128)(2,1)}, bf16[512,512]{1,0:T(8,128)(2,1)S(1)}, u32[]{:S(2)}) copy-start(bf16[512,512]{1,0:T(8,128)(2,1)S(1)} %collective-permute-done.29.refs_1_) | copy-start | bytes 1572868
  113.7 44.1 %collective-permute-start.40 = (bf16[512,384]{1,0:T(8,128)(2,1)S(1)}, bf16[512,384]{1,0:T(8,128)(2,1)}, u32[]{:S(2)}, u32[]{:S(2)}) collective-permute-start(bf16[512,384]{1,0:T(8,128)(2,1)S(1)} %copy-done.9), channel_id=1, source_target_pairs={{0,8},{4,12},{8,0},{12,4},{16,24},{20,28},{24,16},{28,20},{1,9},{5... | collective-permute-start | bytes 1179656 | tf_op jit(solution)/shard_map/ppermute | solution.py:12
  116.6 48.4 %collective-permute-start.41 = (bf16[512,384]{1,0:T(8,128)(2,1)S(1)}, bf16[512,384]{1,0:T(8,128)(2,1)}, u32[]{:S(2)}, u32[]{:S(2)}) collective-permute-start(bf16[512,384]{1,0:T(8,128)(2,1)S(1)} %copy-done.7), channel_id=1, source_target_pairs={{0,12},{4,8},{8,4},{12,0},{16,28},{20,24},{24,20},{28,16},{1,13},{... | collective-permute-start | bytes 1179656 | tf_op jit(solution)/shard_map/ppermute | solution.py:12
  118.4 76.2 %collective-permute-start.26 = (bf16[320,896]{1,0:T(8,128)(2,1)}, bf16[320,896]{1,0:T(8,128)(2,1)}, u32[]{:S(2)}, u32[]{:S(2)}) collective-permute-start(bf16[320,896]{1,0:T(8,128)(2,1)} %convolution_convert_fusion.1), channel_id=1, source_target_pairs={{0,1},{1,0},{2,3},{3,2},{4,5},{5,4},{6,7},{7,6},{8,9},{9,8},{10,11... | collective-permute-start | bytes 1720328 | tf_op jit(solution)/shard_map/ppermute | solution.py:12
  131.0 0.8 copy-start.16
  131.8 63.2 %collective-permute-start.28 = (bf16[320,896]{1,0:T(8,128)(2,1)}, bf16[320,896]{1,0:T(8,128)(2,1)S(1)}, u32[]{:S(2)}, u32[]{:S(2)}) collective-permute-start(bf16[320,896]{1,0:T(8,128)(2,1)} %add_convert_fusion.1), channel_id=1, source_target_pairs={{0,2},{1,3},{2,0},{3,1},{4,6},{5,7},{6,4},{7,5},{8,10},{9,11},{10,... | collective-permute-start | bytes 1720328 | tf_op jit(solution)/shard_map/ppermute | solution.py:12
  137.7 54.1 %collective-permute-start.32 = (bf16[512,512]{1,0:T(8,128)(2,1)}, bf16[512,512]{1,0:T(8,128)(2,1)S(1)}, u32[]{:S(2)}, u32[]{:S(2)}) collective-permute-start(bf16[512,512]{1,0:T(8,128)(2,1)} %get-tuple-element.104), channel_id=1, source_target_pairs={{0,16},{4,20},{8,24},{12,28},{16,0},{20,4},{24,8},{28,12},{1,17},{... | collective-permute-start | bytes 1572872 | tf_op jit(solution)/shard_map/ppermute | solution.py:12
  170.3 19.8 %collective-permute-start.42 = (bf16[512,384]{1,0:T(8,128)(2,1)}, bf16[512,384]{1,0:T(8,128)(2,1)S(1)}, u32[]{:S(2)}, u32[]{:S(2)}) collective-permute-start(bf16[512,384]{1,0:T(8,128)(2,1)} %get-tuple-element.114), channel_id=1, source_target_pairs={{0,16},{4,20},{8,24},{12,28},{16,0},{20,4},{24,8},{28,12},{1,17},{... | collective-permute-start | bytes 1179656 | tf_op jit(solution)/shard_map/ppermute | solution.py:12
  190.0 1.1 copy-start.3
  191.3 11.0 %collective-permute-start.43 = (bf16[128,384]{1,0:T(8,128)(2,1)S(1)}, bf16[128,384]{1,0:T(8,128)(2,1)S(1)}, u32[]{:S(2)}, u32[]{:S(2)}) collective-permute-start(bf16[128,384]{1,0:T(8,128)(2,1)S(1)} %get-tuple-element.116), channel_id=1, source_target_pairs={{0,1},{1,0},{2,3},{3,2},{4,5},{5,4},{6,7},{7,6},{8,9},{9,8},{10,11... | collective-permute-start | bytes 294920 | tf_op jit(solution)/shard_map/ppermute | solution.py:12
  191.4 14.0 %collective-permute-start.44 = (bf16[128,384]{1,0:T(8,128)(2,1)S(1)}, bf16[128,384]{1,0:T(8,128)(2,1)S(1)}, u32[]{:S(2)}, u32[]{:S(2)}) collective-permute-start(bf16[128,384]{1,0:T(8,128)(2,1)S(1)} %get-tuple-element.117), channel_id=1, source_target_pairs={{0,2},{1,3},{2,0},{3,1},{4,6},{5,7},{6,4},{7,5},{8,10},{9,11},{10,... | collective-permute-start | bytes 294920 | tf_op jit(solution)/shard_map/ppermute | solution.py:12
  191.8 13.6 %collective-permute-start.45 = (bf16[128,384]{1,0:T(8,128)(2,1)S(1)}, bf16[128,384]{1,0:T(8,128)(2,1)S(1)}, u32[]{:S(2)}, u32[]{:S(2)}) collective-permute-start(bf16[128,384]{1,0:T(8,128)(2,1)S(1)} %get-tuple-element.118), channel_id=1, source_target_pairs={{0,3},{1,2},{2,1},{3,0},{4,7},{5,6},{6,5},{7,4},{8,11},{9,10},{10,... | collective-permute-start | bytes 294920 | tf_op jit(solution)/shard_map/ppermute | solution.py:12
  193.2 1.2 copy-start.2
  194.6 15.3 %collective-permute-start.33 = (bf16[128,512]{1,0:T(8,128)(2,1)S(1)}, bf16[128,512]{1,0:T(8,128)(2,1)S(1)}, u32[]{:S(2)}, u32[]{:S(2)}) collective-permute-start(bf16[128,512]{1,0:T(8,128)(2,1)S(1)} %get-tuple-element.106), channel_id=1, source_target_pairs={{0,1},{1,0},{2,3},{3,2},{4,5},{5,4},{6,7},{7,6},{8,9},{9,8},{10,11... | collective-permute-start | bytes 393224 | tf_op jit(solution)/shard_map/ppermute | solution.py:12
  195.0 14.9 %collective-permute-start.34 = (bf16[128,512]{1,0:T(8,128)(2,1)S(1)}, bf16[128,512]{1,0:T(8,128)(2,1)S(1)}, u32[]{:S(2)}, u32[]{:S(2)}) collective-permute-start(bf16[128,512]{1,0:T(8,128)(2,1)S(1)} %get-tuple-element.107), channel_id=1, source_target_pairs={{0,2},{1,3},{2,0},{3,1},{4,6},{5,7},{6,4},{7,5},{8,10},{9,11},{10,... | collective-permute-start | bytes 393224 | tf_op jit(solution)/shard_map/ppermute | solution.py:12
  198.1 29.2 %all-to-all-start.1 = ((bf16[8,40,896]{2,1,0:T(8,128)(2,1)}), bf16[8,40,896]{2,1,0:T(8,128)(2,1)}, u32[]{:S(2)}, u32[]{:S(2)}) async-start(bf16[8,40,896]{2,1,0:T(8,128)(2,1)} %bitcast.44), calls=%async_computation.1 | async-start | bytes 1146880 | tf_op jit(solution)/shard_map/all_to_all | solution.py:467
  202.3 7.6 %collective-permute-start.35 = (bf16[128,512]{1,0:T(8,128)(2,1)S(1)}, bf16[128,512]{1,0:T(8,128)(2,1)S(1)}, u32[]{:S(2)}, u32[]{:S(2)}) collective-permute-start(bf16[128,512]{1,0:T(8,128)(2,1)S(1)} %get-tuple-element.108), channel_id=1, source_target_pairs={{0,3},{1,2},{2,1},{3,0},{4,7},{5,6},{6,5},{7,4},{8,11},{9,10},{10,... | collective-permute-start | bytes 393224 | tf_op jit(solution)/shard_map/ppermute | solution.py:12
  206.2 17.3 %collective-permute-start.48 = (bf16[4,128,384]{2,1,0:T(8,128)(2,1)}, bf16[4,128,384]{2,1,0:T(8,128)(2,1)S(1)}, u32[]{:S(2)}, u32[]{:S(2)}) collective-permute-start(bf16[4,128,384]{2,1,0:T(8,128)(2,1)} %pad_maximum_fusion.4.refs_4_), channel_id=1, source_target_pairs={{0,12},{4,8},{8,4},{12,0},{16,28},{20,24},{24,20},{28,16},{1,13},{... | collective-permute-start | bytes 1179656 | tf_op jit(solution)/shard_map/ppermute | solution.py:12
  208.7 22.9 %collective-permute-start.47 = (bf16[4,128,384]{2,1,0:T(8,128)(2,1)}, bf16[4,128,384]{2,1,0:T(8,128)(2,1)}, u32[]{:S(2)}, u32[]{:S(2)}) collective-permute-start(bf16[4,128,384]{2,1,0:T(8,128)(2,1)} %pad_maximum_fusion.4.refs_4_), channel_id=1, source_target_pairs={{0,8},{4,12},{8,0},{12,4},{16,24},{20,28},{24,16},{28,20},{1,9},{5... | collective-permute-start | bytes 1179656 | tf_op jit(solution)/shard_map/ppermute | solution.py:12
  210.6 16.7 %copy-start.35 = (f32[128,2]{0,1:T(2,128)S(1)}, f32[128,2]{0,1:T(2,128)}, u32[]{:S(2)}) copy-start(f32[128,2]{0,1:T(2,128)} %param.14) | copy-start | bytes 3076
  211.6 17.9 %copy-start.18 = (bf16[4,128,512]{2,1,0:T(8,128)(2,1)}, bf16[4,128,512]{2,1,0:T(8,128)(2,1)S(1)}, u32[]{:S(2)}) copy-start(bf16[4,128,512]{2,1,0:T(8,128)(2,1)S(1)} %pad_maximum_fusion.3.refs_0_) | copy-start | bytes 1572868
  211.6 41.5 %collective-permute-start.38 = (bf16[4,128,512]{2,1,0:T(8,128)(2,1)S(1)}, bf16[4,128,512]{2,1,0:T(8,128)(2,1)S(1)}, u32[]{:S(2)}, u32[]{:S(2)}) collective-permute-start(bf16[4,128,512]{2,1,0:T(8,128)(2,1)S(1)} %pad_maximum_fusion.3.refs_0_), channel_id=1, source_target_pairs={{0,12},{4,8},{8,4},{12,0},{16,28},{20,24},{24,20},{28,16},{1,13},{... | collective-permute-start | bytes 1572872 | tf_op jit(solution)/shard_map/ppermute | solution.py:12
  212.5 41.5 %collective-permute-start.37 = (bf16[4,128,512]{2,1,0:T(8,128)(2,1)S(1)}, bf16[4,128,512]{2,1,0:T(8,128)(2,1)}, u32[]{:S(2)}, u32[]{:S(2)}) collective-permute-start(bf16[4,128,512]{2,1,0:T(8,128)(2,1)S(1)} %pad_maximum_fusion.3.refs_0_), channel_id=1, source_target_pairs={{0,8},{4,12},{8,0},{12,4},{16,24},{20,28},{24,16},{28,20},{1,9},{5... | collective-permute-start | bytes 1572872 | tf_op jit(solution)/shard_map/ppermute | solution.py:12
  213.0 41.0 %collective-permute-start.36 = (bf16[4,128,512]{2,1,0:T(8,128)(2,1)S(1)}, bf16[4,128,512]{2,1,0:T(8,128)(2,1)}, u32[]{:S(2)}, u32[]{:S(2)}) collective-permute-start(bf16[4,128,512]{2,1,0:T(8,128)(2,1)S(1)} %pad_maximum_fusion.3.refs_0_), channel_id=1, source_target_pairs={{0,4},{4,0},{8,12},{12,8},{16,20},{20,16},{24,28},{28,24},{1,5},{5... | collective-permute-start | bytes 1572872 | tf_op jit(solution)/shard_map/ppermute | solution.py:12
  223.5 3.7 copy-start.27
  223.5 29.6 %collective-permute-start.46 = (bf16[4,128,384]{2,1,0:T(8,128)(2,1)}, bf16[4,128,384]{2,1,0:T(8,128)(2,1)}, u32[]{:S(2)}, u32[]{:S(2)}) collective-permute-start(bf16[4,128,384]{2,1,0:T(8,128)(2,1)} %pad_maximum_fusion.4.refs_4_), channel_id=1, source_target_pairs={{0,4},{4,0},{8,12},{12,8},{16,20},{20,16},{24,28},{28,24},{1,5},{5... | collective-permute-start | bytes 1179656 | tf_op jit(solution)/shard_map/ppermute | solution.py:12
  229.5 137.6 %copy-start.15 = (bf16[512,512]{1,0:T(8,128)(2,1)S(1)}, bf16[512,512]{1,0:T(8,128)(2,1)}, u32[]{:S(2)}) copy-start(bf16[512,512]{1,0:T(8,128)(2,1)} %copy-done.14) | copy-start | bytes 1572868
  229.5 137.6 %copy-start.17 = (bf16[512,512]{1,0:T(8,128)(2,1)S(1)}, bf16[512,512]{1,0:T(8,128)(2,1)}, u32[]{:S(2)}) copy-start(bf16[512,512]{1,0:T(8,128)(2,1)} %copy-done.16) | copy-start | bytes 1572868
  229.5 137.6 %copy-start.20 = (bf16[512,384]{1,0:T(8,128)(2,1)S(1)}, bf16[512,384]{1,0:T(8,128)(2,1)}, u32[]{:S(2)}) copy-start(bf16[512,384]{1,0:T(8,128)(2,1)} %get-tuple-element.158.refs_0_) | copy-start | bytes 1179652
  253.1 0.9 copy-start.22
  367.2 0.9 copy-start.1
  (2 other events, 1.3 us)
Sparse Core Ops, SparseCore 0:
  101.5 55.7 all-gather.2

commit v4 on v3

--- a/solution.py
+++ b/solution.py
@@ -12,7 +12,7 @@
     return lax.ppermute(value, axis, [(i, i ^ k) for i in range(size)])
 
 
-def gather_tensor(value, size):
+def gather_small(value, size):
     held = {0: value}
     bit = size // 2
     while bit:
@@ -22,37 +22,101 @@
     return [held[k] for k in range(size)]
 
 
-def scatter_tensor(parts, size):
-    held = dict(enumerate(parts))
+def gather_even(value, size):
+    stack, order = value[None], [0]
+    bit = size // 2
+    while bit > 1:
+        stack = jnp.concatenate([stack, xor_permute(stack, "tensor", size, bit)])
+        order = order + [k ^ bit for k in order]
+        bit //= 2
+    return stack, order
+
+
+def down_kernel(count, where_ref, rows_ref, weight_ref, send_ref, keep_ref):
+    step = pl.program_id(0)
+    part = jnp.dot(rows_ref[...], weight_ref[...], preferred_element_type=jnp.float32)
+
+    @pl.when(step < count // 2)
+    def _():
+        send_ref[0] = part.astype(send_ref.dtype)
+
+    @pl.when(step >= count // 2)
+    def _():
+        keep_ref[0] = part.astype(keep_ref.dtype)
+
+
+def down(hidden, routed, own, t, count):
+    units, model = own.shape
+    block = model // count
+    half = count // 2
+
+    def column(i, where):
+        return (0, where[0] ^ jnp.where(i < half, 2 * i + 1, 2 * (i - half)))
+
+    shape = jax.ShapeDtypeStruct((half, routed, block), jnp.bfloat16)
+    return pl.pallas_call(
+        functools.partial(down_kernel, count),
+        out_shape=[shape, shape],
+        grid_spec=pltpu.PrefetchScalarGridSpec(
+            num_scalar_prefetch=1,
+            grid=(count,),
+            in_specs=[
+                pl.BlockSpec((routed, units), lambda i, where: (0, 0)),
+                pl.BlockSpec((units, block), column),
+            ],
+            out_specs=[
+                pl.BlockSpec(
+                    (1, routed, block), lambda i, where: (jnp.minimum(i, half - 1), 0, 0)
+                ),
+                pl.BlockSpec(
+                    (1, routed, block), lambda i, where: (jnp.maximum(i - half, 0), 0, 0)
+                ),
+            ],
+        ),
+        compiler_params=pltpu.CompilerParams(vmem_limit_bytes=BIG_VMEM),
+        cost_estimate=SMALL_COST,
+        name="down",
+    )(t.reshape(1).astype(jnp.int32), hidden, own)
+
+
+def sum_tensor(send, keep, size):
     bit = 1
     while bit < size:
-        for k in sorted(held):
-            if k & bit:
-                arrived = xor_permute(
-                    held.pop(k).astype(jnp.bfloat16), "tensor", size, bit
-                )
-                held[k ^ bit] = held[k ^ bit] + arrived.astype(jnp.float32)
+        if send.shape[0] == 1:
+            send, keep = send[0], keep[0]
+        arrived = xor_permute(send, "tensor", size, bit)
+        total = keep.astype(jnp.float32) + arrived.astype(jnp.float32)
         bit *= 2
-    return held[0]
-
-
-def ffn_kernel(count, where_ref, *refs):
-    parts = refs[:count]
-    gate_ref, up_ref, out_ref, gate_sum, up_sum = refs[count:]
+        if bit < size:
+            send, keep = total[1::2].astype(jnp.bfloat16), total[0::2]
+    return total.astype(jnp.bfloat16)
+
+
+SMALL_COST = pl.CostEstimate(flops=1024, bytes_accessed=1024, transcendentals=0)
+BIG_VMEM = 48 * 1024 * 1024
+
+
+def all_after(values, *others):
+    return list(lax.optimization_barrier((*values, *others))[: len(values)])
+
+
+def ffn_kernel(order, where_ref, even_ref, odd_ref, gate_ref, up_ref, out_ref, gate_sum, up_sum):
     step = pl.program_id(0)
+    count = 2 * len(order)
 
     @pl.when(step == 0)
     def _():
         gate_sum[...] = jnp.zeros_like(gate_sum)
         up_sum[...] = jnp.zeros_like(up_sum)
 
-    for k in range(count):
-
-        @pl.when(step == k)
-        def _(k=k):
-            rows = parts[k][...]
-            gate_sum[...] += jnp.dot(rows, gate_ref[0], preferred_element_type=jnp.float32)
-            up_sum[...] += jnp.dot(rows, up_ref[0], preferred_element_type=jnp.float32)
+    for place, k in enumerate(order):
+        for odd, stack in enumerate((even_ref, odd_ref)):
+
+            @pl.when(step == k + odd)
+            def _(place=place, stack=stack):
+                rows = stack[place]
+                gate_sum[...] += jnp.dot(rows, gate_ref[0], preferred_element_type=jnp.float32)
+                up_sum[...] += jnp.dot(rows, up_ref[0], preferred_element_type=jnp.float32)
 
     @pl.when(step == count - 1)
     def _():
@@ -60,30 +124,25 @@
         out_ref[...] = (gate / (1.0 + jnp.exp(-gate)) * up_sum[...]).astype(out_ref.dtype)
 
 
-def ffn(parts, gate_weight, up_weight, t):
-    count = len(parts)
-    rows, width = parts[0].shape
+def ffn(stacks, order, gate_weight, up_weight, t):
+    n, rows, width = stacks[0].shape
     units = gate_weight.shape[2]
     weight_spec = pl.BlockSpec((1, width, units), lambda k, where: (0, where[0] ^ k, 0))
     return pl.pallas_call(
-        functools.partial(ffn_kernel, count),
+        functools.partial(ffn_kernel, order),
         out_shape=jax.ShapeDtypeStruct((rows, units), jnp.bfloat16),
         grid_spec=pltpu.PrefetchScalarGridSpec(
             num_scalar_prefetch=1,
-            grid=(count,),
-            in_specs=[pl.BlockSpec((rows, width), lambda k, where: (0, 0))] * count
+            grid=(2 * n,),
+            in_specs=[pl.BlockSpec((n, rows, width), lambda k, where: (0, 0, 0))] * 2
             + [weight_spec, weight_spec],
             out_specs=pl.BlockSpec((rows, units), lambda k, where: (0, 0)),
             scratch_shapes=[pltpu.VMEM((rows, units), jnp.float32)] * 2,
         ),
-        compiler_params=pltpu.CompilerParams(vmem_limit_bytes=48 * 1024 * 1024),
-        cost_estimate=pl.CostEstimate(
-            flops=4 * rows * width * count * units,
-            bytes_accessed=2 * (2 * width * count * units + rows * width * count + rows * units),
-            transcendentals=rows * units,
-        ),
+        compiler_params=pltpu.CompilerParams(vmem_limit_bytes=BIG_VMEM),
+        cost_estimate=SMALL_COST,
         name="ffn",
-    )(t.reshape(1).astype(jnp.int32), *parts, gate_weight, up_weight)
+    )(t.reshape(1).astype(jnp.int32), *stacks, gate_weight, up_weight)
 
 
 def chunks_of(width):
@@ -106,6 +165,8 @@
 
 
 def after(value, *others):
+    if not others:
+        return value
     return lax.optimization_barrier((value,) + others)[0]
 
 
@@ -118,12 +179,22 @@
     return found
 
 
+def columns_in_two(own, t, off, width, *earlier):
+    block = own.shape[1] // 4
+    mine, near, far, both = [
+        lax.dynamic_slice(own, (0, (t ^ k) * block + off), (own.shape[0], width)) for k in range(4)
+    ]
+    before_far, before_near = earlier or ((), ())
+    first = xor_permute(after(jnp.stack([far, both]), *before_far), "tensor", 4, 2)
+    pair = after(jnp.stack([near, first[1]]), *before_near)
+    return [mine, first, xor_permute(pair, "tensor", 4, 1)]
+
+
 def rows_to_device(pieces, nt):
     return [xor_permute(pieces[k], "tensor", nt, k) if k else pieces[k] for k in range(nt)]
 
 
 T_AT, Q_AT, KEEP_AT, GIVE_AT, MINE_AT, MEMBER_AT = range(6)
-BIG_VMEM = 48 * 1024 * 1024
 
 
 def full_spec(shape):
@@ -131,76 +202,71 @@
 
 
 def align_kernel(nt, half, sub, flags_ref, place_ref, *refs):
-    sources, outs = refs[:nt], refs[nt:]
-    rows, width = sources[0].shape
+    mine, first, second = refs[:3]
+    outs = refs[3:]
+    rows, width = mine.shape
     lane = lax.broadcasted_iota(jnp.int32, (rows, rows), 1)
     q = flags_ref[Q_AT]
     for k in range(half):
-        first = pl.multiple_of((q ^ k) * sub, sub)
+        start = pl.multiple_of((q ^ k) * sub, sub)
         place = jnp.concatenate(
-            [place_ref[pl.ds(first + b * half * sub, sub), :] for b in range(nt)], axis=0
+            [place_ref[pl.ds(start + b * half * sub, sub), :] for b in range(nt)], axis=0
         )
         total = jnp.zeros((rows, width), jnp.float32)
         for m in range(nt):
             selector = jnp.where(place - m * rows == lane, 1.0, 0.0).astype(jnp.bfloat16)
-            total = total + jnp.dot(
-                selector, sources[m][...], preferred_element_type=jnp.float32
-            )
+            source = (mine[...], second[0], first[0], second[1])[m]
+            total = total + jnp.dot(selector, source, preferred_element_type=jnp.float32)
         outs[k][...] = total.astype(jnp.bfloat16)
 
 
 def align(flags, place, sources, half, sub):
-    nt = len(sources)
+    nt = 4
     rows, width = sources[0].shape
     piece = jax.ShapeDtypeStruct((rows, width), jnp.bfloat16)
     return pl.pallas_call(
         functools.partial(align_kernel, nt, half, sub),
         out_shape=[piece] * half,
         in_specs=[pl.BlockSpec(memory_space=pltpu.SMEM), full_spec(place.shape)]
-        + [full_spec((rows, width))] * nt,
+        + [full_spec(source.shape) for source in sources],
         out_specs=[full_spec((rows, width))] * half,
         compiler_params=pltpu.CompilerParams(vmem_limit_bytes=BIG_VMEM),
-        cost_estimate=pl.CostEstimate(
-            flops=2 * half * nt * rows * rows * width,
-            bytes_accessed=2 * (half + nt) * rows * width,
-            transcendentals=0,
-        ),
+        cost_estimate=SMALL_COST,
         name="align",
     )(flags, place, *sources)
 
 
-def sums_kernel(half, flags_ref, *refs):
+def sums_kernel(half, tile, flags_ref, *refs):
     parts, sent_ref, kept_ref = refs[:half], refs[half], refs[half + 1]
-    keep, give = flags_ref[KEEP_AT], flags_ref[GIVE_AT]
-    sent = jnp.zeros(sent_ref.shape, jnp.float32)
-    kept = jnp.zeros(kept_ref.shape, jnp.float32)
-    for k in range(half):
-        member = flags_ref[MEMBER_AT + k]
-        part = parts[k][...].astype(jnp.float32)
-        sent = sent + jnp.where(member == give, part, 0.0)
-        kept = kept + jnp.where(member == keep, part, 0.0)
-    sent_ref[...] = sent.astype(sent_ref.dtype)
-    kept_ref[...] = kept
-
-
-def sums(flags, parts, tile=64):
+    gives = [jnp.where(flags_ref[MEMBER_AT + k] == flags_ref[GIVE_AT], 1.0, 0.0) for k in range(half)]
+    keeps = [jnp.where(flags_ref[MEMBER_AT + k] == flags_ref[KEEP_AT], 1.0, 0.0) for k in range(half)]
+
+    @pl.loop(0, sent_ref.shape[0] // tile)
+    def _(i):
+        at = pl.ds(pl.multiple_of(i * tile, tile), tile)
+        sent = kept = None
+        for k in range(half):
+            part = parts[k][at, :].astype(jnp.float32)
+            sent = part * gives[k] if k == 0 else sent + part * gives[k]
+            kept = part * keeps[k] if k == 0 else kept + part * keeps[k]
+        sent_ref[at, :] = sent.astype(sent_ref.dtype)
+        kept_ref[at, :] = kept
+
+
+def sums(flags, parts):
     rows, width = parts[0].shape
-    tile = min(tile, rows)
-    spec = pl.BlockSpec((tile, width), lambda i: (i, 0))
+    tile = min(32, rows)
+    spec = full_spec((rows, width))
     return pl.pallas_call(
-        functools.partial(sums_kernel, len(parts)),
-        grid=(rows // tile,),
+        functools.partial(sums_kernel, len(parts), tile),
         out_shape=[
             jax.ShapeDtypeStruct((rows, width), jnp.bfloat16),
             jax.ShapeDtypeStruct((rows, width), jnp.float32),
         ],
         in_specs=[pl.BlockSpec(memory_space=pltpu.SMEM)] + [spec] * len(parts),
         out_specs=[spec, spec],
-        cost_estimate=pl.CostEstimate(
-            flops=2 * len(parts) * rows * width,
-            bytes_accessed=2 * (len(parts) + 3) * rows * width,
-            transcendentals=0,
-        ),
+        compiler_params=pltpu.CompilerParams(vmem_limit_bytes=BIG_VMEM),
+        cost_estimate=SMALL_COST,
         name="sums",
     )(flags, *parts)
 
@@ -223,73 +289,43 @@
         in_specs=[pl.BlockSpec(memory_space=pltpu.SMEM)] + [full_spec((rows, width))] * 2,
         out_specs=[full_spec((sub, width))] * nt,
         compiler_params=pltpu.CompilerParams(vmem_limit_bytes=BIG_VMEM),
-        cost_estimate=pl.CostEstimate(
-            flops=2 * rows * width, bytes_accessed=8 * rows * width, transcendentals=0
-        ),
+        cost_estimate=SMALL_COST,
         name="mean",
     )(scale, kept, other)
 
 
 def assemble_kernel(half, nt, spans, flags_ref, *refs):
-    count = half * len(spans)
-    groups, out_ref, blank, sems, blank_sems = refs[:count], *refs[count:]
-    sub = blank.shape[0]
+    groups, out_ref = refs[:-1], refs[-1]
+    sub = groups[0].shape[1]
     block = out_ref.shape[1] // nt
     mine = flags_ref[MINE_AT] != 0
 
     @pl.when(mine)
     def _():
-        copies = []
         for k in range(half):
             at = pl.multiple_of((flags_ref[Q_AT] ^ k) * sub, sub)
             for m in range(nt):
                 left = pl.multiple_of((flags_ref[T_AT] ^ m) * block, 128)
                 for c, (off, width) in enumerate(spans):
-                    copies.append(
-                        pltpu.make_async_copy(
-                            groups[c * half + k].at[m],
-                            out_ref.at[pl.ds(at, sub), pl.ds(left + off, width)],
-                            sems.at[len(copies)],
-                        )
-                    )
-        for copy in copies:
-            copy.start()
-        for copy in copies:
-            copy.wait()
+                    out_ref[pl.ds(at, sub), pl.ds(left + off, width)] = groups[c * half + k][m]
 
     @pl.when(jnp.logical_not(mine))
     def _():
-        blank[...] = jnp.zeros_like(blank)
-        copies = [
-            pltpu.make_async_copy(
-                blank, out_ref.at[pl.ds(j * sub, sub), :], blank_sems.at[j]
-            )
-            for j in range(half)
-        ]
-        for copy in copies:
-            copy.start()
-        for copy in copies:
-            copy.wait()
+        out_ref[...] = jnp.zeros_like(out_ref)
 
 
 def assemble(flags, gathered, spans, rows, model):
     half = len(gathered[0])
-    nt, sub = gathered[0][0].shape[:2]
-    anywhere = pl.BlockSpec(memory_space=pl.ANY)
+    nt = gathered[0][0].shape[0]
     groups = [piece for group in gathered for piece in group]
     return pl.pallas_call(
         functools.partial(assemble_kernel, half, nt, spans),
         out_shape=jax.ShapeDtypeStruct((rows, model), jnp.bfloat16),
-        in_specs=[pl.BlockSpec(memory_space=pltpu.SMEM)] + [anywhere] * len(groups),
-        out_specs=anywhere,
-        scratch_shapes=[
-            pltpu.VMEM((sub, model), jnp.bfloat16),
-            pltpu.SemaphoreType.DMA((half * nt * len(spans),)),
-            pltpu.SemaphoreType.DMA((half,)),
-        ],
-        cost_estimate=pl.CostEstimate(
-            flops=0, bytes_accessed=4 * rows * model, transcendentals=0
-        ),
+        in_specs=[pl.BlockSpec(memory_space=pltpu.SMEM)]
+        + [full_spec(piece.shape) for piece in groups],
+        out_specs=full_spec((rows, model)),
+        compiler_params=pltpu.CompilerParams(vmem_limit_bytes=BIG_VMEM),
+        cost_estimate=SMALL_COST,
         name="assemble",
     )(flags, *groups)
 
@@ -319,22 +355,23 @@
             axis=1,
         )
         self.scale = 1.0 / jnp.where(keep == 0, self.sizes[0:1], self.sizes[1:2])
-        self.sources = [
-            columns_to_device(own, t, nt, off, width) for off, width in self.spans
-        ]
-
-    def send_aligned(self, c):
-        pieces = align(self.flags, self.place, self.sources[c], self.half, self.sub)
+
+    def columns(self, c, *earlier):
+        return columns_in_two(self.own, self.t, *self.spans[c], *earlier)
+
+    def send_aligned(self, sources, *earlier):
+        sources = all_after(sources, *earlier)
+        pieces = align(self.flags, self.place, sources, self.half, self.sub)
         sent = [
             xor_permute(piece, "expert", self.ne, k) if k else piece
             for k, piece in enumerate(pieces)
         ]
         return pieces[0], sent
 
-    def back_and_out(self, pieces, *others):
-        lines = jnp.stack(rows_to_device(pieces, self.nt))
-        if others:
-            lines = after(lines, *others)
+    def back(self, pieces):
+        return jnp.stack(rows_to_device(pieces, self.nt))
+
+    def out(self, lines):
         return [
             xor_permute(lines, "expert", self.ne, k) if k else lines for k in range(self.half)
         ]
@@ -354,7 +391,7 @@
                     total = total + jnp.where(near[k] == 1, parts[k].astype(jnp.float32), 0.0)
                 other = xor_permute(total.astype(jnp.bfloat16), "expert", self.ne, self.half)
                 scale = (1.0 / self.sizes[1]).reshape(1)
-                again.append(self.back_and_out(mean_of(scale, total, other, self.nt)))
+                again.append(self.out(self.back(mean_of(scale, total, other, self.nt))))
             mine = jnp.where(self.owners[1:2] == self.e, 1, 0).astype(jnp.int32)
             flags = jnp.concatenate(
                 [self.flags[:MINE_AT], mine, self.flags[MINE_AT + 1 :]]
@@ -417,9 +454,9 @@
     model = own.shape[1]
     block = model // nt
 
-    perm = jnp.concatenate(gather_tensor(hidden_perm[0], nt))
+    perm = jnp.concatenate(gather_small(hidden_perm[0], nt))
     two = None
-    if ne == 8 and owners.shape[0] == 2:
+    if ne == 8 and nt == 4 and owners.shape[0] == 2:
         two = TwoClusters(own, perm, cluster, owners, e, t, ne, nt)
 
     flat = routes.reshape(-1)
@@ -436,34 +473,35 @@
     ).astype(jnp.bfloat16)
     arrived = lax.all_to_all(outgoing, "expert", split_axis=0, concat_axis=0, tiled=True)
     routed = arrived.shape[0]
-    stacked = gather_tensor(jnp.concatenate([arrived, probe_rows], axis=0), nt)
-
+    stacked = jnp.concatenate([arrived, probe_rows], axis=0)
     if two is not None:
-        parts, others, kept, marks = [], [], [], []
-        for c in range(len(two.spans)):
-            mark, sent = two.send_aligned(c)
+        last = len(two.spans) - 1
+        sources, marks, parts = [], [], []
+        for c in range(last + 1):
+            earlier = ((sources[-1][1],), parts[-1][1:]) if c else ()
+            sources.append(two.columns(c, *earlier))
+            mark, sent = two.send_aligned(sources[c], *marks[-1:])
             marks.append(mark)
             parts.append(sent)
-        stacked = list(lax.optimization_barrier((*stacked, *marks))[:nt])
-    hidden = ffn(stacked, gate_weight, up_weight, t)
-    routed_hidden, probe_hidden = hidden[:routed], hidden[routed:]
+        stacked = after(stacked, sources[-1][1])
+        given, own_sum = sums(two.flags, all_after(parts[0], marks[-1]))
+        others, kept = [xor_permute(given, "expert", ne, two.half)], [own_sum]
+    even, order = gather_even(stacked, nt)
     if two is not None:
-        for c in range(len(two.spans)):
-            given, own_sum = sums(two.flags, parts[c])
-            if c == 0:
-                given = after(given, hidden)
+        even = after(even, kept[0])
+    odd = xor_permute(even, "tensor", nt, 1)
+    if two is not None:
+        for c in range(1, last + 1):
+            given, own_sum = sums(two.flags, all_after(parts[c], kept[-1]))
             others.append(xor_permute(given, "expert", ne, two.half))
             kept.append(own_sum)
-
-    partials = [
-        jnp.dot(
-            routed_hidden,
-            lax.dynamic_slice(own, (0, (t ^ k) * block), (own.shape[0], block)),
-            preferred_element_type=jnp.float32,
-        )
-        for k in range(nt)
-    ]
-    returned = scatter_tensor(partials, nt).astype(jnp.bfloat16)
+        odd = after(odd, kept[-1])
+    hidden = ffn((even, odd), order, gate_weight, up_weight, t)
+    probe_hidden = hidden[routed:]
+    send, keep = down(hidden, routed, own, t, nt)
+    if two is not None:
+        keep = after(keep, others[0])
+    returned = sum_tensor(send, keep, nt)
     home = lax.all_to_all(returned, "expert", split_axis=0, concat_axis=0, tiled=True)
     chooser = (target.T.reshape(-1)[:, None] == slots[None, :]).astype(jnp.bfloat16)
     picked = jnp.dot(chooser, home, preferred_element_type=jnp.float32)
@@ -485,8 +523,12 @@
     if two is not None:
         gathered = []
         for c in range(len(two.spans)):
-            means = mean_of(two.scale, kept[c], others[c], nt)
-            gathered.append(two.back_and_out(means, *((returned,) if c == 0 else ())))
+            other = after(others[c], lines) if c else others[c]
+            means = mean_of(two.scale, kept[c], other, nt)
+            lines = two.back(means)
+            if c == len(two.spans) - 1:
+                lines = after(lines, returned)
+            gathered.append(two.out(lines))
         gathered[-1][0] = after(gathered[-1][0], mixed, correlation)
         merged = two.finish(gathered, parts)
     else:

time: 377 us -> 251 us (0.67)
  Pallas kernels: 142 us -> 32.9 us
  matrix products: 16.6 us -> 6.16 us
  local copies, waits for them, and re-layouts: 19.9 us -> 11.1 us
  starting transfers between devices: 45.2 us -> 38.8 us
  other arithmetic: 7.49 us -> 13.1 us
    pallas_call x1, Pallas kernels: 113 us -> 3.25 us  [assemble(): pl.pallas_call(functools.partial(assemble_kernel, half, nt, spans), out_s...]
    dot_general x4 -> x0, matrix products: 10.4 us -> none  [on_device(): jnp.dot(routed_hidden, lax.dynamic_slice(own, (0, (t ^ k) * block), (own....]
    ppermute x35 -> x31, waiting for transfers between devices: 109 us -> 119 us  [xor_permute(): return lax.ppermute(value, axis, [(i, i ^ k) for i in range(size)])]
    unnamed x57 -> x31, local copies, waits for them, and re-layouts: 9.78 us -> 1.93 us
    ppermute x35 -> x31, starting transfers between devices: 33.6 us -> 27 us  [xor_permute(): return lax.ppermute(value, axis, [(i, i ^ k) for i in range(size)])]
    all_to_all x1, waiting for transfers between devices: 6.5 us -> 0.01 us  [on_device(): lax.all_to_all(outgoing, 'expert', split_axis=0, concat_axis=0, tiled=True)]
    pallas_call x3 -> x4, Pallas kernels: 17.4 us -> 16.7 us  [the longest x1 6.42 us: ffn(): pl.pallas_call(functools.partial(ffn_kernel, order), out_shape=jax.ShapeD...]
  transfers between devices with their start and end apart: 38 -> 34, of which waited for: 14 -> 19; matrix products, arithmetic and copies ran while one was open for 8% -> 11% of each run, Pallas kernels for 6% -> 4%
where the time goes in v4:
time: 251 us; the launch traced here: 250 us
  waiting for transfers between devices  119 us (47%)
  starting transfers between devices  38.8 us (15%)
  Pallas kernels  32.9 us (13%)
  between operations  21.4 us (9%)
  other arithmetic  13.1 us (5%)
  local copies, waits for them, and re-layouts  11.1 us (4%)
  blocking collectives  7.23 us (3%)
  matrix products  6.16 us (2%)
    ppermute x31, waiting for transfers between devices, xor_permute(): return lax.ppermute(value, axis, [(i, i ^ k) for i in range(size)])  119 us
    ppermute x31, starting transfers between devices, xor_permute(): return lax.ppermute(value, axis, [(i, i ^ k) for i in range(size)])  27 us
    pallas_call x2, Pallas kernels, align(): pl.pallas_call(functools.partial(align_kernel, nt, half, sub), out_shape=...  11.7 us
    all_gather x1, blocking collectives, on_device(): partner_full = lax.all_gather(partner, 'tensor', axis=1, tiled=True)  7.23 us
    pallas_call x1, Pallas kernels, ffn(): pl.pallas_call(functools.partial(ffn_kernel, order), out_shape=jax.ShapeD...  6.42 us
    all_to_all x1, starting transfers between devices, on_device(): lax.all_to_all(outgoing, 'expert', split_axis=0, concat_axis=0, tiled=True)  6.18 us
    all_to_all x1, starting transfers between devices, on_device(): lax.all_to_all(returned, 'expert', split_axis=0, concat_axis=0, tiled=True)  5.57 us
    pallas_call x1, Pallas kernels, down(): pl.pallas_call(functools.partial(down_kernel, count), out_shape=[shape, s...  5.18 us
  transfers between devices with their start and end apart: 34, of which 19 were waited for; matrix products, arithmetic and copies ran while one was open for 11% of the time, Pallas kernels for 4%

profile of v4, /device:TPU:0, one launch (start us, length us, event | category | flops | bytes accessed | tf_op | source)
XLA Modules:
  0.0 250.1 jit_solution(6760803411000180643)
XLA Ops:
  7.2 3.0 %collective-permute-start.18 = (s32[512]{0:T(512)}, s32[512]{0:T(512)S(1)}, u32[]{:S(2)}, u32[]{:S(2)}) collective-permute-start(s32[512]{0:T(512)} %bitcast.97), channel_id=1, source_target_pairs={{0,2},{1,3},{2,0},{3,1},{4,6},{5,7},{6,4},{7,5},{8,10},{9,11},{10,... | collective-permute-start | bytes 6152 | tf_op jit(solution)/shard_map/ppermute | solution.py:12
  10.2 1.7 constant_dynamic-slice_fusion.1
  11.9 1.1 pad_maximum_fusion.3
  13.8 1.1 convolution_convert_fusion
  14.9 6.2 %all-to-all-start = ((bf16[8,40,896]{2,1,0:T(8,128)(2,1)}), bf16[8,40,896]{2,1,0:T(8,128)(2,1)}, u32[]{:S(2)}, u32[]{:S(2)}) async-start(bf16[8,40,896]{2,1,0:T(8,128)(2,1)} %bitcast.22), calls=%async_computation | async-start | bytes 1146880 | tf_op jit(solution)/shard_map/all_to_all | solution.py:474
  21.2 0.6 dynamic_slice.44
  23.7 2.4 constant_dynamic-slice_fusion
  26.2 1.0 pad_maximum_fusion.6
  27.2 11.6 %collective-permute-done.14.refs_1_ = bf16[2,512,512]{2,1,0:T(8,128)(2,1)S(1)} collective-permute-done((bf16[2,512,512]{2,1,0:T(8,128)(2,1)}, bf16[2,512,512]{2,1,0:T(8,128)(2,1)S(1)}, u32[]{:S(2)}, u32[]{:S(2)}) %collective-permute-start.14) | collective-permute-done | bytes 1048608 | tf_op jit(solution)/shard_map/ppermute | solution.py:12
  38.8 1.1 pad_maximum_fusion.4
  40.0 0.7 fusion.28
  41.2 0.6 fusion.27
  44.4 1.3 copy.47
  46.0 2.2 fusion.7.place_ref
  48.2 6.6 %align.2 = (bf16[512,512]{1,0:T(8,128)(2,1)}, bf16[512,512]{1,0:T(8,128)(2,1)}, bf16[512,512]{1,0:T(8,128)(2,1)}, bf16[512,512]{1,0:T(8,128)(2,1)}) custom-call(s32[9]{0:T(128)S(1)} %concatenate.56.flags_ref, s32[2048,1]{1,0:T(8,128)S(1)} %fusion.7.place_ref, bf16[512,512]{1,0:T(8,128)(2,1)S(1)} %get-tuple-element.113.refs_0_, ...), custom_call_target="tpu_custom_call" | custom-call | flops 1024 | bytes 1024 | tf_op jit(solution)/shard_map/align/pallas_call | solution.py:227
  54.9 1.7 collective-permute-start.21
  56.6 1.6 collective-permute-start.22
  58.4 1.2 pad_maximum_fusion.5
  59.6 5.8 %collective-permute-done.15.refs_1_ = bf16[2,512,384]{2,1,0:T(8,128)(2,1)S(1)} collective-permute-done((bf16[2,512,384]{2,1,0:T(8,128)(2,1)}, bf16[2,512,384]{2,1,0:T(8,128)(2,1)S(1)}, u32[]{:S(2)}, u32[]{:S(2)}) %collective-permute-start.15) | collective-permute-done | bytes 786464 | tf_op jit(solution)/shard_map/ppermute | solution.py:12
  65.7 1.1 pad_maximum_fusion.7
  66.9 2.1 collective-permute-done.21.refs_1_
  69.0 2.6 %collective-permute-done.22.refs_2_ = bf16[512,512]{1,0:T(8,128)(2,1)S(1)} collective-permute-done((bf16[512,512]{1,0:T(8,128)(2,1)}, bf16[512,512]{1,0:T(8,128)(2,1)S(1)}, u32[]{:S(2)}, u32[]{:S(2)}) %collective-permute-start.22) | collective-permute-done | bytes 524320 | tf_op jit(solution)/shard_map/ppermute | solution.py:12
  71.7 0.8 copy-done.6
  72.5 8.7 %collective-permute-done.23.refs_3_ = bf16[512,512]{1,0:T(8,128)(2,1)} collective-permute-done((bf16[512,512]{1,0:T(8,128)(2,1)}, bf16[512,512]{1,0:T(8,128)(2,1)}, u32[]{:S(2)}, u32[]{:S(2)}) %collective-permute-start.23) | collective-permute-done | bytes 524320 | tf_op jit(solution)/shard_map/ppermute | solution.py:12
  81.2 3.2 %collective-permute-done.16 = bf16[1,448,896]{2,1,0:T(8,128)(2,1)S(1)} collective-permute-done((bf16[1,448,896]{2,1,0:T(8,128)(2,1)S(1)}, bf16[1,448,896]{2,1,0:T(8,128)(2,1)S(1)}, u32[]{:S(2)}, u32[]{:S(2)}) %collective-permute-start.16) | collective-permute-done | bytes 802848 | tf_op jit(solution)/shard_map/ppermute | solution.py:12
  84.7 5.1 %align.3 = (bf16[512,384]{1,0:T(8,128)(2,1)S(1)}, bf16[512,384]{1,0:T(8,128)(2,1)S(1)}, bf16[512,384]{1,0:T(8,128)(2,1)S(1)}, bf16[512,384]{1,0:T(8,128)(2,1)S(1)}) custom-call(s32[9]{0:T(128)S(1)} %concatenate.56.flags_ref, s32[2048,1]{1,0:T(8,128)S(1)} %fusion.7.place_ref, bf16[512,384]{1,0:T(8,128)(2,1)S(1)} %copy-done.2, ...), custom_call_target="tpu_custom_call" | custom-call | flops 1024 | bytes 1024 | tf_op jit(solution)/shard_map/align/pallas_call | solution.py:227
  89.8 3.1 %sums.2 = (bf16[512,512]{1,0:T(8,128)(2,1)}, f32[512,512]{1,0:T(8,128)S(1)}) custom-call(s32[9]{0:T(128)S(1)} %concatenate.56.flags_ref, bf16[512,512]{1,0:T(8,128)(2,1)S(1)} %copy-done.4, bf16[512,512]{1,0:T(8,128)(2,1)} %collective-permute-done.21.refs_1_, bf16[512,512]{1,0:T(8,128)(2,1)S(1)} %copy-done.7, bf16[512,512]{1,0:T(8,128)(2,1)} %collective-permute-done.23.refs_3_), custom_call_target="tpu_custom_call" | custom-call | flops 1024 | bytes 1024 | tf_op jit(solution)/shard_map/sums/pallas_call | solution.py:260
  92.9 1.5 collective-permute-start.26
  94.4 1.6 collective-permute-start.27
  96.4 8.0 %collective-permute-done.26.refs_1_ = bf16[512,384]{1,0:T(8,128)(2,1)S(1)} collective-permute-done((bf16[512,384]{1,0:T(8,128)(2,1)S(1)}, bf16[512,384]{1,0:T(8,128)(2,1)S(1)}, u32[]{:S(2)}, u32[]{:S(2)}) %collective-permute-start.26) | collective-permute-done | bytes 393248 | tf_op jit(solution)/shard_map/ppermute | solution.py:12
  104.5 1.9 collective-permute-done.27.refs_2_
  106.4 7.7 %collective-permute-done.28.refs_3_ = bf16[512,384]{1,0:T(8,128)(2,1)S(1)} collective-permute-done((bf16[512,384]{1,0:T(8,128)(2,1)S(1)}, bf16[512,384]{1,0:T(8,128)(2,1)S(1)}, u32[]{:S(2)}, u32[]{:S(2)}) %collective-permute-start.28) | collective-permute-done | bytes 393248 | tf_op jit(solution)/shard_map/ppermute | solution.py:12
  114.1 1.9 sums.3
  116.0 6.4 %ffn.1.rows_ref = bf16[448,512]{1,0:T(8,128)(2,1)S(1)} custom-call(s32[1]{0:T(128)} %bitcast.19.where_ref, bf16[2,448,896]{2,1,0:T(8,128)(2,1)S(1)} %pad_maximum_fusion.2.even_ref, bf16[2,448,896]{2,1,0:T(8,128)(2,1)S(1)} %collective-permute-done.25.odd_ref, bf16[1,3584,512]{2,1,0:T(8,128)(2,1)} %gate_ref.1, bf16[1,3584,512]{2,1,0:T(8,128)(2,1)} %up_ref.1), custom_call_target="tpu_custom_call" | custom-call | flops 1024 | bytes 1024 | tf_op jit(solution)/shard_map/ffn/pallas_call | solution.py:131
  122.5 5.2 %down.1 = (bf16[2,320,896]{2,1,0:T(8,128)(2,1)}, bf16[2,320,896]{2,1,0:T(8,128)(2,1)S(1)}) custom-call(s32[1]{0:T(128)} %bitcast.19.where_ref, bf16[448,512]{1,0:T(8,128)(2,1)S(1)} %ffn.1.rows_ref, bf16[512,3584]{1,0:T(8,128)(2,1)} %bitcast.78), custom_call_target="tpu_custom_call" | custom-call | flops 1024 | bytes 1024 | tf_op jit(solution)/shard_map/down/pallas_call | solution.py:57
  127.7 2.6 %collective-permute-start.29 = (bf16[512,512]{1,0:T(8,128)(2,1)}, bf16[512,512]{1,0:T(8,128)(2,1)}, u32[]{:S(2)}, u32[]{:S(2)}) collective-permute-start(bf16[512,512]{1,0:T(8,128)(2,1)} %get-tuple-element.141), channel_id=1, source_target_pairs={{0,16},{4,20},{8,24},{12,28},{16,0},{20,4},{24,8},{28,12},{1,17},{... | collective-permute-start | bytes 1572872 | tf_op jit(solution)/shard_map/ppermute | solution.py:12
  130.3 0.7 slice.89
  130.9 27.8 %collective-permute-done.29.other_ref = bf16[512,512]{1,0:T(8,128)(2,1)} collective-permute-done((bf16[512,512]{1,0:T(8,128)(2,1)}, bf16[512,512]{1,0:T(8,128)(2,1)}, u32[]{:S(2)}, u32[]{:S(2)}) %collective-permute-start.29) | collective-permute-done | bytes 524320 | tf_op jit(solution)/shard_map/ppermute | solution.py:12
  158.8 1.5 convert_add_fusion
  160.3 0.6 collective-permute-start.31
  161.0 0.6 fusion.26
  163.0 1.2 mean.6
  164.3 1.6 collective-permute-start.33
  166.1 10.2 %collective-permute-done.31 = bf16[320,896]{1,0:T(8,128)(2,1)S(1)} collective-permute-done((bf16[320,896]{1,0:T(8,128)(2,1)S(1)}, bf16[320,896]{1,0:T(8,128)(2,1)S(1)}, u32[]{:S(2)}, u32[]{:S(2)}) %collective-permute-start.31) | collective-permute-done | bytes 573472 | tf_op jit(solution)/shard_map/ppermute | solution.py:12
  176.3 1.0 fusion.4
  177.2 5.6 %all-to-all-start.1 = ((bf16[8,40,896]{2,1,0:T(8,128)(2,1)}), bf16[8,40,896]{2,1,0:T(8,128)(2,1)}, u32[]{:S(2)}, u32[]{:S(2)}) async-start(bf16[8,40,896]{2,1,0:T(8,128)(2,1)} %bitcast.38), calls=%async_computation.1 | async-start | bytes 1146880 | tf_op jit(solution)/shard_map/all_to_all | solution.py:505
  182.9 3.0 %collective-permute-start.37 = (bf16[4,128,512]{2,1,0:T(8,128)(2,1)S(1)}, bf16[4,128,512]{2,1,0:T(8,128)(2,1)S(1)}, u32[]{:S(2)}, u32[]{:S(2)}) collective-permute-start(bf16[4,128,512]{2,1,0:T(8,128)(2,1)S(1)} %pad_maximum_fusion.8.refs_0_), channel_id=1, source_target_pairs={{0,12},{4,8},{8,4},{12,0},{16,28},{20,24},{24,20},{28,16},{1,13},{... | collective-permute-start | bytes 1572872 | tf_op jit(solution)/shard_map/ppermute | solution.py:12
  185.9 9.8 %collective-permute-done.38.other_ref = bf16[512,384]{1,0:T(8,128)(2,1)S(1)} collective-permute-done((bf16[512,384]{1,0:T(8,128)(2,1)}, bf16[512,384]{1,0:T(8,128)(2,1)S(1)}, u32[]{:S(2)}, u32[]{:S(2)}) %collective-permute-start.38) | collective-permute-done | bytes 393248 | tf_op jit(solution)/shard_map/ppermute | solution.py:12
  195.8 2.5 collective-permute-start.40
  198.4 0.6 iota_compare_fusion.6
  200.3 1.3 collective-permute-start.35
  202.0 1.6 collective-permute-done.41
  204.0 2.5 collective-permute-start.43
  206.4 1.5 fusion.1
  207.9 7.2 %all_gather.11 = bf16[128,2048]{1,0:T(8,128)(2,1)S(1)} all-gather(bf16[128,512]{1,0:T(8,128)(2,1)S(1)} %fusion.1), channel_id=1, replica_groups=mesh['expert'=8,'tensor'=4] {'tensor'}, dimensions={1}, use_global_device_ids=true | all-gather | bytes 655360 | tf_op jit(solution)/shard_map/all_gather | solution.py:516
  215.2 0.7 collective-permute-start.42
  215.9 2.7 %convolution_multiply_fusion = f32[512,2048]{1,0:T(8,128)} fusion(bf16[128,2048]{1,0:T(8,128)(2,1)S(1)} %all_gather.11, bf16[448,512]{1,0:T(8,128)(2,1)S(1)} %ffn.1.rows_ref), kind=kOutput, calls=%fused_computation.10 | convolution fusion | flops 269484032 | bytes 4849664 | tf_op jit(solution)/shard_map/dot_general | solution.py:518
  218.7 2.3 fusion.2
  220.9 0.8 collective-permute-done.36.refs_2_
  221.8 1.9 collective-permute-done.35.refs_1_
  223.7 8.4 %collective-permute-done.44.refs_7_ = bf16[4,128,384]{2,1,0:T(8,128)(2,1)S(1)} collective-permute-done((bf16[4,128,384]{2,1,0:T(8,128)(2,1)S(1)}, bf16[4,128,384]{2,1,0:T(8,128)(2,1)S(1)}, u32[]{:S(2)}, u32[]{:S(2)}) %collective-permute-start.44) | collective-permute-done | bytes 393248 | tf_op jit(solution)/shard_map/ppermute | solution.py:12
  232.1 6.5 %collective-permute-done.43.refs_6_ = bf16[4,128,384]{2,1,0:T(8,128)(2,1)} collective-permute-done((bf16[4,128,384]{2,1,0:T(8,128)(2,1)S(1)}, bf16[4,128,384]{2,1,0:T(8,128)(2,1)}, u32[]{:S(2)}, u32[]{:S(2)}) %collective-permute-start.43) | collective-permute-done | bytes 393248 | tf_op jit(solution)/shard_map/ppermute | solution.py:12
  239.0 3.2 %assemble.3 = bf16[512,3584]{1,0:T(8,128)(2,1)} custom-call(s32[9]{0:T(128)S(1)} %concatenate.56.flags_ref, bf16[4,128,512]{2,1,0:T(8,128)(2,1)S(1)} %pad_maximum_fusion.8.refs_0_, bf16[4,128,512]{2,1,0:T(8,128)(2,1)S(1)} %collective-permute-done.35.refs_1_, bf16[4,128,512]{2,1,0:T(8,128)(2,1)S(1)} %collective-permute-done.36.refs_2_, ...), custom_call_target="tpu_custom_call" | custom-call | flops 1024 | bytes 1024 | tf_op jit(solution)/shard_map/assemble/pallas_call | solution.py:321
  242.3 0.9 copy-done.1
  (86 shorter events, 5.2 us)
Async XLA Ops:
  7.2 6.6 %copy-start = (bf16[128,896]{1,0:T(8,128)(2,1)S(1)}, bf16[128,896]{1,0:T(8,128)(2,1)}, u32[]{:S(2)}) copy-start(bf16[128,896]{1,0:T(8,128)(2,1)} %param.12) | copy-start | bytes 688132
  7.2 33.5 %collective-permute-start.18 = (s32[512]{0:T(512)}, s32[512]{0:T(512)S(1)}, u32[]{:S(2)}, u32[]{:S(2)}) collective-permute-start(s32[512]{0:T(512)} %bitcast.97), channel_id=1, source_target_pairs={{0,2},{1,3},{2,0},{3,1},{4,6},{5,7},{6,4},{7,5},{8,10},{9,11},{10,... | collective-permute-start | bytes 6152 | tf_op jit(solution)/shard_map/ppermute | solution.py:12
  10.2 34.1 %collective-permute-start.17 = (s32[512]{0:T(512)}, s32[512]{0:T(512)S(1)}, u32[]{:S(2)}, u32[]{:S(2)}) collective-permute-start(s32[512]{0:T(512)} %bitcast.98), channel_id=1, source_target_pairs={{0,1},{1,0},{2,3},{3,2},{4,5},{5,4},{6,7},{7,6},{8,9},{9,8},{10,11... | collective-permute-start | bytes 6152 | tf_op jit(solution)/shard_map/ppermute | solution.py:12
  10.2 2.9 %copy-start.14 = (s32[128,2]{0,1:T(2,128)S(1)}, s32[128,2]{0,1:T(2,128)}, u32[]{:S(2)}) copy-start(s32[128,2]{0,1:T(2,128)} %param.13) | copy-start | bytes 3076
  11.9 9.3 %copy-start.3 = (s32[8]{0:T(128)S(1)}, s32[8]{0:T(128)}, u32[]{:S(2)}) copy-start(s32[8]{0:T(128)} %param.20) | copy-start | bytes 100
  13.0 25.8 %collective-permute-start.14 = (bf16[2,512,512]{2,1,0:T(8,128)(2,1)}, bf16[2,512,512]{2,1,0:T(8,128)(2,1)S(1)}, u32[]{:S(2)}, u32[]{:S(2)}) collective-permute-start(bf16[2,512,512]{2,1,0:T(8,128)(2,1)} %pad_maximum_fusion.3), channel_id=1, source_target_pairs={{0,2},{1,3},{2,0},{3,1},{4,6},{5,7},{6,4},{7,5},{8,10},{9,11},{10,... | collective-permute-start | bytes 3145736 | tf_op jit(solution)/shard_map/ppermute | solution.py:12
  14.9 43.4 %all-to-all-start = ((bf16[8,40,896]{2,1,0:T(8,128)(2,1)}), bf16[8,40,896]{2,1,0:T(8,128)(2,1)}, u32[]{:S(2)}, u32[]{:S(2)}) async-start(bf16[8,40,896]{2,1,0:T(8,128)(2,1)} %bitcast.22), calls=%async_computation | async-start | bytes 1146880 | tf_op jit(solution)/shard_map/all_to_all | solution.py:474
  21.1 185.3 %all-gather.3.cloned.1.call-start = ((), (), s32[]{:S(2)}) async-start(), calls=%async_computation.2 | async-start | bytes 1179648 | tf_op jit(solution)/shard_map/all_gather | solution.py:511
  23.7 3.4 %copy-start.13 = (s32[2]{0:T(128)S(1)}, s32[2]{0:T(128)}, u32[]{:S(2)}) copy-start(s32[2]{0:T(128)} %param.21) | copy-start | bytes 28
  26.2 18.2 %copy-start.15 = (s32[1,512]{1,0:T(1,128)S(1)}, s32[1,512]{1,0:T(1,128)}, u32[]{:S(2)}) copy-start(s32[1,512]{1,0:T(1,128)} %param.19) | copy-start | bytes 6148
  39.9 8.4 %collective-permute-start.20 = (bf16[2,512,512]{2,1,0:T(8,128)(2,1)}, bf16[2,512,512]{2,1,0:T(8,128)(2,1)}, u32[]{:S(2)}, u32[]{:S(2)}) collective-permute-start(bf16[2,512,512]{2,1,0:T(8,128)(2,1)} %pad_maximum_fusion.4), channel_id=1, source_target_pairs={{0,1},{1,0},{2,3},{3,2},{4,5},{5,4},{6,7},{7,6},{8,9},{9,8},{10,11... | collective-permute-start | bytes 3145736 | tf_op jit(solution)/shard_map/ppermute | solution.py:12
  40.7 3.7 %collective-permute-start.19 = (s32[512]{0:T(512)S(1)}, s32[512]{0:T(512)S(1)}, u32[]{:S(2)}, u32[]{:S(2)}) collective-permute-start(s32[512]{0:T(512)S(1)} %collective-permute-done.18), channel_id=1, source_target_pairs={{0,1},{1,0},{2,3},{3,2},{4,5},{5,4},{6,7},{7,6},{8,9},{9,8},{10,11... | collective-permute-start | bytes 6152 | tf_op jit(solution)/shard_map/ppermute | solution.py:12
  45.7 19.7 %collective-permute-start.15 = (bf16[2,512,384]{2,1,0:T(8,128)(2,1)}, bf16[2,512,384]{2,1,0:T(8,128)(2,1)S(1)}, u32[]{:S(2)}, u32[]{:S(2)}) collective-permute-start(bf16[2,512,384]{2,1,0:T(8,128)(2,1)} %pad_maximum_fusion.6), channel_id=1, source_target_pairs={{0,2},{1,3},{2,0},{3,1},{4,6},{5,7},{6,4},{7,5},{8,10},{9,11},{10,... | collective-permute-start | bytes 2359304 | tf_op jit(solution)/shard_map/ppermute | solution.py:12
  54.9 14.1 %collective-permute-start.21 = (bf16[512,512]{1,0:T(8,128)(2,1)}, bf16[512,512]{1,0:T(8,128)(2,1)}, u32[]{:S(2)}, u32[]{:S(2)}) collective-permute-start(bf16[512,512]{1,0:T(8,128)(2,1)} %get-tuple-element.117), channel_id=1, source_target_pairs={{0,4},{4,0},{8,12},{12,8},{16,20},{20,16},{24,28},{28,24},{1,5},{5... | collective-permute-start | bytes 1572872 | tf_op jit(solution)/shard_map/ppermute | solution.py:12
  56.6 15.1 %collective-permute-start.22 = (bf16[512,512]{1,0:T(8,128)(2,1)}, bf16[512,512]{1,0:T(8,128)(2,1)S(1)}, u32[]{:S(2)}, u32[]{:S(2)}) collective-permute-start(bf16[512,512]{1,0:T(8,128)(2,1)} %get-tuple-element.118), channel_id=1, source_target_pairs={{0,8},{4,12},{8,0},{12,4},{16,24},{20,28},{24,16},{28,20},{1,9},{5... | collective-permute-start | bytes 1572872 | tf_op jit(solution)/shard_map/ppermute | solution.py:12
  58.2 23.1 %collective-permute-start.23 = (bf16[512,512]{1,0:T(8,128)(2,1)}, bf16[512,512]{1,0:T(8,128)(2,1)}, u32[]{:S(2)}, u32[]{:S(2)}) collective-permute-start(bf16[512,512]{1,0:T(8,128)(2,1)} %get-tuple-element.119), channel_id=1, source_target_pairs={{0,12},{4,8},{8,4},{12,0},{16,28},{20,24},{24,20},{28,16},{1,13},{... | collective-permute-start | bytes 1572872 | tf_op jit(solution)/shard_map/ppermute | solution.py:12
  65.4 19.1 %collective-permute-start.16 = (bf16[1,448,896]{2,1,0:T(8,128)(2,1)S(1)}, bf16[1,448,896]{2,1,0:T(8,128)(2,1)S(1)}, u32[]{:S(2)}, u32[]{:S(2)}) collective-permute-start(bf16[1,448,896]{2,1,0:T(8,128)(2,1)S(1)} %bitcast.80), channel_id=1, source_target_pairs={{0,2},{1,3},{2,0},{3,1},{4,6},{5,7},{6,4},{7,5},{8,10},{9,11},{10,... | collective-permute-start | bytes 2408456 | tf_op jit(solution)/shard_map/ppermute | solution.py:12
  65.7 18.9 %copy-start.2 = (bf16[512,384]{1,0:T(8,128)(2,1)S(1)}, bf16[512,384]{1,0:T(8,128)(2,1)}, u32[]{:S(2)}) copy-start(bf16[512,384]{1,0:T(8,128)(2,1)} %get-tuple-element.121.refs_0_) | copy-start | bytes 1179652
  71.7 0.8 copy-start.6
  81.2 3.4 %collective-permute-start.24 = (bf16[2,512,384]{2,1,0:T(8,128)(2,1)S(1)}, bf16[2,512,384]{2,1,0:T(8,128)(2,1)S(1)}, u32[]{:S(2)}, u32[]{:S(2)}) collective-permute-start(bf16[2,512,384]{2,1,0:T(8,128)(2,1)S(1)} %pad_maximum_fusion.7), channel_id=1, source_target_pairs={{0,1},{1,0},{2,3},{3,2},{4,5},{5,4},{6,7},{7,6},{8,9},{9,8},{10,11... | collective-permute-start | bytes 2359304 | tf_op jit(solution)/shard_map/ppermute | solution.py:12
  84.6 5.2 %copy-start.4 = (bf16[512,512]{1,0:T(8,128)(2,1)S(1)}, bf16[512,512]{1,0:T(8,128)(2,1)}, u32[]{:S(2)}) copy-start(bf16[512,512]{1,0:T(8,128)(2,1)} %get-tuple-element.125.refs_0_) | copy-start | bytes 1572868
  84.6 5.2 %copy-start.7 = (bf16[512,512]{1,0:T(8,128)(2,1)S(1)}, bf16[512,512]{1,0:T(8,128)(2,1)}, u32[]{:S(2)}) copy-start(bf16[512,512]{1,0:T(8,128)(2,1)} %copy-done.6) | copy-start | bytes 1572868
  89.8 32.7 %copy-start.9 = (bf16[512,384]{1,0:T(8,128)(2,1)}, bf16[512,384]{1,0:T(8,128)(2,1)S(1)}, u32[]{:S(2)}) copy-start(bf16[512,384]{1,0:T(8,128)(2,1)S(1)} %get-tuple-element.134.refs_0_) | copy-start | bytes 1179652
  92.9 23.1 %collective-permute-start.25 = (bf16[2,448,896]{2,1,0:T(8,128)(2,1)S(1)}, bf16[2,448,896]{2,1,0:T(8,128)(2,1)S(1)}, u32[]{:S(2)}, u32[]{:S(2)}) collective-permute-start(bf16[2,448,896]{2,1,0:T(8,128)(2,1)S(1)} %pad_maximum_fusion.2.even_ref), channel_id=1, source_target_pairs={{0,1},{1,0},{2,3},{3,2},{4,5},{5,4},{6,7},{7,6},{8,9},{9,8},{10,11... | collective-permute-start | bytes 4816904 | tf_op jit(solution)/shard_map/ppermute | solution.py:12
  92.9 11.5 %collective-permute-start.26 = (bf16[512,384]{1,0:T(8,128)(2,1)S(1)}, bf16[512,384]{1,0:T(8,128)(2,1)S(1)}, u32[]{:S(2)}, u32[]{:S(2)}) collective-permute-start(bf16[512,384]{1,0:T(8,128)(2,1)S(1)} %get-tuple-element.131), channel_id=1, source_target_pairs={{0,4},{4,0},{8,12},{12,8},{16,20},{20,16},{24,28},{28,24},{1,5},{5... | collective-permute-start | bytes 1179656 | tf_op jit(solution)/shard_map/ppermute | solution.py:12
  94.4 11.9 %collective-permute-start.27 = (bf16[512,384]{1,0:T(8,128)(2,1)S(1)}, bf16[512,384]{1,0:T(8,128)(2,1)S(1)}, u32[]{:S(2)}, u32[]{:S(2)}) collective-permute-start(bf16[512,384]{1,0:T(8,128)(2,1)S(1)} %get-tuple-element.132), channel_id=1, source_target_pairs={{0,8},{4,12},{8,0},{12,4},{16,24},{20,28},{24,16},{28,20},{1,9},{5... | collective-permute-start | bytes 1179656 | tf_op jit(solution)/shard_map/ppermute | solution.py:12
  96.0 18.1 %collective-permute-start.28 = (bf16[512,384]{1,0:T(8,128)(2,1)S(1)}, bf16[512,384]{1,0:T(8,128)(2,1)S(1)}, u32[]{:S(2)}, u32[]{:S(2)}) collective-permute-start(bf16[512,384]{1,0:T(8,128)(2,1)S(1)} %get-tuple-element.133), channel_id=1, source_target_pairs={{0,12},{4,8},{8,4},{12,0},{16,28},{20,24},{24,20},{28,16},{1,13},{... | collective-permute-start | bytes 1179656 | tf_op jit(solution)/shard_map/ppermute | solution.py:12
  104.5 18.0 %copy-start.10 = (bf16[512,384]{1,0:T(8,128)(2,1)}, bf16[512,384]{1,0:T(8,128)(2,1)S(1)}, u32[]{:S(2)}) copy-start(bf16[512,384]{1,0:T(8,128)(2,1)S(1)} %collective-permute-done.26.refs_1_) | copy-start | bytes 1179652
  106.4 16.1 %copy-start.11 = (bf16[512,384]{1,0:T(8,128)(2,1)}, bf16[512,384]{1,0:T(8,128)(2,1)S(1)}, u32[]{:S(2)}) copy-start(bf16[512,384]{1,0:T(8,128)(2,1)S(1)} %collective-permute-done.27.refs_2_) | copy-start | bytes 1179652
  114.1 8.4 %copy-start.12 = (bf16[512,384]{1,0:T(8,128)(2,1)}, bf16[512,384]{1,0:T(8,128)(2,1)S(1)}, u32[]{:S(2)}) copy-start(bf16[512,384]{1,0:T(8,128)(2,1)S(1)} %collective-permute-done.28.refs_3_) | copy-start | bytes 1179652
  127.7 31.1 %collective-permute-start.30 = (bf16[2,320,896]{2,1,0:T(8,128)(2,1)}, bf16[2,320,896]{2,1,0:T(8,128)(2,1)}, u32[]{:S(2)}, u32[]{:S(2)}) collective-permute-start(bf16[2,320,896]{2,1,0:T(8,128)(2,1)} %get-tuple-element.143), channel_id=1, source_target_pairs={{0,1},{1,0},{2,3},{3,2},{4,5},{5,4},{6,7},{7,6},{8,9},{9,8},{10,11... | collective-permute-start | bytes 3440648 | tf_op jit(solution)/shard_map/ppermute | solution.py:12
  127.7 31.1 %collective-permute-start.29 = (bf16[512,512]{1,0:T(8,128)(2,1)}, bf16[512,512]{1,0:T(8,128)(2,1)}, u32[]{:S(2)}, u32[]{:S(2)}) collective-permute-start(bf16[512,512]{1,0:T(8,128)(2,1)} %get-tuple-element.141), channel_id=1, source_target_pairs={{0,16},{4,20},{8,24},{12,28},{16,0},{20,4},{24,8},{28,12},{1,17},{... | collective-permute-start | bytes 1572872 | tf_op jit(solution)/shard_map/ppermute | solution.py:12
  160.3 16.0 %collective-permute-start.31 = (bf16[320,896]{1,0:T(8,128)(2,1)S(1)}, bf16[320,896]{1,0:T(8,128)(2,1)S(1)}, u32[]{:S(2)}, u32[]{:S(2)}) collective-permute-start(bf16[320,896]{1,0:T(8,128)(2,1)S(1)} %fusion.12), channel_id=1, source_target_pairs={{0,2},{1,3},{2,0},{3,1},{4,6},{5,7},{6,4},{7,5},{8,10},{9,11},{10,... | collective-permute-start | bytes 1720328 | tf_op jit(solution)/shard_map/ppermute | solution.py:12
  162.9 32.7 %collective-permute-start.38 = (bf16[512,384]{1,0:T(8,128)(2,1)}, bf16[512,384]{1,0:T(8,128)(2,1)S(1)}, u32[]{:S(2)}, u32[]{:S(2)}) collective-permute-start(bf16[512,384]{1,0:T(8,128)(2,1)} %get-tuple-element.148), channel_id=1, source_target_pairs={{0,16},{4,20},{8,24},{12,28},{16,0},{20,4},{24,8},{28,12},{1,17},{... | collective-permute-start | bytes 1179656 | tf_op jit(solution)/shard_map/ppermute | solution.py:12
  164.2 18.6 %collective-permute-start.32 = (bf16[128,512]{1,0:T(8,128)(2,1)S(1)}, bf16[128,512]{1,0:T(8,128)(2,1)S(1)}, u32[]{:S(2)}, u32[]{:S(2)}) collective-permute-start(bf16[128,512]{1,0:T(8,128)(2,1)S(1)} %get-tuple-element.145), channel_id=1, source_target_pairs={{0,1},{1,0},{2,3},{3,2},{4,5},{5,4},{6,7},{7,6},{8,9},{9,8},{10,11... | collective-permute-start | bytes 393224 | tf_op jit(solution)/shard_map/ppermute | solution.py:12
  164.3 18.6 %collective-permute-start.33 = (bf16[128,512]{1,0:T(8,128)(2,1)S(1)}, bf16[128,512]{1,0:T(8,128)(2,1)S(1)}, u32[]{:S(2)}, u32[]{:S(2)}) collective-permute-start(bf16[128,512]{1,0:T(8,128)(2,1)S(1)} %get-tuple-element.146), channel_id=1, source_target_pairs={{0,2},{1,3},{2,0},{3,1},{4,6},{5,7},{6,4},{7,5},{8,10},{9,11},{10,... | collective-permute-start | bytes 393224 | tf_op jit(solution)/shard_map/ppermute | solution.py:12
  165.9 17.0 %collective-permute-start.34 = (bf16[128,512]{1,0:T(8,128)(2,1)S(1)}, bf16[128,512]{1,0:T(8,128)(2,1)S(1)}, u32[]{:S(2)}, u32[]{:S(2)}) collective-permute-start(bf16[128,512]{1,0:T(8,128)(2,1)S(1)} %get-tuple-element.147), channel_id=1, source_target_pairs={{0,3},{1,2},{2,1},{3,0},{4,7},{5,6},{6,5},{7,4},{8,11},{9,10},{10,... | collective-permute-start | bytes 393224 | tf_op jit(solution)/shard_map/ppermute | solution.py:12
  177.2 41.4 %all-to-all-start.1 = ((bf16[8,40,896]{2,1,0:T(8,128)(2,1)}), bf16[8,40,896]{2,1,0:T(8,128)(2,1)}, u32[]{:S(2)}, u32[]{:S(2)}) async-start(bf16[8,40,896]{2,1,0:T(8,128)(2,1)} %bitcast.38), calls=%async_computation.1 | async-start | bytes 1146880 | tf_op jit(solution)/shard_map/all_to_all | solution.py:505
  182.9 32.3 %collective-permute-start.37 = (bf16[4,128,512]{2,1,0:T(8,128)(2,1)S(1)}, bf16[4,128,512]{2,1,0:T(8,128)(2,1)S(1)}, u32[]{:S(2)}, u32[]{:S(2)}) collective-permute-start(bf16[4,128,512]{2,1,0:T(8,128)(2,1)S(1)} %pad_maximum_fusion.8.refs_0_), channel_id=1, source_target_pairs={{0,12},{4,8},{8,4},{12,0},{16,28},{20,24},{24,20},{28,16},{1,13},{... | collective-permute-start | bytes 1572872 | tf_op jit(solution)/shard_map/ppermute | solution.py:12
  195.7 4.6 %collective-permute-start.39 = (bf16[128,384]{1,0:T(8,128)(2,1)S(1)}, bf16[128,384]{1,0:T(8,128)(2,1)S(1)}, u32[]{:S(2)}, u32[]{:S(2)}) collective-permute-start(bf16[128,384]{1,0:T(8,128)(2,1)S(1)} %get-tuple-element.151), channel_id=1, source_target_pairs={{0,1},{1,0},{2,3},{3,2},{4,5},{5,4},{6,7},{7,6},{8,9},{9,8},{10,11... | collective-permute-start | bytes 294920 | tf_op jit(solution)/shard_map/ppermute | solution.py:12
  195.8 6.1 %collective-permute-start.40 = (bf16[128,384]{1,0:T(8,128)(2,1)S(1)}, bf16[128,384]{1,0:T(8,128)(2,1)S(1)}, u32[]{:S(2)}, u32[]{:S(2)}) collective-permute-start(bf16[128,384]{1,0:T(8,128)(2,1)S(1)} %get-tuple-element.152), channel_id=1, source_target_pairs={{0,2},{1,3},{2,0},{3,1},{4,6},{5,7},{6,4},{7,5},{8,10},{9,11},{10,... | collective-permute-start | bytes 294920 | tf_op jit(solution)/shard_map/ppermute | solution.py:12
  198.3 5.2 %collective-permute-start.41 = (bf16[128,384]{1,0:T(8,128)(2,1)S(1)}, bf16[128,384]{1,0:T(8,128)(2,1)S(1)}, u32[]{:S(2)}, u32[]{:S(2)}) collective-permute-start(bf16[128,384]{1,0:T(8,128)(2,1)S(1)} %get-tuple-element.153), channel_id=1, source_target_pairs={{0,3},{1,2},{2,1},{3,0},{4,7},{5,6},{6,5},{7,4},{8,11},{9,10},{10,... | collective-permute-start | bytes 294920 | tf_op jit(solution)/shard_map/ppermute | solution.py:12
  200.3 21.5 %collective-permute-start.36 = (bf16[4,128,512]{2,1,0:T(8,128)(2,1)S(1)}, bf16[4,128,512]{2,1,0:T(8,128)(2,1)S(1)}, u32[]{:S(2)}, u32[]{:S(2)}) collective-permute-start(bf16[4,128,512]{2,1,0:T(8,128)(2,1)S(1)} %pad_maximum_fusion.8.refs_0_), channel_id=1, source_target_pairs={{0,8},{4,12},{8,0},{12,4},{16,24},{20,28},{24,16},{28,20},{1,9},{5... | collective-permute-start | bytes 1572872 | tf_op jit(solution)/shard_map/ppermute | solution.py:12
  200.3 23.3 %collective-permute-start.35 = (bf16[4,128,512]{2,1,0:T(8,128)(2,1)S(1)}, bf16[4,128,512]{2,1,0:T(8,128)(2,1)S(1)}, u32[]{:S(2)}, u32[]{:S(2)}) collective-permute-start(bf16[4,128,512]{2,1,0:T(8,128)(2,1)S(1)} %pad_maximum_fusion.8.refs_0_), channel_id=1, source_target_pairs={{0,4},{4,0},{8,12},{12,8},{16,20},{20,16},{24,28},{28,24},{1,5},{5... | collective-permute-start | bytes 1572872 | tf_op jit(solution)/shard_map/ppermute | solution.py:12
  203.6 28.5 %collective-permute-start.44 = (bf16[4,128,384]{2,1,0:T(8,128)(2,1)S(1)}, bf16[4,128,384]{2,1,0:T(8,128)(2,1)S(1)}, u32[]{:S(2)}, u32[]{:S(2)}) collective-permute-start(bf16[4,128,384]{2,1,0:T(8,128)(2,1)S(1)} %pad_maximum_fusion.9.refs_4_), channel_id=1, source_target_pairs={{0,12},{4,8},{8,4},{12,0},{16,28},{20,24},{24,20},{28,16},{1,13},{... | collective-permute-start | bytes 1179656 | tf_op jit(solution)/shard_map/ppermute | solution.py:12
  204.0 34.7 %collective-permute-start.43 = (bf16[4,128,384]{2,1,0:T(8,128)(2,1)S(1)}, bf16[4,128,384]{2,1,0:T(8,128)(2,1)}, u32[]{:S(2)}, u32[]{:S(2)}) collective-permute-start(bf16[4,128,384]{2,1,0:T(8,128)(2,1)S(1)} %pad_maximum_fusion.9.refs_4_), channel_id=1, source_target_pairs={{0,8},{4,12},{8,0},{12,4},{16,24},{20,28},{24,16},{28,20},{1,9},{5... | collective-permute-start | bytes 1179656 | tf_op jit(solution)/shard_map/ppermute | solution.py:12
  215.2 3.5 %copy-start.16 = (f32[128,2]{0,1:T(2,128)S(1)}, f32[128,2]{0,1:T(2,128)}, u32[]{:S(2)}) copy-start(f32[128,2]{0,1:T(2,128)} %param.14) | copy-start | bytes 3076
  215.2 23.9 %collective-permute-start.42 = (bf16[4,128,384]{2,1,0:T(8,128)(2,1)S(1)}, bf16[4,128,384]{2,1,0:T(8,128)(2,1)}, u32[]{:S(2)}, u32[]{:S(2)}) collective-permute-start(bf16[4,128,384]{2,1,0:T(8,128)(2,1)S(1)} %pad_maximum_fusion.9.refs_4_), channel_id=1, source_target_pairs={{0,4},{4,0},{8,12},{12,8},{16,20},{20,16},{24,28},{28,24},{1,5},{5... | collective-permute-start | bytes 1179656 | tf_op jit(solution)/shard_map/ppermute | solution.py:12
  242.3 0.9 copy-start.1
Sparse Core Ops, SparseCore 0:
  131.1 54.3 all-gather.2

commit v5 on v4

--- a/solution.py
+++ b/solution.py
@@ -22,11 +22,12 @@
     return [held[k] for k in range(size)]
 
 
-def gather_even(value, size):
+def gather_even(value, size, *others):
     stack, order = value[None], [0]
     bit = size // 2
     while bit > 1:
-        stack = jnp.concatenate([stack, xor_permute(stack, "tensor", size, bit)])
+        arrived = after(xor_permute(stack, "tensor", size, bit), *others)
+        stack = jnp.concatenate([stack, arrived])
         order = order + [k ^ bit for k in order]
         bit //= 2
     return stack, order
@@ -186,7 +187,7 @@
     ]
     before_far, before_near = earlier or ((), ())
     first = xor_permute(after(jnp.stack([far, both]), *before_far), "tensor", 4, 2)
-    pair = after(jnp.stack([near, first[1]]), *before_near)
+    pair = jnp.stack([near, after(first, *before_near)[1]])
     return [mine, first, xor_permute(pair, "tensor", 4, 1)]
 
 
@@ -476,31 +477,28 @@
     stacked = jnp.concatenate([arrived, probe_rows], axis=0)
     if two is not None:
         last = len(two.spans) - 1
-        sources, marks, parts = [], [], []
-        for c in range(last + 1):
-            earlier = ((sources[-1][1],), parts[-1][1:]) if c else ()
-            sources.append(two.columns(c, *earlier))
-            mark, sent = two.send_aligned(sources[c], *marks[-1:])
-            marks.append(mark)
-            parts.append(sent)
-        stacked = after(stacked, sources[-1][1])
-        given, own_sum = sums(two.flags, all_after(parts[0], marks[-1]))
-        others, kept = [xor_permute(given, "expert", ne, two.half)], [own_sum]
-    even, order = gather_even(stacked, nt)
-    if two is not None:
-        even = after(even, kept[0])
+        source = two.columns(0)
+        mark, sent = two.send_aligned(source)
+        parts = [sent]
+        stacked = after(stacked, source[1])
+    even, order = gather_even(stacked, nt, *([] if two is None else [mark]))
     odd = xor_permute(even, "tensor", nt, 1)
-    if two is not None:
-        for c in range(1, last + 1):
-            given, own_sum = sums(two.flags, all_after(parts[c], kept[-1]))
-            others.append(xor_permute(given, "expert", ne, two.half))
-            kept.append(own_sum)
-        odd = after(odd, kept[-1])
     hidden = ffn((even, odd), order, gate_weight, up_weight, t)
     probe_hidden = hidden[routed:]
     send, keep = down(hidden, routed, own, t, nt)
     if two is not None:
-        keep = after(keep, others[0])
+        others, kept = [], []
+        for c in range(last + 1):
+            if c < last:
+                source = two.columns(c + 1, (even,), (*parts[c][1:], send))
+                mark, sent = two.send_aligned(source, mark)
+                parts.append(sent)
+            ready = all_after(parts[c], *(kept[-1:] if c else (send,)))
+            given, own_sum = sums(two.flags, ready)
+            others.append(xor_permute(given, "expert", ne, two.half))
+            kept.append(own_sum)
+        lines = two.back(mean_of(two.scale, kept[0], after(others[0], kept[-1]), nt))
+        keep = after(keep, kept[-1])
     returned = sum_tensor(send, keep, nt)
     home = lax.all_to_all(returned, "expert", split_axis=0, concat_axis=0, tiled=True)
     chooser = (target.T.reshape(-1)[:, None] == slots[None, :]).astype(jnp.bfloat16)
@@ -521,13 +519,10 @@
         / probe_hidden.shape[0]
     )
     if two is not None:
-        gathered = []
-        for c in range(len(two.spans)):
-            other = after(others[c], lines) if c else others[c]
-            means = mean_of(two.scale, kept[c], other, nt)
-            lines = two.back(means)
-            if c == len(two.spans) - 1:
-                lines = after(lines, returned)
+        gathered = [two.out(lines)]
+        for c in range(1, len(two.spans)):
+            means = mean_of(two.scale, kept[c], after(others[c], lines), nt)
+            lines = after(two.back(means), returned)
             gathered.append(two.out(lines))
         gathered[-1][0] = after(gathered[-1][0], mixed, correlation)
         merged = two.finish(gathered, parts)

time: 251 us -> 243 us (0.968)
  waiting for transfers between devices: 119 us -> 109 us
  starting transfers between devices: 38.8 us -> 43.8 us
    ppermute x31, waiting for transfers between devices: 119 us -> 109 us  [xor_permute(): return lax.ppermute(value, axis, [(i, i ^ k) for i in range(size)])]
    ppermute x31, starting transfers between devices: 27 us -> 31.3 us  [xor_permute(): return lax.ppermute(value, axis, [(i, i ^ k) for i in range(size)])]
  transfers between devices with their start and end apart: 34 -> 34, of which waited for: 19 -> 14; matrix products, arithmetic and copies ran while one was open for 11% -> 9% of each run, Pallas kernels for 4% -> 12%
where the time goes in v5:
time: 243 us; the launch traced here: 242 us
  waiting for transfers between devices  109 us (45%)
  starting transfers between devices  43.8 us (18%)
  Pallas kernels  31.6 us (13%)
  between operations  21.7 us (9%)
  other arithmetic  12.4 us (5%)
  local copies, waits for them, and re-layouts  10.3 us (4%)
  blocking collectives  7.34 us (3%)
  matrix products  6.16 us (3%)
    ppermute x31, waiting for transfers between devices, xor_permute(): return lax.ppermute(value, axis, [(i, i ^ k) for i in range(size)])  109 us
    ppermute x31, starting transfers between devices, xor_permute(): return lax.ppermute(value, axis, [(i, i ^ k) for i in range(size)])  31.3 us
    pallas_call x2, Pallas kernels, align(): pl.pallas_call(functools.partial(align_kernel, nt, half, sub), out_shape=...  11.8 us
    all_gather x1, blocking collectives, on_device(): partner_full = lax.all_gather(partner, 'tensor', axis=1, tiled=True)  7.34 us
    pallas_call x1, Pallas kernels, ffn(): pl.pallas_call(functools.partial(ffn_kernel, order), out_shape=jax.ShapeD...  6.96 us
    all_to_all x1, starting transfers between devices, on_device(): lax.all_to_all(returned, 'expert', split_axis=0, concat_axis=0, tiled=True)  6.51 us
    all_to_all x1, starting transfers between devices, on_device(): lax.all_to_all(outgoing, 'expert', split_axis=0, concat_axis=0, tiled=True)  5.94 us
    pallas_call x1, Pallas kernels, down(): pl.pallas_call(functools.partial(down_kernel, count), out_shape=[shape, s...  5.19 us
  transfers between devices with their start and end apart: 34, of which 14 were waited for; matrix products, arithmetic and copies ran while one was open for 9% of the time, Pallas kernels for 12%

profile of v5, /device:TPU:0, one launch (start us, length us, event | category | flops | bytes accessed | tf_op | source)
XLA Modules:
  0.0 241.8 jit_solution(15361314456914077457)
XLA Ops:
  7.2 2.6 %constant_dynamic-slice_fusion.3 = (bf16[1,512,512]{2,1,0:T(8,128)(2,1)}, bf16[512,512]{1,0:T(8,128)(2,1)S(1)}, bf16[1,512,512]{2,1,0:T(8,128)(2,1)S(1)}, bf16[1,512,512]{2,1,0:T(8,128)(2,1)S(1)}) fusion(bf16[1,512,3584]{2,1,0:T(8,128)(2,1)} %param.18, s32[]{:T(128)S(6)} %select_n.176, s32[]{:T(128)S(6)} %select_n.175, s32[]{:T(128)S(6)} %select_n.164, ...), kind=kLoop, calls=%fused_computation.62 | loop fusion | bytes 4194320 | tf_op jit(solution)/shard_map/dynamic_slice | solution.py:186
  9.8 1.1 pad_maximum_fusion.3
  10.9 3.0 %collective-permute-start.14 = (bf16[2,512,512]{2,1,0:T(8,128)(2,1)}, bf16[2,512,512]{2,1,0:T(8,128)(2,1)S(1)}, u32[]{:S(2)}, u32[]{:S(2)}) collective-permute-start(bf16[2,512,512]{2,1,0:T(8,128)(2,1)} %pad_maximum_fusion.3), channel_id=1, source_target_pairs={{0,2},{1,3},{2,0},{3,1},{4,6},{5,7},{6,4},{7,5},{8,10},{9,11},{10,... | collective-permute-start | bytes 3145736 | tf_op jit(solution)/shard_map/ppermute | solution.py:12
  14.6 1.1 convolution_convert_fusion
  15.7 5.9 %all-to-all-start = ((bf16[8,40,896]{2,1,0:T(8,128)(2,1)}), bf16[8,40,896]{2,1,0:T(8,128)(2,1)S(1)}, u32[]{:S(2)}, u32[]{:S(2)}) async-start(bf16[8,40,896]{2,1,0:T(8,128)(2,1)} %bitcast.22), calls=%async_computation | async-start | bytes 1146880 | tf_op jit(solution)/shard_map/all_to_all | solution.py:475
  21.7 0.6 collective-permute-start.17
  22.3 0.6 dynamic_slice.44
  25.0 12.3 %collective-permute-done.14.refs_1_ = bf16[2,512,512]{2,1,0:T(8,128)(2,1)S(1)} collective-permute-done((bf16[2,512,512]{2,1,0:T(8,128)(2,1)}, bf16[2,512,512]{2,1,0:T(8,128)(2,1)S(1)}, u32[]{:S(2)}, u32[]{:S(2)}) %collective-permute-start.14) | collective-permute-done | bytes 1048608 | tf_op jit(solution)/shard_map/ppermute | solution.py:12
  37.3 2.1 pad_maximum_fusion.4
  39.4 0.7 fusion.28
  40.1 0.5 collective-permute-start.18
  40.7 1.8 collective-permute-start.15
  42.5 0.6 fusion.27
  45.8 1.3 copy.47
  47.1 2.2 fusion.7.place_ref
  49.4 6.6 %align.2 = (bf16[512,512]{1,0:T(8,128)(2,1)}, bf16[512,512]{1,0:T(8,128)(2,1)}, bf16[512,512]{1,0:T(8,128)(2,1)}, bf16[512,512]{1,0:T(8,128)(2,1)}) custom-call(s32[9]{0:T(128)S(1)} %concatenate.55.flags_ref, s32[2048,1]{1,0:T(8,128)S(1)} %fusion.7.place_ref, bf16[512,512]{1,0:T(8,128)(2,1)S(1)} %get-tuple-element.112.refs_0_, ...), custom_call_target="tpu_custom_call" | custom-call | flops 1024 | bytes 1024 | tf_op jit(solution)/shard_map/align/pallas_call | solution.py:228
  56.0 4.6 %collective-permute-done.15 = bf16[1,448,896]{2,1,0:T(8,128)(2,1)} collective-permute-done((bf16[1,448,896]{2,1,0:T(8,128)(2,1)S(1)}, bf16[1,448,896]{2,1,0:T(8,128)(2,1)}, u32[]{:S(2)}, u32[]{:S(2)}) %collective-permute-start.15) | collective-permute-done | bytes 802848 | tf_op jit(solution)/shard_map/ppermute | solution.py:12
  60.6 1.3 pad_maximum_fusion.2.even_ref
  62.1 1.5 constant_dynamic-slice_fusion
  63.7 1.8 collective-permute-start.21
  65.5 1.5 collective-permute-start.22
  67.0 1.6 collective-permute-start.23
  68.6 0.4 collective-permute-start.24
  69.0 7.0 %ffn.1.rows_ref = bf16[448,512]{1,0:T(8,128)(2,1)S(1)} custom-call(s32[1]{0:T(128)} %bitcast.19.where_ref, bf16[2,448,896]{2,1,0:T(8,128)(2,1)S(1)} %pad_maximum_fusion.2.even_ref, bf16[2,448,896]{2,1,0:T(8,128)(2,1)} %collective-permute-done.20.odd_ref, bf16[1,3584,512]{2,1,0:T(8,128)(2,1)} %gate_ref.1, bf16[1,3584,512]{2,1,0:T(8,128)(2,1)} %up_ref.1), custom_call_target="tpu_custom_call" | custom-call | flops 1024 | bytes 1024 | tf_op jit(solution)/shard_map/ffn/pallas_call | solution.py:132
  76.0 5.2 %down.1 = (bf16[2,320,896]{2,1,0:T(8,128)(2,1)}, bf16[2,320,896]{2,1,0:T(8,128)(2,1)S(1)}) custom-call(s32[1]{0:T(128)} %bitcast.19.where_ref, bf16[448,512]{1,0:T(8,128)(2,1)S(1)} %ffn.1.rows_ref, bf16[512,3584]{1,0:T(8,128)(2,1)} %bitcast.78), custom_call_target="tpu_custom_call" | custom-call | flops 1024 | bytes 1024 | tf_op jit(solution)/shard_map/down/pallas_call | solution.py:58
  81.1 0.8 collective-permute-done.23.refs_2_
  82.0 10.1 %collective-permute-done.24.refs_3_ = bf16[512,512]{1,0:T(8,128)(2,1)S(1)} collective-permute-done((bf16[512,512]{1,0:T(8,128)(2,1)}, bf16[512,512]{1,0:T(8,128)(2,1)S(1)}, u32[]{:S(2)}, u32[]{:S(2)}) %collective-permute-start.24) | collective-permute-done | bytes 524320 | tf_op jit(solution)/shard_map/ppermute | solution.py:12
  92.4 0.5 collective-permute-start.29
  92.9 2.1 collective-permute-done.25.refs_2_
  95.0 5.1 %align.3 = (bf16[512,384]{1,0:T(8,128)(2,1)}, bf16[512,384]{1,0:T(8,128)(2,1)}, bf16[512,384]{1,0:T(8,128)(2,1)S(1)}, bf16[512,384]{1,0:T(8,128)(2,1)S(1)}) custom-call(s32[9]{0:T(128)S(1)} %concatenate.55.flags_ref, s32[2048,1]{1,0:T(8,128)S(1)} %fusion.7.place_ref, bf16[512,384]{1,0:T(8,128)(2,1)S(1)} %get-tuple-element.124.refs_0_, ...), custom_call_target="tpu_custom_call" | custom-call | flops 1024 | bytes 1024 | tf_op jit(solution)/shard_map/align/pallas_call | solution.py:228
  100.1 1.6 collective-permute-start.26
  101.7 1.6 collective-permute-start.27
  103.3 0.4 collective-permute-start.28
  103.7 0.7 slice.88
  104.4 2.4 sums.2
  106.8 5.0 %collective-permute-done.26.refs_1_ = bf16[512,384]{1,0:T(8,128)(2,1)S(1)} collective-permute-done((bf16[512,384]{1,0:T(8,128)(2,1)}, bf16[512,384]{1,0:T(8,128)(2,1)S(1)}, u32[]{:S(2)}, u32[]{:S(2)}) %collective-permute-start.26) | collective-permute-done | bytes 393248 | tf_op jit(solution)/shard_map/ppermute | solution.py:12
  111.7 2.1 collective-permute-done.27.refs_2_
  113.8 10.2 %collective-permute-done.28.refs_3_ = bf16[512,384]{1,0:T(8,128)(2,1)} collective-permute-done((bf16[512,384]{1,0:T(8,128)(2,1)S(1)}, bf16[512,384]{1,0:T(8,128)(2,1)}, u32[]{:S(2)}, u32[]{:S(2)}) %collective-permute-start.28) | collective-permute-done | bytes 393248 | tf_op jit(solution)/shard_map/ppermute | solution.py:12
  124.0 1.8 sums.3
  125.8 1.8 convert_add_fusion
  127.7 3.7 %collective-permute-start.31 = (bf16[512,512]{1,0:T(8,128)(2,1)S(1)}, bf16[512,512]{1,0:T(8,128)(2,1)S(1)}, u32[]{:S(2)}, u32[]{:S(2)}) collective-permute-start(bf16[512,512]{1,0:T(8,128)(2,1)S(1)} %get-tuple-element.142), channel_id=1, source_target_pairs={{0,16},{4,20},{8,24},{12,28},{16,0},{20,4},{24,8},{28,12},{1,17},{... | collective-permute-start | bytes 1572872 | tf_op jit(solution)/shard_map/ppermute | solution.py:12
  131.5 0.6 fusion.26
  133.5 27.7 %collective-permute-done.31.other_ref = bf16[512,512]{1,0:T(8,128)(2,1)S(1)} collective-permute-done((bf16[512,512]{1,0:T(8,128)(2,1)S(1)}, bf16[512,512]{1,0:T(8,128)(2,1)S(1)}, u32[]{:S(2)}, u32[]{:S(2)}) %collective-permute-start.31) | collective-permute-done | bytes 524320 | tf_op jit(solution)/shard_map/ppermute | solution.py:12
  161.4 1.7 collective-permute-start.33
  163.3 0.9 fusion.4
  164.2 6.5 %all-to-all-start.1 = ((bf16[8,40,896]{2,1,0:T(8,128)(2,1)}), bf16[8,40,896]{2,1,0:T(8,128)(2,1)}, u32[]{:S(2)}, u32[]{:S(2)}) async-start(bf16[8,40,896]{2,1,0:T(8,128)(2,1)} %bitcast.82), calls=%async_computation.1 | async-start | bytes 1146880 | tf_op jit(solution)/shard_map/all_to_all | solution.py:503
  170.9 3.0 %collective-permute-start.37 = (bf16[4,128,512]{2,1,0:T(8,128)(2,1)S(1)}, bf16[4,128,512]{2,1,0:T(8,128)(2,1)S(1)}, u32[]{:S(2)}, u32[]{:S(2)}) collective-permute-start(bf16[4,128,512]{2,1,0:T(8,128)(2,1)S(1)} %pad_maximum_fusion.8.refs_0_), channel_id=1, source_target_pairs={{0,12},{4,8},{8,4},{12,0},{16,28},{20,24},{24,20},{28,16},{1,13},{... | collective-permute-start | bytes 1572872 | tf_op jit(solution)/shard_map/ppermute | solution.py:12
  173.8 17.0 %collective-permute-done.38.other_ref = bf16[512,384]{1,0:T(8,128)(2,1)S(1)} collective-permute-done((bf16[512,384]{1,0:T(8,128)(2,1)S(1)}, bf16[512,384]{1,0:T(8,128)(2,1)S(1)}, u32[]{:S(2)}, u32[]{:S(2)}) %collective-permute-start.38) | collective-permute-done | bytes 393248 | tf_op jit(solution)/shard_map/ppermute | solution.py:12
  191.0 1.7 collective-permute-start.40
  192.8 0.6 iota_compare_fusion.6
  194.8 1.8 collective-permute-start.35
  196.6 1.2 collective-permute-done.41
  197.9 0.5 collective-permute-start.44
  198.4 2.7 %collective-permute-start.43 = (bf16[4,128,384]{2,1,0:T(8,128)(2,1)S(1)}, bf16[4,128,384]{2,1,0:T(8,128)(2,1)S(1)}, u32[]{:S(2)}, u32[]{:S(2)}) collective-permute-start(bf16[4,128,384]{2,1,0:T(8,128)(2,1)S(1)} %pad_maximum_fusion.9.refs_4_), channel_id=1, source_target_pairs={{0,8},{4,12},{8,0},{12,4},{16,24},{20,28},{24,16},{28,20},{1,9},{5... | collective-permute-start | bytes 1179656 | tf_op jit(solution)/shard_map/ppermute | solution.py:12
  201.1 1.5 fusion.1
  202.6 7.3 %all_gather.11 = bf16[128,2048]{1,0:T(8,128)(2,1)S(1)} all-gather(bf16[128,512]{1,0:T(8,128)(2,1)S(1)} %fusion.1), channel_id=1, replica_groups=mesh['expert'=8,'tensor'=4] {'tensor'}, dimensions={1}, use_global_device_ids=true | all-gather | bytes 655360 | tf_op jit(solution)/shard_map/all_gather | solution.py:514
  210.0 0.3 collective-permute-start.42
  210.3 2.7 %convolution_multiply_fusion = f32[512,2048]{1,0:T(8,128)} fusion(bf16[128,2048]{1,0:T(8,128)(2,1)S(1)} %all_gather.11, bf16[448,512]{1,0:T(8,128)(2,1)S(1)} %ffn.1.rows_ref), kind=kOutput, calls=%fused_computation.10 | convolution fusion | flops 269484032 | bytes 4849664 | tf_op jit(solution)/shard_map/dot_general | solution.py:516
  213.1 2.3 fusion.2
  215.3 7.6 %collective-permute-done.44.refs_7_ = bf16[4,128,384]{2,1,0:T(8,128)(2,1)S(1)} collective-permute-done((bf16[4,128,384]{2,1,0:T(8,128)(2,1)S(1)}, bf16[4,128,384]{2,1,0:T(8,128)(2,1)S(1)}, u32[]{:S(2)}, u32[]{:S(2)}) %collective-permute-start.44) | collective-permute-done | bytes 393248 | tf_op jit(solution)/shard_map/ppermute | solution.py:12
  223.0 6.6 %collective-permute-done.43.refs_6_ = bf16[4,128,384]{2,1,0:T(8,128)(2,1)S(1)} collective-permute-done((bf16[4,128,384]{2,1,0:T(8,128)(2,1)S(1)}, bf16[4,128,384]{2,1,0:T(8,128)(2,1)S(1)}, u32[]{:S(2)}, u32[]{:S(2)}) %collective-permute-start.43) | collective-permute-done | bytes 393248 | tf_op jit(solution)/shard_map/ppermute | solution.py:12
  229.6 1.2 collective-permute-done.42.refs_5_
  230.7 3.3 %assemble.3 = bf16[512,3584]{1,0:T(8,128)(2,1)} custom-call(s32[9]{0:T(128)S(1)} %concatenate.55.flags_ref, bf16[4,128,512]{2,1,0:T(8,128)(2,1)S(1)} %pad_maximum_fusion.8.refs_0_, bf16[4,128,512]{2,1,0:T(8,128)(2,1)} %collective-permute-done.35.refs_1_, bf16[4,128,512]{2,1,0:T(8,128)(2,1)S(1)} %collective-permute-done.36.refs_2_, ...), custom_call_target="tpu_custom_call" | custom-call | flops 1024 | bytes 1024 | tf_op jit(solution)/shard_map/assemble/pallas_call | solution.py:322
  234.0 0.9 copy-done.1
  (88 shorter events, 2.7 us)
Async XLA Ops:
  7.2 7.4 %copy-start = (bf16[128,896]{1,0:T(8,128)(2,1)S(1)}, bf16[128,896]{1,0:T(8,128)(2,1)}, u32[]{:S(2)}) copy-start(bf16[128,896]{1,0:T(8,128)(2,1)} %param.12) | copy-start | bytes 688132
  7.2 6.7 %copy-start.16 = (s32[128,2]{0,1:T(2,128)S(1)}, s32[128,2]{0,1:T(2,128)}, u32[]{:S(2)}) copy-start(s32[128,2]{0,1:T(2,128)} %param.13) | copy-start | bytes 3076
  9.8 11.8 %copy-start.17 = (s32[1,512]{1,0:T(1,128)S(1)}, s32[1,512]{1,0:T(1,128)}, u32[]{:S(2)}) copy-start(s32[1,512]{1,0:T(1,128)} %param.19) | copy-start | bytes 6148
  9.8 12.4 %copy-start.4 = (s32[8]{0:T(128)S(1)}, s32[8]{0:T(128)}, u32[]{:S(2)}) copy-start(s32[8]{0:T(128)} %param.20) | copy-start | bytes 100
  9.8 15.1 %copy-start.15 = (s32[2]{0:T(128)S(1)}, s32[2]{0:T(128)}, u32[]{:S(2)}) copy-start(s32[2]{0:T(128)} %param.21) | copy-start | bytes 28
  10.9 26.4 %collective-permute-start.14 = (bf16[2,512,512]{2,1,0:T(8,128)(2,1)}, bf16[2,512,512]{2,1,0:T(8,128)(2,1)S(1)}, u32[]{:S(2)}, u32[]{:S(2)}) collective-permute-start(bf16[2,512,512]{2,1,0:T(8,128)(2,1)} %pad_maximum_fusion.3), channel_id=1, source_target_pairs={{0,2},{1,3},{2,0},{3,1},{4,6},{5,7},{6,4},{7,5},{8,10},{9,11},{10,... | collective-permute-start | bytes 3145736 | tf_op jit(solution)/shard_map/ppermute | solution.py:12
  15.7 24.9 %copy-start.14 = (bf16[128,896]{1,0:T(8,128)(2,1)S(1)}, bf16[128,896]{1,0:T(8,128)(2,1)}, u32[]{:S(2)}) copy-start(bf16[128,896]{1,0:T(8,128)(2,1)} %param.15) | copy-start | bytes 688132
  15.7 24.9 %all-to-all-start = ((bf16[8,40,896]{2,1,0:T(8,128)(2,1)}), bf16[8,40,896]{2,1,0:T(8,128)(2,1)S(1)}, u32[]{:S(2)}, u32[]{:S(2)}) async-start(bf16[8,40,896]{2,1,0:T(8,128)(2,1)} %bitcast.22), calls=%async_computation | async-start | bytes 1146880 | tf_op jit(solution)/shard_map/all_to_all | solution.py:475
  21.6 179.5 %all-gather.3.cloned.1.call-start = ((), (), s32[]{:S(2)}) async-start(), calls=%async_computation.2 | async-start | bytes 1179648 | tf_op jit(solution)/shard_map/all_gather | solution.py:509
  21.7 18.4 %collective-permute-start.17 = (s32[512]{0:T(512)S(1)}, s32[512]{0:T(512)S(1)}, u32[]{:S(2)}, u32[]{:S(2)}) collective-permute-start(s32[512]{0:T(512)S(1)} %bitcast.99), channel_id=1, source_target_pairs={{0,2},{1,3},{2,0},{3,1},{4,6},{5,7},{6,4},{7,5},{8,10},{9,11},{10,... | collective-permute-start | bytes 6152 | tf_op jit(solution)/shard_map/ppermute | solution.py:12
  22.2 23.5 %collective-permute-start.16 = (s32[512]{0:T(512)S(1)}, s32[512]{0:T(512)S(1)}, u32[]{:S(2)}, u32[]{:S(2)}) collective-permute-start(s32[512]{0:T(512)S(1)} %bitcast.100), channel_id=1, source_target_pairs={{0,1},{1,0},{2,3},{3,2},{4,5},{5,4},{6,7},{7,6},{8,9},{9,8},{10,11... | collective-permute-start | bytes 6152 | tf_op jit(solution)/shard_map/ppermute | solution.py:12
  39.4 10.0 %collective-permute-start.19 = (bf16[2,512,512]{2,1,0:T(8,128)(2,1)}, bf16[2,512,512]{2,1,0:T(8,128)(2,1)}, u32[]{:S(2)}, u32[]{:S(2)}) collective-permute-start(bf16[2,512,512]{2,1,0:T(8,128)(2,1)} %pad_maximum_fusion.4), channel_id=1, source_target_pairs={{0,1},{1,0},{2,3},{3,2},{4,5},{5,4},{6,7},{7,6},{8,9},{9,8},{10,11... | collective-permute-start | bytes 3145736 | tf_op jit(solution)/shard_map/ppermute | solution.py:12
  40.1 5.7 %collective-permute-start.18 = (s32[512]{0:T(512)S(1)}, s32[512]{0:T(512)S(1)}, u32[]{:S(2)}, u32[]{:S(2)}) collective-permute-start(s32[512]{0:T(512)S(1)} %collective-permute-done.17), channel_id=1, source_target_pairs={{0,1},{1,0},{2,3},{3,2},{4,5},{5,4},{6,7},{7,6},{8,9},{9,8},{10,11... | collective-permute-start | bytes 6152 | tf_op jit(solution)/shard_map/ppermute | solution.py:12
  40.7 20.0 %collective-permute-start.15 = (bf16[1,448,896]{2,1,0:T(8,128)(2,1)S(1)}, bf16[1,448,896]{2,1,0:T(8,128)(2,1)}, u32[]{:S(2)}, u32[]{:S(2)}) collective-permute-start(bf16[1,448,896]{2,1,0:T(8,128)(2,1)S(1)} %bitcast.80), channel_id=1, source_target_pairs={{0,2},{1,3},{2,0},{3,1},{4,6},{5,7},{6,4},{7,5},{8,10},{9,11},{10,... | collective-permute-start | bytes 2408456 | tf_op jit(solution)/shard_map/ppermute | solution.py:12
  61.9 7.0 %collective-permute-start.20 = (bf16[2,448,896]{2,1,0:T(8,128)(2,1)S(1)}, bf16[2,448,896]{2,1,0:T(8,128)(2,1)}, u32[]{:S(2)}, u32[]{:S(2)}) collective-permute-start(bf16[2,448,896]{2,1,0:T(8,128)(2,1)S(1)} %pad_maximum_fusion.2.even_ref), channel_id=1, source_target_pairs={{0,1},{1,0},{2,3},{3,2},{4,5},{5,4},{6,7},{7,6},{8,9},{9,8},{10,11... | collective-permute-start | bytes 4816904 | tf_op jit(solution)/shard_map/ppermute | solution.py:12
  63.7 28.4 %collective-permute-start.21 = (bf16[2,512,384]{2,1,0:T(8,128)(2,1)S(1)}, bf16[2,512,384]{2,1,0:T(8,128)(2,1)S(1)}, u32[]{:S(2)}, u32[]{:S(2)}) collective-permute-start(bf16[2,512,384]{2,1,0:T(8,128)(2,1)S(1)} %pad_maximum_fusion.6), channel_id=1, source_target_pairs={{0,2},{1,3},{2,0},{3,1},{4,6},{5,7},{6,4},{7,5},{8,10},{9,11},{10,... | collective-permute-start | bytes 2359304 | tf_op jit(solution)/shard_map/ppermute | solution.py:12
  65.5 15.6 %collective-permute-start.22 = (bf16[512,512]{1,0:T(8,128)(2,1)}, bf16[512,512]{1,0:T(8,128)(2,1)S(1)}, u32[]{:S(2)}, u32[]{:S(2)}) collective-permute-start(bf16[512,512]{1,0:T(8,128)(2,1)} %get-tuple-element.119), channel_id=1, source_target_pairs={{0,4},{4,0},{8,12},{12,8},{16,20},{20,16},{24,28},{28,24},{1,5},{5... | collective-permute-start | bytes 1572872 | tf_op jit(solution)/shard_map/ppermute | solution.py:12
  67.0 15.0 %collective-permute-start.23 = (bf16[512,512]{1,0:T(8,128)(2,1)}, bf16[512,512]{1,0:T(8,128)(2,1)S(1)}, u32[]{:S(2)}, u32[]{:S(2)}) collective-permute-start(bf16[512,512]{1,0:T(8,128)(2,1)} %get-tuple-element.120), channel_id=1, source_target_pairs={{0,8},{4,12},{8,0},{12,4},{16,24},{20,28},{24,16},{28,20},{1,9},{5... | collective-permute-start | bytes 1572872 | tf_op jit(solution)/shard_map/ppermute | solution.py:12
  68.6 23.6 %collective-permute-start.24 = (bf16[512,512]{1,0:T(8,128)(2,1)}, bf16[512,512]{1,0:T(8,128)(2,1)S(1)}, u32[]{:S(2)}, u32[]{:S(2)}) collective-permute-start(bf16[512,512]{1,0:T(8,128)(2,1)} %get-tuple-element.121), channel_id=1, source_target_pairs={{0,12},{4,8},{8,4},{12,0},{16,28},{20,24},{24,20},{28,16},{1,13},{... | collective-permute-start | bytes 1572872 | tf_op jit(solution)/shard_map/ppermute | solution.py:12
  81.1 13.8 %copy-start.6 = (bf16[512,512]{1,0:T(8,128)(2,1)}, bf16[512,512]{1,0:T(8,128)(2,1)S(1)}, u32[]{:S(2)}) copy-start(bf16[512,512]{1,0:T(8,128)(2,1)S(1)} %collective-permute-done.22.refs_1_) | copy-start | bytes 1572868
  82.0 18.1 %copy-start.8 = (bf16[512,512]{1,0:T(8,128)(2,1)}, bf16[512,512]{1,0:T(8,128)(2,1)S(1)}, u32[]{:S(2)}) copy-start(bf16[512,512]{1,0:T(8,128)(2,1)S(1)} %collective-permute-done.23.refs_2_) | copy-start | bytes 1572868
  92.1 8.0 %copy-start.10 = (bf16[512,512]{1,0:T(8,128)(2,1)}, bf16[512,512]{1,0:T(8,128)(2,1)S(1)}, u32[]{:S(2)}) copy-start(bf16[512,512]{1,0:T(8,128)(2,1)S(1)} %collective-permute-done.24.refs_3_) | copy-start | bytes 1572868
  92.3 2.7 %collective-permute-start.25 = (bf16[2,512,384]{2,1,0:T(8,128)(2,1)S(1)}, bf16[2,512,384]{2,1,0:T(8,128)(2,1)S(1)}, u32[]{:S(2)}, u32[]{:S(2)}) collective-permute-start(bf16[2,512,384]{2,1,0:T(8,128)(2,1)S(1)} %pad_maximum_fusion.7), channel_id=1, source_target_pairs={{0,1},{1,0},{2,3},{3,2},{4,5},{5,4},{6,7},{7,6},{8,9},{9,8},{10,11... | collective-permute-start | bytes 2359304 | tf_op jit(solution)/shard_map/ppermute | solution.py:12
  92.4 33.4 %collective-permute-start.29 = (bf16[2,320,896]{2,1,0:T(8,128)(2,1)}, bf16[2,320,896]{2,1,0:T(8,128)(2,1)}, u32[]{:S(2)}, u32[]{:S(2)}) collective-permute-start(bf16[2,320,896]{2,1,0:T(8,128)(2,1)} %get-tuple-element.122), channel_id=1, source_target_pairs={{0,1},{1,0},{2,3},{3,2},{4,5},{5,4},{6,7},{7,6},{8,9},{9,8},{10,11... | collective-permute-start | bytes 3440648 | tf_op jit(solution)/shard_map/ppermute | solution.py:12
  100.1 23.9 %copy-start.12 = (bf16[512,384]{1,0:T(8,128)(2,1)S(1)}, bf16[512,384]{1,0:T(8,128)(2,1)}, u32[]{:S(2)}) copy-start(bf16[512,384]{1,0:T(8,128)(2,1)} %get-tuple-element.136.refs_0_) | copy-start | bytes 1179652
  100.1 11.6 %collective-permute-start.26 = (bf16[512,384]{1,0:T(8,128)(2,1)}, bf16[512,384]{1,0:T(8,128)(2,1)S(1)}, u32[]{:S(2)}, u32[]{:S(2)}) collective-permute-start(bf16[512,384]{1,0:T(8,128)(2,1)} %get-tuple-element.128), channel_id=1, source_target_pairs={{0,4},{4,0},{8,12},{12,8},{16,20},{20,16},{24,28},{28,24},{1,5},{5... | collective-permute-start | bytes 1179656 | tf_op jit(solution)/shard_map/ppermute | solution.py:12
  101.7 12.1 %collective-permute-start.27 = (bf16[512,384]{1,0:T(8,128)(2,1)S(1)}, bf16[512,384]{1,0:T(8,128)(2,1)}, u32[]{:S(2)}, u32[]{:S(2)}) collective-permute-start(bf16[512,384]{1,0:T(8,128)(2,1)S(1)} %get-tuple-element.129), channel_id=1, source_target_pairs={{0,8},{4,12},{8,0},{12,4},{16,24},{20,28},{24,16},{28,20},{1,9},{5... | collective-permute-start | bytes 1179656 | tf_op jit(solution)/shard_map/ppermute | solution.py:12
  103.3 20.7 %collective-permute-start.28 = (bf16[512,384]{1,0:T(8,128)(2,1)S(1)}, bf16[512,384]{1,0:T(8,128)(2,1)}, u32[]{:S(2)}, u32[]{:S(2)}) collective-permute-start(bf16[512,384]{1,0:T(8,128)(2,1)S(1)} %get-tuple-element.130), channel_id=1, source_target_pairs={{0,12},{4,8},{8,4},{12,0},{16,28},{20,24},{24,20},{28,16},{1,13},{... | collective-permute-start | bytes 1179656 | tf_op jit(solution)/shard_map/ppermute | solution.py:12
  111.7 15.8 %copy-start.13 = (bf16[512,384]{1,0:T(8,128)(2,1)}, bf16[512,384]{1,0:T(8,128)(2,1)S(1)}, u32[]{:S(2)}) copy-start(bf16[512,384]{1,0:T(8,128)(2,1)S(1)} %collective-permute-done.26.refs_1_) | copy-start | bytes 1179652
  125.8 1.8 copy-start.2
  127.6 35.7 %collective-permute-start.30 = (bf16[320,896]{1,0:T(8,128)(2,1)S(1)}, bf16[320,896]{1,0:T(8,128)(2,1)S(1)}, u32[]{:S(2)}, u32[]{:S(2)}) collective-permute-start(bf16[320,896]{1,0:T(8,128)(2,1)S(1)} %fusion.12), channel_id=1, source_target_pairs={{0,2},{1,3},{2,0},{3,1},{4,6},{5,7},{6,4},{7,5},{8,10},{9,11},{10,... | collective-permute-start | bytes 1720328 | tf_op jit(solution)/shard_map/ppermute | solution.py:12
  127.7 33.5 %collective-permute-start.31 = (bf16[512,512]{1,0:T(8,128)(2,1)S(1)}, bf16[512,512]{1,0:T(8,128)(2,1)S(1)}, u32[]{:S(2)}, u32[]{:S(2)}) collective-permute-start(bf16[512,512]{1,0:T(8,128)(2,1)S(1)} %get-tuple-element.142), channel_id=1, source_target_pairs={{0,16},{4,20},{8,24},{12,28},{16,0},{20,4},{24,8},{28,12},{1,17},{... | collective-permute-start | bytes 1572872 | tf_op jit(solution)/shard_map/ppermute | solution.py:12
  161.3 29.4 %copy-start.3 = (f32[512,384]{1,0:T(8,128)S(1)}, f32[512,384]{1,0:T(8,128)}, u32[]{:S(2)}) copy-start(f32[512,384]{1,0:T(8,128)} %copy-done.2) | copy-start | bytes 2359300
  161.4 9.4 %collective-permute-start.32 = (bf16[128,512]{1,0:T(8,128)(2,1)S(1)}, bf16[128,512]{1,0:T(8,128)(2,1)S(1)}, u32[]{:S(2)}, u32[]{:S(2)}) collective-permute-start(bf16[128,512]{1,0:T(8,128)(2,1)S(1)} %get-tuple-element.145), channel_id=1, source_target_pairs={{0,1},{1,0},{2,3},{3,2},{4,5},{5,4},{6,7},{7,6},{8,9},{9,8},{10,11... | collective-permute-start | bytes 393224 | tf_op jit(solution)/shard_map/ppermute | solution.py:12
  161.4 9.3 %collective-permute-start.33 = (bf16[128,512]{1,0:T(8,128)(2,1)S(1)}, bf16[128,512]{1,0:T(8,128)(2,1)S(1)}, u32[]{:S(2)}, u32[]{:S(2)}) collective-permute-start(bf16[128,512]{1,0:T(8,128)(2,1)S(1)} %get-tuple-element.146), channel_id=1, source_target_pairs={{0,2},{1,3},{2,0},{3,1},{4,6},{5,7},{6,4},{7,5},{8,10},{9,11},{10,... | collective-permute-start | bytes 393224 | tf_op jit(solution)/shard_map/ppermute | solution.py:12
  163.2 7.6 %collective-permute-start.34 = (bf16[128,512]{1,0:T(8,128)(2,1)S(1)}, bf16[128,512]{1,0:T(8,128)(2,1)S(1)}, u32[]{:S(2)}, u32[]{:S(2)}) collective-permute-start(bf16[128,512]{1,0:T(8,128)(2,1)S(1)} %get-tuple-element.147), channel_id=1, source_target_pairs={{0,3},{1,2},{2,1},{3,0},{4,7},{5,6},{6,5},{7,4},{8,11},{9,10},{10,... | collective-permute-start | bytes 393224 | tf_op jit(solution)/shard_map/ppermute | solution.py:12
  163.3 27.5 %collective-permute-start.38 = (bf16[512,384]{1,0:T(8,128)(2,1)S(1)}, bf16[512,384]{1,0:T(8,128)(2,1)S(1)}, u32[]{:S(2)}, u32[]{:S(2)}) collective-permute-start(bf16[512,384]{1,0:T(8,128)(2,1)S(1)} %get-tuple-element.148), channel_id=1, source_target_pairs={{0,16},{4,20},{8,24},{12,28},{16,0},{20,4},{24,8},{28,12},{1,17},{... | collective-permute-start | bytes 1179656 | tf_op jit(solution)/shard_map/ppermute | solution.py:12
  164.2 48.8 %all-to-all-start.1 = ((bf16[8,40,896]{2,1,0:T(8,128)(2,1)}), bf16[8,40,896]{2,1,0:T(8,128)(2,1)}, u32[]{:S(2)}, u32[]{:S(2)}) async-start(bf16[8,40,896]{2,1,0:T(8,128)(2,1)} %bitcast.82), calls=%async_computation.1 | async-start | bytes 1146880 | tf_op jit(solution)/shard_map/all_to_all | solution.py:503
  170.9 39.1 %collective-permute-start.37 = (bf16[4,128,512]{2,1,0:T(8,128)(2,1)S(1)}, bf16[4,128,512]{2,1,0:T(8,128)(2,1)S(1)}, u32[]{:S(2)}, u32[]{:S(2)}) collective-permute-start(bf16[4,128,512]{2,1,0:T(8,128)(2,1)S(1)} %pad_maximum_fusion.8.refs_0_), channel_id=1, source_target_pairs={{0,12},{4,8},{8,4},{12,0},{16,28},{20,24},{24,20},{28,16},{1,13},{... | collective-permute-start | bytes 1572872 | tf_op jit(solution)/shard_map/ppermute | solution.py:12
  190.9 3.9 %collective-permute-start.39 = (bf16[128,384]{1,0:T(8,128)(2,1)S(1)}, bf16[128,384]{1,0:T(8,128)(2,1)S(1)}, u32[]{:S(2)}, u32[]{:S(2)}) collective-permute-start(bf16[128,384]{1,0:T(8,128)(2,1)S(1)} %get-tuple-element.151), channel_id=1, source_target_pairs={{0,1},{1,0},{2,3},{3,2},{4,5},{5,4},{6,7},{7,6},{8,9},{9,8},{10,11... | collective-permute-start | bytes 294920 | tf_op jit(solution)/shard_map/ppermute | solution.py:12
  191.0 5.7 %collective-permute-start.40 = (bf16[128,384]{1,0:T(8,128)(2,1)S(1)}, bf16[128,384]{1,0:T(8,128)(2,1)S(1)}, u32[]{:S(2)}, u32[]{:S(2)}) collective-permute-start(bf16[128,384]{1,0:T(8,128)(2,1)S(1)} %get-tuple-element.152), channel_id=1, source_target_pairs={{0,2},{1,3},{2,0},{3,1},{4,6},{5,7},{6,4},{7,5},{8,10},{9,11},{10,... | collective-permute-start | bytes 294920 | tf_op jit(solution)/shard_map/ppermute | solution.py:12
  192.7 5.1 %collective-permute-start.41 = (bf16[128,384]{1,0:T(8,128)(2,1)S(1)}, bf16[128,384]{1,0:T(8,128)(2,1)S(1)}, u32[]{:S(2)}, u32[]{:S(2)}) collective-permute-start(bf16[128,384]{1,0:T(8,128)(2,1)S(1)} %get-tuple-element.153), channel_id=1, source_target_pairs={{0,3},{1,2},{2,1},{3,0},{4,7},{5,6},{6,5},{7,4},{8,11},{9,10},{10,... | collective-permute-start | bytes 294920 | tf_op jit(solution)/shard_map/ppermute | solution.py:12
  194.7 20.6 %collective-permute-start.36 = (bf16[4,128,512]{2,1,0:T(8,128)(2,1)S(1)}, bf16[4,128,512]{2,1,0:T(8,128)(2,1)S(1)}, u32[]{:S(2)}, u32[]{:S(2)}) collective-permute-start(bf16[4,128,512]{2,1,0:T(8,128)(2,1)S(1)} %pad_maximum_fusion.8.refs_0_), channel_id=1, source_target_pairs={{0,8},{4,12},{8,0},{12,4},{16,24},{20,28},{24,16},{28,20},{1,9},{5... | collective-permute-start | bytes 1572872 | tf_op jit(solution)/shard_map/ppermute | solution.py:12
  194.8 20.5 %collective-permute-start.35 = (bf16[4,128,512]{2,1,0:T(8,128)(2,1)S(1)}, bf16[4,128,512]{2,1,0:T(8,128)(2,1)}, u32[]{:S(2)}, u32[]{:S(2)}) collective-permute-start(bf16[4,128,512]{2,1,0:T(8,128)(2,1)S(1)} %pad_maximum_fusion.8.refs_0_), channel_id=1, source_target_pairs={{0,4},{4,0},{8,12},{12,8},{16,20},{20,16},{24,28},{28,24},{1,5},{5... | collective-permute-start | bytes 1572872 | tf_op jit(solution)/shard_map/ppermute | solution.py:12
  197.9 25.1 %collective-permute-start.44 = (bf16[4,128,384]{2,1,0:T(8,128)(2,1)S(1)}, bf16[4,128,384]{2,1,0:T(8,128)(2,1)S(1)}, u32[]{:S(2)}, u32[]{:S(2)}) collective-permute-start(bf16[4,128,384]{2,1,0:T(8,128)(2,1)S(1)} %pad_maximum_fusion.9.refs_4_), channel_id=1, source_target_pairs={{0,12},{4,8},{8,4},{12,0},{16,28},{20,24},{24,20},{28,16},{1,13},{... | collective-permute-start | bytes 1179656 | tf_op jit(solution)/shard_map/ppermute | solution.py:12
  198.4 31.1 %collective-permute-start.43 = (bf16[4,128,384]{2,1,0:T(8,128)(2,1)S(1)}, bf16[4,128,384]{2,1,0:T(8,128)(2,1)S(1)}, u32[]{:S(2)}, u32[]{:S(2)}) collective-permute-start(bf16[4,128,384]{2,1,0:T(8,128)(2,1)S(1)} %pad_maximum_fusion.9.refs_4_), channel_id=1, source_target_pairs={{0,8},{4,12},{8,0},{12,4},{16,24},{20,28},{24,16},{28,20},{1,9},{5... | collective-permute-start | bytes 1179656 | tf_op jit(solution)/shard_map/ppermute | solution.py:12
  210.0 3.1 %copy-start.18 = (f32[128,2]{0,1:T(2,128)S(1)}, f32[128,2]{0,1:T(2,128)}, u32[]{:S(2)}) copy-start(f32[128,2]{0,1:T(2,128)} %param.14) | copy-start | bytes 3076
  210.0 20.7 %collective-permute-start.42 = (bf16[4,128,384]{2,1,0:T(8,128)(2,1)S(1)}, bf16[4,128,384]{2,1,0:T(8,128)(2,1)}, u32[]{:S(2)}, u32[]{:S(2)}) collective-permute-start(bf16[4,128,384]{2,1,0:T(8,128)(2,1)S(1)} %pad_maximum_fusion.9.refs_4_), channel_id=1, source_target_pairs={{0,4},{4,0},{8,12},{12,8},{16,20},{20,16},{24,28},{28,24},{1,5},{5... | collective-permute-start | bytes 1179656 | tf_op jit(solution)/shard_map/ppermute | solution.py:12
  215.3 18.7 %copy-start.5 = (bf16[512,512]{1,0:T(8,128)(2,1)S(1)}, bf16[512,512]{1,0:T(8,128)(2,1)}, u32[]{:S(2)}) copy-start(bf16[512,512]{1,0:T(8,128)(2,1)} %get-tuple-element.131.refs_0_) | copy-start | bytes 1572868
  234.0 0.9 copy-start.1
Sparse Core Ops, SparseCore 0:
  104.5 51.5 all-gather.2

commit v6 on v5

--- a/solution.py
+++ b/solution.py
@@ -272,23 +272,27 @@
     )(flags, *parts)
 
 
-def mean_kernel(scale_ref, kept_ref, other_ref, *outs):
-    sub = outs[0].shape[0]
+def mean_kernel(scale_ref, kept_ref, other_ref, mine_ref, near_ref, far_ref):
+    sub = mine_ref.shape[0]
     scale = scale_ref[0]
-    for m, out in enumerate(outs):
+    for m in range(4):
         at = pl.ds(m * sub, sub)
         total = kept_ref[at, :] + other_ref[at, :].astype(jnp.float32)
-        out[...] = (total * scale).astype(out.dtype)
-
-
-def mean_of(scale, kept, other, nt):
+        value = (total * scale).astype(mine_ref.dtype)
+        if m < 2:
+            (mine_ref, near_ref)[m][...] = value
+        else:
+            far_ref[m - 2] = value
+
+
+def mean_of(scale, kept, other):
     rows, width = kept.shape
-    sub = rows // nt
+    one, two = (rows // 4, width), (2, rows // 4, width)
     return pl.pallas_call(
         mean_kernel,
-        out_shape=[jax.ShapeDtypeStruct((sub, width), jnp.bfloat16)] * nt,
+        out_shape=[jax.ShapeDtypeStruct(shape, jnp.bfloat16) for shape in (one, one, two)],
         in_specs=[pl.BlockSpec(memory_space=pltpu.SMEM)] + [full_spec((rows, width))] * 2,
-        out_specs=[full_spec((sub, width))] * nt,
+        out_specs=[full_spec(one), full_spec(one), full_spec(two)],
         compiler_params=pltpu.CompilerParams(vmem_limit_bytes=BIG_VMEM),
         cost_estimate=SMALL_COST,
         name="mean",
@@ -370,7 +374,10 @@
         return pieces[0], sent
 
     def back(self, pieces):
-        return jnp.stack(rows_to_device(pieces, self.nt))
+        mine, near, far = pieces
+        first = xor_permute(far, "tensor", 4, 2)
+        second = xor_permute(jnp.stack([near, first[1]]), "tensor", 4, 1)
+        return jnp.stack([mine, second[0], first[0], second[1]])
 
     def out(self, lines):
         return [
@@ -392,7 +399,7 @@
                     total = total + jnp.where(near[k] == 1, parts[k].astype(jnp.float32), 0.0)
                 other = xor_permute(total.astype(jnp.bfloat16), "expert", self.ne, self.half)
                 scale = (1.0 / self.sizes[1]).reshape(1)
-                again.append(self.out(self.back(mean_of(scale, total, other, self.nt))))
+                again.append(self.out(self.back(mean_of(scale, total, other))))
             mine = jnp.where(self.owners[1:2] == self.e, 1, 0).astype(jnp.int32)
             flags = jnp.concatenate(
                 [self.flags[:MINE_AT], mine, self.flags[MINE_AT + 1 :]]
@@ -493,13 +500,15 @@
                 source = two.columns(c + 1, (even,), (*parts[c][1:], send))
                 mark, sent = two.send_aligned(source, mark)
                 parts.append(sent)
-            ready = all_after(parts[c], *(kept[-1:] if c else (send,)))
+            ready = all_after(parts[c], *((others[-1],) if c else (send,)))
             given, own_sum = sums(two.flags, ready)
             others.append(xor_permute(given, "expert", ne, two.half))
             kept.append(own_sum)
-        lines = two.back(mean_of(two.scale, kept[0], after(others[0], kept[-1]), nt))
-        keep = after(keep, kept[-1])
-    returned = sum_tensor(send, keep, nt)
+            if not c:
+                returned = sum_tensor(send, after(keep, others[0]), nt)
+        lines = two.back(mean_of(two.scale, kept[0], after(others[0], kept[-1])))
+    else:
+        returned = sum_tensor(send, keep, nt)
     home = lax.all_to_all(returned, "expert", split_axis=0, concat_axis=0, tiled=True)
     chooser = (target.T.reshape(-1)[:, None] == slots[None, :]).astype(jnp.bfloat16)
     picked = jnp.dot(chooser, home, preferred_element_type=jnp.float32)
@@ -521,7 +530,7 @@
     if two is not None:
         gathered = [two.out(lines)]
         for c in range(1, len(two.spans)):
-            means = mean_of(two.scale, kept[c], after(others[c], lines), nt)
+            means = mean_of(two.scale, kept[c], after(others[c], returned, *gathered[-1][1:]))
             lines = after(two.back(means), returned)
             gathered.append(two.out(lines))
         gathered[-1][0] = after(gathered[-1][0], mixed, correlation)

time: 243 us -> 235 us (0.967)
  starting transfers between devices: 43.8 us -> 38.1 us
  waiting for transfers between devices: 109 us -> 106 us
    ppermute x31 -> x29, starting transfers between devices: 31.3 us -> 28 us  [xor_permute(): return lax.ppermute(value, axis, [(i, i ^ k) for i in range(size)])]
    ppermute x31 -> x29, waiting for transfers between devices: 109 us -> 106 us  [xor_permute(): return lax.ppermute(value, axis, [(i, i ^ k) for i in range(size)])]
  transfers between devices with their start and end apart: 34 -> 32, of which waited for: 14 -> 14; matrix products, arithmetic and copies ran while one was open for 9% -> 10% of each run, Pallas kernels for 12% -> 13%
where the time goes in v6:
time: 235 us; the launch traced here: 234 us
  waiting for transfers between devices  106 us (45%)
  starting transfers between devices  38.1 us (16%)
  Pallas kernels  32.6 us (14%)
  between operations  21.3 us (9%)
  other arithmetic  12.2 us (5%)
  local copies, waits for them, and re-layouts  10.4 us (4%)
  blocking collectives  7.43 us (3%)
  matrix products  6.16 us (3%)
    ppermute x29, waiting for transfers between devices, xor_permute(): return lax.ppermute(value, axis, [(i, i ^ k) for i in range(size)])  106 us
    ppermute x29, starting transfers between devices, xor_permute(): return lax.ppermute(value, axis, [(i, i ^ k) for i in range(size)])  28 us
    pallas_call x2, Pallas kernels, align(): pl.pallas_call(functools.partial(align_kernel, nt, half, sub), out_shape=...  11.7 us
    all_gather x1, blocking collectives, on_device(): partner_full = lax.all_gather(partner, 'tensor', axis=1, tiled=True)  7.43 us
    pallas_call x1, Pallas kernels, ffn(): pl.pallas_call(functools.partial(ffn_kernel, order), out_shape=jax.ShapeD...  6.96 us
    all_to_all x1, starting transfers between devices, on_device(): lax.all_to_all(outgoing, 'expert', split_axis=0, concat_axis=0, tiled=True)  5.94 us
    pallas_call x1, Pallas kernels, down(): pl.pallas_call(functools.partial(down_kernel, count), out_shape=[shape, s...  5.24 us
  transfers between devices with their start and end apart: 32, of which 14 were waited for; matrix products, arithmetic and copies ran while one was open for 10% of the time, Pallas kernels for 13%

profile of v6, /device:TPU:0, one launch (start us, length us, event | category | flops | bytes accessed | tf_op | source)
XLA Modules:
  0.0 234.2 jit_solution(16155497153473337162)
XLA Ops:
  7.2 2.6 %constant_dynamic-slice_fusion.3 = (bf16[1,512,512]{2,1,0:T(8,128)(2,1)}, bf16[512,512]{1,0:T(8,128)(2,1)S(1)}, bf16[1,512,512]{2,1,0:T(8,128)(2,1)S(1)}, bf16[1,512,512]{2,1,0:T(8,128)(2,1)S(1)}) fusion(bf16[1,512,3584]{2,1,0:T(8,128)(2,1)} %param.18, s32[]{:T(128)S(6)} %select_n.176, s32[]{:T(128)S(6)} %select_n.175, s32[]{:T(128)S(6)} %select_n.164, ...), kind=kLoop, calls=%fused_computation.66 | loop fusion | bytes 4194320 | tf_op jit(solution)/shard_map/dynamic_slice | solution.py:186
  9.8 1.1 pad_maximum_fusion.5
  10.9 3.0 %collective-permute-start.12 = (bf16[2,512,512]{2,1,0:T(8,128)(2,1)}, bf16[2,512,512]{2,1,0:T(8,128)(2,1)S(1)}, u32[]{:S(2)}, u32[]{:S(2)}) collective-permute-start(bf16[2,512,512]{2,1,0:T(8,128)(2,1)} %pad_maximum_fusion.5), channel_id=1, source_target_pairs={{0,2},{1,3},{2,0},{3,1},{4,6},{5,7},{6,4},{7,5},{8,10},{9,11},{10,... | collective-permute-start | bytes 3145736 | tf_op jit(solution)/shard_map/ppermute | solution.py:12
  14.6 1.1 convolution_convert_fusion
  15.7 5.9 %all-to-all-start = ((bf16[8,40,896]{2,1,0:T(8,128)(2,1)}), bf16[8,40,896]{2,1,0:T(8,128)(2,1)S(1)}, u32[]{:S(2)}, u32[]{:S(2)}) async-start(bf16[8,40,896]{2,1,0:T(8,128)(2,1)} %bitcast.18), calls=%async_computation | async-start | bytes 1146880 | tf_op jit(solution)/shard_map/all_to_all | solution.py:482
  21.7 0.6 collective-permute-start.15
  22.3 0.6 dynamic_slice.39
  25.0 12.3 %collective-permute-done.12.refs_1_ = bf16[2,512,512]{2,1,0:T(8,128)(2,1)S(1)} collective-permute-done((bf16[2,512,512]{2,1,0:T(8,128)(2,1)}, bf16[2,512,512]{2,1,0:T(8,128)(2,1)S(1)}, u32[]{:S(2)}, u32[]{:S(2)}) %collective-permute-start.12) | collective-permute-done | bytes 1048608 | tf_op jit(solution)/shard_map/ppermute | solution.py:12
  37.3 2.1 pad_maximum_fusion.6
  39.4 0.6 fusion.36
  40.0 0.5 collective-permute-start.16
  40.6 1.8 collective-permute-start.13
  42.4 0.6 fusion.35
  45.6 1.3 copy.47
  46.9 2.2 fusion.7.place_ref
  49.2 6.6 %align.2 = (bf16[512,512]{1,0:T(8,128)(2,1)}, bf16[512,512]{1,0:T(8,128)(2,1)}, bf16[512,512]{1,0:T(8,128)(2,1)}, bf16[512,512]{1,0:T(8,128)(2,1)}) custom-call(s32[9]{0:T(128)S(1)} %concatenate.55.flags_ref, s32[2048,1]{1,0:T(8,128)S(1)} %fusion.7.place_ref, bf16[512,512]{1,0:T(8,128)(2,1)S(1)} %get-tuple-element.108.refs_0_, ...), custom_call_target="tpu_custom_call" | custom-call | flops 1024 | bytes 1024 | tf_op jit(solution)/shard_map/align/pallas_call | solution.py:228
  55.8 4.8 %collective-permute-done.13 = bf16[1,448,896]{2,1,0:T(8,128)(2,1)} collective-permute-done((bf16[1,448,896]{2,1,0:T(8,128)(2,1)S(1)}, bf16[1,448,896]{2,1,0:T(8,128)(2,1)}, u32[]{:S(2)}, u32[]{:S(2)}) %collective-permute-start.13) | collective-permute-done | bytes 802848 | tf_op jit(solution)/shard_map/ppermute | solution.py:12
  60.6 1.3 pad_maximum_fusion.4.even_ref
  62.0 1.5 constant_dynamic-slice_fusion
  63.7 1.8 collective-permute-start.25
  65.5 1.5 collective-permute-start.19
  67.0 1.6 collective-permute-start.20
  69.0 7.0 %ffn.1.rows_ref = bf16[448,512]{1,0:T(8,128)(2,1)S(1)} custom-call(s32[1]{0:T(128)} %bitcast.15.where_ref, bf16[2,448,896]{2,1,0:T(8,128)(2,1)S(1)} %pad_maximum_fusion.4.even_ref, bf16[2,448,896]{2,1,0:T(8,128)(2,1)} %collective-permute-done.18.odd_ref, bf16[1,3584,512]{2,1,0:T(8,128)(2,1)} %gate_ref.1, bf16[1,3584,512]{2,1,0:T(8,128)(2,1)} %up_ref.1), custom_call_target="tpu_custom_call" | custom-call | flops 1024 | bytes 1024 | tf_op jit(solution)/shard_map/ffn/pallas_call | solution.py:132
  75.9 5.2 %down.1 = (bf16[2,320,896]{2,1,0:T(8,128)(2,1)}, bf16[2,320,896]{2,1,0:T(8,128)(2,1)S(1)}) custom-call(s32[1]{0:T(128)} %bitcast.15.where_ref, bf16[448,512]{1,0:T(8,128)(2,1)S(1)} %ffn.1.rows_ref, bf16[512,3584]{1,0:T(8,128)(2,1)} %bitcast.74), custom_call_target="tpu_custom_call" | custom-call | flops 1024 | bytes 1024 | tf_op jit(solution)/shard_map/down/pallas_call | solution.py:58
  81.2 0.8 collective-permute-done.20.refs_2_
  82.0 10.1 %collective-permute-done.21.refs_3_ = bf16[512,512]{1,0:T(8,128)(2,1)S(1)} collective-permute-done((bf16[512,512]{1,0:T(8,128)(2,1)}, bf16[512,512]{1,0:T(8,128)(2,1)S(1)}, u32[]{:S(2)}, u32[]{:S(2)}) %collective-permute-start.21) | collective-permute-done | bytes 524320 | tf_op jit(solution)/shard_map/ppermute | solution.py:12
  92.3 0.5 collective-permute-start.23
  92.8 2.2 sums.2
  95.0 2.6 %collective-permute-start.22 = (bf16[512,512]{1,0:T(8,128)(2,1)}, bf16[512,512]{1,0:T(8,128)(2,1)}, u32[]{:S(2)}, u32[]{:S(2)}) collective-permute-start(bf16[512,512]{1,0:T(8,128)(2,1)} %get-tuple-element.122), channel_id=1, source_target_pairs={{0,16},{4,20},{8,24},{12,28},{16,0},{20,4},{24,8},{28,12},{1,17},{... | collective-permute-start | bytes 1572872 | tf_op jit(solution)/shard_map/ppermute | solution.py:12
  97.6 5.1 %align.3 = (bf16[512,384]{1,0:T(8,128)(2,1)}, bf16[512,384]{1,0:T(8,128)(2,1)}, bf16[512,384]{1,0:T(8,128)(2,1)S(1)}, bf16[512,384]{1,0:T(8,128)(2,1)S(1)}) custom-call(s32[9]{0:T(128)S(1)} %concatenate.55.flags_ref, s32[2048,1]{1,0:T(8,128)S(1)} %fusion.7.place_ref, bf16[512,384]{1,0:T(8,128)(2,1)S(1)} %get-tuple-element.127.refs_0_, ...), custom_call_target="tpu_custom_call" | custom-call | flops 1024 | bytes 1024 | tf_op jit(solution)/shard_map/align/pallas_call | solution.py:228
  102.7 1.6 collective-permute-start.27
  104.3 1.6 collective-permute-start.28
  106.4 0.6 fusion.34
  108.3 0.7 slice.152
  109.0 13.8 %collective-permute-done.22.other_ref = bf16[512,512]{1,0:T(8,128)(2,1)} collective-permute-done((bf16[512,512]{1,0:T(8,128)(2,1)}, bf16[512,512]{1,0:T(8,128)(2,1)}, u32[]{:S(2)}, u32[]{:S(2)}) %collective-permute-start.22) | collective-permute-done | bytes 524320 | tf_op jit(solution)/shard_map/ppermute | solution.py:12
  122.8 6.9 %collective-permute-done.28.refs_2_ = bf16[512,384]{1,0:T(8,128)(2,1)} collective-permute-done((bf16[512,384]{1,0:T(8,128)(2,1)S(1)}, bf16[512,384]{1,0:T(8,128)(2,1)}, u32[]{:S(2)}, u32[]{:S(2)}) %collective-permute-start.28) | collective-permute-done | bytes 393248 | tf_op jit(solution)/shard_map/ppermute | solution.py:12
  129.7 7.9 %collective-permute-done.29.refs_3_ = bf16[512,384]{1,0:T(8,128)(2,1)} collective-permute-done((bf16[512,384]{1,0:T(8,128)(2,1)S(1)}, bf16[512,384]{1,0:T(8,128)(2,1)}, u32[]{:S(2)}, u32[]{:S(2)}) %collective-permute-start.29) | collective-permute-done | bytes 393248 | tf_op jit(solution)/shard_map/ppermute | solution.py:12
  137.7 2.0 sums.3
  139.7 1.2 mean.6
  140.9 0.7 collective-permute-start.30
  141.6 1.5 convert_add_fusion
  143.0 4.8 %collective-permute-done.30 = bf16[2,128,512]{2,1,0:T(8,128)(2,1)S(1)} collective-permute-done((bf16[2,128,512]{2,1,0:T(8,128)(2,1)S(1)}, bf16[2,128,512]{2,1,0:T(8,128)(2,1)S(1)}, u32[]{:S(2)}, u32[]{:S(2)}) %collective-permute-start.30) | collective-permute-done | bytes 262176 | tf_op jit(solution)/shard_map/ppermute | solution.py:12
  148.1 0.5 collective-permute-start.24
  148.5 1.0 collective-permute-done.31
  149.7 2.8 %collective-permute-start.33 = (bf16[4,128,512]{2,1,0:T(8,128)(2,1)S(1)}, bf16[4,128,512]{2,1,0:T(8,128)(2,1)S(1)}, u32[]{:S(2)}, u32[]{:S(2)}) collective-permute-start(bf16[4,128,512]{2,1,0:T(8,128)(2,1)S(1)} %pad_maximum_fusion.10.refs_0_), channel_id=1, source_target_pairs={{0,8},{4,12},{8,0},{12,4},{16,24},{20,28},{24,16},{28,20},{1,9},{5... | collective-permute-start | bytes 1572872 | tf_op jit(solution)/shard_map/ppermute | solution.py:12
  152.5 0.7 collective-permute-start.32
  153.2 0.9 collective-permute-start.35
  154.1 9.5 %collective-permute-done.24 = bf16[320,896]{1,0:T(8,128)(2,1)S(1)} collective-permute-done((bf16[320,896]{1,0:T(8,128)(2,1)S(1)}, bf16[320,896]{1,0:T(8,128)(2,1)S(1)}, u32[]{:S(2)}, u32[]{:S(2)}) %collective-permute-start.24) | collective-permute-done | bytes 573472 | tf_op jit(solution)/shard_map/ppermute | solution.py:12
  163.5 1.0 fusion.4
  164.5 16.7 %collective-permute-done.35.other_ref = bf16[512,384]{1,0:T(8,128)(2,1)S(1)} collective-permute-done((bf16[512,384]{1,0:T(8,128)(2,1)S(1)}, bf16[512,384]{1,0:T(8,128)(2,1)S(1)}, u32[]{:S(2)}, u32[]{:S(2)}) %collective-permute-start.35) | collective-permute-done | bytes 393248 | tf_op jit(solution)/shard_map/ppermute | solution.py:12
  181.2 3.0 %collective-permute-done.33.refs_2_ = bf16[4,128,512]{2,1,0:T(8,128)(2,1)S(1)} collective-permute-done((bf16[4,128,512]{2,1,0:T(8,128)(2,1)S(1)}, bf16[4,128,512]{2,1,0:T(8,128)(2,1)S(1)}, u32[]{:S(2)}, u32[]{:S(2)}) %collective-permute-start.33) | collective-permute-done | bytes 524320 | tf_op jit(solution)/shard_map/ppermute | solution.py:12
  184.3 0.8 collective-permute-start.36
  185.1 0.6 iota_compare_fusion.6
  186.9 4.2 %all-to-all-start.1 = ((bf16[8,40,896]{2,1,0:T(8,128)(2,1)}), bf16[8,40,896]{2,1,0:T(8,128)(2,1)}, u32[]{:S(2)}, u32[]{:S(2)}) async-start(bf16[8,40,896]{2,1,0:T(8,128)(2,1)} %bitcast.78), calls=%async_computation.1 | async-start | bytes 1146880 | tf_op jit(solution)/shard_map/all_to_all | solution.py:512
  191.2 1.5 fusion.1
  192.8 7.4 %all_gather.11 = bf16[128,2048]{1,0:T(8,128)(2,1)S(1)} all-gather(bf16[128,512]{1,0:T(8,128)(2,1)S(1)} %fusion.1), channel_id=1, replica_groups=mesh['expert'=8,'tensor'=4] {'tensor'}, dimensions={1}, use_global_device_ids=true | all-gather | bytes 655360 | tf_op jit(solution)/shard_map/all_gather | solution.py:523
  200.4 2.8 %collective-permute-start.40 = (bf16[4,128,384]{2,1,0:T(8,128)(2,1)S(1)}, bf16[4,128,384]{2,1,0:T(8,128)(2,1)S(1)}, u32[]{:S(2)}, u32[]{:S(2)}) collective-permute-start(bf16[4,128,384]{2,1,0:T(8,128)(2,1)S(1)} %pad_maximum_fusion.11.refs_4_), channel_id=1, source_target_pairs={{0,12},{4,8},{8,4},{12,0},{16,28},{20,24},{24,20},{28,16},{1,13},{... | collective-permute-start | bytes 1179656 | tf_op jit(solution)/shard_map/ppermute | solution.py:12
  203.2 0.5 collective-permute-start.39
  203.9 2.7 %convolution_multiply_fusion = f32[512,2048]{1,0:T(8,128)} fusion(bf16[128,2048]{1,0:T(8,128)(2,1)S(1)} %all_gather.11, bf16[448,512]{1,0:T(8,128)(2,1)S(1)} %ffn.1.rows_ref), kind=kOutput, calls=%fused_computation.12 | convolution fusion | flops 269484032 | bytes 4849664 | tf_op jit(solution)/shard_map/dot_general | solution.py:525
  206.7 2.3 fusion.2
  208.9 5.6 %collective-permute-done.40.refs_7_ = bf16[4,128,384]{2,1,0:T(8,128)(2,1)S(1)} collective-permute-done((bf16[4,128,384]{2,1,0:T(8,128)(2,1)S(1)}, bf16[4,128,384]{2,1,0:T(8,128)(2,1)S(1)}, u32[]{:S(2)}, u32[]{:S(2)}) %collective-permute-start.40) | collective-permute-done | bytes 393248 | tf_op jit(solution)/shard_map/ppermute | solution.py:12
  214.5 8.7 %collective-permute-done.39.refs_6_ = bf16[4,128,384]{2,1,0:T(8,128)(2,1)} collective-permute-done((bf16[4,128,384]{2,1,0:T(8,128)(2,1)S(1)}, bf16[4,128,384]{2,1,0:T(8,128)(2,1)}, u32[]{:S(2)}, u32[]{:S(2)}) %collective-permute-start.39) | collective-permute-done | bytes 393248 | tf_op jit(solution)/shard_map/ppermute | solution.py:12
  223.2 3.2 %assemble.3 = bf16[512,3584]{1,0:T(8,128)(2,1)} custom-call(s32[9]{0:T(128)S(1)} %concatenate.55.flags_ref, bf16[4,128,512]{2,1,0:T(8,128)(2,1)S(1)} %pad_maximum_fusion.10.refs_0_, bf16[4,128,512]{2,1,0:T(8,128)(2,1)S(1)} %collective-permute-done.32.refs_1_, bf16[4,128,512]{2,1,0:T(8,128)(2,1)S(1)} %collective-permute-done.33.refs_2_, ...), custom_call_target="tpu_custom_call" | custom-call | flops 1024 | bytes 1024 | tf_op jit(solution)/shard_map/assemble/pallas_call | solution.py:326
  226.4 0.9 copy-done.1
  (88 shorter events, 3.4 us)
Async XLA Ops:
  7.2 7.4 %copy-start = (bf16[128,896]{1,0:T(8,128)(2,1)S(1)}, bf16[128,896]{1,0:T(8,128)(2,1)}, u32[]{:S(2)}) copy-start(bf16[128,896]{1,0:T(8,128)(2,1)} %param.12) | copy-start | bytes 688132
  7.2 6.7 %copy-start.15 = (s32[128,2]{0,1:T(2,128)S(1)}, s32[128,2]{0,1:T(2,128)}, u32[]{:S(2)}) copy-start(s32[128,2]{0,1:T(2,128)} %param.13) | copy-start | bytes 3076
  9.8 11.8 %copy-start.16 = (s32[1,512]{1,0:T(1,128)S(1)}, s32[1,512]{1,0:T(1,128)}, u32[]{:S(2)}) copy-start(s32[1,512]{1,0:T(1,128)} %param.19) | copy-start | bytes 6148
  9.8 12.4 %copy-start.4 = (s32[8]{0:T(128)S(1)}, s32[8]{0:T(128)}, u32[]{:S(2)}) copy-start(s32[8]{0:T(128)} %param.20) | copy-start | bytes 100
  9.8 15.2 %copy-start.14 = (s32[2]{0:T(128)S(1)}, s32[2]{0:T(128)}, u32[]{:S(2)}) copy-start(s32[2]{0:T(128)} %param.21) | copy-start | bytes 28
  10.9 26.4 %collective-permute-start.12 = (bf16[2,512,512]{2,1,0:T(8,128)(2,1)}, bf16[2,512,512]{2,1,0:T(8,128)(2,1)S(1)}, u32[]{:S(2)}, u32[]{:S(2)}) collective-permute-start(bf16[2,512,512]{2,1,0:T(8,128)(2,1)} %pad_maximum_fusion.5), channel_id=1, source_target_pairs={{0,2},{1,3},{2,0},{3,1},{4,6},{5,7},{6,4},{7,5},{8,10},{9,11},{10,... | collective-permute-start | bytes 3145736 | tf_op jit(solution)/shard_map/ppermute | solution.py:12
  15.7 24.8 %copy-start.13 = (bf16[128,896]{1,0:T(8,128)(2,1)S(1)}, bf16[128,896]{1,0:T(8,128)(2,1)}, u32[]{:S(2)}) copy-start(bf16[128,896]{1,0:T(8,128)(2,1)} %param.15) | copy-start | bytes 688132
  15.7 24.8 %all-to-all-start = ((bf16[8,40,896]{2,1,0:T(8,128)(2,1)}), bf16[8,40,896]{2,1,0:T(8,128)(2,1)S(1)}, u32[]{:S(2)}, u32[]{:S(2)}) async-start(bf16[8,40,896]{2,1,0:T(8,128)(2,1)} %bitcast.18), calls=%async_computation | async-start | bytes 1146880 | tf_op jit(solution)/shard_map/all_to_all | solution.py:482
  21.6 169.5 %all-gather.3.cloned.1.call-start = ((), (), s32[]{:S(2)}) async-start(), calls=%async_computation.2 | async-start | bytes 1179648 | tf_op jit(solution)/shard_map/all_gather | solution.py:518
  21.7 18.3 %collective-permute-start.15 = (s32[512]{0:T(512)S(1)}, s32[512]{0:T(512)S(1)}, u32[]{:S(2)}, u32[]{:S(2)}) collective-permute-start(s32[512]{0:T(512)S(1)} %bitcast.83), channel_id=1, source_target_pairs={{0,2},{1,3},{2,0},{3,1},{4,6},{5,7},{6,4},{7,5},{8,10},{9,11},{10,... | collective-permute-start | bytes 6152 | tf_op jit(solution)/shard_map/ppermute | solution.py:12
  22.3 23.3 %collective-permute-start.14 = (s32[512]{0:T(512)S(1)}, s32[512]{0:T(512)S(1)}, u32[]{:S(2)}, u32[]{:S(2)}) collective-permute-start(s32[512]{0:T(512)S(1)} %bitcast.84), channel_id=1, source_target_pairs={{0,1},{1,0},{2,3},{3,2},{4,5},{5,4},{6,7},{7,6},{8,9},{9,8},{10,11... | collective-permute-start | bytes 6152 | tf_op jit(solution)/shard_map/ppermute | solution.py:12
  39.4 9.7 %collective-permute-start.17 = (bf16[2,512,512]{2,1,0:T(8,128)(2,1)}, bf16[2,512,512]{2,1,0:T(8,128)(2,1)}, u32[]{:S(2)}, u32[]{:S(2)}) collective-permute-start(bf16[2,512,512]{2,1,0:T(8,128)(2,1)} %pad_maximum_fusion.6), channel_id=1, source_target_pairs={{0,1},{1,0},{2,3},{3,2},{4,5},{5,4},{6,7},{7,6},{8,9},{9,8},{10,11... | collective-permute-start | bytes 3145736 | tf_op jit(solution)/shard_map/ppermute | solution.py:12
  40.0 5.6 %collective-permute-start.16 = (s32[512]{0:T(512)S(1)}, s32[512]{0:T(512)S(1)}, u32[]{:S(2)}, u32[]{:S(2)}) collective-permute-start(s32[512]{0:T(512)S(1)} %collective-permute-done.15), channel_id=1, source_target_pairs={{0,1},{1,0},{2,3},{3,2},{4,5},{5,4},{6,7},{7,6},{8,9},{9,8},{10,11... | collective-permute-start | bytes 6152 | tf_op jit(solution)/shard_map/ppermute | solution.py:12
  40.6 20.0 %collective-permute-start.13 = (bf16[1,448,896]{2,1,0:T(8,128)(2,1)S(1)}, bf16[1,448,896]{2,1,0:T(8,128)(2,1)}, u32[]{:S(2)}, u32[]{:S(2)}) collective-permute-start(bf16[1,448,896]{2,1,0:T(8,128)(2,1)S(1)} %bitcast.76), channel_id=1, source_target_pairs={{0,2},{1,3},{2,0},{3,1},{4,6},{5,7},{6,4},{7,5},{8,10},{9,11},{10,... | collective-permute-start | bytes 2408456 | tf_op jit(solution)/shard_map/ppermute | solution.py:12
  61.9 7.0 %collective-permute-start.18 = (bf16[2,448,896]{2,1,0:T(8,128)(2,1)S(1)}, bf16[2,448,896]{2,1,0:T(8,128)(2,1)}, u32[]{:S(2)}, u32[]{:S(2)}) collective-permute-start(bf16[2,448,896]{2,1,0:T(8,128)(2,1)S(1)} %pad_maximum_fusion.4.even_ref), channel_id=1, source_target_pairs={{0,1},{1,0},{2,3},{3,2},{4,5},{5,4},{6,7},{7,6},{8,9},{9,8},{10,11... | collective-permute-start | bytes 4816904 | tf_op jit(solution)/shard_map/ppermute | solution.py:12
  63.7 28.4 %collective-permute-start.25 = (bf16[2,512,384]{2,1,0:T(8,128)(2,1)S(1)}, bf16[2,512,384]{2,1,0:T(8,128)(2,1)S(1)}, u32[]{:S(2)}, u32[]{:S(2)}) collective-permute-start(bf16[2,512,384]{2,1,0:T(8,128)(2,1)S(1)} %pad_maximum_fusion.8), channel_id=1, source_target_pairs={{0,2},{1,3},{2,0},{3,1},{4,6},{5,7},{6,4},{7,5},{8,10},{9,11},{10,... | collective-permute-start | bytes 2359304 | tf_op jit(solution)/shard_map/ppermute | solution.py:12
  65.5 15.7 %collective-permute-start.19 = (bf16[512,512]{1,0:T(8,128)(2,1)}, bf16[512,512]{1,0:T(8,128)(2,1)S(1)}, u32[]{:S(2)}, u32[]{:S(2)}) collective-permute-start(bf16[512,512]{1,0:T(8,128)(2,1)} %get-tuple-element.114), channel_id=1, source_target_pairs={{0,4},{4,0},{8,12},{12,8},{16,20},{20,16},{24,28},{28,24},{1,5},{5... | collective-permute-start | bytes 1572872 | tf_op jit(solution)/shard_map/ppermute | solution.py:12
  67.0 15.0 %collective-permute-start.20 = (bf16[512,512]{1,0:T(8,128)(2,1)}, bf16[512,512]{1,0:T(8,128)(2,1)S(1)}, u32[]{:S(2)}, u32[]{:S(2)}) collective-permute-start(bf16[512,512]{1,0:T(8,128)(2,1)} %get-tuple-element.115), channel_id=1, source_target_pairs={{0,8},{4,12},{8,0},{12,4},{16,24},{20,28},{24,16},{28,20},{1,9},{5... | collective-permute-start | bytes 1572872 | tf_op jit(solution)/shard_map/ppermute | solution.py:12
  68.5 23.6 %collective-permute-start.21 = (bf16[512,512]{1,0:T(8,128)(2,1)}, bf16[512,512]{1,0:T(8,128)(2,1)S(1)}, u32[]{:S(2)}, u32[]{:S(2)}) collective-permute-start(bf16[512,512]{1,0:T(8,128)(2,1)} %get-tuple-element.116), channel_id=1, source_target_pairs={{0,12},{4,8},{8,4},{12,0},{16,28},{20,24},{24,20},{28,16},{1,13},{... | collective-permute-start | bytes 1572872 | tf_op jit(solution)/shard_map/ppermute | solution.py:12
  75.9 16.9 %copy-start.5 = (bf16[512,512]{1,0:T(8,128)(2,1)S(1)}, bf16[512,512]{1,0:T(8,128)(2,1)}, u32[]{:S(2)}) copy-start(bf16[512,512]{1,0:T(8,128)(2,1)} %get-tuple-element.118.refs_0_) | copy-start | bytes 1572868
  81.2 16.4 %copy-start.7 = (bf16[512,512]{1,0:T(8,128)(2,1)}, bf16[512,512]{1,0:T(8,128)(2,1)S(1)}, u32[]{:S(2)}) copy-start(bf16[512,512]{1,0:T(8,128)(2,1)S(1)} %collective-permute-done.19.refs_1_) | copy-start | bytes 1572868
  82.0 20.7 %copy-start.9 = (bf16[512,512]{1,0:T(8,128)(2,1)}, bf16[512,512]{1,0:T(8,128)(2,1)S(1)}, u32[]{:S(2)}) copy-start(bf16[512,512]{1,0:T(8,128)(2,1)S(1)} %collective-permute-done.20.refs_2_) | copy-start | bytes 1572868
  92.1 10.6 %copy-start.11 = (bf16[512,512]{1,0:T(8,128)(2,1)}, bf16[512,512]{1,0:T(8,128)(2,1)S(1)}, u32[]{:S(2)}) copy-start(bf16[512,512]{1,0:T(8,128)(2,1)S(1)} %collective-permute-done.21.refs_3_) | copy-start | bytes 1572868
  92.2 5.3 %collective-permute-start.26 = (bf16[2,512,384]{2,1,0:T(8,128)(2,1)S(1)}, bf16[2,512,384]{2,1,0:T(8,128)(2,1)S(1)}, u32[]{:S(2)}, u32[]{:S(2)}) collective-permute-start(bf16[2,512,384]{2,1,0:T(8,128)(2,1)S(1)} %pad_maximum_fusion.9), channel_id=1, source_target_pairs={{0,1},{1,0},{2,3},{3,2},{4,5},{5,4},{6,7},{7,6},{8,9},{9,8},{10,11... | collective-permute-start | bytes 2359304 | tf_op jit(solution)/shard_map/ppermute | solution.py:12
  92.3 49.2 %collective-permute-start.23 = (bf16[2,320,896]{2,1,0:T(8,128)(2,1)}, bf16[2,320,896]{2,1,0:T(8,128)(2,1)}, u32[]{:S(2)}, u32[]{:S(2)}) collective-permute-start(bf16[2,320,896]{2,1,0:T(8,128)(2,1)} %get-tuple-element.117), channel_id=1, source_target_pairs={{0,1},{1,0},{2,3},{3,2},{4,5},{5,4},{6,7},{7,6},{8,9},{9,8},{10,11... | collective-permute-start | bytes 3440648 | tf_op jit(solution)/shard_map/ppermute | solution.py:12
  95.0 7.7 %copy-start.2 = (f32[512,512]{1,0:T(8,128)}, f32[512,512]{1,0:T(8,128)S(1)}, u32[]{:S(2)}) copy-start(f32[512,512]{1,0:T(8,128)S(1)} %get-tuple-element.124.kept_ref) | copy-start | bytes 3145732
  95.0 27.8 %collective-permute-start.22 = (bf16[512,512]{1,0:T(8,128)(2,1)}, bf16[512,512]{1,0:T(8,128)(2,1)}, u32[]{:S(2)}, u32[]{:S(2)}) collective-permute-start(bf16[512,512]{1,0:T(8,128)(2,1)} %get-tuple-element.122), channel_id=1, source_target_pairs={{0,16},{4,20},{8,24},{12,28},{16,0},{20,4},{24,8},{28,12},{1,17},{... | collective-permute-start | bytes 1572872 | tf_op jit(solution)/shard_map/ppermute | solution.py:12
  102.7 37.0 %copy-start.3 = (f32[512,512]{1,0:T(8,128)S(1)}, f32[512,512]{1,0:T(8,128)}, u32[]{:S(2)}) copy-start(f32[512,512]{1,0:T(8,128)} %copy-done.2) | copy-start | bytes 3145732
  102.7 20.1 %collective-permute-start.27 = (bf16[512,384]{1,0:T(8,128)(2,1)}, bf16[512,384]{1,0:T(8,128)(2,1)}, u32[]{:S(2)}, u32[]{:S(2)}) collective-permute-start(bf16[512,384]{1,0:T(8,128)(2,1)} %get-tuple-element.131), channel_id=1, source_target_pairs={{0,4},{4,0},{8,12},{12,8},{16,20},{20,16},{24,28},{28,24},{1,5},{5... | collective-permute-start | bytes 1179656 | tf_op jit(solution)/shard_map/ppermute | solution.py:12
  104.3 25.4 %collective-permute-start.28 = (bf16[512,384]{1,0:T(8,128)(2,1)S(1)}, bf16[512,384]{1,0:T(8,128)(2,1)}, u32[]{:S(2)}, u32[]{:S(2)}) collective-permute-start(bf16[512,384]{1,0:T(8,128)(2,1)S(1)} %get-tuple-element.132), channel_id=1, source_target_pairs={{0,8},{4,12},{8,0},{12,4},{16,24},{20,28},{24,16},{28,20},{1,9},{5... | collective-permute-start | bytes 1179656 | tf_op jit(solution)/shard_map/ppermute | solution.py:12
  105.9 31.8 %collective-permute-start.29 = (bf16[512,384]{1,0:T(8,128)(2,1)S(1)}, bf16[512,384]{1,0:T(8,128)(2,1)}, u32[]{:S(2)}, u32[]{:S(2)}) collective-permute-start(bf16[512,384]{1,0:T(8,128)(2,1)S(1)} %get-tuple-element.133), channel_id=1, source_target_pairs={{0,12},{4,8},{8,4},{12,0},{16,28},{20,24},{24,20},{28,16},{1,13},{... | collective-permute-start | bytes 1179656 | tf_op jit(solution)/shard_map/ppermute | solution.py:12
  140.9 7.0 %collective-permute-start.30 = (bf16[2,128,512]{2,1,0:T(8,128)(2,1)S(1)}, bf16[2,128,512]{2,1,0:T(8,128)(2,1)S(1)}, u32[]{:S(2)}, u32[]{:S(2)}) collective-permute-start(bf16[2,128,512]{2,1,0:T(8,128)(2,1)S(1)} %get-tuple-element.142), channel_id=1, source_target_pairs={{0,2},{1,3},{2,0},{3,1},{4,6},{5,7},{6,4},{7,5},{8,10},{9,11},{10,... | collective-permute-start | bytes 786440 | tf_op jit(solution)/shard_map/ppermute | solution.py:12
  147.9 1.6 collective-permute-start.31
  148.1 15.4 %collective-permute-start.24 = (bf16[320,896]{1,0:T(8,128)(2,1)S(1)}, bf16[320,896]{1,0:T(8,128)(2,1)S(1)}, u32[]{:S(2)}, u32[]{:S(2)}) collective-permute-start(bf16[320,896]{1,0:T(8,128)(2,1)S(1)} %fusion.12), channel_id=1, source_target_pairs={{0,2},{1,3},{2,0},{3,1},{4,6},{5,7},{6,4},{7,5},{8,10},{9,11},{10,... | collective-permute-start | bytes 1720328 | tf_op jit(solution)/shard_map/ppermute | solution.py:12
  149.6 31.5 %collective-permute-start.34 = (bf16[4,128,512]{2,1,0:T(8,128)(2,1)S(1)}, bf16[4,128,512]{2,1,0:T(8,128)(2,1)S(1)}, u32[]{:S(2)}, u32[]{:S(2)}) collective-permute-start(bf16[4,128,512]{2,1,0:T(8,128)(2,1)S(1)} %pad_maximum_fusion.10.refs_0_), channel_id=1, source_target_pairs={{0,12},{4,8},{8,4},{12,0},{16,28},{20,24},{24,20},{28,16},{1,13},{... | collective-permute-start | bytes 1572872 | tf_op jit(solution)/shard_map/ppermute | solution.py:12
  149.7 34.5 %collective-permute-start.33 = (bf16[4,128,512]{2,1,0:T(8,128)(2,1)S(1)}, bf16[4,128,512]{2,1,0:T(8,128)(2,1)S(1)}, u32[]{:S(2)}, u32[]{:S(2)}) collective-permute-start(bf16[4,128,512]{2,1,0:T(8,128)(2,1)S(1)} %pad_maximum_fusion.10.refs_0_), channel_id=1, source_target_pairs={{0,8},{4,12},{8,0},{12,4},{16,24},{20,28},{24,16},{28,20},{1,9},{5... | collective-permute-start | bytes 1572872 | tf_op jit(solution)/shard_map/ppermute | solution.py:12
  152.5 31.7 %collective-permute-start.32 = (bf16[4,128,512]{2,1,0:T(8,128)(2,1)S(1)}, bf16[4,128,512]{2,1,0:T(8,128)(2,1)S(1)}, u32[]{:S(2)}, u32[]{:S(2)}) collective-permute-start(bf16[4,128,512]{2,1,0:T(8,128)(2,1)S(1)} %pad_maximum_fusion.10.refs_0_), channel_id=1, source_target_pairs={{0,4},{4,0},{8,12},{12,8},{16,20},{20,16},{24,28},{28,24},{1,5},{5... | collective-permute-start | bytes 1572872 | tf_op jit(solution)/shard_map/ppermute | solution.py:12
  153.2 28.0 %collective-permute-start.35 = (bf16[512,384]{1,0:T(8,128)(2,1)S(1)}, bf16[512,384]{1,0:T(8,128)(2,1)S(1)}, u32[]{:S(2)}, u32[]{:S(2)}) collective-permute-start(bf16[512,384]{1,0:T(8,128)(2,1)S(1)} %get-tuple-element.143), channel_id=1, source_target_pairs={{0,16},{4,20},{8,24},{12,28},{16,0},{20,4},{24,8},{28,12},{1,17},{... | collective-permute-start | bytes 1179656 | tf_op jit(solution)/shard_map/ppermute | solution.py:12
  184.3 8.4 %collective-permute-start.36 = (bf16[2,128,384]{2,1,0:T(8,128)(2,1)S(1)}, bf16[2,128,384]{2,1,0:T(8,128)(2,1)S(1)}, u32[]{:S(2)}, u32[]{:S(2)}) collective-permute-start(bf16[2,128,384]{2,1,0:T(8,128)(2,1)S(1)} %get-tuple-element.147), channel_id=1, source_target_pairs={{0,2},{1,3},{2,0},{3,1},{4,6},{5,7},{6,4},{7,5},{8,10},{9,11},{10,... | collective-permute-start | bytes 589832 | tf_op jit(solution)/shard_map/ppermute | solution.py:12
  186.9 19.7 %all-to-all-start.1 = ((bf16[8,40,896]{2,1,0:T(8,128)(2,1)}), bf16[8,40,896]{2,1,0:T(8,128)(2,1)}, u32[]{:S(2)}, u32[]{:S(2)}) async-start(bf16[8,40,896]{2,1,0:T(8,128)(2,1)} %bitcast.78), calls=%async_computation.1 | async-start | bytes 1146880 | tf_op jit(solution)/shard_map/all_to_all | solution.py:512
  192.7 7.5 %collective-permute-start.37 = (bf16[2,128,384]{2,1,0:T(8,128)(2,1)S(1)}, bf16[2,128,384]{2,1,0:T(8,128)(2,1)S(1)}, u32[]{:S(2)}, u32[]{:S(2)}) collective-permute-start(bf16[2,128,384]{2,1,0:T(8,128)(2,1)S(1)} %pad_maximum_fusion.13), channel_id=1, source_target_pairs={{0,1},{1,0},{2,3},{3,2},{4,5},{5,4},{6,7},{7,6},{8,9},{9,8},{10,11... | collective-permute-start | bytes 589832 | tf_op jit(solution)/shard_map/ppermute | solution.py:12
  200.4 6.3 %copy-start.17 = (f32[128,2]{0,1:T(2,128)S(1)}, f32[128,2]{0,1:T(2,128)}, u32[]{:S(2)}) copy-start(f32[128,2]{0,1:T(2,128)} %param.14) | copy-start | bytes 3076
  200.4 14.1 %collective-permute-start.40 = (bf16[4,128,384]{2,1,0:T(8,128)(2,1)S(1)}, bf16[4,128,384]{2,1,0:T(8,128)(2,1)S(1)}, u32[]{:S(2)}, u32[]{:S(2)}) collective-permute-start(bf16[4,128,384]{2,1,0:T(8,128)(2,1)S(1)} %pad_maximum_fusion.11.refs_4_), channel_id=1, source_target_pairs={{0,12},{4,8},{8,4},{12,0},{16,28},{20,24},{24,20},{28,16},{1,13},{... | collective-permute-start | bytes 1179656 | tf_op jit(solution)/shard_map/ppermute | solution.py:12
  203.2 20.0 %collective-permute-start.39 = (bf16[4,128,384]{2,1,0:T(8,128)(2,1)S(1)}, bf16[4,128,384]{2,1,0:T(8,128)(2,1)}, u32[]{:S(2)}, u32[]{:S(2)}) collective-permute-start(bf16[4,128,384]{2,1,0:T(8,128)(2,1)S(1)} %pad_maximum_fusion.11.refs_4_), channel_id=1, source_target_pairs={{0,8},{4,12},{8,0},{12,4},{16,24},{20,28},{24,16},{28,20},{1,9},{5... | collective-permute-start | bytes 1179656 | tf_op jit(solution)/shard_map/ppermute | solution.py:12
  203.8 19.4 %collective-permute-start.38 = (bf16[4,128,384]{2,1,0:T(8,128)(2,1)S(1)}, bf16[4,128,384]{2,1,0:T(8,128)(2,1)}, u32[]{:S(2)}, u32[]{:S(2)}) collective-permute-start(bf16[4,128,384]{2,1,0:T(8,128)(2,1)S(1)} %pad_maximum_fusion.11.refs_4_), channel_id=1, source_target_pairs={{0,4},{4,0},{8,12},{12,8},{16,20},{20,16},{24,28},{28,24},{1,5},{5... | collective-permute-start | bytes 1179656 | tf_op jit(solution)/shard_map/ppermute | solution.py:12
  208.9 17.5 %copy-start.6 = (bf16[512,512]{1,0:T(8,128)(2,1)S(1)}, bf16[512,512]{1,0:T(8,128)(2,1)}, u32[]{:S(2)}) copy-start(bf16[512,512]{1,0:T(8,128)(2,1)} %get-tuple-element.118.refs_0_) | copy-start | bytes 1572868
  226.4 0.9 copy-start.1
Sparse Core Ops, SparseCore 0:
  109.1 43.2 all-gather.2

commit v7 on v6

--- a/solution.py
+++ b/solution.py
@@ -492,6 +492,19 @@
     odd = xor_permute(even, "tensor", nt, 1)
     hidden = ffn((even, odd), order, gate_weight, up_weight, t)
     probe_hidden = hidden[routed:]
+    everyone = lax.all_gather(probe_hidden, "expert", axis=0)
+    at_owner = jnp.arange(ne, dtype=jnp.int32) == owners[cluster[e]]
+    partner = jnp.sum(
+        jnp.where(at_owner[:, None, None], everyone.astype(jnp.float32), 0.0), axis=0
+    ).astype(jnp.bfloat16)
+
+    def correlate(partner):
+        partner_full = lax.all_gather(partner, "tensor", axis=1, tiled=True)
+        found = lax.dot_general(
+            probe_hidden, partner_full, (((0,), (0,)), ((), ())), preferred_element_type=jnp.float32
+        )
+        return found / probe_hidden.shape[0]
+
     send, keep = down(hidden, routed, own, t, nt)
     if two is not None:
         others, kept = [], []
@@ -500,40 +513,31 @@
                 source = two.columns(c + 1, (even,), (*parts[c][1:], send))
                 mark, sent = two.send_aligned(source, mark)
                 parts.append(sent)
-            ready = all_after(parts[c], *((others[-1],) if c else (send,)))
+            ready = all_after(parts[c], *((others[-1], returned, correlation) if c else (send,)))
             given, own_sum = sums(two.flags, ready)
             others.append(xor_permute(given, "expert", ne, two.half))
             kept.append(own_sum)
             if not c:
-                returned = sum_tensor(send, after(keep, others[0]), nt)
+                returned = sum_tensor(send, after(keep, mark), nt)
+                correlation = correlate(after(partner, own_sum))
         lines = two.back(mean_of(two.scale, kept[0], after(others[0], kept[-1])))
+        lines = after(lines, others[-1])
     else:
         returned = sum_tensor(send, keep, nt)
+        correlation = correlate(partner)
     home = lax.all_to_all(returned, "expert", split_axis=0, concat_axis=0, tiled=True)
     chooser = (target.T.reshape(-1)[:, None] == slots[None, :]).astype(jnp.bfloat16)
     picked = jnp.dot(chooser, home, preferred_element_type=jnp.float32)
     picked = picked.reshape(top, tok_rows, block)
     mixed = jnp.sum(gate_values.T[:, :, None] * picked, axis=0).astype(jnp.bfloat16)
 
-    everyone = lax.all_gather(probe_hidden, "expert", axis=0)
-    at_owner = jnp.arange(ne, dtype=jnp.int32) == owners[cluster[e]]
-    partner = jnp.sum(
-        jnp.where(at_owner[:, None, None], everyone.astype(jnp.float32), 0.0), axis=0
-    ).astype(jnp.bfloat16)
-    partner_full = lax.all_gather(partner, "tensor", axis=1, tiled=True)
-    correlation = (
-        lax.dot_general(
-            probe_hidden, partner_full, (((0,), (0,)), ((), ())), preferred_element_type=jnp.float32
-        )
-        / probe_hidden.shape[0]
-    )
     if two is not None:
         gathered = [two.out(lines)]
         for c in range(1, len(two.spans)):
-            means = mean_of(two.scale, kept[c], after(others[c], returned, *gathered[-1][1:]))
-            lines = after(two.back(means), returned)
+            means = mean_of(two.scale, kept[c], others[c])
+            lines = two.back(means)
             gathered.append(two.out(lines))
-        gathered[-1][0] = after(gathered[-1][0], mixed, correlation)
+        gathered[-1][0] = after(gathered[-1][0], mixed)
         merged = two.finish(gathered, parts)
     else:
         merged = merge_any(own, perm, cluster, owners, e, t, ne, nt)

time: 235 us -> 255 us (1.085)
  waiting for transfers between devices: 106 us -> 122 us
  local copies, waits for them, and re-layouts: 10.4 us -> 14.8 us
    all_gather x1, waiting for transfers between devices: 0.02 us -> 32.2 us  [on_device(): everyone = lax.all_gather(probe_hidden, 'expert', axis=0)]
    ppermute x29, waiting for transfers between devices: 106 us -> 89.8 us  [xor_permute(): return lax.ppermute(value, axis, [(i, i ^ k) for i in range(size)])]
    unnamed x31 -> x53, local copies, waits for them, and re-layouts: 1.12 us -> 5.47 us
  transfers between devices with their start and end apart: 32 -> 32, of which waited for: 14 -> 15; matrix products, arithmetic and copies ran while one was open for 10% -> 9% of each run, Pallas kernels for 13% -> 10%
where the time goes in v7:
time: 255 us; the launch traced here: 254 us
  waiting for transfers between devices  122 us (48%)
  starting transfers between devices  38.8 us (15%)
  Pallas kernels  30.5 us (12%)
  between operations  21.7 us (9%)
  local copies, waits for them, and re-layouts  14.8 us (6%)
  other arithmetic  13.2 us (5%)
  blocking collectives  7.08 us (3%)
  matrix products  6.16 us (2%)
    ppermute x29, waiting for transfers between devices, xor_permute(): return lax.ppermute(value, axis, [(i, i ^ k) for i in range(size)])  89.8 us
    all_gather x1, waiting for transfers between devices, on_device(): everyone = lax.all_gather(probe_hidden, 'expert', axis=0)  32.2 us
    ppermute x29, starting transfers between devices, xor_permute(): return lax.ppermute(value, axis, [(i, i ^ k) for i in range(size)])  28.6 us
    pallas_call x2, Pallas kernels, align(): pl.pallas_call(functools.partial(align_kernel, nt, half, sub), out_shape=...  11.7 us
    all_gather x1, blocking collectives, correlate(): partner_full = lax.all_gather(partner, 'tensor', axis=1, tiled=True)  7.08 us
    pallas_call x1, Pallas kernels, ffn(): pl.pallas_call(functools.partial(ffn_kernel, order), out_shape=jax.ShapeD...  6.96 us
    all_to_all x1, starting transfers between devices, on_device(): lax.all_to_all(outgoing, 'expert', split_axis=0, concat_axis=0, tiled=True)  5.94 us
    unnamed x53, local copies, waits for them, and re-layouts  5.47 us
  transfers between devices with their start and end apart: 32, of which 15 were waited for; matrix products, arithmetic and copies ran while one was open for 9% of the time, Pallas kernels for 10%

profile of v7, /device:TPU:0, one launch (start us, length us, event | category | flops | bytes accessed | tf_op | source)
XLA Modules:
  0.0 254.2 jit_solution(147245854031924240)
XLA Ops:
  7.2 2.6 %constant_dynamic-slice_fusion.3 = (bf16[1,512,512]{2,1,0:T(8,128)(2,1)}, bf16[512,512]{1,0:T(8,128)(2,1)S(1)}, bf16[1,512,512]{2,1,0:T(8,128)(2,1)S(1)}, bf16[1,512,512]{2,1,0:T(8,128)(2,1)S(1)}) fusion(bf16[1,512,3584]{2,1,0:T(8,128)(2,1)} %param.18, s32[]{:T(128)S(6)} %select_n.176, s32[]{:T(128)S(6)} %select_n.175, s32[]{:T(128)S(6)} %select_n.164, ...), kind=kLoop, calls=%fused_computation.66 | loop fusion | bytes 4194320 | tf_op jit(solution)/shard_map/dynamic_slice | solution.py:186
  9.8 1.1 pad_maximum_fusion.5
  10.9 3.0 %collective-permute-start.12 = (bf16[2,512,512]{2,1,0:T(8,128)(2,1)}, bf16[2,512,512]{2,1,0:T(8,128)(2,1)S(1)}, u32[]{:S(2)}, u32[]{:S(2)}) collective-permute-start(bf16[2,512,512]{2,1,0:T(8,128)(2,1)} %pad_maximum_fusion.5), channel_id=1, source_target_pairs={{0,2},{1,3},{2,0},{3,1},{4,6},{5,7},{6,4},{7,5},{8,10},{9,11},{10,... | collective-permute-start | bytes 3145736 | tf_op jit(solution)/shard_map/ppermute | solution.py:12
  14.5 1.1 convolution_convert_fusion
  15.7 5.9 %all-to-all-start = ((bf16[8,40,896]{2,1,0:T(8,128)(2,1)}), bf16[8,40,896]{2,1,0:T(8,128)(2,1)S(1)}, u32[]{:S(2)}, u32[]{:S(2)}) async-start(bf16[8,40,896]{2,1,0:T(8,128)(2,1)} %bitcast.18), calls=%async_computation | async-start | bytes 1146880 | tf_op jit(solution)/shard_map/all_to_all | solution.py:482
  22.2 0.6 dynamic_slice.44
  25.0 12.2 %collective-permute-done.12.refs_1_ = bf16[2,512,512]{2,1,0:T(8,128)(2,1)S(1)} collective-permute-done((bf16[2,512,512]{2,1,0:T(8,128)(2,1)}, bf16[2,512,512]{2,1,0:T(8,128)(2,1)S(1)}, u32[]{:S(2)}, u32[]{:S(2)}) %collective-permute-start.12) | collective-permute-done | bytes 1048608 | tf_op jit(solution)/shard_map/ppermute | solution.py:12
  37.3 2.1 pad_maximum_fusion.6
  39.4 0.6 fusion.36
  40.6 1.8 collective-permute-start.13
  42.4 0.7 fusion.35
  45.7 1.3 copy.47
  47.1 2.2 fusion.7.place_ref
  49.3 5.8 %align.2 = (bf16[512,512]{1,0:T(8,128)(2,1)}, bf16[512,512]{1,0:T(8,128)(2,1)S(1)}, bf16[512,512]{1,0:T(8,128)(2,1)S(1)}, bf16[512,512]{1,0:T(8,128)(2,1)S(1)}) custom-call(s32[9]{0:T(128)S(1)} %concatenate.55.flags_ref, s32[2048,1]{1,0:T(8,128)S(1)} %fusion.7.place_ref, bf16[512,512]{1,0:T(8,128)(2,1)S(1)} %get-tuple-element.108.refs_0_, ...), custom_call_target="tpu_custom_call" | custom-call | flops 1024 | bytes 1024 | tf_op jit(solution)/shard_map/align/pallas_call | solution.py:228
  55.2 0.8 copy-done.6
  56.0 0.8 copy-done.8
  56.7 0.8 copy-done.10
  57.5 3.1 %collective-permute-done.13 = bf16[1,448,896]{2,1,0:T(8,128)(2,1)} collective-permute-done((bf16[1,448,896]{2,1,0:T(8,128)(2,1)S(1)}, bf16[1,448,896]{2,1,0:T(8,128)(2,1)}, u32[]{:S(2)}, u32[]{:S(2)}) %collective-permute-start.13) | collective-permute-done | bytes 802848 | tf_op jit(solution)/shard_map/ppermute | solution.py:12
  60.6 1.3 pad_maximum_fusion.4.even_ref
  62.1 1.6 constant_dynamic-slice_fusion
  63.8 1.8 collective-permute-start.19
  65.6 1.5 collective-permute-start.20
  67.1 1.6 collective-permute-start.21
  69.1 7.0 %ffn.1.rows_ref = bf16[448,512]{1,0:T(8,128)(2,1)S(1)} custom-call(s32[1]{0:T(128)} %bitcast.15.where_ref, bf16[2,448,896]{2,1,0:T(8,128)(2,1)S(1)} %pad_maximum_fusion.4.even_ref, bf16[2,448,896]{2,1,0:T(8,128)(2,1)} %collective-permute-done.18.odd_ref, bf16[1,3584,512]{2,1,0:T(8,128)(2,1)} %gate_ref.1, bf16[1,3584,512]{2,1,0:T(8,128)(2,1)} %up_ref.1), custom_call_target="tpu_custom_call" | custom-call | flops 1024 | bytes 1024 | tf_op jit(solution)/shard_map/ffn/pallas_call | solution.py:132
  76.1 5.2 %down.1 = (bf16[2,320,896]{2,1,0:T(8,128)(2,1)}, bf16[2,320,896]{2,1,0:T(8,128)(2,1)S(1)}) custom-call(s32[1]{0:T(128)} %bitcast.15.where_ref, bf16[448,512]{1,0:T(8,128)(2,1)S(1)} %ffn.1.rows_ref, bf16[512,3584]{1,0:T(8,128)(2,1)} %bitcast.74), custom_call_target="tpu_custom_call" | custom-call | flops 1024 | bytes 1024 | tf_op jit(solution)/shard_map/down/pallas_call | solution.py:58
  81.3 1.0 copy-done.4
  82.3 9.7 %collective-permute-done.22.refs_3_ = bf16[512,512]{1,0:T(8,128)(2,1)S(1)} collective-permute-done((bf16[512,512]{1,0:T(8,128)(2,1)S(1)}, bf16[512,512]{1,0:T(8,128)(2,1)S(1)}, u32[]{:S(2)}, u32[]{:S(2)}) %collective-permute-start.22) | collective-permute-done | bytes 524320 | tf_op jit(solution)/shard_map/ppermute | solution.py:12
  92.1 0.9 copy-done.2
  93.0 1.0 pad_maximum_fusion.9
  94.0 0.7 slice.152
  94.7 1.8 collective-permute-done.23.refs_2_
  96.5 5.9 %align.3 = (bf16[512,384]{1,0:T(8,128)(2,1)}, bf16[512,384]{1,0:T(8,128)(2,1)}, bf16[512,384]{1,0:T(8,128)(2,1)}, bf16[512,384]{1,0:T(8,128)(2,1)}) custom-call(s32[9]{0:T(128)S(1)} %concatenate.55.flags_ref, s32[2048,1]{1,0:T(8,128)S(1)} %fusion.7.place_ref, bf16[512,384]{1,0:T(8,128)(2,1)S(1)} %get-tuple-element.120.refs_0_, ...), custom_call_target="tpu_custom_call" | custom-call | flops 1024 | bytes 1024 | tf_op jit(solution)/shard_map/align/pallas_call | solution.py:228
  102.4 1.6 convert_add_fusion
  104.6 0.6 fusion.34
  106.6 0.6 iota_compare_fusion.6
  107.2 1.4 sums.2
  108.6 2.8 %collective-permute-start.26 = (bf16[512,512]{1,0:T(8,128)(2,1)S(1)}, bf16[512,512]{1,0:T(8,128)(2,1)S(1)}, u32[]{:S(2)}, u32[]{:S(2)}) collective-permute-start(bf16[512,512]{1,0:T(8,128)(2,1)S(1)} %get-tuple-element.131), channel_id=1, source_target_pairs={{0,16},{4,20},{8,24},{12,28},{16,0},{20,4},{24,8},{28,12},{1,17},{... | collective-permute-start | bytes 1572872 | tf_op jit(solution)/shard_map/ppermute | solution.py:12
  111.4 1.5 collective-permute-start.27
  112.9 1.6 collective-permute-start.28
  114.9 4.3 %collective-permute-done.25 = bf16[320,896]{1,0:T(8,128)(2,1)S(1)} collective-permute-done((bf16[320,896]{1,0:T(8,128)(2,1)S(1)}, bf16[320,896]{1,0:T(8,128)(2,1)S(1)}, u32[]{:S(2)}, u32[]{:S(2)}) %collective-permute-start.25) | collective-permute-done | bytes 573472 | tf_op jit(solution)/shard_map/ppermute | solution.py:12
  119.2 0.9 fusion.4
  120.1 32.2 %all-gather.3.cloned.1.call-done = bf16[1024,512]{1,0:T(8,128)(2,1)} async-done(((bf16[128,512]{1,0:T(8,128)(2,1)}), bf16[1024,512]{1,0:T(8,128)(2,1)}) %all-gather.3.cloned.1.call-update) | async-done | bytes 1048592 | tf_op jit(solution)/shard_map/all_gather | solution.py:495
  152.3 1.5 fusion.1
  153.8 7.1 %all_gather.11 = bf16[128,2048]{1,0:T(8,128)(2,1)S(1)} all-gather(bf16[128,512]{1,0:T(8,128)(2,1)S(1)} %fusion.1), channel_id=1, replica_groups=mesh['expert'=8,'tensor'=4] {'tensor'}, dimensions={1}, use_global_device_ids=true | all-gather | bytes 655360 | tf_op jit(solution)/shard_map/all_gather | solution.py:502
  160.9 2.7 %convolution_multiply_fusion = f32[512,2048]{1,0:T(8,128)} fusion(bf16[128,2048]{1,0:T(8,128)(2,1)S(1)} %all_gather.11, bf16[448,512]{1,0:T(8,128)(2,1)S(1)} %ffn.1.rows_ref), kind=kOutput, calls=%fused_computation.12 | convolution fusion | flops 269484032 | bytes 4849664 | tf_op jit(solution)/shard_map/dot_general | solution.py:503
  163.7 1.9 sums.3
  165.7 1.0 collective-permute-start.30
  166.7 1.2 collective-permute-start.32
  167.9 6.4 %collective-permute-done.30 = bf16[2,128,512]{2,1,0:T(8,128)(2,1)S(1)} collective-permute-done((bf16[2,128,512]{2,1,0:T(8,128)(2,1)S(1)}, bf16[2,128,512]{2,1,0:T(8,128)(2,1)S(1)}, u32[]{:S(2)}, u32[]{:S(2)}) %collective-permute-start.30) | collective-permute-done | bytes 262176 | tf_op jit(solution)/shard_map/ppermute | solution.py:12
  174.5 4.2 %all-to-all-start.1 = ((bf16[8,40,896]{2,1,0:T(8,128)(2,1)}), bf16[8,40,896]{2,1,0:T(8,128)(2,1)}, u32[]{:S(2)}, u32[]{:S(2)}) async-start(bf16[8,40,896]{2,1,0:T(8,128)(2,1)} %bitcast.34), calls=%async_computation.1 | async-start | bytes 1146880 | tf_op jit(solution)/shard_map/all_to_all | solution.py:528
  178.7 15.1 %collective-permute-done.32.other_ref = bf16[512,384]{1,0:T(8,128)(2,1)S(1)} collective-permute-done((bf16[512,384]{1,0:T(8,128)(2,1)S(1)}, bf16[512,384]{1,0:T(8,128)(2,1)S(1)}, u32[]{:S(2)}, u32[]{:S(2)}) %collective-permute-start.32) | collective-permute-done | bytes 393248 | tf_op jit(solution)/shard_map/ppermute | solution.py:12
  193.9 1.3 collective-permute-start.36
  195.2 4.5 %collective-permute-done.36 = bf16[2,128,384]{2,1,0:T(8,128)(2,1)S(1)} collective-permute-done((bf16[2,128,384]{2,1,0:T(8,128)(2,1)S(1)}, bf16[2,128,384]{2,1,0:T(8,128)(2,1)S(1)}, u32[]{:S(2)}, u32[]{:S(2)}) %collective-permute-start.36) | collective-permute-done | bytes 196640 | tf_op jit(solution)/shard_map/ppermute | solution.py:12
  200.1 2.3 collective-permute-start.34
  202.4 1.0 collective-permute-start.33
  204.0 2.0 collective-permute-start.39
  206.1 9.5 %collective-permute-done.35.refs_3_ = bf16[4,128,512]{2,1,0:T(8,128)(2,1)S(1)} collective-permute-done((bf16[4,128,512]{2,1,0:T(8,128)(2,1)S(1)}, bf16[4,128,512]{2,1,0:T(8,128)(2,1)S(1)}, u32[]{:S(2)}, u32[]{:S(2)}) %collective-permute-start.35) | collective-permute-done | bytes 524320 | tf_op jit(solution)/shard_map/ppermute | solution.py:12
  215.6 1.0 collective-permute-start.38
  217.9 2.3 fusion.2
  220.2 6.2 %collective-permute-done.34.refs_2_ = bf16[4,128,512]{2,1,0:T(8,128)(2,1)S(1)} collective-permute-done((bf16[4,128,512]{2,1,0:T(8,128)(2,1)S(1)}, bf16[4,128,512]{2,1,0:T(8,128)(2,1)S(1)}, u32[]{:S(2)}, u32[]{:S(2)}) %collective-permute-start.34) | collective-permute-done | bytes 524320 | tf_op jit(solution)/shard_map/ppermute | solution.py:12
  226.9 8.4 %collective-permute-done.40.refs_7_ = bf16[4,128,384]{2,1,0:T(8,128)(2,1)S(1)} collective-permute-done((bf16[4,128,384]{2,1,0:T(8,128)(2,1)S(1)}, bf16[4,128,384]{2,1,0:T(8,128)(2,1)S(1)}, u32[]{:S(2)}, u32[]{:S(2)}) %collective-permute-start.40) | collective-permute-done | bytes 393248 | tf_op jit(solution)/shard_map/ppermute | solution.py:12
  235.3 7.6 %collective-permute-done.39.refs_6_ = bf16[4,128,384]{2,1,0:T(8,128)(2,1)S(1)} collective-permute-done((bf16[4,128,384]{2,1,0:T(8,128)(2,1)S(1)}, bf16[4,128,384]{2,1,0:T(8,128)(2,1)S(1)}, u32[]{:S(2)}, u32[]{:S(2)}) %collective-permute-start.39) | collective-permute-done | bytes 393248 | tf_op jit(solution)/shard_map/ppermute | solution.py:12
  243.3 3.1 %assemble.3 = bf16[512,3584]{1,0:T(8,128)(2,1)} custom-call(s32[9]{0:T(128)S(1)} %concatenate.55.flags_ref, bf16[4,128,512]{2,1,0:T(8,128)(2,1)S(1)} %pad_maximum_fusion.10.refs_0_, bf16[4,128,512]{2,1,0:T(8,128)(2,1)S(1)} %collective-permute-done.33.refs_1_, bf16[4,128,512]{2,1,0:T(8,128)(2,1)S(1)} %collective-permute-done.34.refs_2_, ...), custom_call_target="tpu_custom_call" | custom-call | flops 1024 | bytes 1024 | tf_op jit(solution)/shard_map/assemble/pallas_call | solution.py:326
  246.5 0.9 copy-done.1
  (110 shorter events, 6.3 us)
Async XLA Ops:
  7.2 7.4 %copy-start = (bf16[128,896]{1,0:T(8,128)(2,1)S(1)}, bf16[128,896]{1,0:T(8,128)(2,1)}, u32[]{:S(2)}) copy-start(bf16[128,896]{1,0:T(8,128)(2,1)} %param.12) | copy-start | bytes 688132
  7.2 6.6 %copy-start.27 = (s32[128,2]{0,1:T(2,128)S(1)}, s32[128,2]{0,1:T(2,128)}, u32[]{:S(2)}) copy-start(s32[128,2]{0,1:T(2,128)} %param.13) | copy-start | bytes 3076
  9.8 11.8 %copy-start.28 = (s32[1,512]{1,0:T(1,128)S(1)}, s32[1,512]{1,0:T(1,128)}, u32[]{:S(2)}) copy-start(s32[1,512]{1,0:T(1,128)} %param.19) | copy-start | bytes 6148
  9.8 12.4 %copy-start.12 = (s32[8]{0:T(128)S(1)}, s32[8]{0:T(128)}, u32[]{:S(2)}) copy-start(s32[8]{0:T(128)} %param.20) | copy-start | bytes 100
  9.8 15.2 %copy-start.26 = (s32[2]{0:T(128)S(1)}, s32[2]{0:T(128)}, u32[]{:S(2)}) copy-start(s32[2]{0:T(128)} %param.21) | copy-start | bytes 28
  10.9 26.4 %collective-permute-start.12 = (bf16[2,512,512]{2,1,0:T(8,128)(2,1)}, bf16[2,512,512]{2,1,0:T(8,128)(2,1)S(1)}, u32[]{:S(2)}, u32[]{:S(2)}) collective-permute-start(bf16[2,512,512]{2,1,0:T(8,128)(2,1)} %pad_maximum_fusion.5), channel_id=1, source_target_pairs={{0,2},{1,3},{2,0},{3,1},{4,6},{5,7},{6,4},{7,5},{8,10},{9,11},{10,... | collective-permute-start | bytes 3145736 | tf_op jit(solution)/shard_map/ppermute | solution.py:12
  15.7 24.9 %copy-start.25 = (bf16[128,896]{1,0:T(8,128)(2,1)S(1)}, bf16[128,896]{1,0:T(8,128)(2,1)}, u32[]{:S(2)}) copy-start(bf16[128,896]{1,0:T(8,128)(2,1)} %param.15) | copy-start | bytes 688132
  15.7 24.9 %all-to-all-start = ((bf16[8,40,896]{2,1,0:T(8,128)(2,1)}), bf16[8,40,896]{2,1,0:T(8,128)(2,1)S(1)}, u32[]{:S(2)}, u32[]{:S(2)}) async-start(bf16[8,40,896]{2,1,0:T(8,128)(2,1)} %bitcast.18), calls=%async_computation | async-start | bytes 1146880 | tf_op jit(solution)/shard_map/all_to_all | solution.py:482
  21.6 130.7 %all-gather.3.cloned.1.call-start = ((), (), s32[]{:S(2)}) async-start(), calls=%async_computation.2 | async-start | bytes 1179648 | tf_op jit(solution)/shard_map/all_gather | solution.py:495
  21.7 18.4 %collective-permute-start.15 = (s32[512]{0:T(512)S(1)}, s32[512]{0:T(512)S(1)}, u32[]{:S(2)}, u32[]{:S(2)}) collective-permute-start(s32[512]{0:T(512)S(1)} %bitcast.82), channel_id=1, source_target_pairs={{0,2},{1,3},{2,0},{3,1},{4,6},{5,7},{6,4},{7,5},{8,10},{9,11},{10,... | collective-permute-start | bytes 6152 | tf_op jit(solution)/shard_map/ppermute | solution.py:12
  22.2 23.5 %collective-permute-start.14 = (s32[512]{0:T(512)S(1)}, s32[512]{0:T(512)S(1)}, u32[]{:S(2)}, u32[]{:S(2)}) collective-permute-start(s32[512]{0:T(512)S(1)} %bitcast.83), channel_id=1, source_target_pairs={{0,1},{1,0},{2,3},{3,2},{4,5},{5,4},{6,7},{7,6},{8,9},{9,8},{10,11... | collective-permute-start | bytes 6152 | tf_op jit(solution)/shard_map/ppermute | solution.py:12
  39.4 9.9 %collective-permute-start.17 = (bf16[2,512,512]{2,1,0:T(8,128)(2,1)}, bf16[2,512,512]{2,1,0:T(8,128)(2,1)}, u32[]{:S(2)}, u32[]{:S(2)}) collective-permute-start(bf16[2,512,512]{2,1,0:T(8,128)(2,1)} %pad_maximum_fusion.6), channel_id=1, source_target_pairs={{0,1},{1,0},{2,3},{3,2},{4,5},{5,4},{6,7},{7,6},{8,9},{9,8},{10,11... | collective-permute-start | bytes 3145736 | tf_op jit(solution)/shard_map/ppermute | solution.py:12
  40.0 5.7 %collective-permute-start.16 = (s32[512]{0:T(512)S(1)}, s32[512]{0:T(512)S(1)}, u32[]{:S(2)}, u32[]{:S(2)}) collective-permute-start(s32[512]{0:T(512)S(1)} %collective-permute-done.15), channel_id=1, source_target_pairs={{0,1},{1,0},{2,3},{3,2},{4,5},{5,4},{6,7},{7,6},{8,9},{9,8},{10,11... | collective-permute-start | bytes 6152 | tf_op jit(solution)/shard_map/ppermute | solution.py:12
  40.6 20.0 %collective-permute-start.13 = (bf16[1,448,896]{2,1,0:T(8,128)(2,1)S(1)}, bf16[1,448,896]{2,1,0:T(8,128)(2,1)}, u32[]{:S(2)}, u32[]{:S(2)}) collective-permute-start(bf16[1,448,896]{2,1,0:T(8,128)(2,1)S(1)} %bitcast.76), channel_id=1, source_target_pairs={{0,2},{1,3},{2,0},{3,1},{4,6},{5,7},{6,4},{7,5},{8,10},{9,11},{10,... | collective-permute-start | bytes 2408456 | tf_op jit(solution)/shard_map/ppermute | solution.py:12
  55.1 0.8 copy-start.6
  56.0 0.8 copy-start.8
  56.7 0.8 copy-start.10
  61.9 7.2 %collective-permute-start.18 = (bf16[2,448,896]{2,1,0:T(8,128)(2,1)S(1)}, bf16[2,448,896]{2,1,0:T(8,128)(2,1)}, u32[]{:S(2)}, u32[]{:S(2)}) collective-permute-start(bf16[2,448,896]{2,1,0:T(8,128)(2,1)S(1)} %pad_maximum_fusion.4.even_ref), channel_id=1, source_target_pairs={{0,1},{1,0},{2,3},{3,2},{4,5},{5,4},{6,7},{7,6},{8,9},{9,8},{10,11... | collective-permute-start | bytes 4816904 | tf_op jit(solution)/shard_map/ppermute | solution.py:12
  62.0 3.6 %copy-start.11 = (bf16[512,512]{1,0:T(8,128)(2,1)S(1)}, bf16[512,512]{1,0:T(8,128)(2,1)}, u32[]{:S(2)}) copy-start(bf16[512,512]{1,0:T(8,128)(2,1)} %copy-done.10) | copy-start | bytes 1572868
  62.0 5.1 %copy-start.9 = (bf16[512,512]{1,0:T(8,128)(2,1)S(1)}, bf16[512,512]{1,0:T(8,128)(2,1)}, u32[]{:S(2)}) copy-start(bf16[512,512]{1,0:T(8,128)(2,1)} %copy-done.8) | copy-start | bytes 1572868
  62.0 6.6 %copy-start.7 = (bf16[512,512]{1,0:T(8,128)(2,1)S(1)}, bf16[512,512]{1,0:T(8,128)(2,1)}, u32[]{:S(2)}) copy-start(bf16[512,512]{1,0:T(8,128)(2,1)} %copy-done.6) | copy-start | bytes 1572868
  63.8 28.2 %collective-permute-start.19 = (bf16[2,512,384]{2,1,0:T(8,128)(2,1)S(1)}, bf16[2,512,384]{2,1,0:T(8,128)(2,1)S(1)}, u32[]{:S(2)}, u32[]{:S(2)}) collective-permute-start(bf16[2,512,384]{2,1,0:T(8,128)(2,1)S(1)} %pad_maximum_fusion.8), channel_id=1, source_target_pairs={{0,2},{1,3},{2,0},{3,1},{4,6},{5,7},{6,4},{7,5},{8,10},{9,11},{10,... | collective-permute-start | bytes 2359304 | tf_op jit(solution)/shard_map/ppermute | solution.py:12
  65.6 16.7 %collective-permute-start.20 = (bf16[512,512]{1,0:T(8,128)(2,1)S(1)}, bf16[512,512]{1,0:T(8,128)(2,1)S(1)}, u32[]{:S(2)}, u32[]{:S(2)}) collective-permute-start(bf16[512,512]{1,0:T(8,128)(2,1)S(1)} %copy-done.11), channel_id=1, source_target_pairs={{0,4},{4,0},{8,12},{12,8},{16,20},{20,16},{24,28},{28,24},{1,5},{5... | collective-permute-start | bytes 1572872 | tf_op jit(solution)/shard_map/ppermute | solution.py:12
  67.1 15.2 %collective-permute-start.21 = (bf16[512,512]{1,0:T(8,128)(2,1)S(1)}, bf16[512,512]{1,0:T(8,128)(2,1)S(1)}, u32[]{:S(2)}, u32[]{:S(2)}) collective-permute-start(bf16[512,512]{1,0:T(8,128)(2,1)S(1)} %copy-done.9), channel_id=1, source_target_pairs={{0,8},{4,12},{8,0},{12,4},{16,24},{20,28},{24,16},{28,20},{1,9},{5... | collective-permute-start | bytes 1572872 | tf_op jit(solution)/shard_map/ppermute | solution.py:12
  68.7 23.3 %collective-permute-start.22 = (bf16[512,512]{1,0:T(8,128)(2,1)S(1)}, bf16[512,512]{1,0:T(8,128)(2,1)S(1)}, u32[]{:S(2)}, u32[]{:S(2)}) collective-permute-start(bf16[512,512]{1,0:T(8,128)(2,1)S(1)} %copy-done.7), channel_id=1, source_target_pairs={{0,12},{4,8},{8,4},{12,0},{16,28},{20,24},{24,20},{28,16},{1,13},{... | collective-permute-start | bytes 1572872 | tf_op jit(solution)/shard_map/ppermute | solution.py:12
  81.3 1.0 copy-start.4
  82.3 20.1 %collective-permute-start.24 = (bf16[2,320,896]{2,1,0:T(8,128)(2,1)}, bf16[2,320,896]{2,1,0:T(8,128)(2,1)}, u32[]{:S(2)}, u32[]{:S(2)}) collective-permute-start(bf16[2,320,896]{2,1,0:T(8,128)(2,1)} %get-tuple-element.118), channel_id=1, source_target_pairs={{0,1},{1,0},{2,3},{3,2},{4,5},{5,4},{6,7},{7,6},{8,9},{9,8},{10,11... | collective-permute-start | bytes 3440648 | tf_op jit(solution)/shard_map/ppermute | solution.py:12
  82.3 10.7 %copy-start.15 = (bf16[512,512]{1,0:T(8,128)(2,1)}, bf16[512,512]{1,0:T(8,128)(2,1)S(1)}, u32[]{:S(2)}) copy-start(bf16[512,512]{1,0:T(8,128)(2,1)S(1)} %collective-permute-done.20.refs_1_) | copy-start | bytes 1572868
  82.3 11.7 %copy-start.18 = (bf16[512,512]{1,0:T(8,128)(2,1)}, bf16[512,512]{1,0:T(8,128)(2,1)S(1)}, u32[]{:S(2)}) copy-start(bf16[512,512]{1,0:T(8,128)(2,1)S(1)} %collective-permute-done.21.refs_2_) | copy-start | bytes 1572868
  92.0 2.0 copy-start.21
  92.1 0.9 copy-start.2
  93.0 3.5 %copy-start.3 = (bf16[2,512,384]{2,1,0:T(8,128)(2,1)S(1)}, bf16[2,512,384]{2,1,0:T(8,128)(2,1)}, u32[]{:S(2)}) copy-start(bf16[2,512,384]{2,1,0:T(8,128)(2,1)} %copy-done.2) | copy-start | bytes 2359300
  94.0 2.5 collective-permute-start.23
  94.7 7.7 %copy-start.5 = (bf16[2,320,896]{2,1,0:T(8,128)(2,1)S(1)}, bf16[2,320,896]{2,1,0:T(8,128)(2,1)}, u32[]{:S(2)}) copy-start(bf16[2,320,896]{2,1,0:T(8,128)(2,1)} %copy-done.4) | copy-start | bytes 3440644
  102.4 4.8 %copy-start.13 = (bf16[512,512]{1,0:T(8,128)(2,1)S(1)}, bf16[512,512]{1,0:T(8,128)(2,1)}, u32[]{:S(2)}) copy-start(bf16[512,512]{1,0:T(8,128)(2,1)} %get-tuple-element.125.refs_0_) | copy-start | bytes 1572868
  102.4 4.9 %copy-start.16 = (bf16[512,512]{1,0:T(8,128)(2,1)S(1)}, bf16[512,512]{1,0:T(8,128)(2,1)}, u32[]{:S(2)}) copy-start(bf16[512,512]{1,0:T(8,128)(2,1)} %copy-done.15) | copy-start | bytes 1572868
  102.4 4.9 %copy-start.19 = (bf16[512,512]{1,0:T(8,128)(2,1)S(1)}, bf16[512,512]{1,0:T(8,128)(2,1)}, u32[]{:S(2)}) copy-start(bf16[512,512]{1,0:T(8,128)(2,1)} %copy-done.18) | copy-start | bytes 1572868
  102.4 4.9 %copy-start.22 = (bf16[512,512]{1,0:T(8,128)(2,1)S(1)}, bf16[512,512]{1,0:T(8,128)(2,1)}, u32[]{:S(2)}) copy-start(bf16[512,512]{1,0:T(8,128)(2,1)} %copy-done.21) | copy-start | bytes 1572868
  104.1 15.1 %collective-permute-start.25 = (bf16[320,896]{1,0:T(8,128)(2,1)S(1)}, bf16[320,896]{1,0:T(8,128)(2,1)S(1)}, u32[]{:S(2)}, u32[]{:S(2)}) collective-permute-start(bf16[320,896]{1,0:T(8,128)(2,1)S(1)} %fusion.12), channel_id=1, source_target_pairs={{0,2},{1,3},{2,0},{3,1},{4,6},{5,7},{6,4},{7,5},{8,10},{9,11},{10,... | collective-permute-start | bytes 1720328 | tf_op jit(solution)/shard_map/ppermute | solution.py:12
  108.6 55.0 %collective-permute-start.26 = (bf16[512,512]{1,0:T(8,128)(2,1)S(1)}, bf16[512,512]{1,0:T(8,128)(2,1)S(1)}, u32[]{:S(2)}, u32[]{:S(2)}) collective-permute-start(bf16[512,512]{1,0:T(8,128)(2,1)S(1)} %get-tuple-element.131), channel_id=1, source_target_pairs={{0,16},{4,20},{8,24},{12,28},{16,0},{20,4},{24,8},{28,12},{1,17},{... | collective-permute-start | bytes 1572872 | tf_op jit(solution)/shard_map/ppermute | solution.py:12
  111.4 52.2 %collective-permute-start.27 = (bf16[512,384]{1,0:T(8,128)(2,1)}, bf16[512,384]{1,0:T(8,128)(2,1)}, u32[]{:S(2)}, u32[]{:S(2)}) collective-permute-start(bf16[512,384]{1,0:T(8,128)(2,1)} %get-tuple-element.132), channel_id=1, source_target_pairs={{0,4},{4,0},{8,12},{12,8},{16,20},{20,16},{24,28},{28,24},{1,5},{5... | collective-permute-start | bytes 1179656 | tf_op jit(solution)/shard_map/ppermute | solution.py:12
  112.9 50.7 %collective-permute-start.28 = (bf16[512,384]{1,0:T(8,128)(2,1)}, bf16[512,384]{1,0:T(8,128)(2,1)}, u32[]{:S(2)}, u32[]{:S(2)}) collective-permute-start(bf16[512,384]{1,0:T(8,128)(2,1)} %get-tuple-element.133), channel_id=1, source_target_pairs={{0,8},{4,12},{8,0},{12,4},{16,24},{20,28},{24,16},{28,20},{1,9},{5... | collective-permute-start | bytes 1179656 | tf_op jit(solution)/shard_map/ppermute | solution.py:12
  114.5 49.1 %collective-permute-start.29 = (bf16[512,384]{1,0:T(8,128)(2,1)}, bf16[512,384]{1,0:T(8,128)(2,1)}, u32[]{:S(2)}, u32[]{:S(2)}) collective-permute-start(bf16[512,384]{1,0:T(8,128)(2,1)} %get-tuple-element.134), channel_id=1, source_target_pairs={{0,12},{4,8},{8,4},{12,0},{16,28},{20,24},{24,20},{28,16},{1,13},{... | collective-permute-start | bytes 1179656 | tf_op jit(solution)/shard_map/ppermute | solution.py:12
  160.9 2.8 %copy-start.24 = (bf16[512,384]{1,0:T(8,128)(2,1)S(1)}, bf16[512,384]{1,0:T(8,128)(2,1)}, u32[]{:S(2)}) copy-start(bf16[512,384]{1,0:T(8,128)(2,1)} %get-tuple-element.135.refs_0_) | copy-start | bytes 1179652
  165.7 8.6 %collective-permute-start.30 = (bf16[2,128,512]{2,1,0:T(8,128)(2,1)S(1)}, bf16[2,128,512]{2,1,0:T(8,128)(2,1)S(1)}, u32[]{:S(2)}, u32[]{:S(2)}) collective-permute-start(bf16[2,128,512]{2,1,0:T(8,128)(2,1)S(1)} %get-tuple-element.143), channel_id=1, source_target_pairs={{0,2},{1,3},{2,0},{3,1},{4,6},{5,7},{6,4},{7,5},{8,10},{9,11},{10,... | collective-permute-start | bytes 786440 | tf_op jit(solution)/shard_map/ppermute | solution.py:12
  166.7 27.1 %collective-permute-start.32 = (bf16[512,384]{1,0:T(8,128)(2,1)S(1)}, bf16[512,384]{1,0:T(8,128)(2,1)S(1)}, u32[]{:S(2)}, u32[]{:S(2)}) collective-permute-start(bf16[512,384]{1,0:T(8,128)(2,1)S(1)} %get-tuple-element.144), channel_id=1, source_target_pairs={{0,16},{4,20},{8,24},{12,28},{16,0},{20,4},{24,8},{28,12},{1,17},{... | collective-permute-start | bytes 1179656 | tf_op jit(solution)/shard_map/ppermute | solution.py:12
  174.4 20.8 %collective-permute-start.31 = (bf16[2,128,512]{2,1,0:T(8,128)(2,1)S(1)}, bf16[2,128,512]{2,1,0:T(8,128)(2,1)S(1)}, u32[]{:S(2)}, u32[]{:S(2)}) collective-permute-start(bf16[2,128,512]{2,1,0:T(8,128)(2,1)S(1)} %pad_maximum_fusion.12), channel_id=1, source_target_pairs={{0,1},{1,0},{2,3},{3,2},{4,5},{5,4},{6,7},{7,6},{8,9},{9,8},{10,11... | collective-permute-start | bytes 786440 | tf_op jit(solution)/shard_map/ppermute | solution.py:12
  174.5 43.4 %all-to-all-start.1 = ((bf16[8,40,896]{2,1,0:T(8,128)(2,1)}), bf16[8,40,896]{2,1,0:T(8,128)(2,1)}, u32[]{:S(2)}, u32[]{:S(2)}) async-start(bf16[8,40,896]{2,1,0:T(8,128)(2,1)} %bitcast.34), calls=%async_computation.1 | async-start | bytes 1146880 | tf_op jit(solution)/shard_map/all_to_all | solution.py:528
  178.7 39.2 %copy-start.29 = (f32[128,2]{0,1:T(2,128)S(1)}, f32[128,2]{0,1:T(2,128)}, u32[]{:S(2)}) copy-start(f32[128,2]{0,1:T(2,128)} %param.14) | copy-start | bytes 3076
  193.9 5.7 %collective-permute-start.36 = (bf16[2,128,384]{2,1,0:T(8,128)(2,1)S(1)}, bf16[2,128,384]{2,1,0:T(8,128)(2,1)S(1)}, u32[]{:S(2)}, u32[]{:S(2)}) collective-permute-start(bf16[2,128,384]{2,1,0:T(8,128)(2,1)S(1)} %get-tuple-element.148), channel_id=1, source_target_pairs={{0,2},{1,3},{2,0},{3,1},{4,6},{5,7},{6,4},{7,5},{8,10},{9,11},{10,... | collective-permute-start | bytes 589832 | tf_op jit(solution)/shard_map/ppermute | solution.py:12
  199.7 3.7 %collective-permute-start.37 = (bf16[2,128,384]{2,1,0:T(8,128)(2,1)S(1)}, bf16[2,128,384]{2,1,0:T(8,128)(2,1)S(1)}, u32[]{:S(2)}, u32[]{:S(2)}) collective-permute-start(bf16[2,128,384]{2,1,0:T(8,128)(2,1)S(1)} %pad_maximum_fusion.13), channel_id=1, source_target_pairs={{0,1},{1,0},{2,3},{3,2},{4,5},{5,4},{6,7},{7,6},{8,9},{9,8},{10,11... | collective-permute-start | bytes 589832 | tf_op jit(solution)/shard_map/ppermute | solution.py:12
  199.9 15.7 %collective-permute-start.35 = (bf16[4,128,512]{2,1,0:T(8,128)(2,1)S(1)}, bf16[4,128,512]{2,1,0:T(8,128)(2,1)S(1)}, u32[]{:S(2)}, u32[]{:S(2)}) collective-permute-start(bf16[4,128,512]{2,1,0:T(8,128)(2,1)S(1)} %pad_maximum_fusion.10.refs_0_), channel_id=1, source_target_pairs={{0,12},{4,8},{8,4},{12,0},{16,28},{20,24},{24,20},{28,16},{1,13},{... | collective-permute-start | bytes 1572872 | tf_op jit(solution)/shard_map/ppermute | solution.py:12
  200.1 26.3 %collective-permute-start.34 = (bf16[4,128,512]{2,1,0:T(8,128)(2,1)S(1)}, bf16[4,128,512]{2,1,0:T(8,128)(2,1)S(1)}, u32[]{:S(2)}, u32[]{:S(2)}) collective-permute-start(bf16[4,128,512]{2,1,0:T(8,128)(2,1)S(1)} %pad_maximum_fusion.10.refs_0_), channel_id=1, source_target_pairs={{0,8},{4,12},{8,0},{12,4},{16,24},{20,28},{24,16},{28,20},{1,9},{5... | collective-permute-start | bytes 1572872 | tf_op jit(solution)/shard_map/ppermute | solution.py:12
  202.4 24.5 %collective-permute-start.33 = (bf16[4,128,512]{2,1,0:T(8,128)(2,1)S(1)}, bf16[4,128,512]{2,1,0:T(8,128)(2,1)S(1)}, u32[]{:S(2)}, u32[]{:S(2)}) collective-permute-start(bf16[4,128,512]{2,1,0:T(8,128)(2,1)S(1)} %pad_maximum_fusion.10.refs_0_), channel_id=1, source_target_pairs={{0,4},{4,0},{8,12},{12,8},{16,20},{20,16},{24,28},{28,24},{1,5},{5... | collective-permute-start | bytes 1572872 | tf_op jit(solution)/shard_map/ppermute | solution.py:12
  203.5 31.8 %collective-permute-start.40 = (bf16[4,128,384]{2,1,0:T(8,128)(2,1)S(1)}, bf16[4,128,384]{2,1,0:T(8,128)(2,1)S(1)}, u32[]{:S(2)}, u32[]{:S(2)}) collective-permute-start(bf16[4,128,384]{2,1,0:T(8,128)(2,1)S(1)} %pad_maximum_fusion.11.refs_4_), channel_id=1, source_target_pairs={{0,12},{4,8},{8,4},{12,0},{16,28},{20,24},{24,20},{28,16},{1,13},{... | collective-permute-start | bytes 1179656 | tf_op jit(solution)/shard_map/ppermute | solution.py:12
  204.0 38.8 %collective-permute-start.39 = (bf16[4,128,384]{2,1,0:T(8,128)(2,1)S(1)}, bf16[4,128,384]{2,1,0:T(8,128)(2,1)S(1)}, u32[]{:S(2)}, u32[]{:S(2)}) collective-permute-start(bf16[4,128,384]{2,1,0:T(8,128)(2,1)S(1)} %pad_maximum_fusion.11.refs_4_), channel_id=1, source_target_pairs={{0,8},{4,12},{8,0},{12,4},{16,24},{20,28},{24,16},{28,20},{1,9},{5... | collective-permute-start | bytes 1179656 | tf_op jit(solution)/shard_map/ppermute | solution.py:12
  215.6 27.7 %collective-permute-start.38 = (bf16[4,128,384]{2,1,0:T(8,128)(2,1)S(1)}, bf16[4,128,384]{2,1,0:T(8,128)(2,1)}, u32[]{:S(2)}, u32[]{:S(2)}) collective-permute-start(bf16[4,128,384]{2,1,0:T(8,128)(2,1)S(1)} %pad_maximum_fusion.11.refs_4_), channel_id=1, source_target_pairs={{0,4},{4,0},{8,12},{12,8},{16,20},{20,16},{24,28},{28,24},{1,5},{5... | collective-permute-start | bytes 1179656 | tf_op jit(solution)/shard_map/ppermute | solution.py:12
  246.5 0.9 copy-start.1
Sparse Core Ops, SparseCore 0:
  94.8 57.4 all-gather.2

commit v8 on v7

--- a/solution.py
+++ b/solution.py
@@ -513,13 +513,12 @@
                 source = two.columns(c + 1, (even,), (*parts[c][1:], send))
                 mark, sent = two.send_aligned(source, mark)
                 parts.append(sent)
-            ready = all_after(parts[c], *((others[-1], returned, correlation) if c else (send,)))
+            ready = all_after(parts[c], *((others[-1], returned) if c else (send,)))
             given, own_sum = sums(two.flags, ready)
             others.append(xor_permute(given, "expert", ne, two.half))
             kept.append(own_sum)
             if not c:
                 returned = sum_tensor(send, after(keep, mark), nt)
-                correlation = correlate(after(partner, own_sum))
         lines = two.back(mean_of(two.scale, kept[0], after(others[0], kept[-1])))
         lines = after(lines, others[-1])
     else:
@@ -537,7 +536,8 @@
             means = mean_of(two.scale, kept[c], others[c])
             lines = two.back(means)
             gathered.append(two.out(lines))
-        gathered[-1][0] = after(gathered[-1][0], mixed)
+        correlation = correlate(after(partner, lines))
+        gathered[-1][0] = after(gathered[-1][0], mixed, correlation)
         merged = two.finish(gathered, parts)
     else:
         merged = merge_any(own, perm, cluster, owners, e, t, ne, nt)

time: 255 us -> 237 us (0.929)
  waiting for transfers between devices: 122 us -> 104 us
    all_gather x1, waiting for transfers between devices: 32.2 us -> 3.14 us  [on_device(): everyone = lax.all_gather(probe_hidden, 'expert', axis=0)]
    ppermute x29, waiting for transfers between devices: 89.8 us -> 101 us  [xor_permute(): return lax.ppermute(value, axis, [(i, i ^ k) for i in range(size)])]
    unnamed x53 -> x61, local copies, waits for them, and re-layouts: 5.47 us -> 5.49 us
  transfers between devices with their start and end apart: 32 -> 32, of which waited for: 15 -> 16; matrix products, arithmetic and copies ran while one was open for 9% -> 10% of each run, Pallas kernels for 10% -> 11%
where the time goes in v8:
time: 237 us; the launch traced here: 236 us
  waiting for transfers between devices  104 us (44%)
  starting transfers between devices  39.9 us (17%)
  Pallas kernels  29.4 us (12%)
  between operations  21.4 us (9%)
  local copies, waits for them, and re-layouts  14.8 us (6%)
  other arithmetic  13.2 us (6%)
  blocking collectives  6.99 us (3%)
  matrix products  6.16 us (3%)
    ppermute x29, waiting for transfers between devices, xor_permute(): return lax.ppermute(value, axis, [(i, i ^ k) for i in range(size)])  101 us
    ppermute x29, starting transfers between devices, xor_permute(): return lax.ppermute(value, axis, [(i, i ^ k) for i in range(size)])  29.3 us
    pallas_call x2, Pallas kernels, align(): pl.pallas_call(functools.partial(align_kernel, nt, half, sub), out_shape=...  10.9 us
    all_gather x1, blocking collectives, correlate(): partner_full = lax.all_gather(partner, 'tensor', axis=1, tiled=True)  6.99 us
    pallas_call x1, Pallas kernels, ffn(): pl.pallas_call(functools.partial(ffn_kernel, order), out_shape=jax.ShapeD...  6.96 us
    all_to_all x1, starting transfers between devices, on_device(): lax.all_to_all(outgoing, 'expert', split_axis=0, concat_axis=0, tiled=True)  5.93 us
    unnamed x61, local copies, waits for them, and re-layouts  5.49 us
    pallas_call x1, Pallas kernels, down(): pl.pallas_call(functools.partial(down_kernel, count), out_shape=[shape, s...  5.19 us
  transfers between devices with their start and end apart: 32, of which 16 were waited for; matrix products, arithmetic and copies ran while one was open for 10% of the time, Pallas kernels for 11%

profile of v8, /device:TPU:0, one launch (start us, length us, event | category | flops | bytes accessed | tf_op | source)
XLA Modules:
  0.0 236.0 jit_solution(3612682105035408940)
XLA Ops:
  7.2 2.6 %constant_dynamic-slice_fusion.3 = (bf16[1,512,512]{2,1,0:T(8,128)(2,1)}, bf16[512,512]{1,0:T(8,128)(2,1)S(1)}, bf16[1,512,512]{2,1,0:T(8,128)(2,1)S(1)}, bf16[1,512,512]{2,1,0:T(8,128)(2,1)S(1)}) fusion(bf16[1,512,3584]{2,1,0:T(8,128)(2,1)} %param.18, s32[]{:T(128)S(6)} %select_n.176, s32[]{:T(128)S(6)} %select_n.175, s32[]{:T(128)S(6)} %select_n.164, ...), kind=kLoop, calls=%fused_computation.66 | loop fusion | bytes 4194320 | tf_op jit(solution)/shard_map/dynamic_slice | solution.py:186
  9.8 1.1 pad_maximum_fusion.5
  10.9 3.0 %collective-permute-start.12 = (bf16[2,512,512]{2,1,0:T(8,128)(2,1)}, bf16[2,512,512]{2,1,0:T(8,128)(2,1)S(1)}, u32[]{:S(2)}, u32[]{:S(2)}) collective-permute-start(bf16[2,512,512]{2,1,0:T(8,128)(2,1)} %pad_maximum_fusion.5), channel_id=1, source_target_pairs={{0,2},{1,3},{2,0},{3,1},{4,6},{5,7},{6,4},{7,5},{8,10},{9,11},{10,... | collective-permute-start | bytes 3145736 | tf_op jit(solution)/shard_map/ppermute | solution.py:12
  14.5 1.1 convolution_convert_fusion
  15.7 5.9 %all-to-all-start = ((bf16[8,40,896]{2,1,0:T(8,128)(2,1)}), bf16[8,40,896]{2,1,0:T(8,128)(2,1)S(1)}, u32[]{:S(2)}, u32[]{:S(2)}) async-start(bf16[8,40,896]{2,1,0:T(8,128)(2,1)} %bitcast.18), calls=%async_computation | async-start | bytes 1146880 | tf_op jit(solution)/shard_map/all_to_all | solution.py:482
  22.3 0.6 dynamic_slice.44
  25.0 12.3 %collective-permute-done.12.refs_1_ = bf16[2,512,512]{2,1,0:T(8,128)(2,1)S(1)} collective-permute-done((bf16[2,512,512]{2,1,0:T(8,128)(2,1)}, bf16[2,512,512]{2,1,0:T(8,128)(2,1)S(1)}, u32[]{:S(2)}, u32[]{:S(2)}) %collective-permute-start.12) | collective-permute-done | bytes 1048608 | tf_op jit(solution)/shard_map/ppermute | solution.py:12
  37.3 2.1 pad_maximum_fusion.6
  39.4 0.7 fusion.36
  40.6 1.8 collective-permute-start.13
  45.6 1.3 copy.47
  46.9 2.2 fusion.7.place_ref
  49.1 5.8 %align.2 = (bf16[512,512]{1,0:T(8,128)(2,1)}, bf16[512,512]{1,0:T(8,128)(2,1)S(1)}, bf16[512,512]{1,0:T(8,128)(2,1)S(1)}, bf16[512,512]{1,0:T(8,128)(2,1)S(1)}) custom-call(s32[9]{0:T(128)S(1)} %concatenate.55.flags_ref, s32[2048,1]{1,0:T(8,128)S(1)} %fusion.7.place_ref, bf16[512,512]{1,0:T(8,128)(2,1)S(1)} %get-tuple-element.108.refs_0_, ...), custom_call_target="tpu_custom_call" | custom-call | flops 1024 | bytes 1024 | tf_op jit(solution)/shard_map/align/pallas_call | solution.py:228
  55.0 0.8 copy-done.6
  55.8 0.8 copy-done.8
  56.6 0.8 copy-done.10
  57.4 3.3 %collective-permute-done.13 = bf16[1,448,896]{2,1,0:T(8,128)(2,1)} collective-permute-done((bf16[1,448,896]{2,1,0:T(8,128)(2,1)S(1)}, bf16[1,448,896]{2,1,0:T(8,128)(2,1)}, u32[]{:S(2)}, u32[]{:S(2)}) %collective-permute-start.13) | collective-permute-done | bytes 802848 | tf_op jit(solution)/shard_map/ppermute | solution.py:12
  60.6 1.3 pad_maximum_fusion.4.even_ref
  62.1 1.6 constant_dynamic-slice_fusion
  63.8 1.8 collective-permute-start.19
  65.6 1.5 collective-permute-start.20
  67.1 1.6 collective-permute-start.21
  69.1 7.0 %ffn.1.rows_ref = bf16[448,512]{1,0:T(8,128)(2,1)S(1)} custom-call(s32[1]{0:T(128)} %bitcast.15.where_ref, bf16[2,448,896]{2,1,0:T(8,128)(2,1)S(1)} %pad_maximum_fusion.4.even_ref, bf16[2,448,896]{2,1,0:T(8,128)(2,1)} %collective-permute-done.18.odd_ref, bf16[1,3584,512]{2,1,0:T(8,128)(2,1)} %gate_ref.1, bf16[1,3584,512]{2,1,0:T(8,128)(2,1)} %up_ref.1), custom_call_target="tpu_custom_call" | custom-call | flops 1024 | bytes 1024 | tf_op jit(solution)/shard_map/ffn/pallas_call | solution.py:132
  76.1 5.2 %down.1 = (bf16[2,320,896]{2,1,0:T(8,128)(2,1)}, bf16[2,320,896]{2,1,0:T(8,128)(2,1)S(1)}) custom-call(s32[1]{0:T(128)} %bitcast.15.where_ref, bf16[448,512]{1,0:T(8,128)(2,1)S(1)} %ffn.1.rows_ref, bf16[512,3584]{1,0:T(8,128)(2,1)} %bitcast.74), custom_call_target="tpu_custom_call" | custom-call | flops 1024 | bytes 1024 | tf_op jit(solution)/shard_map/down/pallas_call | solution.py:58
  81.3 1.0 copy-done.4
  82.3 9.7 %collective-permute-done.22.refs_3_ = bf16[512,512]{1,0:T(8,128)(2,1)S(1)} collective-permute-done((bf16[512,512]{1,0:T(8,128)(2,1)S(1)}, bf16[512,512]{1,0:T(8,128)(2,1)S(1)}, u32[]{:S(2)}, u32[]{:S(2)}) %collective-permute-start.22) | collective-permute-done | bytes 524320 | tf_op jit(solution)/shard_map/ppermute | solution.py:12
  92.1 0.9 copy-done.2
  93.0 1.0 pad_maximum_fusion.9
  94.0 0.7 slice.152
  94.7 1.8 collective-permute-done.23.refs_2_
  96.5 5.1 %align.3 = (bf16[512,384]{1,0:T(8,128)(2,1)S(1)}, bf16[512,384]{1,0:T(8,128)(2,1)S(1)}, bf16[512,384]{1,0:T(8,128)(2,1)S(1)}, bf16[512,384]{1,0:T(8,128)(2,1)S(1)}) custom-call(s32[9]{0:T(128)S(1)} %concatenate.55.flags_ref, s32[2048,1]{1,0:T(8,128)S(1)} %fusion.7.place_ref, bf16[512,384]{1,0:T(8,128)(2,1)S(1)} %get-tuple-element.120.refs_0_, ...), custom_call_target="tpu_custom_call" | custom-call | flops 1024 | bytes 1024 | tf_op jit(solution)/shard_map/align/pallas_call | solution.py:228
  101.7 1.7 convert_add_fusion
  103.9 1.4 sums.2
  105.3 2.8 %collective-permute-start.29 = (bf16[512,512]{1,0:T(8,128)(2,1)S(1)}, bf16[512,512]{1,0:T(8,128)(2,1)S(1)}, u32[]{:S(2)}, u32[]{:S(2)}) collective-permute-start(bf16[512,512]{1,0:T(8,128)(2,1)S(1)} %get-tuple-element.132), channel_id=1, source_target_pairs={{0,16},{4,20},{8,24},{12,28},{16,0},{20,4},{24,8},{28,12},{1,17},{... | collective-permute-start | bytes 1572872 | tf_op jit(solution)/shard_map/ppermute | solution.py:12
  109.2 1.6 collective-permute-start.26
  110.8 1.6 collective-permute-start.27
  112.9 5.7 %collective-permute-done.25 = bf16[320,896]{1,0:T(8,128)(2,1)S(1)} collective-permute-done((bf16[320,896]{1,0:T(8,128)(2,1)S(1)}, bf16[320,896]{1,0:T(8,128)(2,1)S(1)}, u32[]{:S(2)}, u32[]{:S(2)}) %collective-permute-start.25) | collective-permute-done | bytes 573472 | tf_op jit(solution)/shard_map/ppermute | solution.py:12
  118.5 0.9 fusion.4
  119.5 14.8 %collective-permute-done.29.other_ref = bf16[512,512]{1,0:T(8,128)(2,1)S(1)} collective-permute-done((bf16[512,512]{1,0:T(8,128)(2,1)S(1)}, bf16[512,512]{1,0:T(8,128)(2,1)S(1)}, u32[]{:S(2)}, u32[]{:S(2)}) %collective-permute-start.29) | collective-permute-done | bytes 524320 | tf_op jit(solution)/shard_map/ppermute | solution.py:12
  134.3 12.6 %collective-permute-done.28.refs_3_ = bf16[512,384]{1,0:T(8,128)(2,1)S(1)} collective-permute-done((bf16[512,384]{1,0:T(8,128)(2,1)S(1)}, bf16[512,384]{1,0:T(8,128)(2,1)S(1)}, u32[]{:S(2)}, u32[]{:S(2)}) %collective-permute-start.28) | collective-permute-done | bytes 393248 | tf_op jit(solution)/shard_map/ppermute | solution.py:12
  146.9 1.2 sums.3
  148.6 0.6 fusion.35
  150.7 1.5 collective-permute-start.33
  152.2 0.6 iota_compare_fusion.6
  152.8 4.6 %all-to-all-start.1 = ((bf16[8,40,896]{2,1,0:T(8,128)(2,1)}), bf16[8,40,896]{2,1,0:T(8,128)(2,1)}, u32[]{:S(2)}, u32[]{:S(2)}) async-start(bf16[8,40,896]{2,1,0:T(8,128)(2,1)} %bitcast.78), calls=%async_computation.1 | async-start | bytes 1146880 | tf_op jit(solution)/shard_map/all_to_all | solution.py:527
  157.5 3.1 %all-gather.3.cloned.1.call-done = bf16[1024,512]{1,0:T(8,128)(2,1)} async-done(((bf16[128,512]{1,0:T(8,128)(2,1)}), bf16[1024,512]{1,0:T(8,128)(2,1)}) %all-gather.3.cloned.1.call-update) | async-done | bytes 1048592 | tf_op jit(solution)/shard_map/all_gather | solution.py:495
  160.6 1.5 fusion.1
  162.1 12.5 %collective-permute-done.30.other_ref = bf16[512,384]{1,0:T(8,128)(2,1)S(1)} collective-permute-done((bf16[512,384]{1,0:T(8,128)(2,1)S(1)}, bf16[512,384]{1,0:T(8,128)(2,1)S(1)}, u32[]{:S(2)}, u32[]{:S(2)}) %collective-permute-start.30) | collective-permute-done | bytes 393248 | tf_op jit(solution)/shard_map/ppermute | solution.py:12
  174.7 1.6 collective-permute-start.31
  176.4 4.6 %collective-permute-done.31 = bf16[2,128,384]{2,1,0:T(8,128)(2,1)S(1)} collective-permute-done((bf16[2,128,384]{2,1,0:T(8,128)(2,1)S(1)}, bf16[2,128,384]{2,1,0:T(8,128)(2,1)S(1)}, u32[]{:S(2)}, u32[]{:S(2)}) %collective-permute-start.31) | collective-permute-done | bytes 196640 | tf_op jit(solution)/shard_map/ppermute | solution.py:12
  181.3 2.7 %collective-permute-start.36 = (bf16[4,128,512]{2,1,0:T(8,128)(2,1)S(1)}, bf16[4,128,512]{2,1,0:T(8,128)(2,1)S(1)}, u32[]{:S(2)}, u32[]{:S(2)}) collective-permute-start(bf16[4,128,512]{2,1,0:T(8,128)(2,1)S(1)} %pad_maximum_fusion.10.refs_0_), channel_id=1, source_target_pairs={{0,8},{4,12},{8,0},{12,4},{16,24},{20,28},{24,16},{28,20},{1,9},{5... | collective-permute-start | bytes 1572872 | tf_op jit(solution)/shard_map/ppermute | solution.py:12
  184.1 0.8 collective-permute-start.35
  184.9 0.8 collective-permute-start.40
  185.7 2.0 collective-permute-start.39
  187.7 7.0 %all_gather.11 = bf16[128,2048]{1,0:T(8,128)(2,1)S(1)} all-gather(bf16[128,512]{1,0:T(8,128)(2,1)S(1)} %fusion.1), channel_id=1, replica_groups=mesh['expert'=8,'tensor'=4] {'tensor'}, dimensions={1}, use_global_device_ids=true | all-gather | bytes 655360 | tf_op jit(solution)/shard_map/all_gather | solution.py:502
  194.7 2.3 collective-permute-done.37.refs_3_
  197.0 1.3 collective-permute-start.38
  198.3 2.7 %convolution_multiply_fusion = f32[512,2048]{1,0:T(8,128)} fusion(bf16[128,2048]{1,0:T(8,128)(2,1)S(1)} %all_gather.11, bf16[448,512]{1,0:T(8,128)(2,1)S(1)} %ffn.1.rows_ref), kind=kOutput, calls=%fused_computation.12 | convolution fusion | flops 269484032 | bytes 4849664 | tf_op jit(solution)/shard_map/dot_general | solution.py:503
  201.0 2.3 fusion.2
  203.3 4.7 %collective-permute-done.36.refs_2_ = bf16[4,128,512]{2,1,0:T(8,128)(2,1)S(1)} collective-permute-done((bf16[4,128,512]{2,1,0:T(8,128)(2,1)S(1)}, bf16[4,128,512]{2,1,0:T(8,128)(2,1)S(1)}, u32[]{:S(2)}, u32[]{:S(2)}) %collective-permute-start.36) | collective-permute-done | bytes 524320 | tf_op jit(solution)/shard_map/ppermute | solution.py:12
  208.3 8.4 %collective-permute-done.40.refs_7_ = bf16[4,128,384]{2,1,0:T(8,128)(2,1)S(1)} collective-permute-done((bf16[4,128,384]{2,1,0:T(8,128)(2,1)S(1)}, bf16[4,128,384]{2,1,0:T(8,128)(2,1)S(1)}, u32[]{:S(2)}, u32[]{:S(2)}) %collective-permute-start.40) | collective-permute-done | bytes 393248 | tf_op jit(solution)/shard_map/ppermute | solution.py:12
  216.7 7.9 %collective-permute-done.39.refs_6_ = bf16[4,128,384]{2,1,0:T(8,128)(2,1)} collective-permute-done((bf16[4,128,384]{2,1,0:T(8,128)(2,1)S(1)}, bf16[4,128,384]{2,1,0:T(8,128)(2,1)}, u32[]{:S(2)}, u32[]{:S(2)}) %collective-permute-start.39) | collective-permute-done | bytes 393248 | tf_op jit(solution)/shard_map/ppermute | solution.py:12
  224.7 3.5 %assemble.3 = bf16[512,3584]{1,0:T(8,128)(2,1)} custom-call(s32[9]{0:T(128)S(1)} %concatenate.55.flags_ref, bf16[4,128,512]{2,1,0:T(8,128)(2,1)S(1)} %pad_maximum_fusion.10.refs_0_, bf16[4,128,512]{2,1,0:T(8,128)(2,1)S(1)} %collective-permute-done.35.refs_1_, bf16[4,128,512]{2,1,0:T(8,128)(2,1)S(1)} %collective-permute-done.36.refs_2_, ...), custom_call_target="tpu_custom_call" | custom-call | flops 1024 | bytes 1024 | tf_op jit(solution)/shard_map/assemble/pallas_call | solution.py:326
  228.2 0.9 copy-done.1
  (118 shorter events, 6.1 us)
Async XLA Ops:
  7.2 7.4 %copy-start = (bf16[128,896]{1,0:T(8,128)(2,1)S(1)}, bf16[128,896]{1,0:T(8,128)(2,1)}, u32[]{:S(2)}) copy-start(bf16[128,896]{1,0:T(8,128)(2,1)} %param.12) | copy-start | bytes 688132
  7.2 6.7 %copy-start.30 = (s32[128,2]{0,1:T(2,128)S(1)}, s32[128,2]{0,1:T(2,128)}, u32[]{:S(2)}) copy-start(s32[128,2]{0,1:T(2,128)} %param.13) | copy-start | bytes 3076
  9.8 11.8 %copy-start.31 = (s32[1,512]{1,0:T(1,128)S(1)}, s32[1,512]{1,0:T(1,128)}, u32[]{:S(2)}) copy-start(s32[1,512]{1,0:T(1,128)} %param.19) | copy-start | bytes 6148
  9.8 12.4 %copy-start.12 = (s32[8]{0:T(128)S(1)}, s32[8]{0:T(128)}, u32[]{:S(2)}) copy-start(s32[8]{0:T(128)} %param.20) | copy-start | bytes 100
  9.8 15.1 %copy-start.29 = (s32[2]{0:T(128)S(1)}, s32[2]{0:T(128)}, u32[]{:S(2)}) copy-start(s32[2]{0:T(128)} %param.21) | copy-start | bytes 28
  10.9 26.4 %collective-permute-start.12 = (bf16[2,512,512]{2,1,0:T(8,128)(2,1)}, bf16[2,512,512]{2,1,0:T(8,128)(2,1)S(1)}, u32[]{:S(2)}, u32[]{:S(2)}) collective-permute-start(bf16[2,512,512]{2,1,0:T(8,128)(2,1)} %pad_maximum_fusion.5), channel_id=1, source_target_pairs={{0,2},{1,3},{2,0},{3,1},{4,6},{5,7},{6,4},{7,5},{8,10},{9,11},{10,... | collective-permute-start | bytes 3145736 | tf_op jit(solution)/shard_map/ppermute | solution.py:12
  15.7 24.9 %copy-start.28 = (bf16[128,896]{1,0:T(8,128)(2,1)S(1)}, bf16[128,896]{1,0:T(8,128)(2,1)}, u32[]{:S(2)}) copy-start(bf16[128,896]{1,0:T(8,128)(2,1)} %param.15) | copy-start | bytes 688132
  15.7 24.9 %all-to-all-start = ((bf16[8,40,896]{2,1,0:T(8,128)(2,1)}), bf16[8,40,896]{2,1,0:T(8,128)(2,1)S(1)}, u32[]{:S(2)}, u32[]{:S(2)}) async-start(bf16[8,40,896]{2,1,0:T(8,128)(2,1)} %bitcast.18), calls=%async_computation | async-start | bytes 1146880 | tf_op jit(solution)/shard_map/all_to_all | solution.py:482
  21.6 139.0 %all-gather.3.cloned.1.call-start = ((), (), s32[]{:S(2)}) async-start(), calls=%async_computation.2 | async-start | bytes 1179648 | tf_op jit(solution)/shard_map/all_gather | solution.py:495
  21.7 18.4 %collective-permute-start.15 = (s32[512]{0:T(512)S(1)}, s32[512]{0:T(512)S(1)}, u32[]{:S(2)}, u32[]{:S(2)}) collective-permute-start(s32[512]{0:T(512)S(1)} %bitcast.83), channel_id=1, source_target_pairs={{0,2},{1,3},{2,0},{3,1},{4,6},{5,7},{6,4},{7,5},{8,10},{9,11},{10,... | collective-permute-start | bytes 6152 | tf_op jit(solution)/shard_map/ppermute | solution.py:12
  22.2 23.3 %collective-permute-start.14 = (s32[512]{0:T(512)S(1)}, s32[512]{0:T(512)S(1)}, u32[]{:S(2)}, u32[]{:S(2)}) collective-permute-start(s32[512]{0:T(512)S(1)} %bitcast.84), channel_id=1, source_target_pairs={{0,1},{1,0},{2,3},{3,2},{4,5},{5,4},{6,7},{7,6},{8,9},{9,8},{10,11... | collective-permute-start | bytes 6152 | tf_op jit(solution)/shard_map/ppermute | solution.py:12
  39.4 9.7 %collective-permute-start.17 = (bf16[2,512,512]{2,1,0:T(8,128)(2,1)}, bf16[2,512,512]{2,1,0:T(8,128)(2,1)}, u32[]{:S(2)}, u32[]{:S(2)}) collective-permute-start(bf16[2,512,512]{2,1,0:T(8,128)(2,1)} %pad_maximum_fusion.6), channel_id=1, source_target_pairs={{0,1},{1,0},{2,3},{3,2},{4,5},{5,4},{6,7},{7,6},{8,9},{9,8},{10,11... | collective-permute-start | bytes 3145736 | tf_op jit(solution)/shard_map/ppermute | solution.py:12
  40.1 5.5 %collective-permute-start.16 = (s32[512]{0:T(512)S(1)}, s32[512]{0:T(512)S(1)}, u32[]{:S(2)}, u32[]{:S(2)}) collective-permute-start(s32[512]{0:T(512)S(1)} %collective-permute-done.15), channel_id=1, source_target_pairs={{0,1},{1,0},{2,3},{3,2},{4,5},{5,4},{6,7},{7,6},{8,9},{9,8},{10,11... | collective-permute-start | bytes 6152 | tf_op jit(solution)/shard_map/ppermute | solution.py:12
  40.6 20.0 %collective-permute-start.13 = (bf16[1,448,896]{2,1,0:T(8,128)(2,1)S(1)}, bf16[1,448,896]{2,1,0:T(8,128)(2,1)}, u32[]{:S(2)}, u32[]{:S(2)}) collective-permute-start(bf16[1,448,896]{2,1,0:T(8,128)(2,1)S(1)} %bitcast.76), channel_id=1, source_target_pairs={{0,2},{1,3},{2,0},{3,1},{4,6},{5,7},{6,4},{7,5},{8,10},{9,11},{10,... | collective-permute-start | bytes 2408456 | tf_op jit(solution)/shard_map/ppermute | solution.py:12
  55.0 0.8 copy-start.6
  55.8 0.8 copy-start.8
  56.6 0.8 copy-start.10
  61.9 7.2 %collective-permute-start.18 = (bf16[2,448,896]{2,1,0:T(8,128)(2,1)S(1)}, bf16[2,448,896]{2,1,0:T(8,128)(2,1)}, u32[]{:S(2)}, u32[]{:S(2)}) collective-permute-start(bf16[2,448,896]{2,1,0:T(8,128)(2,1)S(1)} %pad_maximum_fusion.4.even_ref), channel_id=1, source_target_pairs={{0,1},{1,0},{2,3},{3,2},{4,5},{5,4},{6,7},{7,6},{8,9},{9,8},{10,11... | collective-permute-start | bytes 4816904 | tf_op jit(solution)/shard_map/ppermute | solution.py:12
  62.0 3.6 %copy-start.11 = (bf16[512,512]{1,0:T(8,128)(2,1)S(1)}, bf16[512,512]{1,0:T(8,128)(2,1)}, u32[]{:S(2)}) copy-start(bf16[512,512]{1,0:T(8,128)(2,1)} %copy-done.10) | copy-start | bytes 1572868
  62.1 5.1 %copy-start.9 = (bf16[512,512]{1,0:T(8,128)(2,1)S(1)}, bf16[512,512]{1,0:T(8,128)(2,1)}, u32[]{:S(2)}) copy-start(bf16[512,512]{1,0:T(8,128)(2,1)} %copy-done.8) | copy-start | bytes 1572868
  62.1 6.6 %copy-start.7 = (bf16[512,512]{1,0:T(8,128)(2,1)S(1)}, bf16[512,512]{1,0:T(8,128)(2,1)}, u32[]{:S(2)}) copy-start(bf16[512,512]{1,0:T(8,128)(2,1)} %copy-done.6) | copy-start | bytes 1572868
  63.8 28.2 %collective-permute-start.19 = (bf16[2,512,384]{2,1,0:T(8,128)(2,1)S(1)}, bf16[2,512,384]{2,1,0:T(8,128)(2,1)S(1)}, u32[]{:S(2)}, u32[]{:S(2)}) collective-permute-start(bf16[2,512,384]{2,1,0:T(8,128)(2,1)S(1)} %pad_maximum_fusion.8), channel_id=1, source_target_pairs={{0,2},{1,3},{2,0},{3,1},{4,6},{5,7},{6,4},{7,5},{8,10},{9,11},{10,... | collective-permute-start | bytes 2359304 | tf_op jit(solution)/shard_map/ppermute | solution.py:12
  65.6 16.7 %collective-permute-start.20 = (bf16[512,512]{1,0:T(8,128)(2,1)S(1)}, bf16[512,512]{1,0:T(8,128)(2,1)S(1)}, u32[]{:S(2)}, u32[]{:S(2)}) collective-permute-start(bf16[512,512]{1,0:T(8,128)(2,1)S(1)} %copy-done.11), channel_id=1, source_target_pairs={{0,4},{4,0},{8,12},{12,8},{16,20},{20,16},{24,28},{28,24},{1,5},{5... | collective-permute-start | bytes 1572872 | tf_op jit(solution)/shard_map/ppermute | solution.py:12
  67.1 15.2 %collective-permute-start.21 = (bf16[512,512]{1,0:T(8,128)(2,1)S(1)}, bf16[512,512]{1,0:T(8,128)(2,1)S(1)}, u32[]{:S(2)}, u32[]{:S(2)}) collective-permute-start(bf16[512,512]{1,0:T(8,128)(2,1)S(1)} %copy-done.9), channel_id=1, source_target_pairs={{0,8},{4,12},{8,0},{12,4},{16,24},{20,28},{24,16},{28,20},{1,9},{5... | collective-permute-start | bytes 1572872 | tf_op jit(solution)/shard_map/ppermute | solution.py:12
  68.7 23.3 %collective-permute-start.22 = (bf16[512,512]{1,0:T(8,128)(2,1)S(1)}, bf16[512,512]{1,0:T(8,128)(2,1)S(1)}, u32[]{:S(2)}, u32[]{:S(2)}) collective-permute-start(bf16[512,512]{1,0:T(8,128)(2,1)S(1)} %copy-done.7), channel_id=1, source_target_pairs={{0,12},{4,8},{8,4},{12,0},{16,28},{20,24},{24,20},{28,16},{1,13},{... | collective-permute-start | bytes 1572872 | tf_op jit(solution)/shard_map/ppermute | solution.py:12
  81.3 1.0 copy-start.4
  82.3 19.4 %collective-permute-start.24 = (bf16[2,320,896]{2,1,0:T(8,128)(2,1)}, bf16[2,320,896]{2,1,0:T(8,128)(2,1)}, u32[]{:S(2)}, u32[]{:S(2)}) collective-permute-start(bf16[2,320,896]{2,1,0:T(8,128)(2,1)} %get-tuple-element.118), channel_id=1, source_target_pairs={{0,1},{1,0},{2,3},{3,2},{4,5},{5,4},{6,7},{7,6},{8,9},{9,8},{10,11... | collective-permute-start | bytes 3440648 | tf_op jit(solution)/shard_map/ppermute | solution.py:12
  82.3 10.7 %copy-start.15 = (bf16[512,512]{1,0:T(8,128)(2,1)}, bf16[512,512]{1,0:T(8,128)(2,1)S(1)}, u32[]{:S(2)}) copy-start(bf16[512,512]{1,0:T(8,128)(2,1)S(1)} %collective-permute-done.20.refs_1_) | copy-start | bytes 1572868
  82.3 11.7 %copy-start.18 = (bf16[512,512]{1,0:T(8,128)(2,1)}, bf16[512,512]{1,0:T(8,128)(2,1)S(1)}, u32[]{:S(2)}) copy-start(bf16[512,512]{1,0:T(8,128)(2,1)S(1)} %collective-permute-done.21.refs_2_) | copy-start | bytes 1572868
  92.0 2.0 copy-start.21
  92.1 0.9 copy-start.2
  93.0 3.5 %copy-start.3 = (bf16[2,512,384]{2,1,0:T(8,128)(2,1)S(1)}, bf16[2,512,384]{2,1,0:T(8,128)(2,1)}, u32[]{:S(2)}) copy-start(bf16[2,512,384]{2,1,0:T(8,128)(2,1)} %copy-done.2) | copy-start | bytes 2359300
  94.0 2.5 %collective-permute-start.23 = (bf16[2,512,384]{2,1,0:T(8,128)(2,1)}, bf16[2,512,384]{2,1,0:T(8,128)(2,1)S(1)}, u32[]{:S(2)}, u32[]{:S(2)}) collective-permute-start(bf16[2,512,384]{2,1,0:T(8,128)(2,1)} %pad_maximum_fusion.9), channel_id=1, source_target_pairs={{0,1},{1,0},{2,3},{3,2},{4,5},{5,4},{6,7},{7,6},{8,9},{9,8},{10,11... | collective-permute-start | bytes 2359304 | tf_op jit(solution)/shard_map/ppermute | solution.py:12
  94.7 7.0 %copy-start.5 = (bf16[2,320,896]{2,1,0:T(8,128)(2,1)S(1)}, bf16[2,320,896]{2,1,0:T(8,128)(2,1)}, u32[]{:S(2)}) copy-start(bf16[2,320,896]{2,1,0:T(8,128)(2,1)} %copy-done.4) | copy-start | bytes 3440644
  101.6 45.3 %copy-start.24 = (bf16[512,384]{1,0:T(8,128)(2,1)}, bf16[512,384]{1,0:T(8,128)(2,1)S(1)}, u32[]{:S(2)}) copy-start(bf16[512,384]{1,0:T(8,128)(2,1)S(1)} %get-tuple-element.133.refs_0_) | copy-start | bytes 1179652
  101.6 2.2 copy-start.13
  101.6 2.2 copy-start.16
  101.6 2.2 copy-start.19
  101.7 2.2 copy-start.22
  103.4 15.1 %collective-permute-start.25 = (bf16[320,896]{1,0:T(8,128)(2,1)S(1)}, bf16[320,896]{1,0:T(8,128)(2,1)S(1)}, u32[]{:S(2)}, u32[]{:S(2)}) collective-permute-start(bf16[320,896]{1,0:T(8,128)(2,1)S(1)} %fusion.12), channel_id=1, source_target_pairs={{0,2},{1,3},{2,0},{3,1},{4,6},{5,7},{6,4},{7,5},{8,10},{9,11},{10,... | collective-permute-start | bytes 1720328 | tf_op jit(solution)/shard_map/ppermute | solution.py:12
  105.3 29.0 %collective-permute-start.29 = (bf16[512,512]{1,0:T(8,128)(2,1)S(1)}, bf16[512,512]{1,0:T(8,128)(2,1)S(1)}, u32[]{:S(2)}, u32[]{:S(2)}) collective-permute-start(bf16[512,512]{1,0:T(8,128)(2,1)S(1)} %get-tuple-element.132), channel_id=1, source_target_pairs={{0,16},{4,20},{8,24},{12,28},{16,0},{20,4},{24,8},{28,12},{1,17},{... | collective-permute-start | bytes 1572872 | tf_op jit(solution)/shard_map/ppermute | solution.py:12
  109.2 25.1 %collective-permute-start.26 = (bf16[512,384]{1,0:T(8,128)(2,1)S(1)}, bf16[512,384]{1,0:T(8,128)(2,1)S(1)}, u32[]{:S(2)}, u32[]{:S(2)}) collective-permute-start(bf16[512,384]{1,0:T(8,128)(2,1)S(1)} %get-tuple-element.125), channel_id=1, source_target_pairs={{0,4},{4,0},{8,12},{12,8},{16,20},{20,16},{24,28},{28,24},{1,5},{5... | collective-permute-start | bytes 1179656 | tf_op jit(solution)/shard_map/ppermute | solution.py:12
  110.8 23.5 %collective-permute-start.27 = (bf16[512,384]{1,0:T(8,128)(2,1)S(1)}, bf16[512,384]{1,0:T(8,128)(2,1)S(1)}, u32[]{:S(2)}, u32[]{:S(2)}) collective-permute-start(bf16[512,384]{1,0:T(8,128)(2,1)S(1)} %get-tuple-element.126), channel_id=1, source_target_pairs={{0,8},{4,12},{8,0},{12,4},{16,24},{20,28},{24,16},{28,20},{1,9},{5... | collective-permute-start | bytes 1179656 | tf_op jit(solution)/shard_map/ppermute | solution.py:12
  112.3 34.6 %collective-permute-start.28 = (bf16[512,384]{1,0:T(8,128)(2,1)S(1)}, bf16[512,384]{1,0:T(8,128)(2,1)S(1)}, u32[]{:S(2)}, u32[]{:S(2)}) collective-permute-start(bf16[512,384]{1,0:T(8,128)(2,1)S(1)} %get-tuple-element.127), channel_id=1, source_target_pairs={{0,12},{4,8},{8,4},{12,0},{16,28},{20,24},{24,20},{28,16},{1,13},{... | collective-permute-start | bytes 1179656 | tf_op jit(solution)/shard_map/ppermute | solution.py:12
  134.3 17.9 %copy-start.25 = (bf16[512,384]{1,0:T(8,128)(2,1)}, bf16[512,384]{1,0:T(8,128)(2,1)S(1)}, u32[]{:S(2)}) copy-start(bf16[512,384]{1,0:T(8,128)(2,1)S(1)} %collective-permute-done.26.refs_1_) | copy-start | bytes 1179652
  134.3 27.8 %copy-start.26 = (bf16[512,384]{1,0:T(8,128)(2,1)}, bf16[512,384]{1,0:T(8,128)(2,1)S(1)}, u32[]{:S(2)}) copy-start(bf16[512,384]{1,0:T(8,128)(2,1)S(1)} %collective-permute-done.27.refs_2_) | copy-start | bytes 1179652
  146.9 1.2 copy-start.27
  148.1 26.5 %collective-permute-start.30 = (bf16[512,384]{1,0:T(8,128)(2,1)S(1)}, bf16[512,384]{1,0:T(8,128)(2,1)S(1)}, u32[]{:S(2)}, u32[]{:S(2)}) collective-permute-start(bf16[512,384]{1,0:T(8,128)(2,1)S(1)} %get-tuple-element.138), channel_id=1, source_target_pairs={{0,16},{4,20},{8,24},{12,28},{16,0},{20,4},{24,8},{28,12},{1,17},{... | collective-permute-start | bytes 1179656 | tf_op jit(solution)/shard_map/ppermute | solution.py:12
  150.7 25.6 %collective-permute-start.33 = (bf16[2,128,512]{2,1,0:T(8,128)(2,1)S(1)}, bf16[2,128,512]{2,1,0:T(8,128)(2,1)S(1)}, u32[]{:S(2)}, u32[]{:S(2)}) collective-permute-start(bf16[2,128,512]{2,1,0:T(8,128)(2,1)S(1)} %get-tuple-element.147), channel_id=1, source_target_pairs={{0,2},{1,3},{2,0},{3,1},{4,6},{5,7},{6,4},{7,5},{8,10},{9,11},{10,... | collective-permute-start | bytes 786440 | tf_op jit(solution)/shard_map/ppermute | solution.py:12
  152.8 48.2 %all-to-all-start.1 = ((bf16[8,40,896]{2,1,0:T(8,128)(2,1)}), bf16[8,40,896]{2,1,0:T(8,128)(2,1)}, u32[]{:S(2)}, u32[]{:S(2)}) async-start(bf16[8,40,896]{2,1,0:T(8,128)(2,1)} %bitcast.78), calls=%async_computation.1 | async-start | bytes 1146880 | tf_op jit(solution)/shard_map/all_to_all | solution.py:527
  174.7 6.3 %collective-permute-start.31 = (bf16[2,128,384]{2,1,0:T(8,128)(2,1)S(1)}, bf16[2,128,384]{2,1,0:T(8,128)(2,1)S(1)}, u32[]{:S(2)}, u32[]{:S(2)}) collective-permute-start(bf16[2,128,384]{2,1,0:T(8,128)(2,1)S(1)} %get-tuple-element.141), channel_id=1, source_target_pairs={{0,2},{1,3},{2,0},{3,1},{4,6},{5,7},{6,4},{7,5},{8,10},{9,11},{10,... | collective-permute-start | bytes 589832 | tf_op jit(solution)/shard_map/ppermute | solution.py:12
  176.3 4.8 %collective-permute-start.34 = (bf16[2,128,512]{2,1,0:T(8,128)(2,1)S(1)}, bf16[2,128,512]{2,1,0:T(8,128)(2,1)S(1)}, u32[]{:S(2)}, u32[]{:S(2)}) collective-permute-start(bf16[2,128,512]{2,1,0:T(8,128)(2,1)S(1)} %pad_maximum_fusion.12), channel_id=1, source_target_pairs={{0,1},{1,0},{2,3},{3,2},{4,5},{5,4},{6,7},{7,6},{8,9},{9,8},{10,11... | collective-permute-start | bytes 786440 | tf_op jit(solution)/shard_map/ppermute | solution.py:12
  181.1 3.8 %collective-permute-start.32 = (bf16[2,128,384]{2,1,0:T(8,128)(2,1)S(1)}, bf16[2,128,384]{2,1,0:T(8,128)(2,1)S(1)}, u32[]{:S(2)}, u32[]{:S(2)}) collective-permute-start(bf16[2,128,384]{2,1,0:T(8,128)(2,1)S(1)} %pad_maximum_fusion.13), channel_id=1, source_target_pairs={{0,1},{1,0},{2,3},{3,2},{4,5},{5,4},{6,7},{7,6},{8,9},{9,8},{10,11... | collective-permute-start | bytes 589832 | tf_op jit(solution)/shard_map/ppermute | solution.py:12
  181.3 15.7 %collective-permute-start.37 = (bf16[4,128,512]{2,1,0:T(8,128)(2,1)S(1)}, bf16[4,128,512]{2,1,0:T(8,128)(2,1)S(1)}, u32[]{:S(2)}, u32[]{:S(2)}) collective-permute-start(bf16[4,128,512]{2,1,0:T(8,128)(2,1)S(1)} %pad_maximum_fusion.10.refs_0_), channel_id=1, source_target_pairs={{0,12},{4,8},{8,4},{12,0},{16,28},{20,24},{24,20},{28,16},{1,13},{... | collective-permute-start | bytes 1572872 | tf_op jit(solution)/shard_map/ppermute | solution.py:12
  181.3 26.7 %collective-permute-start.36 = (bf16[4,128,512]{2,1,0:T(8,128)(2,1)S(1)}, bf16[4,128,512]{2,1,0:T(8,128)(2,1)S(1)}, u32[]{:S(2)}, u32[]{:S(2)}) collective-permute-start(bf16[4,128,512]{2,1,0:T(8,128)(2,1)S(1)} %pad_maximum_fusion.10.refs_0_), channel_id=1, source_target_pairs={{0,8},{4,12},{8,0},{12,4},{16,24},{20,28},{24,16},{28,20},{1,9},{5... | collective-permute-start | bytes 1572872 | tf_op jit(solution)/shard_map/ppermute | solution.py:12
  184.1 24.2 %collective-permute-start.35 = (bf16[4,128,512]{2,1,0:T(8,128)(2,1)S(1)}, bf16[4,128,512]{2,1,0:T(8,128)(2,1)S(1)}, u32[]{:S(2)}, u32[]{:S(2)}) collective-permute-start(bf16[4,128,512]{2,1,0:T(8,128)(2,1)S(1)} %pad_maximum_fusion.10.refs_0_), channel_id=1, source_target_pairs={{0,4},{4,0},{8,12},{12,8},{16,20},{20,16},{24,28},{28,24},{1,5},{5... | collective-permute-start | bytes 1572872 | tf_op jit(solution)/shard_map/ppermute | solution.py:12
  184.9 31.8 %collective-permute-start.40 = (bf16[4,128,384]{2,1,0:T(8,128)(2,1)S(1)}, bf16[4,128,384]{2,1,0:T(8,128)(2,1)S(1)}, u32[]{:S(2)}, u32[]{:S(2)}) collective-permute-start(bf16[4,128,384]{2,1,0:T(8,128)(2,1)S(1)} %pad_maximum_fusion.11.refs_4_), channel_id=1, source_target_pairs={{0,12},{4,8},{8,4},{12,0},{16,28},{20,24},{24,20},{28,16},{1,13},{... | collective-permute-start | bytes 1179656 | tf_op jit(solution)/shard_map/ppermute | solution.py:12
  185.7 38.9 %collective-permute-start.39 = (bf16[4,128,384]{2,1,0:T(8,128)(2,1)S(1)}, bf16[4,128,384]{2,1,0:T(8,128)(2,1)}, u32[]{:S(2)}, u32[]{:S(2)}) collective-permute-start(bf16[4,128,384]{2,1,0:T(8,128)(2,1)S(1)} %pad_maximum_fusion.11.refs_4_), channel_id=1, source_target_pairs={{0,8},{4,12},{8,0},{12,4},{16,24},{20,28},{24,16},{28,20},{1,9},{5... | collective-permute-start | bytes 1179656 | tf_op jit(solution)/shard_map/ppermute | solution.py:12
  194.7 6.3 %copy-start.32 = (f32[128,2]{0,1:T(2,128)S(1)}, f32[128,2]{0,1:T(2,128)}, u32[]{:S(2)}) copy-start(f32[128,2]{0,1:T(2,128)} %param.14) | copy-start | bytes 3076
  197.0 27.7 %collective-permute-start.38 = (bf16[4,128,384]{2,1,0:T(8,128)(2,1)S(1)}, bf16[4,128,384]{2,1,0:T(8,128)(2,1)}, u32[]{:S(2)}, u32[]{:S(2)}) collective-permute-start(bf16[4,128,384]{2,1,0:T(8,128)(2,1)S(1)} %pad_maximum_fusion.11.refs_4_), channel_id=1, source_target_pairs={{0,4},{4,0},{8,12},{12,8},{16,20},{20,16},{24,28},{28,24},{1,5},{5... | collective-permute-start | bytes 1179656 | tf_op jit(solution)/shard_map/ppermute | solution.py:12
  203.3 24.9 %copy-start.14 = (bf16[512,512]{1,0:T(8,128)(2,1)S(1)}, bf16[512,512]{1,0:T(8,128)(2,1)}, u32[]{:S(2)}) copy-start(bf16[512,512]{1,0:T(8,128)(2,1)} %get-tuple-element.128.refs_0_) | copy-start | bytes 1572868
  228.2 0.9 copy-start.1
Sparse Core Ops, SparseCore 0:
  94.8 65.7 all-gather.2

commit v9 on v8

--- a/solution.py
+++ b/solution.py
@@ -520,7 +520,6 @@
             if not c:
                 returned = sum_tensor(send, after(keep, mark), nt)
         lines = two.back(mean_of(two.scale, kept[0], after(others[0], kept[-1])))
-        lines = after(lines, others[-1])
     else:
         returned = sum_tensor(send, keep, nt)
         correlation = correlate(partner)
@@ -533,7 +532,7 @@
     if two is not None:
         gathered = [two.out(lines)]
         for c in range(1, len(two.spans)):
-            means = mean_of(two.scale, kept[c], others[c])
+            means = mean_of(two.scale, kept[c], after(others[c], *gathered[-1][1:]))
             lines = two.back(means)
             gathered.append(two.out(lines))
         correlation = correlate(after(partner, lines))

time: 237 us -> 242 us (1.021)
  waiting for transfers between devices: 104 us -> 116 us
  local copies, waits for them, and re-layouts: 14.8 us -> 10.8 us
    ppermute x29, waiting for transfers between devices: 101 us -> 116 us  [xor_permute(): return lax.ppermute(value, axis, [(i, i ^ k) for i in range(size)])]
    unnamed x61 -> x37, local copies, waits for them, and re-layouts: 5.49 us -> 1.56 us
    all_gather x1, waiting for transfers between devices: 3.14 us -> 0.02 us  [on_device(): everyone = lax.all_gather(probe_hidden, 'expert', axis=0)]
  transfers between devices with their start and end apart: 32 -> 32, of which waited for: 16 -> 16; matrix products, arithmetic and copies ran while one was open for 10% -> 9% of each run, Pallas kernels for 11% -> 10%
where the time goes in v9:
time: 242 us; the launch traced here: 241 us
  waiting for transfers between devices  116 us (48%)
  starting transfers between devices  39.5 us (16%)
  Pallas kernels  29.9 us (12%)
  between operations  21.5 us (9%)
  local copies, waits for them, and re-layouts  10.8 us (4%)
  other arithmetic  10.8 us (4%)
  blocking collectives  6.98 us (3%)
  matrix products  6.14 us (3%)
    ppermute x29, waiting for transfers between devices, xor_permute(): return lax.ppermute(value, axis, [(i, i ^ k) for i in range(size)])  116 us
    ppermute x29, starting transfers between devices, xor_permute(): return lax.ppermute(value, axis, [(i, i ^ k) for i in range(size)])  29.3 us
    pallas_call x2, Pallas kernels, align(): pl.pallas_call(functools.partial(align_kernel, nt, half, sub), out_shape=...  11.8 us
    all_gather x1, blocking collectives, correlate(): partner_full = lax.all_gather(partner, 'tensor', axis=1, tiled=True)  6.98 us
    pallas_call x1, Pallas kernels, ffn(): pl.pallas_call(functools.partial(ffn_kernel, order), out_shape=jax.ShapeD...  6.96 us
    all_to_all x1, starting transfers between devices, on_device(): lax.all_to_all(outgoing, 'expert', split_axis=0, concat_axis=0, tiled=True)  5.94 us
  transfers between devices with their start and end apart: 32, of which 16 were waited for; matrix products, arithmetic and copies ran while one was open for 9% of the time, Pallas kernels for 10%

profile of v9, /device:TPU:0, one launch (start us, length us, event | category | flops | bytes accessed | tf_op | source)
XLA Modules:
  0.0 241.4 jit_solution(3050609010761481829)
XLA Ops:
  7.2 2.6 %constant_dynamic-slice_fusion.3 = (bf16[1,512,512]{2,1,0:T(8,128)(2,1)}, bf16[512,512]{1,0:T(8,128)(2,1)S(1)}, bf16[1,512,512]{2,1,0:T(8,128)(2,1)S(1)}, bf16[1,512,512]{2,1,0:T(8,128)(2,1)S(1)}) fusion(bf16[1,512,3584]{2,1,0:T(8,128)(2,1)} %param.18, s32[]{:T(128)S(6)} %select_n.176, s32[]{:T(128)S(6)} %select_n.175, s32[]{:T(128)S(6)} %select_n.164, ...), kind=kLoop, calls=%fused_computation.66 | loop fusion | bytes 4194320 | tf_op jit(solution)/shard_map/dynamic_slice | solution.py:186
  9.8 1.1 pad_maximum_fusion.5
  10.9 3.0 %collective-permute-start.12 = (bf16[2,512,512]{2,1,0:T(8,128)(2,1)}, bf16[2,512,512]{2,1,0:T(8,128)(2,1)S(1)}, u32[]{:S(2)}, u32[]{:S(2)}) collective-permute-start(bf16[2,512,512]{2,1,0:T(8,128)(2,1)} %pad_maximum_fusion.5), channel_id=1, source_target_pairs={{0,2},{1,3},{2,0},{3,1},{4,6},{5,7},{6,4},{7,5},{8,10},{9,11},{10,... | collective-permute-start | bytes 3145736 | tf_op jit(solution)/shard_map/ppermute | solution.py:12
  14.6 1.1 convolution_convert_fusion
  15.7 5.9 %all-to-all-start = ((bf16[8,40,896]{2,1,0:T(8,128)(2,1)}), bf16[8,40,896]{2,1,0:T(8,128)(2,1)S(1)}, u32[]{:S(2)}, u32[]{:S(2)}) async-start(bf16[8,40,896]{2,1,0:T(8,128)(2,1)} %bitcast.18), calls=%async_computation | async-start | bytes 1146880 | tf_op jit(solution)/shard_map/all_to_all | solution.py:482
  21.7 0.6 collective-permute-start.15
  22.3 0.6 dynamic_slice.44
  25.0 12.3 %collective-permute-done.12.refs_1_ = bf16[2,512,512]{2,1,0:T(8,128)(2,1)S(1)} collective-permute-done((bf16[2,512,512]{2,1,0:T(8,128)(2,1)}, bf16[2,512,512]{2,1,0:T(8,128)(2,1)S(1)}, u32[]{:S(2)}, u32[]{:S(2)}) %collective-permute-start.12) | collective-permute-done | bytes 1048608 | tf_op jit(solution)/shard_map/ppermute | solution.py:12
  37.3 2.1 pad_maximum_fusion.6
  39.4 0.6 fusion.36
  40.0 0.5 collective-permute-start.16
  40.6 1.8 collective-permute-start.13
  42.4 0.6 fusion.34
  45.6 1.3 copy.47
  47.0 2.2 fusion.7.place_ref
  49.2 6.6 %align.2 = (bf16[512,512]{1,0:T(8,128)(2,1)}, bf16[512,512]{1,0:T(8,128)(2,1)}, bf16[512,512]{1,0:T(8,128)(2,1)}, bf16[512,512]{1,0:T(8,128)(2,1)}) custom-call(s32[9]{0:T(128)S(1)} %concatenate.55.flags_ref, s32[2048,1]{1,0:T(8,128)S(1)} %fusion.7.place_ref, bf16[512,512]{1,0:T(8,128)(2,1)S(1)} %get-tuple-element.108.refs_0_, ...), custom_call_target="tpu_custom_call" | custom-call | flops 1024 | bytes 1024 | tf_op jit(solution)/shard_map/align/pallas_call | solution.py:228
  55.8 4.8 %collective-permute-done.13 = bf16[1,448,896]{2,1,0:T(8,128)(2,1)} collective-permute-done((bf16[1,448,896]{2,1,0:T(8,128)(2,1)S(1)}, bf16[1,448,896]{2,1,0:T(8,128)(2,1)}, u32[]{:S(2)}, u32[]{:S(2)}) %collective-permute-start.13) | collective-permute-done | bytes 802848 | tf_op jit(solution)/shard_map/ppermute | solution.py:12
  60.6 1.3 pad_maximum_fusion.4.even_ref
  62.0 1.5 constant_dynamic-slice_fusion
  63.6 1.8 collective-permute-start.19
  65.4 1.5 collective-permute-start.20
  66.9 1.6 collective-permute-start.21
  68.5 0.4 collective-permute-start.22
  68.9 7.0 %ffn.1.rows_ref = bf16[448,512]{1,0:T(8,128)(2,1)S(1)} custom-call(s32[1]{0:T(128)} %bitcast.15.where_ref, bf16[2,448,896]{2,1,0:T(8,128)(2,1)S(1)} %pad_maximum_fusion.4.even_ref, bf16[2,448,896]{2,1,0:T(8,128)(2,1)} %collective-permute-done.18.odd_ref, bf16[1,3584,512]{2,1,0:T(8,128)(2,1)} %gate_ref.1, bf16[1,3584,512]{2,1,0:T(8,128)(2,1)} %up_ref.1), custom_call_target="tpu_custom_call" | custom-call | flops 1024 | bytes 1024 | tf_op jit(solution)/shard_map/ffn/pallas_call | solution.py:132
  75.9 4.2 %down.1 = (bf16[2,320,896]{2,1,0:T(8,128)(2,1)S(1)}, bf16[2,320,896]{2,1,0:T(8,128)(2,1)S(1)}) custom-call(s32[1]{0:T(128)} %bitcast.15.where_ref, bf16[448,512]{1,0:T(8,128)(2,1)S(1)} %ffn.1.rows_ref, bf16[512,3584]{1,0:T(8,128)(2,1)} %bitcast.74), custom_call_target="tpu_custom_call" | custom-call | flops 1024 | bytes 1024 | tf_op jit(solution)/shard_map/down/pallas_call | solution.py:58
  80.2 1.8 collective-permute-done.21.refs_2_
  81.9 10.1 %collective-permute-done.22.refs_3_ = bf16[512,512]{1,0:T(8,128)(2,1)S(1)} collective-permute-done((bf16[512,512]{1,0:T(8,128)(2,1)}, bf16[512,512]{1,0:T(8,128)(2,1)S(1)}, u32[]{:S(2)}, u32[]{:S(2)}) %collective-permute-start.22) | collective-permute-done | bytes 524320 | tf_op jit(solution)/shard_map/ppermute | solution.py:12
  92.3 2.3 collective-permute-done.23.refs_2_
  94.6 5.1 %align.3 = (bf16[512,384]{1,0:T(8,128)(2,1)S(1)}, bf16[512,384]{1,0:T(8,128)(2,1)S(1)}, bf16[512,384]{1,0:T(8,128)(2,1)S(1)}, bf16[512,384]{1,0:T(8,128)(2,1)S(1)}) custom-call(s32[9]{0:T(128)S(1)} %concatenate.55.flags_ref, s32[2048,1]{1,0:T(8,128)S(1)} %fusion.7.place_ref, bf16[512,384]{1,0:T(8,128)(2,1)S(1)} %get-tuple-element.120.refs_0_, ...), custom_call_target="tpu_custom_call" | custom-call | flops 1024 | bytes 1024 | tf_op jit(solution)/shard_map/align/pallas_call | solution.py:228
  100.5 0.4 copy-done.3
  100.9 1.4 sums.2
  102.3 2.7 %collective-permute-start.29 = (bf16[512,512]{1,0:T(8,128)(2,1)S(1)}, bf16[512,512]{1,0:T(8,128)(2,1)S(1)}, u32[]{:S(2)}, u32[]{:S(2)}) collective-permute-start(bf16[512,512]{1,0:T(8,128)(2,1)S(1)} %get-tuple-element.132), channel_id=1, source_target_pairs={{0,16},{4,20},{8,24},{12,28},{16,0},{20,4},{24,8},{28,12},{1,17},{... | collective-permute-start | bytes 1572872 | tf_op jit(solution)/shard_map/ppermute | solution.py:12
  105.1 1.5 collective-permute-start.26
  106.6 1.6 collective-permute-start.27
  108.6 0.6 fusion.35
  110.5 4.6 %collective-permute-done.25 = bf16[320,896]{1,0:T(8,128)(2,1)S(1)} collective-permute-done((bf16[320,896]{1,0:T(8,128)(2,1)S(1)}, bf16[320,896]{1,0:T(8,128)(2,1)S(1)}, u32[]{:S(2)}, u32[]{:S(2)}) %collective-permute-start.25) | collective-permute-done | bytes 573472 | tf_op jit(solution)/shard_map/ppermute | solution.py:12
  115.1 0.9 fusion.4
  116.1 12.5 %collective-permute-done.29.other_ref = bf16[512,512]{1,0:T(8,128)(2,1)S(1)} collective-permute-done((bf16[512,512]{1,0:T(8,128)(2,1)S(1)}, bf16[512,512]{1,0:T(8,128)(2,1)S(1)}, u32[]{:S(2)}, u32[]{:S(2)}) %collective-permute-start.29) | collective-permute-done | bytes 524320 | tf_op jit(solution)/shard_map/ppermute | solution.py:12
  128.8 7.0 %collective-permute-done.28.refs_3_ = bf16[512,384]{1,0:T(8,128)(2,1)S(1)} collective-permute-done((bf16[512,384]{1,0:T(8,128)(2,1)S(1)}, bf16[512,384]{1,0:T(8,128)(2,1)S(1)}, u32[]{:S(2)}, u32[]{:S(2)}) %collective-permute-start.28) | collective-permute-done | bytes 393248 | tf_op jit(solution)/shard_map/ppermute | solution.py:12
  135.8 1.9 sums.3
  137.8 1.0 collective-permute-start.31
  138.9 0.7 slice.152
  139.6 5.2 %collective-permute-done.31 = bf16[2,128,512]{2,1,0:T(8,128)(2,1)S(1)} collective-permute-done((bf16[2,128,512]{2,1,0:T(8,128)(2,1)S(1)}, bf16[2,128,512]{2,1,0:T(8,128)(2,1)S(1)}, u32[]{:S(2)}, u32[]{:S(2)}) %collective-permute-start.31) | collective-permute-done | bytes 262176 | tf_op jit(solution)/shard_map/ppermute | solution.py:12
  144.9 1.5 collective-permute-done.32
  146.6 1.7 collective-permute-start.35
  148.2 1.3 collective-permute-start.34
  149.6 0.5 collective-permute-start.33
  150.1 1.5 collective-permute-start.30
  151.6 4.2 %all-to-all-start.1 = ((bf16[8,40,896]{2,1,0:T(8,128)(2,1)}), bf16[8,40,896]{2,1,0:T(8,128)(2,1)}, u32[]{:S(2)}, u32[]{:S(2)}) async-start(bf16[8,40,896]{2,1,0:T(8,128)(2,1)} %bitcast.78), calls=%async_computation.1 | async-start | bytes 1146880 | tf_op jit(solution)/shard_map/all_to_all | solution.py:526
  155.9 35.9 %collective-permute-done.30.other_ref = bf16[512,384]{1,0:T(8,128)(2,1)S(1)} collective-permute-done((bf16[512,384]{1,0:T(8,128)(2,1)}, bf16[512,384]{1,0:T(8,128)(2,1)S(1)}, u32[]{:S(2)}, u32[]{:S(2)}) %collective-permute-start.30) | collective-permute-done | bytes 393248 | tf_op jit(solution)/shard_map/ppermute | solution.py:12
  191.8 7.5 %collective-permute-done.34.refs_2_ = bf16[4,128,512]{2,1,0:T(8,128)(2,1)S(1)} collective-permute-done((bf16[4,128,512]{2,1,0:T(8,128)(2,1)S(1)}, bf16[4,128,512]{2,1,0:T(8,128)(2,1)S(1)}, u32[]{:S(2)}, u32[]{:S(2)}) %collective-permute-start.34) | collective-permute-done | bytes 524320 | tf_op jit(solution)/shard_map/ppermute | solution.py:12
  199.4 1.5 collective-permute-start.36
  202.2 0.6 iota_compare_fusion.6
  202.8 2.5 %collective-permute-done.36 = bf16[2,128,384]{2,1,0:T(8,128)(2,1)S(1)} collective-permute-done((bf16[2,128,384]{2,1,0:T(8,128)(2,1)S(1)}, bf16[2,128,384]{2,1,0:T(8,128)(2,1)S(1)}, u32[]{:S(2)}, u32[]{:S(2)}) %collective-permute-start.36) | collective-permute-done | bytes 196640 | tf_op jit(solution)/shard_map/ppermute | solution.py:12
  205.5 1.5 fusion.1
  207.0 2.3 fusion.2
  209.4 0.5 collective-permute-start.39
  210.0 3.0 %collective-permute-start.38 = (bf16[4,128,384]{2,1,0:T(8,128)(2,1)S(1)}, bf16[4,128,384]{2,1,0:T(8,128)(2,1)S(1)}, u32[]{:S(2)}, u32[]{:S(2)}) collective-permute-start(bf16[4,128,384]{2,1,0:T(8,128)(2,1)S(1)} %pad_maximum_fusion.11.refs_4_), channel_id=1, source_target_pairs={{0,4},{4,0},{8,12},{12,8},{16,20},{20,16},{24,28},{28,24},{1,5},{5... | collective-permute-start | bytes 1179656 | tf_op jit(solution)/shard_map/ppermute | solution.py:12
  212.9 7.0 %all_gather.11 = bf16[128,2048]{1,0:T(8,128)(2,1)S(1)} all-gather(bf16[128,512]{1,0:T(8,128)(2,1)S(1)} %fusion.1), channel_id=1, replica_groups=mesh['expert'=8,'tensor'=4] {'tensor'}, dimensions={1}, use_global_device_ids=true | all-gather | bytes 655360 | tf_op jit(solution)/shard_map/all_gather | solution.py:502
  219.9 2.7 %convolution_multiply_fusion = f32[512,2048]{1,0:T(8,128)} fusion(bf16[128,2048]{1,0:T(8,128)(2,1)S(1)} %all_gather.11, bf16[448,512]{1,0:T(8,128)(2,1)S(1)} %ffn.1.rows_ref), kind=kOutput, calls=%fused_computation.12 | convolution fusion | flops 269484032 | bytes 4849664 | tf_op jit(solution)/shard_map/dot_general | solution.py:503
  222.6 5.2 %collective-permute-done.39.refs_6_ = bf16[4,128,384]{2,1,0:T(8,128)(2,1)S(1)} collective-permute-done((bf16[4,128,384]{2,1,0:T(8,128)(2,1)S(1)}, bf16[4,128,384]{2,1,0:T(8,128)(2,1)S(1)}, u32[]{:S(2)}, u32[]{:S(2)}) %collective-permute-start.39) | collective-permute-done | bytes 393248 | tf_op jit(solution)/shard_map/ppermute | solution.py:12
  227.9 2.4 collective-permute-done.38.refs_5_
  230.2 3.4 %assemble.3 = bf16[512,3584]{1,0:T(8,128)(2,1)} custom-call(s32[9]{0:T(128)S(1)} %concatenate.55.flags_ref, bf16[4,128,512]{2,1,0:T(8,128)(2,1)S(1)} %pad_maximum_fusion.10.refs_0_, bf16[4,128,512]{2,1,0:T(8,128)(2,1)} %collective-permute-done.33.refs_1_, bf16[4,128,512]{2,1,0:T(8,128)(2,1)S(1)} %collective-permute-done.34.refs_2_, ...), custom_call_target="tpu_custom_call" | custom-call | flops 1024 | bytes 1024 | tf_op jit(solution)/shard_map/assemble/pallas_call | solution.py:326
  233.6 0.9 copy-done.1
  (94 shorter events, 3.8 us)
Async XLA Ops:
  7.2 7.4 %copy-start = (bf16[128,896]{1,0:T(8,128)(2,1)S(1)}, bf16[128,896]{1,0:T(8,128)(2,1)}, u32[]{:S(2)}) copy-start(bf16[128,896]{1,0:T(8,128)(2,1)} %param.12) | copy-start | bytes 688132
  7.2 6.7 %copy-start.17 = (s32[128,2]{0,1:T(2,128)S(1)}, s32[128,2]{0,1:T(2,128)}, u32[]{:S(2)}) copy-start(s32[128,2]{0,1:T(2,128)} %param.13) | copy-start | bytes 3076
  9.8 11.8 %copy-start.18 = (s32[1,512]{1,0:T(1,128)S(1)}, s32[1,512]{1,0:T(1,128)}, u32[]{:S(2)}) copy-start(s32[1,512]{1,0:T(1,128)} %param.19) | copy-start | bytes 6148
  9.8 12.4 %copy-start.2 = (s32[8]{0:T(128)S(1)}, s32[8]{0:T(128)}, u32[]{:S(2)}) copy-start(s32[8]{0:T(128)} %param.20) | copy-start | bytes 100
  9.8 15.1 %copy-start.16 = (s32[2]{0:T(128)S(1)}, s32[2]{0:T(128)}, u32[]{:S(2)}) copy-start(s32[2]{0:T(128)} %param.21) | copy-start | bytes 28
  10.9 26.4 %collective-permute-start.12 = (bf16[2,512,512]{2,1,0:T(8,128)(2,1)}, bf16[2,512,512]{2,1,0:T(8,128)(2,1)S(1)}, u32[]{:S(2)}, u32[]{:S(2)}) collective-permute-start(bf16[2,512,512]{2,1,0:T(8,128)(2,1)} %pad_maximum_fusion.5), channel_id=1, source_target_pairs={{0,2},{1,3},{2,0},{3,1},{4,6},{5,7},{6,4},{7,5},{8,10},{9,11},{10,... | collective-permute-start | bytes 3145736 | tf_op jit(solution)/shard_map/ppermute | solution.py:12
  15.7 24.8 %copy-start.15 = (bf16[128,896]{1,0:T(8,128)(2,1)S(1)}, bf16[128,896]{1,0:T(8,128)(2,1)}, u32[]{:S(2)}) copy-start(bf16[128,896]{1,0:T(8,128)(2,1)} %param.15) | copy-start | bytes 688132
  15.7 24.8 %all-to-all-start = ((bf16[8,40,896]{2,1,0:T(8,128)(2,1)}), bf16[8,40,896]{2,1,0:T(8,128)(2,1)S(1)}, u32[]{:S(2)}, u32[]{:S(2)}) async-start(bf16[8,40,896]{2,1,0:T(8,128)(2,1)} %bitcast.18), calls=%async_computation | async-start | bytes 1146880 | tf_op jit(solution)/shard_map/all_to_all | solution.py:482
  21.6 183.8 %all-gather.3.cloned.1.call-start = ((), (), s32[]{:S(2)}) async-start(), calls=%async_computation.2 | async-start | bytes 1179648 | tf_op jit(solution)/shard_map/all_gather | solution.py:495
  21.7 18.3 %collective-permute-start.15 = (s32[512]{0:T(512)S(1)}, s32[512]{0:T(512)S(1)}, u32[]{:S(2)}, u32[]{:S(2)}) collective-permute-start(s32[512]{0:T(512)S(1)} %bitcast.83), channel_id=1, source_target_pairs={{0,2},{1,3},{2,0},{3,1},{4,6},{5,7},{6,4},{7,5},{8,10},{9,11},{10,... | collective-permute-start | bytes 6152 | tf_op jit(solution)/shard_map/ppermute | solution.py:12
  22.2 23.4 %collective-permute-start.14 = (s32[512]{0:T(512)S(1)}, s32[512]{0:T(512)S(1)}, u32[]{:S(2)}, u32[]{:S(2)}) collective-permute-start(s32[512]{0:T(512)S(1)} %bitcast.84), channel_id=1, source_target_pairs={{0,1},{1,0},{2,3},{3,2},{4,5},{5,4},{6,7},{7,6},{8,9},{9,8},{10,11... | collective-permute-start | bytes 6152 | tf_op jit(solution)/shard_map/ppermute | solution.py:12
  39.4 9.8 %collective-permute-start.17 = (bf16[2,512,512]{2,1,0:T(8,128)(2,1)}, bf16[2,512,512]{2,1,0:T(8,128)(2,1)}, u32[]{:S(2)}, u32[]{:S(2)}) collective-permute-start(bf16[2,512,512]{2,1,0:T(8,128)(2,1)} %pad_maximum_fusion.6), channel_id=1, source_target_pairs={{0,1},{1,0},{2,3},{3,2},{4,5},{5,4},{6,7},{7,6},{8,9},{9,8},{10,11... | collective-permute-start | bytes 3145736 | tf_op jit(solution)/shard_map/ppermute | solution.py:12
  40.0 5.6 %collective-permute-start.16 = (s32[512]{0:T(512)S(1)}, s32[512]{0:T(512)S(1)}, u32[]{:S(2)}, u32[]{:S(2)}) collective-permute-start(s32[512]{0:T(512)S(1)} %collective-permute-done.15), channel_id=1, source_target_pairs={{0,1},{1,0},{2,3},{3,2},{4,5},{5,4},{6,7},{7,6},{8,9},{9,8},{10,11... | collective-permute-start | bytes 6152 | tf_op jit(solution)/shard_map/ppermute | solution.py:12
  40.6 20.0 %collective-permute-start.13 = (bf16[1,448,896]{2,1,0:T(8,128)(2,1)S(1)}, bf16[1,448,896]{2,1,0:T(8,128)(2,1)}, u32[]{:S(2)}, u32[]{:S(2)}) collective-permute-start(bf16[1,448,896]{2,1,0:T(8,128)(2,1)S(1)} %bitcast.76), channel_id=1, source_target_pairs={{0,2},{1,3},{2,0},{3,1},{4,6},{5,7},{6,4},{7,5},{8,10},{9,11},{10,... | collective-permute-start | bytes 2408456 | tf_op jit(solution)/shard_map/ppermute | solution.py:12
  61.9 7.0 %collective-permute-start.18 = (bf16[2,448,896]{2,1,0:T(8,128)(2,1)S(1)}, bf16[2,448,896]{2,1,0:T(8,128)(2,1)}, u32[]{:S(2)}, u32[]{:S(2)}) collective-permute-start(bf16[2,448,896]{2,1,0:T(8,128)(2,1)S(1)} %pad_maximum_fusion.4.even_ref), channel_id=1, source_target_pairs={{0,1},{1,0},{2,3},{3,2},{4,5},{5,4},{6,7},{7,6},{8,9},{9,8},{10,11... | collective-permute-start | bytes 4816904 | tf_op jit(solution)/shard_map/ppermute | solution.py:12
  63.6 28.4 %collective-permute-start.19 = (bf16[2,512,384]{2,1,0:T(8,128)(2,1)S(1)}, bf16[2,512,384]{2,1,0:T(8,128)(2,1)S(1)}, u32[]{:S(2)}, u32[]{:S(2)}) collective-permute-start(bf16[2,512,384]{2,1,0:T(8,128)(2,1)S(1)} %pad_maximum_fusion.8), channel_id=1, source_target_pairs={{0,2},{1,3},{2,0},{3,1},{4,6},{5,7},{6,4},{7,5},{8,10},{9,11},{10,... | collective-permute-start | bytes 2359304 | tf_op jit(solution)/shard_map/ppermute | solution.py:12
  65.4 14.7 %collective-permute-start.20 = (bf16[512,512]{1,0:T(8,128)(2,1)}, bf16[512,512]{1,0:T(8,128)(2,1)S(1)}, u32[]{:S(2)}, u32[]{:S(2)}) collective-permute-start(bf16[512,512]{1,0:T(8,128)(2,1)} %get-tuple-element.115), channel_id=1, source_target_pairs={{0,4},{4,0},{8,12},{12,8},{16,20},{20,16},{24,28},{28,24},{1,5},{5... | collective-permute-start | bytes 1572872 | tf_op jit(solution)/shard_map/ppermute | solution.py:12
  66.9 15.0 %collective-permute-start.21 = (bf16[512,512]{1,0:T(8,128)(2,1)}, bf16[512,512]{1,0:T(8,128)(2,1)S(1)}, u32[]{:S(2)}, u32[]{:S(2)}) collective-permute-start(bf16[512,512]{1,0:T(8,128)(2,1)} %get-tuple-element.116), channel_id=1, source_target_pairs={{0,8},{4,12},{8,0},{12,4},{16,24},{20,28},{24,16},{28,20},{1,9},{5... | collective-permute-start | bytes 1572872 | tf_op jit(solution)/shard_map/ppermute | solution.py:12
  68.5 23.6 %collective-permute-start.22 = (bf16[512,512]{1,0:T(8,128)(2,1)}, bf16[512,512]{1,0:T(8,128)(2,1)S(1)}, u32[]{:S(2)}, u32[]{:S(2)}) collective-permute-start(bf16[512,512]{1,0:T(8,128)(2,1)} %get-tuple-element.117), channel_id=1, source_target_pairs={{0,12},{4,8},{8,4},{12,0},{16,28},{20,24},{24,20},{28,16},{1,13},{... | collective-permute-start | bytes 1572872 | tf_op jit(solution)/shard_map/ppermute | solution.py:12
  80.1 19.7 %collective-permute-start.24 = (bf16[2,320,896]{2,1,0:T(8,128)(2,1)S(1)}, bf16[2,320,896]{2,1,0:T(8,128)(2,1)S(1)}, u32[]{:S(2)}, u32[]{:S(2)}) collective-permute-start(bf16[2,320,896]{2,1,0:T(8,128)(2,1)S(1)} %get-tuple-element.118), channel_id=1, source_target_pairs={{0,1},{1,0},{2,3},{3,2},{4,5},{5,4},{6,7},{7,6},{8,9},{9,8},{10,11... | collective-permute-start | bytes 3440648 | tf_op jit(solution)/shard_map/ppermute | solution.py:12
  80.2 20.3 %copy-start.5 = (bf16[512,512]{1,0:T(8,128)(2,1)}, bf16[512,512]{1,0:T(8,128)(2,1)S(1)}, u32[]{:S(2)}) copy-start(bf16[512,512]{1,0:T(8,128)(2,1)S(1)} %collective-permute-done.20.refs_1_) | copy-start | bytes 1572868
  81.9 34.1 %copy-start.7 = (bf16[512,512]{1,0:T(8,128)(2,1)}, bf16[512,512]{1,0:T(8,128)(2,1)S(1)}, u32[]{:S(2)}) copy-start(bf16[512,512]{1,0:T(8,128)(2,1)S(1)} %collective-permute-done.21.refs_2_) | copy-start | bytes 1572868
  92.1 8.4 %copy-start.9 = (bf16[512,512]{1,0:T(8,128)(2,1)}, bf16[512,512]{1,0:T(8,128)(2,1)S(1)}, u32[]{:S(2)}) copy-start(bf16[512,512]{1,0:T(8,128)(2,1)S(1)} %collective-permute-done.22.refs_3_) | copy-start | bytes 1572868
  92.2 2.4 collective-permute-start.23
  99.7 36.0 %copy-start.11 = (bf16[512,384]{1,0:T(8,128)(2,1)}, bf16[512,384]{1,0:T(8,128)(2,1)S(1)}, u32[]{:S(2)}) copy-start(bf16[512,384]{1,0:T(8,128)(2,1)S(1)} %get-tuple-element.133.refs_0_) | copy-start | bytes 1179652
  99.7 1.2 copy-start.3
  100.1 15.1 %collective-permute-start.25 = (bf16[320,896]{1,0:T(8,128)(2,1)S(1)}, bf16[320,896]{1,0:T(8,128)(2,1)S(1)}, u32[]{:S(2)}, u32[]{:S(2)}) collective-permute-start(bf16[320,896]{1,0:T(8,128)(2,1)S(1)} %fusion.12), channel_id=1, source_target_pairs={{0,2},{1,3},{2,0},{3,1},{4,6},{5,7},{6,4},{7,5},{8,10},{9,11},{10,... | collective-permute-start | bytes 1720328 | tf_op jit(solution)/shard_map/ppermute | solution.py:12
  102.3 26.3 %collective-permute-start.29 = (bf16[512,512]{1,0:T(8,128)(2,1)S(1)}, bf16[512,512]{1,0:T(8,128)(2,1)S(1)}, u32[]{:S(2)}, u32[]{:S(2)}) collective-permute-start(bf16[512,512]{1,0:T(8,128)(2,1)S(1)} %get-tuple-element.132), channel_id=1, source_target_pairs={{0,16},{4,20},{8,24},{12,28},{16,0},{20,4},{24,8},{28,12},{1,17},{... | collective-permute-start | bytes 1572872 | tf_op jit(solution)/shard_map/ppermute | solution.py:12
  105.1 23.5 %collective-permute-start.26 = (bf16[512,384]{1,0:T(8,128)(2,1)S(1)}, bf16[512,384]{1,0:T(8,128)(2,1)S(1)}, u32[]{:S(2)}, u32[]{:S(2)}) collective-permute-start(bf16[512,384]{1,0:T(8,128)(2,1)S(1)} %get-tuple-element.125), channel_id=1, source_target_pairs={{0,4},{4,0},{8,12},{12,8},{16,20},{20,16},{24,28},{28,24},{1,5},{5... | collective-permute-start | bytes 1179656 | tf_op jit(solution)/shard_map/ppermute | solution.py:12
  106.6 22.2 %collective-permute-start.27 = (bf16[512,384]{1,0:T(8,128)(2,1)S(1)}, bf16[512,384]{1,0:T(8,128)(2,1)S(1)}, u32[]{:S(2)}, u32[]{:S(2)}) collective-permute-start(bf16[512,384]{1,0:T(8,128)(2,1)S(1)} %get-tuple-element.126), channel_id=1, source_target_pairs={{0,8},{4,12},{8,0},{12,4},{16,24},{20,28},{24,16},{28,20},{1,9},{5... | collective-permute-start | bytes 1179656 | tf_op jit(solution)/shard_map/ppermute | solution.py:12
  108.2 27.5 %collective-permute-start.28 = (bf16[512,384]{1,0:T(8,128)(2,1)S(1)}, bf16[512,384]{1,0:T(8,128)(2,1)S(1)}, u32[]{:S(2)}, u32[]{:S(2)}) collective-permute-start(bf16[512,384]{1,0:T(8,128)(2,1)S(1)} %get-tuple-element.127), channel_id=1, source_target_pairs={{0,12},{4,8},{8,4},{12,0},{16,28},{20,24},{24,20},{28,16},{1,13},{... | collective-permute-start | bytes 1179656 | tf_op jit(solution)/shard_map/ppermute | solution.py:12
  128.6 10.3 %copy-start.12 = (bf16[512,384]{1,0:T(8,128)(2,1)}, bf16[512,384]{1,0:T(8,128)(2,1)S(1)}, u32[]{:S(2)}) copy-start(bf16[512,384]{1,0:T(8,128)(2,1)S(1)} %collective-permute-done.26.refs_1_) | copy-start | bytes 1179652
  128.8 10.1 %copy-start.13 = (bf16[512,384]{1,0:T(8,128)(2,1)}, bf16[512,384]{1,0:T(8,128)(2,1)S(1)}, u32[]{:S(2)}) copy-start(bf16[512,384]{1,0:T(8,128)(2,1)S(1)} %collective-permute-done.27.refs_2_) | copy-start | bytes 1179652
  135.7 1.9 copy-start.14
  137.8 7.0 %collective-permute-start.31 = (bf16[2,128,512]{2,1,0:T(8,128)(2,1)S(1)}, bf16[2,128,512]{2,1,0:T(8,128)(2,1)S(1)}, u32[]{:S(2)}, u32[]{:S(2)}) collective-permute-start(bf16[2,128,512]{2,1,0:T(8,128)(2,1)S(1)} %get-tuple-element.143), channel_id=1, source_target_pairs={{0,2},{1,3},{2,0},{3,1},{4,6},{5,7},{6,4},{7,5},{8,10},{9,11},{10,... | collective-permute-start | bytes 786440 | tf_op jit(solution)/shard_map/ppermute | solution.py:12
  144.8 1.6 collective-permute-start.32
  146.6 60.4 %copy-start.19 = (f32[128,2]{0,1:T(2,128)S(1)}, f32[128,2]{0,1:T(2,128)}, u32[]{:S(2)}) copy-start(f32[128,2]{0,1:T(2,128)} %param.14) | copy-start | bytes 3076
  146.6 45.2 %collective-permute-start.35 = (bf16[4,128,512]{2,1,0:T(8,128)(2,1)S(1)}, bf16[4,128,512]{2,1,0:T(8,128)(2,1)S(1)}, u32[]{:S(2)}, u32[]{:S(2)}) collective-permute-start(bf16[4,128,512]{2,1,0:T(8,128)(2,1)S(1)} %pad_maximum_fusion.10.refs_0_), channel_id=1, source_target_pairs={{0,12},{4,8},{8,4},{12,0},{16,28},{20,24},{24,20},{28,16},{1,13},{... | collective-permute-start | bytes 1572872 | tf_op jit(solution)/shard_map/ppermute | solution.py:12
  148.2 51.0 %collective-permute-start.34 = (bf16[4,128,512]{2,1,0:T(8,128)(2,1)S(1)}, bf16[4,128,512]{2,1,0:T(8,128)(2,1)S(1)}, u32[]{:S(2)}, u32[]{:S(2)}) collective-permute-start(bf16[4,128,512]{2,1,0:T(8,128)(2,1)S(1)} %pad_maximum_fusion.10.refs_0_), channel_id=1, source_target_pairs={{0,8},{4,12},{8,0},{12,4},{16,24},{20,28},{24,16},{28,20},{1,9},{5... | collective-permute-start | bytes 1572872 | tf_op jit(solution)/shard_map/ppermute | solution.py:12
  149.6 49.7 %collective-permute-start.33 = (bf16[4,128,512]{2,1,0:T(8,128)(2,1)S(1)}, bf16[4,128,512]{2,1,0:T(8,128)(2,1)}, u32[]{:S(2)}, u32[]{:S(2)}) collective-permute-start(bf16[4,128,512]{2,1,0:T(8,128)(2,1)S(1)} %pad_maximum_fusion.10.refs_0_), channel_id=1, source_target_pairs={{0,4},{4,0},{8,12},{12,8},{16,20},{20,16},{24,28},{28,24},{1,5},{5... | collective-permute-start | bytes 1572872 | tf_op jit(solution)/shard_map/ppermute | solution.py:12
  150.1 41.7 %collective-permute-start.30 = (bf16[512,384]{1,0:T(8,128)(2,1)}, bf16[512,384]{1,0:T(8,128)(2,1)S(1)}, u32[]{:S(2)}, u32[]{:S(2)}) collective-permute-start(bf16[512,384]{1,0:T(8,128)(2,1)} %get-tuple-element.138), channel_id=1, source_target_pairs={{0,16},{4,20},{8,24},{12,28},{16,0},{20,4},{24,8},{28,12},{1,17},{... | collective-permute-start | bytes 1179656 | tf_op jit(solution)/shard_map/ppermute | solution.py:12
  151.6 55.3 %all-to-all-start.1 = ((bf16[8,40,896]{2,1,0:T(8,128)(2,1)}), bf16[8,40,896]{2,1,0:T(8,128)(2,1)}, u32[]{:S(2)}, u32[]{:S(2)}) async-start(bf16[8,40,896]{2,1,0:T(8,128)(2,1)} %bitcast.78), calls=%async_computation.1 | async-start | bytes 1146880 | tf_op jit(solution)/shard_map/all_to_all | solution.py:526
  199.4 5.9 %collective-permute-start.36 = (bf16[2,128,384]{2,1,0:T(8,128)(2,1)S(1)}, bf16[2,128,384]{2,1,0:T(8,128)(2,1)S(1)}, u32[]{:S(2)}, u32[]{:S(2)}) collective-permute-start(bf16[2,128,384]{2,1,0:T(8,128)(2,1)S(1)} %get-tuple-element.147), channel_id=1, source_target_pairs={{0,2},{1,3},{2,0},{3,1},{4,6},{5,7},{6,4},{7,5},{8,10},{9,11},{10,... | collective-permute-start | bytes 589832 | tf_op jit(solution)/shard_map/ppermute | solution.py:12
  205.4 3.9 %collective-permute-start.37 = (bf16[2,128,384]{2,1,0:T(8,128)(2,1)S(1)}, bf16[2,128,384]{2,1,0:T(8,128)(2,1)S(1)}, u32[]{:S(2)}, u32[]{:S(2)}) collective-permute-start(bf16[2,128,384]{2,1,0:T(8,128)(2,1)S(1)} %pad_maximum_fusion.13), channel_id=1, source_target_pairs={{0,1},{1,0},{2,3},{3,2},{4,5},{5,4},{6,7},{7,6},{8,9},{9,8},{10,11... | collective-permute-start | bytes 589832 | tf_op jit(solution)/shard_map/ppermute | solution.py:12
  209.4 13.3 %collective-permute-start.40 = (bf16[4,128,384]{2,1,0:T(8,128)(2,1)S(1)}, bf16[4,128,384]{2,1,0:T(8,128)(2,1)S(1)}, u32[]{:S(2)}, u32[]{:S(2)}) collective-permute-start(bf16[4,128,384]{2,1,0:T(8,128)(2,1)S(1)} %pad_maximum_fusion.11.refs_4_), channel_id=1, source_target_pairs={{0,12},{4,8},{8,4},{12,0},{16,28},{20,24},{24,20},{28,16},{1,13},{... | collective-permute-start | bytes 1179656 | tf_op jit(solution)/shard_map/ppermute | solution.py:12
  209.4 18.4 %collective-permute-start.39 = (bf16[4,128,384]{2,1,0:T(8,128)(2,1)S(1)}, bf16[4,128,384]{2,1,0:T(8,128)(2,1)S(1)}, u32[]{:S(2)}, u32[]{:S(2)}) collective-permute-start(bf16[4,128,384]{2,1,0:T(8,128)(2,1)S(1)} %pad_maximum_fusion.11.refs_4_), channel_id=1, source_target_pairs={{0,8},{4,12},{8,0},{12,4},{16,24},{20,28},{24,16},{28,20},{1,9},{5... | collective-permute-start | bytes 1179656 | tf_op jit(solution)/shard_map/ppermute | solution.py:12
  210.0 20.3 %collective-permute-start.38 = (bf16[4,128,384]{2,1,0:T(8,128)(2,1)S(1)}, bf16[4,128,384]{2,1,0:T(8,128)(2,1)S(1)}, u32[]{:S(2)}, u32[]{:S(2)}) collective-permute-start(bf16[4,128,384]{2,1,0:T(8,128)(2,1)S(1)} %pad_maximum_fusion.11.refs_4_), channel_id=1, source_target_pairs={{0,4},{4,0},{8,12},{12,8},{16,20},{20,16},{24,28},{28,24},{1,5},{5... | collective-permute-start | bytes 1179656 | tf_op jit(solution)/shard_map/ppermute | solution.py:12
  222.6 11.0 %copy-start.4 = (bf16[512,512]{1,0:T(8,128)(2,1)S(1)}, bf16[512,512]{1,0:T(8,128)(2,1)}, u32[]{:S(2)}) copy-start(bf16[512,512]{1,0:T(8,128)(2,1)} %get-tuple-element.128.refs_0_) | copy-start | bytes 1572868
  222.6 11.0 %copy-start.6 = (bf16[512,512]{1,0:T(8,128)(2,1)S(1)}, bf16[512,512]{1,0:T(8,128)(2,1)}, u32[]{:S(2)}) copy-start(bf16[512,512]{1,0:T(8,128)(2,1)} %copy-done.5) | copy-start | bytes 1572868
  233.6 0.9 copy-start.1
Sparse Core Ops, SparseCore 0:
  139.7 52.1 all-gather.2

commit v10 on v2

--- a/solution.py
+++ b/solution.py
@@ -163,13 +163,15 @@
         gathered = []
         for place, (arrived, (off, width)) in enumerate(zip(partials, spans)):
             sent = partial_of(arrived, given).astype(jnp.bfloat16)
-            if place < len(beside):
-                sent = after(sent, beside[place])
+            if place == 0 and beside:
+                sent = after(sent, beside[0])
             other = xor_permute(sent, "expert", ne, half)
             mean = (
                 (partial_of(arrived, kept) + other.astype(jnp.float32)) * inverse[kept]
             ).astype(jnp.bfloat16)
             lines = jnp.stack(rows_to_device(mean.reshape(nt, sub, width), nt))
+            if place == len(spans) - 1 and beside:
+                lines = after(lines, beside[1])
             gathered.append(
                 [xor_permute(lines, "expert", ne, k) if k else lines for k in range(half)]
             )

time: 234 us -> 259 us (1.11)
  waiting for transfers between devices: 63.5 us -> 103 us
  other arithmetic: 20.2 us -> 15.2 us
  starting transfers between devices: 42.4 us -> 37.5 us
  matrix products: 39.2 us -> 36.1 us
    ppermute x35, waiting for transfers between devices: 63.5 us -> 103 us  [xor_permute(): return lax.ppermute(value, axis, [(i, i ^ k) for i in range(size)])]
    ppermute x35, starting transfers between devices: 32 us -> 26.9 us  [xor_permute(): return lax.ppermute(value, axis, [(i, i ^ k) for i in range(size)])]
    select_n x4 -> x3, other arithmetic: 4.7 us -> 1.52 us  [finish(): chosen = jnp.where(q ^ j == k, group[k], chosen)]
    dot_general x8, matrix products: 27.1 us -> 24 us  [pick_rows(): jnp.dot(selector, source, preferred_element_type=jnp.float32)]
  transfers between devices with their start and end apart: 38 -> 38, of which waited for: 9 -> 12; matrix products, arithmetic and copies ran while one was open for 31% -> 25% of each run, Pallas kernels for 3% -> 3%
where the time goes in v10:
time: 259 us; the launch traced here: 258 us
  waiting for transfers between devices  103 us (40%)
  starting transfers between devices  37.5 us (14%)
  matrix products  36.1 us (14%)
  between operations  34.5 us (13%)
  local copies, waits for them, and re-layouts  17.8 us (7%)
  other arithmetic  15.2 us (6%)
  Pallas kernels  6.64 us (3%)
  blocking collectives  6.64 us (3%)
    ppermute x35, waiting for transfers between devices, xor_permute(): return lax.ppermute(value, axis, [(i, i ^ k) for i in range(size)])  103 us
    ppermute x35, starting transfers between devices, xor_permute(): return lax.ppermute(value, axis, [(i, i ^ k) for i in range(size)])  26.9 us
    dot_general x8, matrix products, pick_rows(): jnp.dot(selector, source, preferred_element_type=jnp.float32)  24 us
    pallas_call x1, Pallas kernels, ffn(): pl.pallas_call(functools.partial(ffn_kernel, count), out_shape=jax.ShapeD...  6.64 us
    all_gather x1, blocking collectives, on_device(): partner_full = lax.all_gather(partner, 'tensor', axis=1, tiled=True)  6.64 us
    all_to_all x1, starting transfers between devices, on_device(): lax.all_to_all(outgoing, 'expert', split_axis=0, concat_axis=0, tiled=True)  6.23 us
    dot_general x4, matrix products, on_device(): jnp.dot(routed_hidden, lax.dynamic_slice(own, (0, (t ^ k) * block), (own....  6.01 us
    dynamic_slice x2, local copies, waits for them, and re-layouts, columns_to_device(): lax.dynamic_slice(own, (0, (t ^ k) * block + off), (own.shape[0], width))  5.33 us
  transfers between devices with their start and end apart: 38, of which 12 were waited for; matrix products, arithmetic and copies ran while one was open for 25% of the time, Pallas kernels for 3%

profile of v10, /device:TPU:0, one launch (start us, length us, event | category | flops | bytes accessed | tf_op | source)
XLA Modules:
  0.0 257.9 jit_solution(3298671054418079643)
XLA Ops:
  7.2 3.0 %collective-permute-start.21 = (s32[512]{0:T(512)}, s32[512]{0:T(512)S(1)}, u32[]{:S(2)}, u32[]{:S(2)}) collective-permute-start(s32[512]{0:T(512)} %bitcast.203), channel_id=1, source_target_pairs={{0,2},{1,3},{2,0},{3,1},{4,6},{5,7},{6,4},{7,5},{8,10},{9,11},{10,... | collective-permute-start | bytes 6152 | tf_op jit(solution)/shard_map/ppermute | solution.py:12
  10.2 2.9 %dynamic-slice_bitcast_fusion.3 = (bf16[512,512]{1,0:T(8,128)(2,1)}, bf16[512,512]{1,0:T(8,128)(2,1)}, bf16[512,512]{1,0:T(8,128)(2,1)}, bf16[512,512]{1,0:T(8,128)(2,1)}) fusion(bf16[1,512,3584]{2,1,0:T(8,128)(2,1)} %param.18, s32[]{:T(128)S(6)} %select_n.781, s32[]{:T(128)S(6)} %select_n.784, s32[]{:T(128)S(6)} %select_n.783, s32[]{:T(128)S(6)} %select_n.782), kind=kLoop, calls=%fused_computation.125 | loop fusion | bytes 4194320 | tf_op jit(solution)/shard_map/dynamic_slice | solution.py:116
  14.5 1.1 convolution_convert_fusion.2
  15.6 6.2 %all-to-all-start = ((bf16[8,40,896]{2,1,0:T(8,128)(2,1)}), bf16[8,40,896]{2,1,0:T(8,128)(2,1)S(1)}, u32[]{:S(2)}, u32[]{:S(2)}) async-start(bf16[8,40,896]{2,1,0:T(8,128)(2,1)} %bitcast.42), calls=%async_computation | async-start | bytes 1146880 | tf_op jit(solution)/shard_map/all_to_all | solution.py:275
  21.9 2.4 dynamic-slice_bitcast_fusion.7
  24.5 0.6 gather_fusion
  25.2 0.7 fusion.69
  33.2 0.6 dynamic_slice.114
  33.8 1.5 collective-permute-start.37
  36.7 1.8 collective-permute-start.25
  38.5 7.5 %collective-permute-done.37 = bf16[512,384]{1,0:T(8,128)(2,1)S(1)} collective-permute-done((bf16[512,384]{1,0:T(8,128)(2,1)}, bf16[512,384]{1,0:T(8,128)(2,1)S(1)}, u32[]{:S(2)}, u32[]{:S(2)}) %collective-permute-start.37) | collective-permute-done | bytes 393248 | tf_op jit(solution)/shard_map/ppermute | solution.py:12
  46.0 7.6 %collective-permute-done.38 = bf16[512,384]{1,0:T(8,128)(2,1)S(1)} collective-permute-done((bf16[512,384]{1,0:T(8,128)(2,1)}, bf16[512,384]{1,0:T(8,128)(2,1)S(1)}, u32[]{:S(2)}, u32[]{:S(2)}) %collective-permute-start.38) | collective-permute-done | bytes 393248 | tf_op jit(solution)/shard_map/ppermute | solution.py:12
  53.6 2.9 %convolution_convert_fusion.9 = bf16[512,384]{0,1:T(8,128)(2,1)} fusion(bf16[512,2048]{1,0:T(8,128)(2,1)S(1)} %fusion.5, bf16[512,384]{1,0:T(8,128)(2,1)S(1)} %collective-permute-done.38, bf16[512,384]{1,0:T(8,128)(2,1)S(1)} %collective-permute-done.37, bf16[512,384]{1,0:T(8,128)(2,1)} %collective-permute-done.36, bf16[512,384]{1,0:T(8,128)(2,1)S(1)} %get-tuple-element.178), kind=kOutput, calls=%fused_computation.69 | convolution fusion | flops 811794432 | bytes 4063232 | tf_op jit(solution)/shard_map/dot_general | solution.py:105
  56.5 1.9 collective-permute-start.39
  58.5 2.9 %convolution_convert_fusion.8 = bf16[512,384]{0,1:T(8,128)(2,1)} fusion(bf16[512,2048]{1,0:T(8,128)(2,1)S(1)} %fusion.6, bf16[512,384]{1,0:T(8,128)(2,1)S(1)} %collective-permute-done.38, bf16[512,384]{1,0:T(8,128)(2,1)S(1)} %collective-permute-done.37, bf16[512,384]{1,0:T(8,128)(2,1)} %collective-permute-done.36, bf16[512,384]{1,0:T(8,128)(2,1)} %copy-done.20), kind=kOutput, calls=%fused_computation.68 | convolution fusion | flops 811794432 | bytes 4063232 | tf_op jit(solution)/shard_map/dot_general | solution.py:105
  61.4 1.5 collective-permute-start.40
  62.8 2.8 %convolution_convert_fusion.7 = bf16[512,384]{0,1:T(8,128)(2,1)} fusion(bf16[512,2048]{1,0:T(8,128)(2,1)S(1)} %fusion.7, bf16[512,384]{1,0:T(8,128)(2,1)S(1)} %collective-permute-done.38, bf16[512,384]{1,0:T(8,128)(2,1)S(1)} %collective-permute-done.37, bf16[512,384]{1,0:T(8,128)(2,1)} %collective-permute-done.36, bf16[512,384]{1,0:T(8,128)(2,1)S(1)} %copy-done.21), kind=kOutput, calls=%fused_computation.67 | convolution fusion | flops 811794432 | bytes 4063232 | tf_op jit(solution)/shard_map/dot_general | solution.py:105
  65.8 3.5 %convolution_convert_fusion.5 = bf16[512,512]{0,1:T(8,128)(2,1)} fusion(bf16[512,2048]{1,0:T(8,128)(2,1)S(1)} %fusion.5, bf16[512,512]{1,0:T(8,128)(2,1)S(1)} %collective-permute-done.25, bf16[512,512]{1,0:T(8,128)(2,1)} %collective-permute-done.24, bf16[512,512]{1,0:T(8,128)(2,1)} %collective-permute-done.23, bf16[512,512]{1,0:T(8,128)(2,1)S(1)} %copy-done.17), kind=kOutput, calls=%fused_computation.64 | convolution fusion | flops 1082392576 | bytes 4718592 | tf_op jit(solution)/shard_map/dot_general | solution.py:105
  69.3 1.9 collective-permute-start.26
  71.2 3.3 %convolution_convert_fusion.4 = bf16[512,512]{0,1:T(8,128)(2,1)} fusion(bf16[512,2048]{1,0:T(8,128)(2,1)S(1)} %fusion.6, bf16[512,512]{1,0:T(8,128)(2,1)S(1)} %collective-permute-done.25, bf16[512,512]{1,0:T(8,128)(2,1)} %collective-permute-done.24, bf16[512,512]{1,0:T(8,128)(2,1)} %collective-permute-done.23, bf16[512,512]{1,0:T(8,128)(2,1)S(1)} %copy-done.17), kind=kOutput, calls=%fused_computation.63 | convolution fusion | flops 1082392576 | bytes 4718592 | tf_op jit(solution)/shard_map/dot_general | solution.py:105
  75.2 2.8 %convolution_convert_fusion.3 = bf16[512,512]{0,1:T(8,128)(2,1)S(1)} fusion(bf16[512,2048]{1,0:T(8,128)(2,1)S(1)} %fusion.7, bf16[512,512]{1,0:T(8,128)(2,1)} %copy-done.27, bf16[512,512]{1,0:T(8,128)(2,1)} %collective-permute-done.24, bf16[512,512]{1,0:T(8,128)(2,1)} %collective-permute-done.23, bf16[512,512]{1,0:T(8,128)(2,1)} %get-tuple-element.174), kind=kOutput, calls=%fused_computation.62 | convolution fusion | flops 1082392576 | bytes 4718592 | tf_op jit(solution)/shard_map/dot_general | solution.py:105
  78.1 1.5 collective-permute-start.27
  80.2 1.5 collective-permute-done.41
  81.7 12.7 %collective-permute-done.15.refs_2_ = bf16[448,896]{1,0:T(8,128)(2,1)S(1)} collective-permute-done((bf16[448,896]{1,0:T(8,128)(2,1)S(1)}, bf16[448,896]{1,0:T(8,128)(2,1)S(1)}, u32[]{:S(2)}, u32[]{:S(2)}) %collective-permute-start.15) | collective-permute-done | bytes 802848 | tf_op jit(solution)/shard_map/ppermute | solution.py:12
  94.4 2.4 fusion.39
  96.9 2.4 collective-permute-start.42
  99.3 10.0 %collective-permute-done.28 = bf16[512,512]{0,1:T(8,128)(2,1)S(1)} collective-permute-done((bf16[512,512]{0,1:T(8,128)(2,1)S(1)}, bf16[512,512]{0,1:T(8,128)(2,1)S(1)}, u32[]{:S(2)}, u32[]{:S(2)}) %collective-permute-start.28) | collective-permute-done | bytes 524320 | tf_op jit(solution)/shard_map/ppermute | solution.py:12
  109.3 3.2 %fusion.21 = (bf16[512,512]{0,1:T(8,128)(2,1)S(1)}, bf16[512,512]{0,1:T(8,128)(2,1)S(1)}) fusion(bf16[512,512]{0,1:T(8,128)(2,1)} %collective-permute-done.26, bf16[512,512]{0,1:T(8,128)(2,1)S(1)} %collective-permute-done.27, bf16[512,512]{0,1:T(8,128)(2,1)S(1)} %collective-permute-done.28, pred[]{:T(512)S(6)} %eq.516, pred[]{:T(512)S(6)} %eq.515, ...), kind=kOutput, calls=%fused_computation.80 | convolution fusion | flops 1085538304 | bytes 6815748 | tf_op jit(solution)/shard_map/dot_general | solution.py:105
  112.6 6.6 %ffn.1 = bf16[448,512]{1,0:T(8,128)(2,1)S(1)} custom-call(s32[1]{0:T(128)} %bitcast.39.where_ref, bf16[448,896]{1,0:T(8,128)(2,1)S(1)} %pad_maximum_fusion.6.refs_0_, bf16[448,896]{1,0:T(8,128)(2,1)S(1)} %collective-permute-done.14.refs_1_, bf16[448,896]{1,0:T(8,128)(2,1)S(1)} %collective-permute-done.15.refs_2_, ...), custom_call_target="tpu_custom_call" | custom-call | flops 3288334336 | bytes 11010048 | tf_op jit(solution)/shard_map/ffn/pallas_call | solution.py:68
  119.4 2.1 fusion.35
  122.1 1.3 convolution_convert_fusion.1
  123.9 20.3 %collective-permute-done.29 = bf16[512,512]{0,1:T(8,128)(2,1)S(1)} collective-permute-done((bf16[512,512]{0,1:T(8,128)(2,1)S(1)}, bf16[512,512]{0,1:T(8,128)(2,1)S(1)}, u32[]{:S(2)}, u32[]{:S(2)}) %collective-permute-start.29) | collective-permute-done | bytes 524320 | tf_op jit(solution)/shard_map/ppermute | solution.py:12
  144.2 2.1 fusion.17
  146.6 1.8 collective-permute-start.32
  148.4 1.3 fusion.10
  150.2 2.7 %collective-permute-done.31 = bf16[128,512]{0,1:T(8,128)(2,1)S(1)} collective-permute-done((bf16[128,512]{0,1:T(8,128)(2,1)S(1)}, bf16[128,512]{0,1:T(8,128)(2,1)S(1)}, u32[]{:S(2)}, u32[]{:S(2)}) %collective-permute-start.31) | collective-permute-done | bytes 131104 | tf_op jit(solution)/shard_map/ppermute | solution.py:12
  152.9 1.8 collective-permute-done.32
  155.2 0.9 pad_maximum_fusion.7
  156.3 13.7 %collective-permute-done.44 = bf16[128,384]{0,1:T(8,128)(2,1)S(1)} collective-permute-done((bf16[128,384]{0,1:T(8,128)(2,1)S(1)}, bf16[128,384]{0,1:T(8,128)(2,1)S(1)}, u32[]{:S(2)}, u32[]{:S(2)}) %collective-permute-start.44) | collective-permute-done | bytes 98336 | tf_op jit(solution)/shard_map/ppermute | solution.py:12
  170.1 1.2 collective-permute-done.45
  171.3 1.3 collective-permute-start.35
  172.6 0.7 fusion.68
  180.7 0.7 dynamic_slice.98
  183.4 0.7 fusion.67
  188.2 0.7 slice.278
  188.9 2.9 %fusion.9 = bf16[320,896]{1,0:T(8,128)(2,1)} fusion(bf16[320,896]{1,0:T(8,128)(2,1)} %collective-permute-done.19, bf16[320,896]{1,0:T(8,128)(2,1)} %collective-permute-done.17, bf16[1,512,3584]{2,1,0:T(8,128)(2,1)} %param.18, s32[]{:T(128)S(6)} %select_n.781, bf16[448,512]{1,0:T(8,128)(2,1)S(1)} %ffn.1), kind=kOutput, calls=%fused_computation.51 | convolution fusion | flops 295034880 | bytes 2965508 | tf_op jit(solution)/shard_map/dot_general | solution.py:282
  191.7 1.0 collective-permute-start.46
  192.7 1.2 collective-permute-start.47
  193.9 4.4 %all-to-all-start.1 = ((bf16[8,40,896]{2,1,0:T(8,128)(2,1)}), bf16[8,40,896]{2,1,0:T(8,128)(2,1)}, u32[]{:S(2)}, u32[]{:S(2)}) async-start(bf16[8,40,896]{2,1,0:T(8,128)(2,1)} %bitcast.48), calls=%async_computation.1 | async-start | bytes 1146880 | tf_op jit(solution)/shard_map/all_to_all | solution.py:290
  198.3 2.0 collective-permute-start.48
  200.7 11.2 %collective-permute-done.46 = bf16[4,128,384]{1,2,0:T(8,128)(2,1)S(1)} collective-permute-done((bf16[4,128,384]{1,2,0:T(8,128)(2,1)S(1)}, bf16[4,128,384]{1,2,0:T(8,128)(2,1)S(1)}, u32[]{:S(2)}, u32[]{:S(2)}) %collective-permute-start.46) | collective-permute-done | bytes 393248 | tf_op jit(solution)/shard_map/ppermute | solution.py:12
  211.9 12.9 %collective-permute-done.47 = bf16[4,128,384]{1,2,0:T(8,128)(2,1)} collective-permute-done((bf16[4,128,384]{1,2,0:T(8,128)(2,1)S(1)}, bf16[4,128,384]{1,2,0:T(8,128)(2,1)}, u32[]{:S(2)}, u32[]{:S(2)}) %collective-permute-start.47) | collective-permute-done | bytes 393248 | tf_op jit(solution)/shard_map/ppermute | solution.py:12
  224.8 1.2 select_select_fusion.23
  226.8 1.8 copy-done.3
  228.8 0.6 copy.107
  229.4 1.3 copy.106
  230.7 2.2 select_select_fusion.13
  232.9 1.3 copy.108
  234.2 0.6 copy.109
  234.8 3.4 %maximum_select_fusion.1 = bf16[512,3584]{1,0:T(8,128)(2,1)} fusion(bf16[512,896]{1,0:T(8,128)(2,1)S(1)} %bitcast.165, bf16[512,896]{1,0:T(8,128)(2,1)} %bitcast.164, bf16[512,896]{1,0:T(8,128)(2,1)S(1)} %bitcast.162, bf16[512,896]{1,0:T(8,128)(2,1)} %bitcast.163, pred[]{:T(512)S(6)} %eq.489), kind=kLoop, calls=%fused_computation.42 | loop fusion | flops 16515072 | bytes 7340033 | tf_op jit(solution)/shard_map/jit(_where)/select_n | solution.py:197
  238.5 0.9 constant_dynamic-slice_fusion.4
  239.4 6.6 %all-gather.1 = bf16[1,128,2048]{2,1,0:T(8,128)(2,1)S(1)} all-gather(bf16[1,128,512]{2,1,0:T(8,128)(2,1)S(1)} %constant_dynamic-slice_fusion.4), channel_id=3, replica_groups=mesh['expert'=8,'tensor'=4] {'tensor'}, dimensions={2}, use_global_device_ids=true | all-gather | bytes 655360 | tf_op jit(solution)/shard_map/all_gather | solution.py:301
  246.0 2.7 %multiply_bitcast_fusion = f32[1,512,2048]{2,1,0:T(8,128)} fusion(bf16[1,128,2048]{2,1,0:T(8,128)(2,1)S(1)} %all-gather.1, bf16[448,512]{1,0:T(8,128)(2,1)S(1)} %ffn.1), kind=kOutput, calls=%fused_computation.36 | convolution fusion | flops 269484032 | bytes 4849664 | tf_op jit(solution)/shard_map/dot_general | solution.py:303
  248.8 2.3 fusion.11
  (143 shorter events, 9.6 us)
Async XLA Ops:
  7.2 7.3 %copy-start = (bf16[128,896]{1,0:T(8,128)(2,1)S(1)}, bf16[128,896]{1,0:T(8,128)(2,1)}, u32[]{:S(2)}) copy-start(bf16[128,896]{1,0:T(8,128)(2,1)} %param.12) | copy-start | bytes 688132
  7.2 6.6 %copy-start.24 = (s32[128,2]{0,1:T(2,128)S(1)}, s32[128,2]{0,1:T(2,128)}, u32[]{:S(2)}) copy-start(s32[128,2]{0,1:T(2,128)} %param.13) | copy-start | bytes 3076
  7.2 19.2 %collective-permute-start.21 = (s32[512]{0:T(512)}, s32[512]{0:T(512)S(1)}, u32[]{:S(2)}, u32[]{:S(2)}) collective-permute-start(s32[512]{0:T(512)} %bitcast.203), channel_id=1, source_target_pairs={{0,2},{1,3},{2,0},{3,1},{4,6},{5,7},{6,4},{7,5},{8,10},{9,11},{10,... | collective-permute-start | bytes 6152 | tf_op jit(solution)/shard_map/ppermute | solution.py:12
  10.2 23.6 %collective-permute-start.20 = (s32[512]{0:T(512)}, s32[512]{0:T(512)S(1)}, u32[]{:S(2)}, u32[]{:S(2)}) collective-permute-start(s32[512]{0:T(512)} %bitcast.204), channel_id=1, source_target_pairs={{0,1},{1,0},{2,3},{3,2},{4,5},{5,4},{6,7},{7,6},{8,9},{9,8},{10,11... | collective-permute-start | bytes 6152 | tf_op jit(solution)/shard_map/ppermute | solution.py:12
  13.1 11.2 %copy-start.26 = (s32[2]{0:T(128)S(1)}, s32[2]{0:T(128)}, u32[]{:S(2)}) copy-start(s32[2]{0:T(128)} %param.21) | copy-start | bytes 28
  13.1 11.3 %copy-start.2 = (s32[8]{0:T(128)S(1)}, s32[8]{0:T(128)}, u32[]{:S(2)}) copy-start(s32[8]{0:T(128)} %param.20) | copy-start | bytes 100
  13.1 22.2 %copy-start.25 = (s32[1,512]{1,0:T(1,128)S(1)}, s32[1,512]{1,0:T(1,128)}, u32[]{:S(2)}) copy-start(s32[1,512]{1,0:T(1,128)} %param.19) | copy-start | bytes 6148
  13.1 52.5 %collective-permute-start.23 = (bf16[512,512]{1,0:T(8,128)(2,1)}, bf16[512,512]{1,0:T(8,128)(2,1)}, u32[]{:S(2)}, u32[]{:S(2)}) collective-permute-start(bf16[512,512]{1,0:T(8,128)(2,1)} %get-tuple-element.177), channel_id=1, source_target_pairs={{0,1},{1,0},{2,3},{3,2},{4,5},{5,4},{6,7},{7,6},{8,9},{9,8},{10,11... | collective-permute-start | bytes 1572872 | tf_op jit(solution)/shard_map/ppermute | solution.py:12
  13.7 52.1 %collective-permute-start.24 = (bf16[512,512]{1,0:T(8,128)(2,1)}, bf16[512,512]{1,0:T(8,128)(2,1)}, u32[]{:S(2)}, u32[]{:S(2)}) collective-permute-start(bf16[512,512]{1,0:T(8,128)(2,1)} %get-tuple-element.176), channel_id=1, source_target_pairs={{0,2},{1,3},{2,0},{3,1},{4,6},{5,7},{6,4},{7,5},{8,10},{9,11},{10,... | collective-permute-start | bytes 1572872 | tf_op jit(solution)/shard_map/ppermute | solution.py:12
  15.6 58.9 %all-to-all-start = ((bf16[8,40,896]{2,1,0:T(8,128)(2,1)}), bf16[8,40,896]{2,1,0:T(8,128)(2,1)S(1)}, u32[]{:S(2)}, u32[]{:S(2)}) async-start(bf16[8,40,896]{2,1,0:T(8,128)(2,1)} %bitcast.42), calls=%async_computation | async-start | bytes 1146880 | tf_op jit(solution)/shard_map/all_to_all | solution.py:275
  21.8 216.6 %all-gather.4.cloned.1.call-start = ((), (), s32[]{:S(2)}) async-start(), calls=%async_computation.2 | async-start | bytes 1179648 | tf_op jit(solution)/shard_map/all_gather | solution.py:299
  24.3 29.3 %copy-start.20 = (bf16[512,384]{1,0:T(8,128)(2,1)}, bf16[512,384]{1,0:T(8,128)(2,1)S(1)}, u32[]{:S(2)}) copy-start(bf16[512,384]{1,0:T(8,128)(2,1)S(1)} %get-tuple-element.178) | copy-start | bytes 1179652
  24.3 12.3 %collective-permute-start.36 = (bf16[512,384]{1,0:T(8,128)(2,1)}, bf16[512,384]{1,0:T(8,128)(2,1)}, u32[]{:S(2)}, u32[]{:S(2)}) collective-permute-start(bf16[512,384]{1,0:T(8,128)(2,1)} %get-tuple-element.179), channel_id=1, source_target_pairs={{0,1},{1,0},{2,3},{3,2},{4,5},{5,4},{6,7},{7,6},{8,9},{9,8},{10,11... | collective-permute-start | bytes 1179656 | tf_op jit(solution)/shard_map/ppermute | solution.py:12
  26.4 8.9 %collective-permute-start.22 = (s32[512]{0:T(512)S(1)}, s32[512]{0:T(512)S(1)}, u32[]{:S(2)}, u32[]{:S(2)}) collective-permute-start(s32[512]{0:T(512)S(1)} %collective-permute-done.21), channel_id=1, source_target_pairs={{0,1},{1,0},{2,3},{3,2},{4,5},{5,4},{6,7},{7,6},{8,9},{9,8},{10,11... | collective-permute-start | bytes 6152 | tf_op jit(solution)/shard_map/ppermute | solution.py:12
  33.8 12.2 %collective-permute-start.37 = (bf16[512,384]{1,0:T(8,128)(2,1)}, bf16[512,384]{1,0:T(8,128)(2,1)S(1)}, u32[]{:S(2)}, u32[]{:S(2)}) collective-permute-start(bf16[512,384]{1,0:T(8,128)(2,1)} %get-tuple-element.181), channel_id=1, source_target_pairs={{0,2},{1,3},{2,0},{3,1},{4,6},{5,7},{6,4},{7,5},{8,10},{9,11},{10,... | collective-permute-start | bytes 1179656 | tf_op jit(solution)/shard_map/ppermute | solution.py:12
  35.3 18.2 %collective-permute-start.38 = (bf16[512,384]{1,0:T(8,128)(2,1)}, bf16[512,384]{1,0:T(8,128)(2,1)S(1)}, u32[]{:S(2)}, u32[]{:S(2)}) collective-permute-start(bf16[512,384]{1,0:T(8,128)(2,1)} %get-tuple-element.180), channel_id=1, source_target_pairs={{0,3},{1,2},{2,1},{3,0},{4,7},{5,6},{6,5},{7,4},{8,11},{9,10},{10,... | collective-permute-start | bytes 1179656 | tf_op jit(solution)/shard_map/ppermute | solution.py:12
  36.7 29.1 %collective-permute-start.25 = (bf16[512,512]{1,0:T(8,128)(2,1)S(1)}, bf16[512,512]{1,0:T(8,128)(2,1)S(1)}, u32[]{:S(2)}, u32[]{:S(2)}) collective-permute-start(bf16[512,512]{1,0:T(8,128)(2,1)S(1)} %copy-done.19), channel_id=1, source_target_pairs={{0,3},{1,2},{2,1},{3,0},{4,7},{5,6},{6,5},{7,4},{8,11},{9,10},{10,... | collective-permute-start | bytes 1572872 | tf_op jit(solution)/shard_map/ppermute | solution.py:12
  46.0 16.8 %copy-start.30 = (bf16[512,384]{1,0:T(8,128)(2,1)}, bf16[512,384]{1,0:T(8,128)(2,1)S(1)}, u32[]{:S(2)}) copy-start(bf16[512,384]{1,0:T(8,128)(2,1)S(1)} %collective-permute-done.37) | copy-start | bytes 1179652
  53.6 9.2 %copy-start.32 = (bf16[512,384]{1,0:T(8,128)(2,1)}, bf16[512,384]{1,0:T(8,128)(2,1)S(1)}, u32[]{:S(2)}) copy-start(bf16[512,384]{1,0:T(8,128)(2,1)S(1)} %collective-permute-done.38) | copy-start | bytes 1179652
  56.5 6.3 %copy-start.21 = (bf16[512,384]{1,0:T(8,128)(2,1)S(1)}, bf16[512,384]{1,0:T(8,128)(2,1)}, u32[]{:S(2)}) copy-start(bf16[512,384]{1,0:T(8,128)(2,1)} %copy-done.20) | copy-start | bytes 1179652
  56.5 21.5 %collective-permute-start.39 = (bf16[512,384]{0,1:T(8,128)(2,1)}, bf16[512,384]{0,1:T(8,128)(2,1)S(1)}, u32[]{:S(2)}, u32[]{:S(2)}) collective-permute-start(bf16[512,384]{0,1:T(8,128)(2,1)} %convolution_convert_fusion.9), channel_id=1, source_target_pairs={{0,4},{4,0},{8,12},{12,8},{16,20},{20,16},{24,28},{28,24},{1,5},{5... | collective-permute-start | bytes 1179656 | tf_op jit(solution)/shard_map/ppermute | solution.py:12
  61.4 4.5 %copy-start.17 = (bf16[512,512]{1,0:T(8,128)(2,1)S(1)}, bf16[512,512]{1,0:T(8,128)(2,1)}, u32[]{:S(2)}) copy-start(bf16[512,512]{1,0:T(8,128)(2,1)} %get-tuple-element.174) | copy-start | bytes 1572868
  61.4 18.3 %collective-permute-start.40 = (bf16[512,384]{0,1:T(8,128)(2,1)}, bf16[512,384]{0,1:T(8,128)(2,1)}, u32[]{:S(2)}, u32[]{:S(2)}) collective-permute-start(bf16[512,384]{0,1:T(8,128)(2,1)} %convolution_convert_fusion.8), channel_id=1, source_target_pairs={{0,8},{4,12},{8,0},{12,4},{16,24},{20,28},{24,16},{28,20},{1,9},{5... | collective-permute-start | bytes 1179656 | tf_op jit(solution)/shard_map/ppermute | solution.py:12
  65.7 16.0 %collective-permute-start.41 = (bf16[512,384]{0,1:T(8,128)(2,1)}, bf16[512,384]{0,1:T(8,128)(2,1)}, u32[]{:S(2)}, u32[]{:S(2)}) collective-permute-start(bf16[512,384]{0,1:T(8,128)(2,1)} %convolution_convert_fusion.7), channel_id=1, source_target_pairs={{0,12},{4,8},{8,4},{12,0},{16,28},{20,24},{24,20},{28,16},{1,13},{... | collective-permute-start | bytes 1179656 | tf_op jit(solution)/shard_map/ppermute | solution.py:12
  65.8 5.4 %copy-start.27 = (bf16[512,512]{1,0:T(8,128)(2,1)}, bf16[512,512]{1,0:T(8,128)(2,1)S(1)}, u32[]{:S(2)}) copy-start(bf16[512,512]{1,0:T(8,128)(2,1)S(1)} %collective-permute-done.25) | copy-start | bytes 1572868
  69.3 5.2 %copy-start.23 = (bf16[128,896]{1,0:T(8,128)(2,1)S(1)}, bf16[128,896]{1,0:T(8,128)(2,1)}, u32[]{:S(2)}) copy-start(bf16[128,896]{1,0:T(8,128)(2,1)} %param.15) | copy-start | bytes 688132
  69.3 27.5 %collective-permute-start.26 = (bf16[512,512]{0,1:T(8,128)(2,1)}, bf16[512,512]{0,1:T(8,128)(2,1)}, u32[]{:S(2)}, u32[]{:S(2)}) collective-permute-start(bf16[512,512]{0,1:T(8,128)(2,1)} %convolution_convert_fusion.5), channel_id=1, source_target_pairs={{0,4},{4,0},{8,12},{12,8},{16,20},{20,16},{24,28},{28,24},{1,5},{5... | collective-permute-start | bytes 1572872 | tf_op jit(solution)/shard_map/ppermute | solution.py:12
  74.6 19.8 %copy-start.22 = (bf16[512,384]{1,0:T(8,128)(2,1)S(1)}, bf16[512,384]{1,0:T(8,128)(2,1)}, u32[]{:S(2)}) copy-start(bf16[512,384]{1,0:T(8,128)(2,1)} %copy-done.20) | copy-start | bytes 1179652
  74.6 19.8 %copy-start.31 = (bf16[512,384]{1,0:T(8,128)(2,1)S(1)}, bf16[512,384]{1,0:T(8,128)(2,1)}, u32[]{:S(2)}) copy-start(bf16[512,384]{1,0:T(8,128)(2,1)} %copy-done.30) | copy-start | bytes 1179652
  74.7 19.8 %copy-start.33 = (bf16[512,384]{1,0:T(8,128)(2,1)S(1)}, bf16[512,384]{1,0:T(8,128)(2,1)}, u32[]{:S(2)}) copy-start(bf16[512,384]{1,0:T(8,128)(2,1)} %copy-done.32) | copy-start | bytes 1179652
  74.7 19.7 %collective-permute-start.15 = (bf16[448,896]{1,0:T(8,128)(2,1)S(1)}, bf16[448,896]{1,0:T(8,128)(2,1)S(1)}, u32[]{:S(2)}, u32[]{:S(2)}) collective-permute-start(bf16[448,896]{1,0:T(8,128)(2,1)S(1)} %pad_maximum_fusion.6.refs_0_), channel_id=1, source_target_pairs={{0,2},{1,3},{2,0},{3,1},{4,6},{5,7},{6,4},{7,5},{8,10},{9,11},{10,... | collective-permute-start | bytes 2408456 | tf_op jit(solution)/shard_map/ppermute | solution.py:12
  78.1 18.7 %copy-start.12 = (bf16[512,384]{0,1:T(8,128)(2,1)}, bf16[512,384]{0,1:T(8,128)(2,1)S(1)}, u32[]{:S(2)}) copy-start(bf16[512,384]{0,1:T(8,128)(2,1)S(1)} %collective-permute-done.39) | copy-start | bytes 1179652
  78.1 21.2 %collective-permute-start.27 = (bf16[512,512]{0,1:T(8,128)(2,1)S(1)}, bf16[512,512]{0,1:T(8,128)(2,1)S(1)}, u32[]{:S(2)}, u32[]{:S(2)}) collective-permute-start(bf16[512,512]{0,1:T(8,128)(2,1)S(1)} %copy-done.29), channel_id=1, source_target_pairs={{0,8},{4,12},{8,0},{12,4},{16,24},{20,28},{24,16},{28,20},{1,9},{5... | collective-permute-start | bytes 1572872 | tf_op jit(solution)/shard_map/ppermute | solution.py:12
  79.6 29.7 %collective-permute-start.28 = (bf16[512,512]{0,1:T(8,128)(2,1)S(1)}, bf16[512,512]{0,1:T(8,128)(2,1)S(1)}, u32[]{:S(2)}, u32[]{:S(2)}) collective-permute-start(bf16[512,512]{0,1:T(8,128)(2,1)S(1)} %convolution_convert_fusion.3), channel_id=1, source_target_pairs={{0,12},{4,8},{8,4},{12,0},{16,28},{20,24},{24,20},{28,16},{1,13},{... | collective-permute-start | bytes 1572872 | tf_op jit(solution)/shard_map/ppermute | solution.py:12
  80.2 29.1 %copy-start.18 = (bf16[512,512]{1,0:T(8,128)(2,1)S(1)}, bf16[512,512]{1,0:T(8,128)(2,1)}, u32[]{:S(2)}) copy-start(bf16[512,512]{1,0:T(8,128)(2,1)} %get-tuple-element.174) | copy-start | bytes 1572868
  80.2 29.1 %copy-start.28 = (bf16[512,512]{1,0:T(8,128)(2,1)S(1)}, bf16[512,512]{1,0:T(8,128)(2,1)}, u32[]{:S(2)}) copy-start(bf16[512,512]{1,0:T(8,128)(2,1)} %copy-done.27) | copy-start | bytes 1572868
  81.7 30.9 %collective-permute-start.14 = (bf16[448,896]{1,0:T(8,128)(2,1)S(1)}, bf16[448,896]{1,0:T(8,128)(2,1)S(1)}, u32[]{:S(2)}, u32[]{:S(2)}) collective-permute-start(bf16[448,896]{1,0:T(8,128)(2,1)S(1)} %pad_maximum_fusion.6.refs_0_), channel_id=1, source_target_pairs={{0,1},{1,0},{2,3},{3,2},{4,5},{5,4},{6,7},{7,6},{8,9},{9,8},{10,11... | collective-permute-start | bytes 2408456 | tf_op jit(solution)/shard_map/ppermute | solution.py:12
  94.4 18.2 %collective-permute-start.16 = (bf16[448,896]{1,0:T(8,128)(2,1)S(1)}, bf16[448,896]{1,0:T(8,128)(2,1)S(1)}, u32[]{:S(2)}, u32[]{:S(2)}) collective-permute-start(bf16[448,896]{1,0:T(8,128)(2,1)S(1)} %collective-permute-done.15.refs_2_), channel_id=1, source_target_pairs={{0,1},{1,0},{2,3},{3,2},{4,5},{5,4},{6,7},{7,6},{8,9},{9,8},{10,11... | collective-permute-start | bytes 2408456 | tf_op jit(solution)/shard_map/ppermute | solution.py:12
  96.8 22.5 %copy-start.15 = (bf16[512,384]{0,1:T(8,128)(2,1)}, bf16[512,384]{0,1:T(8,128)(2,1)S(1)}, u32[]{:S(2)}) copy-start(bf16[512,384]{0,1:T(8,128)(2,1)S(1)} %get-tuple-element.236) | copy-start | bytes 1179652
  96.9 22.5 %collective-permute-start.42 = (bf16[512,384]{0,1:T(8,128)(2,1)S(1)}, bf16[512,384]{0,1:T(8,128)(2,1)S(1)}, u32[]{:S(2)}, u32[]{:S(2)}) collective-permute-start(bf16[512,384]{0,1:T(8,128)(2,1)S(1)} %get-tuple-element.216), channel_id=1, source_target_pairs={{0,16},{4,20},{8,24},{12,28},{16,0},{20,4},{24,8},{28,12},{1,17},{... | collective-permute-start | bytes 1179656 | tf_op jit(solution)/shard_map/ppermute | solution.py:12
  99.3 44.9 %copy-start.8 = (bf16[512,512]{0,1:T(8,128)(2,1)}, bf16[512,512]{0,1:T(8,128)(2,1)S(1)}, u32[]{:S(2)}) copy-start(bf16[512,512]{0,1:T(8,128)(2,1)S(1)} %collective-permute-done.27) | copy-start | bytes 1572868
  109.3 34.9 %copy-start.10 = (bf16[512,512]{0,1:T(8,128)(2,1)}, bf16[512,512]{0,1:T(8,128)(2,1)S(1)}, u32[]{:S(2)}) copy-start(bf16[512,512]{0,1:T(8,128)(2,1)S(1)} %collective-permute-done.28) | copy-start | bytes 1572868
  112.6 31.6 %copy-start.11 = (bf16[512,512]{0,1:T(8,128)(2,1)}, bf16[512,512]{0,1:T(8,128)(2,1)S(1)}, u32[]{:S(2)}) copy-start(bf16[512,512]{0,1:T(8,128)(2,1)S(1)} %get-tuple-element.231) | copy-start | bytes 1572868
  112.6 6.8 %copy-start.13 = (bf16[512,384]{0,1:T(8,128)(2,1)S(1)}, bf16[512,384]{0,1:T(8,128)(2,1)}, u32[]{:S(2)}) copy-start(bf16[512,384]{0,1:T(8,128)(2,1)} %copy-done.12) | copy-start | bytes 1179652
  112.6 8.8 %copy-start.4 = (bf16[1,512,3584]{2,1,0:T(8,128)(2,1)S(1)}, bf16[1,512,3584]{2,1,0:T(8,128)(2,1)}, u32[]{:S(2)}) copy-start(bf16[1,512,3584]{2,1,0:T(8,128)(2,1)} %param.18) | copy-start | bytes 11010052
  119.3 24.9 %collective-permute-start.29 = (bf16[512,512]{0,1:T(8,128)(2,1)S(1)}, bf16[512,512]{0,1:T(8,128)(2,1)S(1)}, u32[]{:S(2)}, u32[]{:S(2)}) collective-permute-start(bf16[512,512]{0,1:T(8,128)(2,1)S(1)} %get-tuple-element.60), channel_id=1, source_target_pairs={{0,16},{4,20},{8,24},{12,28},{16,0},{20,4},{24,8},{28,12},{1,17},{... | collective-permute-start | bytes 1572872 | tf_op jit(solution)/shard_map/ppermute | solution.py:12
  122.0 26.4 %collective-permute-start.18 = (bf16[320,896]{1,0:T(8,128)(2,1)S(1)}, bf16[320,896]{1,0:T(8,128)(2,1)S(1)}, u32[]{:S(2)}, u32[]{:S(2)}) collective-permute-start(bf16[320,896]{1,0:T(8,128)(2,1)S(1)} %convolution_convert_fusion), channel_id=1, source_target_pairs={{0,1},{1,0},{2,3},{3,2},{4,5},{5,4},{6,7},{7,6},{8,9},{9,8},{10,11... | collective-permute-start | bytes 1720328 | tf_op jit(solution)/shard_map/ppermute | solution.py:12
  123.4 65.4 %collective-permute-start.17 = (bf16[320,896]{1,0:T(8,128)(2,1)}, bf16[320,896]{1,0:T(8,128)(2,1)}, u32[]{:S(2)}, u32[]{:S(2)}) collective-permute-start(bf16[320,896]{1,0:T(8,128)(2,1)} %convolution_convert_fusion.1), channel_id=1, source_target_pairs={{0,1},{1,0},{2,3},{3,2},{4,5},{5,4},{6,7},{7,6},{8,9},{9,8},{10,11... | collective-permute-start | bytes 1720328 | tf_op jit(solution)/shard_map/ppermute | solution.py:12
  146.4 3.6 %collective-permute-start.30 = (bf16[128,512]{0,1:T(8,128)(2,1)S(1)}, bf16[128,512]{0,1:T(8,128)(2,1)S(1)}, u32[]{:S(2)}, u32[]{:S(2)}) collective-permute-start(bf16[128,512]{0,1:T(8,128)(2,1)S(1)} %get-tuple-element.193), channel_id=1, source_target_pairs={{0,1},{1,0},{2,3},{3,2},{4,5},{5,4},{6,7},{7,6},{8,9},{9,8},{10,11... | collective-permute-start | bytes 393224 | tf_op jit(solution)/shard_map/ppermute | solution.py:12
  146.5 6.3 %collective-permute-start.31 = (bf16[128,512]{0,1:T(8,128)(2,1)S(1)}, bf16[128,512]{0,1:T(8,128)(2,1)S(1)}, u32[]{:S(2)}, u32[]{:S(2)}) collective-permute-start(bf16[128,512]{0,1:T(8,128)(2,1)S(1)} %get-tuple-element.192), channel_id=1, source_target_pairs={{0,2},{1,3},{2,0},{3,1},{4,6},{5,7},{6,4},{7,5},{8,10},{9,11},{10,... | collective-permute-start | bytes 393224 | tf_op jit(solution)/shard_map/ppermute | solution.py:12
  146.6 8.2 %collective-permute-start.32 = (bf16[128,512]{0,1:T(8,128)(2,1)S(1)}, bf16[128,512]{0,1:T(8,128)(2,1)S(1)}, u32[]{:S(2)}, u32[]{:S(2)}) collective-permute-start(bf16[128,512]{0,1:T(8,128)(2,1)S(1)} %get-tuple-element.191), channel_id=1, source_target_pairs={{0,3},{1,2},{2,1},{3,0},{4,7},{5,6},{6,5},{7,4},{8,11},{9,10},{10,... | collective-permute-start | bytes 393224 | tf_op jit(solution)/shard_map/ppermute | solution.py:12
  149.7 39.2 %collective-permute-start.19 = (bf16[320,896]{1,0:T(8,128)(2,1)}, bf16[320,896]{1,0:T(8,128)(2,1)}, u32[]{:S(2)}, u32[]{:S(2)}) collective-permute-start(bf16[320,896]{1,0:T(8,128)(2,1)} %fusion.10), channel_id=1, source_target_pairs={{0,2},{1,3},{2,0},{3,1},{4,6},{5,7},{6,4},{7,5},{8,10},{9,11},{10,... | collective-permute-start | bytes 1720328 | tf_op jit(solution)/shard_map/ppermute | solution.py:12
  150.1 6.0 %collective-permute-start.43 = (bf16[128,384]{0,1:T(8,128)(2,1)S(1)}, bf16[128,384]{0,1:T(8,128)(2,1)S(1)}, u32[]{:S(2)}, u32[]{:S(2)}) collective-permute-start(bf16[128,384]{0,1:T(8,128)(2,1)S(1)} %get-tuple-element.197), channel_id=1, source_target_pairs={{0,1},{1,0},{2,3},{3,2},{4,5},{5,4},{6,7},{7,6},{8,9},{9,8},{10,11... | collective-permute-start | bytes 294920 | tf_op jit(solution)/shard_map/ppermute | solution.py:12
  152.9 17.2 %collective-permute-start.44 = (bf16[128,384]{0,1:T(8,128)(2,1)S(1)}, bf16[128,384]{0,1:T(8,128)(2,1)S(1)}, u32[]{:S(2)}, u32[]{:S(2)}) collective-permute-start(bf16[128,384]{0,1:T(8,128)(2,1)S(1)} %get-tuple-element.196), channel_id=1, source_target_pairs={{0,2},{1,3},{2,0},{3,1},{4,6},{5,7},{6,4},{7,5},{8,10},{9,11},{10,... | collective-permute-start | bytes 294920 | tf_op jit(solution)/shard_map/ppermute | solution.py:12
  154.8 16.5 %collective-permute-start.45 = (bf16[128,384]{0,1:T(8,128)(2,1)S(1)}, bf16[128,384]{0,1:T(8,128)(2,1)S(1)}, u32[]{:S(2)}, u32[]{:S(2)}) collective-permute-start(bf16[128,384]{0,1:T(8,128)(2,1)S(1)} %get-tuple-element.195), channel_id=1, source_target_pairs={{0,3},{1,2},{2,1},{3,0},{4,7},{5,6},{6,5},{7,4},{8,11},{9,10},{10,... | collective-permute-start | bytes 294920 | tf_op jit(solution)/shard_map/ppermute | solution.py:12
  156.1 42.2 %collective-permute-start.33 = (bf16[4,128,512]{1,2,0:T(8,128)(2,1)}, bf16[4,128,512]{1,2,0:T(8,128)(2,1)S(1)}, u32[]{:S(2)}, u32[]{:S(2)}) collective-permute-start(bf16[4,128,512]{1,2,0:T(8,128)(2,1)} %pad_maximum_fusion.7), channel_id=1, source_target_pairs={{0,12},{4,8},{8,4},{12,0},{16,28},{20,24},{24,20},{28,16},{1,13},{... | collective-permute-start | bytes 1572872 | tf_op jit(solution)/shard_map/ppermute | solution.py:12
  170.1 30.2 %collective-permute-start.34 = (bf16[4,128,512]{1,2,0:T(8,128)(2,1)}, bf16[4,128,512]{1,2,0:T(8,128)(2,1)S(1)}, u32[]{:S(2)}, u32[]{:S(2)}) collective-permute-start(bf16[4,128,512]{1,2,0:T(8,128)(2,1)} %pad_maximum_fusion.7), channel_id=1, source_target_pairs={{0,8},{4,12},{8,0},{12,4},{16,24},{20,28},{24,16},{28,20},{1,9},{5... | collective-permute-start | bytes 1572872 | tf_op jit(solution)/shard_map/ppermute | solution.py:12
  171.3 29.0 %collective-permute-start.35 = (bf16[4,128,512]{1,2,0:T(8,128)(2,1)}, bf16[4,128,512]{1,2,0:T(8,128)(2,1)S(1)}, u32[]{:S(2)}, u32[]{:S(2)}) collective-permute-start(bf16[4,128,512]{1,2,0:T(8,128)(2,1)} %pad_maximum_fusion.7), channel_id=1, source_target_pairs={{0,4},{4,0},{8,12},{12,8},{16,20},{20,16},{24,28},{28,24},{1,5},{5... | collective-permute-start | bytes 1572872 | tf_op jit(solution)/shard_map/ppermute | solution.py:12
  191.7 20.2 %collective-permute-start.46 = (bf16[4,128,384]{1,2,0:T(8,128)(2,1)S(1)}, bf16[4,128,384]{1,2,0:T(8,128)(2,1)S(1)}, u32[]{:S(2)}, u32[]{:S(2)}) collective-permute-start(bf16[4,128,384]{1,2,0:T(8,128)(2,1)S(1)} %pad_maximum_fusion.8), channel_id=1, source_target_pairs={{0,12},{4,8},{8,4},{12,0},{16,28},{20,24},{24,20},{28,16},{1,13},{... | collective-permute-start | bytes 1179656 | tf_op jit(solution)/shard_map/ppermute | solution.py:12
  192.7 32.1 %collective-permute-start.47 = (bf16[4,128,384]{1,2,0:T(8,128)(2,1)S(1)}, bf16[4,128,384]{1,2,0:T(8,128)(2,1)}, u32[]{:S(2)}, u32[]{:S(2)}) collective-permute-start(bf16[4,128,384]{1,2,0:T(8,128)(2,1)S(1)} %pad_maximum_fusion.8), channel_id=1, source_target_pairs={{0,8},{4,12},{8,0},{12,4},{16,24},{20,28},{24,16},{28,20},{1,9},{5... | collective-permute-start | bytes 1179656 | tf_op jit(solution)/shard_map/ppermute | solution.py:12
  193.9 54.9 %all-to-all-start.1 = ((bf16[8,40,896]{2,1,0:T(8,128)(2,1)}), bf16[8,40,896]{2,1,0:T(8,128)(2,1)}, u32[]{:S(2)}, u32[]{:S(2)}) async-start(bf16[8,40,896]{2,1,0:T(8,128)(2,1)} %bitcast.48), calls=%async_computation.1 | async-start | bytes 1146880 | tf_op jit(solution)/shard_map/all_to_all | solution.py:290
  198.3 26.5 %collective-permute-start.48 = (bf16[4,128,384]{1,2,0:T(8,128)(2,1)S(1)}, bf16[4,128,384]{1,2,0:T(8,128)(2,1)S(1)}, u32[]{:S(2)}, u32[]{:S(2)}) collective-permute-start(bf16[4,128,384]{1,2,0:T(8,128)(2,1)S(1)} %pad_maximum_fusion.8), channel_id=1, source_target_pairs={{0,4},{4,0},{8,12},{12,8},{16,20},{20,16},{24,28},{28,24},{1,5},{5... | collective-permute-start | bytes 1179656 | tf_op jit(solution)/shard_map/ppermute | solution.py:12
  238.4 10.4 %copy-start.34 = (f32[128,2]{0,1:T(2,128)S(1)}, f32[128,2]{0,1:T(2,128)}, u32[]{:S(2)}) copy-start(f32[128,2]{0,1:T(2,128)} %param.14) | copy-start | bytes 3076
  239.4 11.7 %copy-start.1 = (bf16[128,896]{1,0:T(8,128)(2,1)S(1)}, bf16[128,896]{1,0:T(8,128)(2,1)}, u32[]{:S(2)}) copy-start(bf16[128,896]{1,0:T(8,128)(2,1)} %param.12) | copy-start | bytes 688132
  (5 other events, 13.3 us)
Sparse Core Ops, SparseCore 0:
  189.0 45.0 all-gather.3
